TPU v7x, 32 devices: a whole 2x2x4 slice. The times are simulated.
32 devices in a mesh: dp: 8 (over z, y), fsdp: 4 (over x, core).
Axes of the slice: x: 2, y: 2, z: 4, core: 2. Of those that a mesh axis runs over, the one named last changes fastest.
Arguments:
- tokens: bfloat16 [8192, 960], P(('dp', 'fsdp')), may hold values from -6 to 6
- cotangent: bfloat16 [8192, 960], P(('dp', 'fsdp')), may hold values from -6 to 6
- sequence_ids: int32 [32], P('dp'), may hold values from 0 to 31, as said below
- span_position: int32 [32], P('dp'), may hold values from 0 to 3, as said below
- attention_norm: bfloat16 [960], P('fsdp'), may hold values from 0.5 to 1.5
- query_weight: bfloat16 [960, 960], P('fsdp'), may hold values from -0.1875 to 0.1875
- key_matrix: bfloat16 [960, 320], P('fsdp'), may hold values from -0.1875 to 0.1875
- value_matrix: bfloat16 [960, 320], P('fsdp'), may hold values from -0.1875 to 0.1875
- output_weight: bfloat16 [960, 960], P('fsdp'), may hold values from -0.5 to 0.5
- feedforward_norm: bfloat16 [960], P('fsdp'), may hold values from 0.5 to 1.5
- gate_weight: bfloat16 [960, 2560], P('fsdp'), may hold values from -0.1875 to 0.1875
- up_weight: bfloat16 [960, 2560], P('fsdp'), may hold values from -0.1875 to 0.1875
- down_weight: bfloat16 [2560, 960], P('fsdp'), may hold values from -0.125 to 0.125
Outputs:
- activations: bfloat16 [8192, 960], P(('dp', 'fsdp'))
- input_grad: bfloat16 [8192, 960], P(('dp', 'fsdp'))
- attention_norm_grad: float32 [960], P('fsdp')
- query_grad: float32 [960, 960], P('fsdp')
- key_grad: float32 [960, 320], P('fsdp')
- value_grad: float32 [960, 320], P('fsdp')
- output_grad: float32 [960, 960], P('fsdp')
- feedforward_norm_grad: float32 [960], P('fsdp')
- gate_grad: float32 [960, 2560], P('fsdp')
- up_grad: float32 [960, 2560], P('fsdp')
- down_grad: float32 [2560, 960], P('fsdp')
Inputs may be any that keep to these rules, and one draw needn't show every extreme that they name: `sequence_ids`: spans with equal ids lie in one group of 4 consecutive spans (one index of dp). A group holds either one sequence of 4 spans or 4 sequences of one span each; every draw has a group with one sequence of 4 spans. `span_position`: within a sequence the spans carry the places 0 to its number of spans - 1, each once, in any order over its group; a sequence of one span has place 0.
All inputs are finite; a program needn't handle non-finite values.
Results may differ from a plain program's by a relative error of at most 0.024.
Values may be sent and summed in bfloat16 or wider, within the bound.
No kernel may reach another device: no remote copies, remote signals or barrier semaphores. Data moves between devices by JAX's collectives and lax.ppermute only.
A program may use at most 192 MiB of HBM per device.

v0:
```python
import jax
import jax.numpy as jnp
from jax import lax
from jax.sharding import PartitionSpec as P

QUERY_HEADS = 15
KEY_VALUE_HEADS = 5
HEAD_SIZE = 64


epsilon = 1e-05
rope_base = 10000.0
masked = -1e30


def as_sent(value):

    def short(part):
        return part.astype(jnp.bfloat16) if part.dtype == jnp.float32 else part

    return jax.tree.map(short, value)


def matrix_product(left_side, right_side):
    return jnp.dot(left_side, right_side, preferred_element_type=jnp.float32)


def first_trans(left_side, right_side):
    return lax.dot_general(
        left_side, right_side, (((0,), (0,)), ((), ())), preferred_element_type=jnp.float32
    )


def second_trans(left_side, right_side):
    return lax.dot_general(
        left_side, right_side, (((1,), (1,)), ((), ())), preferred_element_type=jnp.float32
    )


def rotation(token_positions, half_dim):
    frequency = rope_base ** (-jnp.arange(half_dim, dtype=jnp.float32) / half_dim)
    angles = token_positions.astype(jnp.float32)[:, None] * frequency[None, :]
    return (jnp.cos(angles)[:, None, :], jnp.sin(angles)[:, None, :])


def apply_rotation(vector, cosine_table, sine_table):
    half_dim = vector.shape[-1] // 2
    first_half = vector[..., :half_dim]
    second = vector[..., half_dim:]
    return jnp.concatenate(
        [
            first_half * cosine_table - second * sine_table,
            second * cosine_table + first_half * sine_table,
        ],
        axis=-1,
    )


def normalize(hidden):
    return hidden * lax.rsqrt(jnp.mean(hidden * hidden, axis=-1, keepdims=True) + epsilon)


def norm_back(grad_unit, unitized, hidden):
    factor = lax.rsqrt(jnp.mean(hidden * hidden, axis=-1, keepdims=True) + epsilon)
    return factor * (grad_unit - unitized * jnp.mean(grad_unit * unitized, axis=-1, keepdims=True))


def unchanged(carried):
    return carried


def split_slab(key_rows_block):
    key_total_width = KEY_VALUE_HEADS * HEAD_SIZE
    row_number = key_rows_block.shape[0]
    return (
        key_rows_block[:, :key_total_width].reshape(row_number, KEY_VALUE_HEADS, HEAD_SIZE),
        key_rows_block[:, key_total_width:].reshape(row_number, KEY_VALUE_HEADS, HEAD_SIZE),
    )


def raw_scores(query_rows, keys_part, allowed):
    scores = jnp.einsum(
        "qhgd,khd->hgqk", query_rows, keys_part, preferred_element_type=jnp.float32
    ) * HEAD_SIZE ** (-0.5)
    return jnp.where(allowed, scores, masked)


def attention_inputs(hidden, complete_weights, cosine_table, sine_table):
    row_number = hidden.shape[0]
    unitized = normalize(hidden)
    normalized_input = (unitized * complete_weights[0]).astype(jnp.bfloat16)
    query_rows = apply_rotation(
        matrix_product(normalized_input, complete_weights[1]).reshape(
            row_number, QUERY_HEADS, HEAD_SIZE
        ),
        cosine_table,
        sine_table,
    )
    query_rows = query_rows.astype(jnp.bfloat16).reshape(
        row_number, KEY_VALUE_HEADS, QUERY_HEADS // KEY_VALUE_HEADS, HEAD_SIZE
    )
    rotated_keys = apply_rotation(
        matrix_product(normalized_input, complete_weights[2]).reshape(
            row_number, KEY_VALUE_HEADS, HEAD_SIZE
        ),
        cosine_table,
        sine_table,
    )
    rotated_keys = rotated_keys.astype(jnp.bfloat16).reshape(
        row_number, KEY_VALUE_HEADS * HEAD_SIZE
    )
    value_rows = matrix_product(normalized_input, complete_weights[3]).astype(jnp.bfloat16)
    return (
        unitized,
        normalized_input,
        query_rows,
        jnp.concatenate([rotated_keys, value_rows], axis=1),
    )


def feedforward_front(middle, complete_weights):
    unit_ffn = normalize(middle)
    normed_ffn = (unit_ffn * complete_weights[5]).astype(jnp.bfloat16)
    gating = matrix_product(normed_ffn, complete_weights[6])
    upward = matrix_product(normed_ffn, complete_weights[7])
    sigmoid_gate = jax.nn.sigmoid(gating)
    activation = (gating * sigmoid_gate * upward).astype(jnp.bfloat16)
    return (unit_ffn, normed_ffn, gating, upward, sigmoid_gate, activation)


def attention_forward(query_rows, gathered, layout):
    visible, allowed = layout
    row_number = query_rows.shape[0]
    statistics_shape = (KEY_VALUE_HEADS, QUERY_HEADS // KEY_VALUE_HEADS, row_number, 1)
    row_peak = jnp.full(statistics_shape, masked, jnp.float32)
    row_total = jnp.zeros(statistics_shape, jnp.float32)
    for member in range(len(visible)):
        key_rows_block = gathered[member * row_number : (member + 1) * row_number]

        def update(carried, key_rows_block=key_rows_block, mask_here=allowed[member]):
            old_peak, old_total = carried
            scores = raw_scores(query_rows, split_slab(key_rows_block)[0], mask_here)
            new_peak = jnp.maximum(old_peak, jnp.max(scores, axis=-1, keepdims=True))
            new_total = old_total * jnp.exp(old_peak - new_peak) + jnp.sum(
                jnp.exp(scores - new_peak), axis=-1, keepdims=True
            )
            return (new_peak, new_total)

        row_peak, row_total = lax.cond(visible[member], update, unchanged, (row_peak, row_total))
    attended_rows = jnp.zeros(
        (row_number, KEY_VALUE_HEADS, QUERY_HEADS // KEY_VALUE_HEADS, HEAD_SIZE), jnp.float32
    )
    for member in range(len(visible)):
        key_rows_block = gathered[member * row_number : (member + 1) * row_number]

        def accumulate(running, key_rows_block=key_rows_block, mask_here=allowed[member]):
            keys_part, values_part = split_slab(key_rows_block)
            softened = (
                jnp.exp(raw_scores(query_rows, keys_part, mask_here) - row_peak) / row_total
            ).astype(jnp.bfloat16)
            return running + jnp.einsum(
                "hgqk,khd->qhgd", softened, values_part, preferred_element_type=jnp.float32
            )

        attended_rows = lax.cond(visible[member], accumulate, unchanged, attended_rows)
    return (attended_rows.reshape(row_number, QUERY_HEADS * HEAD_SIZE), row_peak, row_total)


def attention_backward(query_rows, gathered, layout, row_peak, row_total, attended_gradient):
    visible, allowed = layout
    row_number = query_rows.shape[0]
    head_gradient = attended_gradient.reshape(
        row_number, KEY_VALUE_HEADS, QUERY_HEADS // KEY_VALUE_HEADS, HEAD_SIZE
    )
    score_scale = HEAD_SIZE ** (-0.5)

    def probabilities(key_rows_block, mask_here):
        keys_part, values_part = split_slab(key_rows_block)
        softened = jnp.exp(raw_scores(query_rows, keys_part, mask_here) - row_peak) / row_total
        grad_prob = jnp.einsum(
            "qhgd,khd->hgqk", head_gradient, values_part, preferred_element_type=jnp.float32
        )
        return (keys_part, softened, grad_prob)

    row_difference = jnp.zeros(
        (KEY_VALUE_HEADS, QUERY_HEADS // KEY_VALUE_HEADS, row_number, 1), jnp.float32
    )
    for member in range(len(visible)):
        key_rows_block = gathered[member * row_number : (member + 1) * row_number]

        def delta_add(running, key_rows_block=key_rows_block, mask_here=allowed[member]):
            parts = probabilities(key_rows_block, mask_here)
            return running + jnp.sum(parts[2] * parts[1], axis=-1, keepdims=True)

        row_difference = lax.cond(visible[member], delta_add, unchanged, row_difference)
    query_gradient = jnp.zeros(
        (row_number, KEY_VALUE_HEADS, QUERY_HEADS // KEY_VALUE_HEADS, HEAD_SIZE), jnp.float32
    )
    empty_buffer = jnp.zeros((row_number, KEY_VALUE_HEADS, HEAD_SIZE), jnp.float32)
    pieces = []
    for member in range(len(visible)):
        key_rows_block = gathered[member * row_number : (member + 1) * row_number]

        def member_grads(running, key_rows_block=key_rows_block, mask_here=allowed[member]):
            keys_part, softened, grad_prob = probabilities(key_rows_block, mask_here)
            grad_score = (softened * (grad_prob - row_difference)).astype(
                jnp.bfloat16
            ) * score_scale
            key_gradient = jnp.einsum(
                "hgqk,qhgd->khd", grad_score, query_rows, preferred_element_type=jnp.float32
            )
            value_gradient = jnp.einsum(
                "hgqk,qhgd->khd",
                softened.astype(jnp.bfloat16),
                head_gradient,
                preferred_element_type=jnp.float32,
            )
            moved = running + jnp.einsum(
                "hgqk,khd->qhgd", grad_score, keys_part, preferred_element_type=jnp.float32
            )
            return (moved, key_gradient, value_gradient)

        def skipped(running):
            return (running, empty_buffer, empty_buffer)

        query_gradient, key_gradient, value_gradient = lax.cond(
            visible[member], member_grads, skipped, query_gradient
        )
        pieces.append(
            jnp.concatenate(
                [
                    key_gradient.reshape(row_number, KEY_VALUE_HEADS * HEAD_SIZE),
                    value_gradient.reshape(row_number, KEY_VALUE_HEADS * HEAD_SIZE),
                ],
                axis=1,
            )
        )
    return (query_gradient, jnp.concatenate(pieces, axis=0))


def forward_run(hidden, complete_weights, cosine_table, sine_table, layout):
    unitized, normalized_input, query_rows, key_rows_block = attention_inputs(
        hidden, complete_weights, cosine_table, sine_table
    )
    gathered = lax.all_gather(key_rows_block, "fsdp", axis=0, tiled=True)
    attended_rows, row_peak, row_total = attention_forward(query_rows, gathered, layout)
    attended_rows = attended_rows.astype(jnp.bfloat16)
    middle = hidden + matrix_product(attended_rows, complete_weights[4])
    activation = feedforward_front(middle, complete_weights)[5]
    return (
        middle + matrix_product(activation, complete_weights[8]),
        attended_rows,
        row_peak,
        row_total,
    )


def backward_run(
    hidden,
    attended_rows,
    row_peak,
    row_total,
    grad_after,
    complete_weights,
    cosine_table,
    sine_table,
    layout,
):
    (
        attention_norm,
        query_weight,
        key_matrix,
        value_matrix,
        output_weight,
        feedforward_norm,
        gate_weight,
        up_weight,
        down_weight,
    ) = complete_weights
    row_number = hidden.shape[0]
    key_total_width = KEY_VALUE_HEADS * HEAD_SIZE
    unitized, normalized_input, query_rows, key_rows_block = attention_inputs(
        hidden, complete_weights, cosine_table, sine_table
    )
    gathered = lax.all_gather(key_rows_block, "fsdp", axis=0, tiled=True)
    middle = hidden + matrix_product(attended_rows, output_weight)
    unit_ffn, normed_ffn, gating, upward, sigmoid_gate, activation = feedforward_front(
        middle, complete_weights
    )
    grad_branch = grad_after.astype(jnp.bfloat16)
    down_grad = first_trans(activation, grad_branch)
    grad_inner = second_trans(grad_branch, down_weight)
    grad_gating = (
        grad_inner * upward * (sigmoid_gate * (1.0 + gating * (1.0 - sigmoid_gate)))
    ).astype(jnp.bfloat16)
    grad_upward = (grad_inner * (gating * sigmoid_gate)).astype(jnp.bfloat16)
    gate_grad = first_trans(normed_ffn, grad_gating)
    up_grad = first_trans(normed_ffn, grad_upward)
    grad_normed_ffn = second_trans(grad_gating, gate_weight) + second_trans(grad_upward, up_weight)
    ffn_gain_grad = jnp.sum(grad_normed_ffn * unit_ffn, axis=0)
    grad_middle = grad_after + norm_back(grad_normed_ffn * feedforward_norm, unit_ffn, middle)
    grad_mixed = grad_middle.astype(jnp.bfloat16)
    output_grad = first_trans(attended_rows, grad_mixed)
    attended_gradient = second_trans(grad_mixed, output_weight).astype(jnp.bfloat16)
    query_gradient, key_terms = attention_backward(
        query_rows, gathered, layout, row_peak, row_total, attended_gradient
    )
    diagonal_terms = lax.psum_scatter(
        key_terms.astype(jnp.bfloat16), "fsdp", scatter_dimension=0, tiled=True
    ).astype(jnp.float32)
    grad_queries = (
        apply_rotation(
            query_gradient.reshape(row_number, QUERY_HEADS, HEAD_SIZE), cosine_table, -sine_table
        )
        .astype(jnp.bfloat16)
        .reshape(row_number, QUERY_HEADS * HEAD_SIZE)
    )
    key_gradient = (
        apply_rotation(
            diagonal_terms[:, :key_total_width].reshape(row_number, KEY_VALUE_HEADS, HEAD_SIZE),
            cosine_table,
            -sine_table,
        )
        .astype(jnp.bfloat16)
        .reshape(row_number, key_total_width)
    )
    value_gradient = diagonal_terms[:, key_total_width:].astype(jnp.bfloat16)
    query_grad = first_trans(normalized_input, grad_queries)
    key_grad = first_trans(normalized_input, key_gradient)
    value_grad = first_trans(normalized_input, value_gradient)
    grad_normed = (
        second_trans(grad_queries, query_weight)
        + second_trans(key_gradient, key_matrix)
        + second_trans(value_gradient, value_matrix)
    )
    attn_gain_grad = jnp.sum(grad_normed * unitized, axis=0)
    grad_hidden = grad_middle + norm_back(grad_normed * attention_norm, unitized, hidden)
    gradients = (
        attn_gain_grad,
        query_grad,
        key_grad,
        value_grad,
        output_grad,
        ffn_gain_grad,
        gate_grad,
        up_grad,
        down_grad,
    )
    return (grad_hidden, gradients)


def body(
    tokens,
    cotangent,
    sequence_ids,
    span_position,
    attention_norm,
    query_weight,
    key_matrix,
    value_matrix,
    output_weight,
    feedforward_norm,
    gate_weight,
    up_weight,
    down_weight,
):
    complete_weights = (
        lax.all_gather(attention_norm, "fsdp", axis=0, tiled=True),
        lax.all_gather(query_weight, "fsdp", axis=0, tiled=True),
        lax.all_gather(key_matrix, "fsdp", axis=0, tiled=True),
        lax.all_gather(value_matrix, "fsdp", axis=0, tiled=True),
        lax.all_gather(output_weight, "fsdp", axis=0, tiled=True),
        lax.all_gather(feedforward_norm, "fsdp", axis=0, tiled=True),
        lax.all_gather(gate_weight, "fsdp", axis=0, tiled=True),
        lax.all_gather(up_weight, "fsdp", axis=0, tiled=True),
        lax.all_gather(down_weight, "fsdp", axis=0, tiled=True),
    )
    row_number = tokens.shape[0]
    member_count = lax.axis_size("fsdp")
    itself = lax.axis_index("fsdp")
    own_sequence = sequence_ids[itself]
    own_place = span_position[itself]
    offsets = jnp.arange(row_number, dtype=jnp.int32)
    query_places = own_place * row_number + offsets
    cosine_table, sine_table = rotation(query_places, HEAD_SIZE // 2)
    visible = []
    allowed = []
    for member in range(member_count):
        visible.append(
            (sequence_ids[member] == own_sequence) & (span_position[member] <= own_place)
        )
        allowed.append(
            (span_position[member] * row_number + offsets)[None, :] <= query_places[:, None]
        )
    layout = (visible, allowed)
    hidden = tokens.astype(jnp.float32)
    stored = []
    for repeat in range(2):
        finish, attended_rows, row_peak, row_total = forward_run(
            hidden, complete_weights, cosine_table, sine_table, layout
        )
        stored.append((hidden, attended_rows, row_peak, row_total))
        hidden = finish
    activations = hidden.astype(jnp.bfloat16)
    complete_weights = (
        lax.all_gather(attention_norm, "fsdp", axis=0, tiled=True),
        lax.all_gather(query_weight, "fsdp", axis=0, tiled=True),
        lax.all_gather(key_matrix, "fsdp", axis=0, tiled=True),
        lax.all_gather(value_matrix, "fsdp", axis=0, tiled=True),
        lax.all_gather(output_weight, "fsdp", axis=0, tiled=True),
        lax.all_gather(feedforward_norm, "fsdp", axis=0, tiled=True),
        lax.all_gather(gate_weight, "fsdp", axis=0, tiled=True),
        lax.all_gather(up_weight, "fsdp", axis=0, tiled=True),
        lax.all_gather(down_weight, "fsdp", axis=0, tiled=True),
    )
    grad_hidden = cotangent.astype(jnp.float32)
    summed = None
    shard_sums = None
    for repeat in (1, 0):
        stored_hidden, attended_rows, row_peak, row_total = stored[repeat]
        grad_hidden, run_grads = backward_run(
            stored_hidden,
            attended_rows,
            row_peak,
            row_total,
            grad_hidden,
            complete_weights,
            cosine_table,
            sine_table,
            layout,
        )
        summed = run_grads if summed is None else jax.tree.map(jnp.add, summed, run_grads)
    shard_sums = jax.tree.map(
        lambda part: part.astype(jnp.float32),
        lax.psum_scatter(as_sent(summed), "fsdp", scatter_dimension=0, tiled=True),
    )
    totals = lax.psum(shard_sums, "dp")
    return (
        activations,
        grad_hidden.astype(jnp.bfloat16),
        totals[0],
        totals[1],
        totals[2],
        totals[3],
        totals[4],
        totals[5],
        totals[6],
        totals[7],
        totals[8],
    )


def solution(mesh):
    return jax.shard_map(
        body,
        mesh=mesh,
        in_specs=(
            P(("dp", "fsdp"), None),
            P(("dp", "fsdp"), None),
            P("dp"),
            P("dp"),
            P("fsdp"),
            P("fsdp", None),
            P("fsdp", None),
            P("fsdp", None),
            P("fsdp", None),
            P("fsdp"),
            P("fsdp", None),
            P("fsdp", None),
            P("fsdp", None),
        ),
        out_specs=(
            P(("dp", "fsdp"), None),
            P(("dp", "fsdp"), None),
            P("fsdp"),
            P("fsdp", None),
            P("fsdp", None),
            P("fsdp", None),
            P("fsdp", None),
            P("fsdp"),
            P("fsdp", None),
            P("fsdp", None),
            P("fsdp", None),
        ),
        check_vma=False,
    )
```

profile of v0, /device:TPU:0, one launch (start us, length us, event | category | flops | bytes accessed | tf_op | source)
XLA Modules:
  0.0 1117.5 jit_solution(2469597443724993456)
XLA Ops:
  12.2 8.3 all-reduce.6
  22.7 7.1 all-gather
  30.9 8.0 all-gather.1
  64.4 21.4 %all-gather.12.cloned.1.call-done = bf16[960,960]{1,0:T(8,128)(2,1)} async-done(((bf16[240,960]{1,0:T(8,128)(2,1)}), bf16[960,960]{1,0:T(8,128)(2,1)}) %all-gather.12.cloned.1.call-update) | async-done | bytes 1843216 | tf_op jit(solution)/shard_map/all_gather | solution.py:369
  94.0 4.5 conditional.35
  98.5 5.1 conditional.36
  100.3 3.4 fusion.10
  103.7 4.5 conditional.37
  104.4 3.8 fusion.19
  108.2 4.0 conditional.39
  108.3 3.6 fusion.37
  116.5 32.8 %all-gather.16.cloned.1.call-done = bf16[960,2560]{1,0:T(8,128)(2,1)} async-done(((bf16[240,2560]{1,0:T(8,128)(2,1)}), bf16[960,2560]{1,0:T(8,128)(2,1)}) %all-gather.16.cloned.1.call-update) | async-done | bytes 4915216 | tf_op jit(solution)/shard_map/all_gather | solution.py:374
  149.3 5.4 fusion.457
  154.7 34.6 %all-gather.18.cloned.1.call-done = bf16[960,2560]{1,0:T(8,128)(2,1)} async-done(((bf16[240,2560]{1,0:T(8,128)(2,1)}), bf16[960,2560]{1,0:T(8,128)(2,1)}) %all-gather.18.cloned.1.call-update) | async-done | bytes 4915216 | tf_op jit(solution)/shard_map/all_gather | solution.py:375
  189.3 7.0 multiply_convert_fusion.5
  196.3 33.0 %all-gather.20.cloned.1.call-done = bf16[2560,960]{0,1:T(8,128)(2,1)} async-done(((bf16[640,960]{0,1:T(8,128)(2,1)}), bf16[2560,960]{0,1:T(8,128)(2,1)}) %all-gather.20.cloned.1.call-update) | async-done | bytes 4915216 | tf_op jit(solution)/shard_map/all_gather | solution.py:376
  229.3 4.3 multiply_reduce_fusion.7
  239.1 15.7 %all-gather.22.cloned.1.call-done = bf16[1024,640]{0,1:T(8,128)(2,1)} async-done(((bf16[256,640]{0,1:T(8,128)(2,1)}), bf16[1024,640]{0,1:T(8,128)(2,1)}) %all-gather.22.cloned.1.call-update) | async-done | bytes 1310736 | tf_op jit(solution)/shard_map/all_gather | solution.py:245
  259.6 3.9 conditional.43
  269.0 4.0 conditional.47
  269.1 3.7 fusion.77
  276.9 4.8 fusion.460
  283.4 3.6 multiply_convert_fusion.2
  292.0 3.9 conditional.48
  302.2 4.8 conditional.52
  307.8 4.8 conditional.53
  314.3 4.8 conditional.55
  319.1 7.7 maximum_maximum_fusion
  327.3 3.4 fusion.468
  330.7 34.2 %reduce-scatter.16.cloned.1.call-done = bf16[256,640]{0,1:T(8,128)(2,1)} async-done(((bf16[1024,640]{0,1:T(8,128)(2,1)}), bf16[256,640]{0,1:T(8,128)(2,1)}) %reduce-scatter.16.cloned.1.call-update) | async-done | bytes 327696 | tf_op jit(solution)/shard_map/reduce_scatter | solution.py:308
  369.1 5.9 multiply_convert_fusion
  390.6 5.7 conditional.60
  397.0 5.7 conditional.61
  404.4 4.8 conditional.63
  419.5 26.7 %reduce-scatter.18.cloned.1.call-done = bf16[256,640]{0,1:T(8,128)(2,1)} async-done(((bf16[1024,640]{0,1:T(8,128)(2,1)}), bf16[256,640]{0,1:T(8,128)(2,1)}) %reduce-scatter.18.cloned.1.call-update) | async-done | bytes 327696 | tf_op jit(solution)/shard_map/reduce_scatter | solution.py:308
  456.3 3.6 add_convert_fusion
  459.9 7.9 copy.284
  471.7 3.6 add_convert_fusion.1
  478.3 3.7 add_convert_fusion.2
  483.2 5.2 fusion.386
  490.7 5.8 all-reduce.5
  497.7 16.2 %reduce-scatter.20.cloned.1.call-done = bf16[240,960]{1,0:T(8,128)(2,1)} async-done(((bf16[960,960]{1,0:T(8,128)(2,1)}), bf16[240,960]{1,0:T(8,128)(2,1)}) %reduce-scatter.20.cloned.1.call-update) | async-done | bytes 460816 | tf_op jit(solution)/shard_map/reduce_scatter | solution.py:435
  513.9 25.4 %reduce-scatter.30.cloned.1.call-done = bf16[240,320]{1,0:T(8,128)(2,1)} async-done(((bf16[960,320]{1,0:T(8,128)(2,1)}), bf16[240,320]{1,0:T(8,128)(2,1)}) %reduce-scatter.30.cloned.1.call-update) | async-done | bytes 153616
  540.3 24.7 %reduce-scatter.28.cloned.1.call-done = bf16[240,320]{1,0:T(8,128)(2,1)} async-done(((bf16[960,320]{1,0:T(8,128)(2,1)}), bf16[240,320]{1,0:T(8,128)(2,1)}) %reduce-scatter.28.cloned.1.call-update) | async-done | bytes 153616
  566.0 52.8 %reduce-scatter.32.cloned.1.call-done = bf16[640,960]{1,0:T(8,128)(2,1)} async-done(((bf16[2560,960]{1,0:T(8,128)(2,1)}), bf16[640,960]{1,0:T(8,128)(2,1)}) %reduce-scatter.32.cloned.1.call-update) | async-done | bytes 1228816
  621.0 49.7 %reduce-scatter.26.cloned.1.call-done = bf16[240,2560]{1,0:T(8,128)(2,1)} async-done(((bf16[960,2560]{1,0:T(8,128)(2,1)}), bf16[240,2560]{1,0:T(8,128)(2,1)}) %reduce-scatter.26.cloned.1.call-update) | async-done | bytes 1228816 | tf_op jit(solution)/shard_map/reduce_scatter | solution.py:435
  670.7 51.7 %reduce-scatter.24.cloned.1.call-done = bf16[240,2560]{1,0:T(8,128)(2,1)} async-done(((bf16[960,2560]{1,0:T(8,128)(2,1)}), bf16[240,2560]{1,0:T(8,128)(2,1)}) %reduce-scatter.24.cloned.1.call-update) | async-done | bytes 1228816 | tf_op jit(solution)/shard_map/reduce_scatter | solution.py:435
  722.3 388.3 %all-reduce.8 = (f32[240]{0:T(256)}, f32[240,960]{1,0:T(8,128)}, f32[240,320]{0,1:T(8,128)}, f32[240,320]{0,1:T(8,128)}, f32[240,960]{1,0:T(8,128)}, /*index=5*/...) all-reduce(f32[240]{0:T(256)S(1)} %dynamic-slice_convert_fusion.1, ...), channel_id=1, replica_groups=mesh['dp'=8,'fsdp'=4] {'dp'}, use_global_device_ids=true, to_apply=%region_101.102 | all-reduce | flops 2458080 | bytes 14749440 | tf_op jit(solution)/shard_map/psum | solution.py:437
  (494 shorter events, 195.4 us)
Async XLA Ops:
  7.2 32.8 %copy-start.6 = (bf16[256,960]{0,1:T(8,128)(2,1)S(1)}, bf16[256,960]{0,1:T(8,128)(2,1)}, u32[]{:S(2)}) copy-start(bf16[256,960]{0,1:T(8,128)(2,1)} %param.77) | copy-start | bytes 1474564
  7.2 23.7 %copy-start.94 = (bf16[240,320]{0,1:T(8,128)(2,1)S(1)}, bf16[240,320]{0,1:T(8,128)(2,1)}, u32[]{:S(2)}) copy-start(bf16[240,320]{0,1:T(8,128)(2,1)} %param.84) | copy-start | bytes 460804
  7.2 55.1 %all-gather.10.cloned.1.call-start = ((), (), s32[]{:S(2)}) async-start(), calls=%async_computation.9 | async-start | bytes 1638400 | tf_op jit(solution)/shard_map/all_gather | solution.py:245
  8.5 77.3 %copy-start.95 = (f32[256]{0:T(256)}, f32[256]{0:T(256)S(1)}, u32[]{:S(2)}) copy-start(f32[256]{0:T(256)S(1)} %add_rsqrt_fusion.3) | copy-start | bytes 3076
  30.9 204.2 %copy-start.18 = (bf16[960,320]{0,1:T(8,128)(2,1)}, bf16[960,320]{0,1:T(8,128)(2,1)S(1)}, u32[]{:S(2)}) copy-start(bf16[960,320]{0,1:T(8,128)(2,1)S(1)} %reshape.665) | copy-start | bytes 1843204
  39.9 194.8 %copy-start.15 = (bf16[960,320]{0,1:T(8,128)(2,1)}, bf16[960,320]{0,1:T(8,128)(2,1)S(1)}, u32[]{:S(2)}) copy-start(bf16[960,320]{0,1:T(8,128)(2,1)S(1)} %reshape.667) | copy-start | bytes 1843204
  41.7 46.8 %copy-start.71 = (f32[256,32]{0,1:T(8,128)}, f32[256,32]{0,1:T(8,128)S(1)}, u32[]{:S(2)}) copy-start(f32[256,32]{0,1:T(8,128)S(1)} %get-tuple-element.1262) | copy-start | bytes 98308
  42.5 43.3 %all-gather.12.cloned.1.call-start = ((), (), s32[]{:S(2)}) async-start(), calls=%async_computation.10 | async-start | bytes 2457600 | tf_op jit(solution)/shard_map/all_gather | solution.py:369
  43.3 70.3 %all-gather.14.cloned.1.call-start = ((), (), s32[]{:S(2)}) async-start(), calls=%async_computation.11 | async-start | bytes 2457600 | tf_op jit(solution)/shard_map/all_gather | solution.py:372
  44.0 105.3 %all-gather.16.cloned.1.call-start = ((), (), s32[]{:S(2)}) async-start(), calls=%async_computation.12 | async-start | bytes 6144000 | tf_op jit(solution)/shard_map/all_gather | solution.py:374
  44.6 144.7 %all-gather.18.cloned.1.call-start = ((), (), s32[]{:S(2)}) async-start(), calls=%async_computation.13 | async-start | bytes 6144000 | tf_op jit(solution)/shard_map/all_gather | solution.py:375
  45.2 184.1 %all-gather.20.cloned.1.call-start = ((), (), s32[]{:S(2)}) async-start(), calls=%async_computation.14 | async-start | bytes 6144000 | tf_op jit(solution)/shard_map/all_gather | solution.py:376
  45.8 209.0 %all-gather.22.cloned.1.call-start = ((), (), s32[]{:S(2)}) async-start(), calls=%async_computation.15 | async-start | bytes 1638400 | tf_op jit(solution)/shard_map/all_gather | solution.py:245
  64.4 39.3 %copy-start.31 = (bf16[256,640]{0,1:T(8,128)(2,1)}, bf16[256,640]{0,1:T(8,128)(2,1)S(1)}, u32[]{:S(2)}) copy-start(bf16[256,640]{0,1:T(8,128)(2,1)S(1)} %get-tuple-element.1243) | copy-start | bytes 983044
  64.4 43.8 %copy-start.29 = (bf16[256,640]{0,1:T(8,128)(2,1)}, bf16[256,640]{0,1:T(8,128)(2,1)S(1)}, u32[]{:S(2)}) copy-start(bf16[256,640]{0,1:T(8,128)(2,1)S(1)} %get-tuple-element.1242) | copy-start | bytes 983044
  64.4 43.8 %copy-start.27 = (bf16[256,640]{0,1:T(8,128)(2,1)}, bf16[256,640]{0,1:T(8,128)(2,1)S(1)}, u32[]{:S(2)}) copy-start(bf16[256,640]{0,1:T(8,128)(2,1)S(1)} %get-tuple-element.1241) | copy-start | bytes 983044
  88.7 19.5 %copy-start = (bf16[256,5,3,64]{0,3,2,1:T(8,128)(2,1)}, bf16[256,5,3,64]{0,3,2,1:T(8,128)(2,1)S(1)}, u32[]{:S(2)}) copy-start(bf16[256,5,3,64]{0,3,2,1:T(8,128)(2,1)S(1)} %pad_maximum_fusion) | copy-start | bytes 1474564
  113.5 41.2 %copy-start.49 = (bf16[256,5,3,64]{0,3,2,1:T(8,128)(2,1)}, bf16[256,5,3,64]{0,3,2,1:T(8,128)(2,1)S(1)}, u32[]{:S(2)}) copy-start(bf16[256,5,3,64]{0,3,2,1:T(8,128)(2,1)S(1)} %convert_element_type.355) | copy-start | bytes 1474564
  116.2 113.1 %copy-start.44 = (f32[256,960]{0,1:T(8,128)}, f32[256,960]{0,1:T(8,128)S(1)}, u32[]{:S(2)}) copy-start(f32[256,960]{0,1:T(8,128)S(1)} %get-tuple-element.1281) | copy-start | bytes 2949124
  116.2 38.5 %copy-start.97 = (f32[256]{0:T(256)}, f32[256]{0:T(256)S(1)}, u32[]{:S(2)}) copy-start(f32[256]{0:T(256)S(1)} %add_rsqrt_fusion.2) | copy-start | bytes 3076
  116.4 72.9 %copy-start.21 = (bf16[256,960]{0,1:T(8,128)(2,1)}, bf16[256,960]{0,1:T(8,128)(2,1)S(1)}, u32[]{:S(2)}) copy-start(bf16[256,960]{0,1:T(8,128)(2,1)S(1)} %multiply_convert_fusion.8) | copy-start | bytes 1474564
  236.3 128.6 %reduce-scatter.16.cloned.1.call-start = ((), (), s32[]{:S(2)}) async-start(), calls=%async_computation.16 | async-start | bytes 1638400 | tf_op jit(solution)/shard_map/reduce_scatter | solution.py:308
  236.3 19.9 %copy-start.57 = (pred[256,256]{0,1:T(8,128)(4,1)S(1)}, pred[256,256]{0,1:T(8,128)(4,1)}, u32[]{:S(2)}) copy-start(pred[256,256]{0,1:T(8,128)(4,1)} %get-tuple-element.1267) | copy-start | bytes 196612
  256.2 7.4 copy-start.39
  256.2 9.6 copy-start.37
  256.2 11.9 %copy-start.35 = (bf16[256,640]{0,1:T(8,128)(2,1)}, bf16[256,640]{0,1:T(8,128)(2,1)S(1)}, u32[]{:S(2)}) copy-start(bf16[256,640]{0,1:T(8,128)(2,1)S(1)} %get-tuple-element.1238) | copy-start | bytes 983044
  274.3 7.4 slice-start
  274.3 9.0 slice-start.9
  276.6 14.2 %copy-start.23 = (f32[256,960]{0,1:T(8,128)}, f32[256,960]{0,1:T(8,128)S(1)}, u32[]{:S(2)}) copy-start(f32[256,960]{0,1:T(8,128)S(1)} %get-tuple-element.1287) | copy-start | bytes 2949124
  281.8 6.8 slice-start.4
  319.0 8.0 copy-start.69
  326.8 119.4 %reduce-scatter.18.cloned.1.call-start = ((), (), s32[]{:S(2)}) async-start(), calls=%async_computation.17 | async-start | bytes 1638400 | tf_op jit(solution)/shard_map/reduce_scatter | solution.py:308
  327.2 40.7 %copy-start.52 = (bf16[256,15,64]{0,2,1:T(8,128)(2,1)}, bf16[256,15,64]{0,2,1:T(8,128)(2,1)S(1)}, u32[]{:S(2)}) copy-start(bf16[256,15,64]{0,2,1:T(8,128)(2,1)S(1)} %pad_maximum_fusion.2) | copy-start | bytes 1474564
  327.2 38.8 %copy-start.19 = (bf16[960,320]{0,1:T(8,128)(2,1)S(1)}, bf16[960,320]{0,1:T(8,128)(2,1)}, u32[]{:S(2)}) copy-start(bf16[960,320]{0,1:T(8,128)(2,1)} %copy-done.18) | copy-start | bytes 1843204
  327.2 40.6 %copy-start.11 = (f32[256,960]{0,1:T(8,128)S(1)}, f32[256,960]{0,1:T(8,128)}, u32[]{:S(2)}) copy-start(f32[256,960]{0,1:T(8,128)} %copy-done.10) | copy-start | bytes 2949124
  327.3 40.6 %copy-start.16 = (bf16[960,320]{0,1:T(8,128)(2,1)S(1)}, bf16[960,320]{0,1:T(8,128)(2,1)}, u32[]{:S(2)}) copy-start(bf16[960,320]{0,1:T(8,128)(2,1)} %copy-done.15) | copy-start | bytes 1843204
  367.9 7.1 slice-start.2
  367.9 8.7 slice-start.6
  369.0 9.7 copy-start.25
  369.1 7.5 slice-start.7
  412.0 85.7 %reduce-scatter.22.cloned.1.call-start = ((), (), s32[]{:S(2)}) async-start(), calls=%async_computation.19 | async-start | bytes 2457600 | tf_op jit(solution)/shard_map/reduce_scatter | solution.py:435
  415.1 98.8 %reduce-scatter.20.cloned.1.call-start = ((), (), s32[]{:S(2)}) async-start(), calls=%async_computation.18 | async-start | bytes 2457600 | tf_op jit(solution)/shard_map/reduce_scatter | solution.py:435
  418.1 32.7 %copy-start.61 = (bf16[256,5,64]{0,2,1:T(8,128)(2,1)S(1)}, bf16[256,5,64]{0,2,1:T(8,128)(2,1)}, u32[]{:S(2)}) copy-start(bf16[256,5,64]{0,2,1:T(8,128)(2,1)} %copy-done.60) | copy-start | bytes 491524
  418.2 121.1 %reduce-scatter.30.cloned.1.call-start = ((), (), s32[]{:S(2)}) async-start(), calls=%async_computation.23 | async-start | bytes 921600
  450.8 114.2 %reduce-scatter.28.cloned.1.call-start = ((), (), s32[]{:S(2)}) async-start(), calls=%async_computation.22 | async-start | bytes 921600
  453.0 165.9 %reduce-scatter.32.cloned.1.call-start = ((), (), s32[]{:S(2)}) async-start(), calls=%async_computation.24 | async-start | bytes 6553600
  467.9 202.8 %reduce-scatter.26.cloned.1.call-start = ((), (), s32[]{:S(2)}) async-start(), calls=%async_computation.21 | async-start | bytes 6144000 | tf_op jit(solution)/shard_map/reduce_scatter | solution.py:435
  475.4 247.0 %reduce-scatter.24.cloned.1.call-start = ((), (), s32[]{:S(2)}) async-start(), calls=%async_computation.20 | async-start | bytes 6144000 | tf_op jit(solution)/shard_map/reduce_scatter | solution.py:435
  (80 other events, 200.5 us)
Sparse Core Ops, SparseCore 0:
  42.6 19.6 all-gather.9
  63.9 21.8 all-gather.11
  87.4 21.8 all-gather.13
  110.7 38.5 all-gather.15
  150.7 38.5 all-gather.17
  190.7 38.5 all-gather.19
  236.4 18.3 all-gather.21
  326.9 37.9 reduce-scatter.15
  412.1 34.0 reduce-scatter.17
  449.2 30.6 reduce-scatter.21
  483.2 30.6 reduce-scatter.19
  516.3 22.9 reduce-scatter.29
  542.0 22.9 reduce-scatter.27
  567.4 51.3 reduce-scatter.31
  621.4 49.1 reduce-scatter.25
  673.1 49.1 reduce-scatter.23
where the time goes:
time: 1130 us; the launch traced here: 1120 us
  waiting for transfers between devices  425 us (38%)
  blocking collectives  417 us (37%)
  matrix products  163 us (14%)
  local copies, waits for them, and re-layouts  44 us (4%)
  other arithmetic  32.9 us (3%)
  between operations  31.3 us (3%)
    psum x1, blocking collectives, body(): totals = lax.psum(shard_sums, 'dp')  388 us
    reduce_scatter x4, waiting for transfers between devices, body(): lax.psum_scatter(as_sent(summed), 'fsdp', scatter_dimension=0, tiled=True)  118 us
    unnamed x19, waiting for transfers between devices  106 us
    reduce_scatter x2, waiting for transfers between devices, backward_run(): lax.psum_scatter(key_terms.astype(jnp.bfloat16), 'fsdp', scatter_dimensio...  61 us
    dot_general x14, matrix products, matrix_product(): return jnp.dot(left_side, right_side, preferred_element_type=jnp.float32)  39.9 us
    all_gather x1, waiting for transfers between devices, body(): lax.all_gather(up_weight, 'fsdp', axis=0, tiled=True)  34.6 us
    all_gather x1, waiting for transfers between devices, body(): lax.all_gather(down_weight, 'fsdp', axis=0, tiled=True)  33 us
    all_gather x1, waiting for transfers between devices, body(): lax.all_gather(gate_weight, 'fsdp', axis=0, tiled=True)  32.8 us
  transfers between devices with their start and end apart: 16, of which 14 were waited for; matrix products, arithmetic and copies ran while one was open for 9% of the time, Pallas kernels for 0%

commit v1 on v0

--- a/solution.py
+++ b/solution.py
@@ -11,14 +11,6 @@
 epsilon = 1e-05
 rope_base = 10000.0
 masked = -1e30
-
-
-def as_sent(value):
-
-    def short(part):
-        return part.astype(jnp.bfloat16) if part.dtype == jnp.float32 else part
-
-    return jax.tree.map(short, value)
 
 
 def matrix_product(left_side, right_side):
@@ -238,11 +230,133 @@
     return (query_gradient, jnp.concatenate(pieces, axis=0))
 
 
+def flip(value, axis_name, distance):
+    size = lax.axis_size(axis_name)
+    return lax.ppermute(value, axis_name, [(i, i ^ distance) for i in range(size)])
+
+
+def pick(condition, when_true, when_false):
+    return jnp.where(condition, when_true, when_false)
+
+
+def quarters(value):
+    width = value.shape[1] // 4
+    return [value[:, i * width : (i + 1) * width] for i in range(4)]
+
+
+def order_by(bit, own, other):
+    return (pick(bit == 1, other, own), pick(bit == 1, own, other))
+
+
+def gather_direct(shard):
+    core = lax.axis_index("fsdp") % 2
+    chip = lax.axis_index("fsdp") // 2
+    beside = flip(shard, "fsdp", 1)
+    across = flip(shard, "fsdp", 2)
+    diagonal = flip(across, "fsdp", 1)
+    near = order_by(core, shard, beside)
+    far = order_by(core, across, diagonal)
+    low = [pick(chip == 1, f, n) for n, f in zip(near, far)]
+    high = [pick(chip == 1, n, f) for n, f in zip(near, far)]
+    return jnp.concatenate(low + high, axis=0)
+
+
+def gather_shared(shard):
+    core = lax.axis_index("fsdp") % 2
+    chip = lax.axis_index("fsdp") // 2
+    first = lax.axis_index("dp") % 2
+    second = (lax.axis_index("dp") // 2) % 2
+    beside = flip(shard, "fsdp", 1)
+    parts = quarters(shard)
+    mine = pick(second == 1, pick(first == 1, parts[3], parts[2]), pick(first == 1, parts[1], parts[0]))
+    got = flip(mine, "fsdp", 2)
+    half = got.shape[1] // 2
+    left, right = got[:, :half], got[:, half:]
+    left_y = flip(left, "dp", 1)
+    right_z = flip(right, "dp", 2)
+    left_pair = order_by(first, left, left_y)
+    right_pair = order_by(second, right, right_z)
+    left_row = jnp.concatenate(left_pair, axis=1)
+    right_row = jnp.concatenate(right_pair, axis=1)
+    left_far = flip(left_row, "dp", 2)
+    right_far = flip(right_row, "dp", 1)
+    left_rows = order_by(second, left_row, left_far)
+    right_rows = order_by(first, right_row, right_far)
+    pieces = []
+    for b2 in range(2):
+        for b1 in range(2):
+            pieces.append(left_rows[b2][:, b1 * half : (b1 + 1) * half])
+            pieces.append(right_rows[b1][:, b2 * half : (b2 + 1) * half])
+    across = jnp.concatenate(pieces, axis=1)
+    diagonal = flip(across, "fsdp", 1)
+    near = order_by(core, shard, beside)
+    far = order_by(core, across, diagonal)
+    low = [pick(chip == 1, f, n) for n, f in zip(near, far)]
+    high = [pick(chip == 1, n, f) for n, f in zip(near, far)]
+    return jnp.concatenate(low + high, axis=0)
+
+
+def gather_rows(block):
+    core = lax.axis_index("fsdp") % 2
+    chip = lax.axis_index("fsdp") // 2
+    beside = flip(block, "fsdp", 1)
+    across = flip(block, "fsdp", 2)
+    diagonal = flip(across, "fsdp", 1)
+    near = order_by(core, block, beside)
+    far = order_by(core, across, diagonal)
+    low = [pick(chip == 1, f, n) for n, f in zip(near, far)]
+    high = [pick(chip == 1, n, f) for n, f in zip(near, far)]
+    return jnp.concatenate(low + high, axis=0)
+
+
+def add_short(one, other):
+    return (one.astype(jnp.float32) + other.astype(jnp.float32)).astype(jnp.bfloat16)
+
+
+def scatter_group(blocks):
+    core = lax.axis_index("fsdp") % 2
+    chip = lax.axis_index("fsdp") // 2
+    keep = [pick(core == 1, row[1], row[0]) for row in blocks]
+    send = [pick(core == 1, row[0], row[1]) for row in blocks]
+    got = flip(jnp.concatenate(send, axis=0), "fsdp", 1)
+    rows = keep[0].shape[0]
+    summed = [add_short(keep[0], got[:rows]), add_short(keep[1], got[rows:])]
+    got = flip(pick(chip == 1, summed[0], summed[1]), "fsdp", 2)
+    return add_short(pick(chip == 1, summed[1], summed[0]), got)
+
+
+def reduce_rows(blocks):
+    size = lax.axis_size("dp")
+    index = lax.axis_index("dp")
+    first = index % 2
+    second = (index // 2) % 2
+    own = scatter_group(blocks)
+    width = own.shape[1] // 2
+    got = flip(pick(first == 1, own[:, :width], own[:, width:]), "dp", 1)
+    own = add_short(pick(first == 1, own[:, width:], own[:, :width]), got)
+    width = width // 2
+    got = flip(pick(second == 1, own[:, :width], own[:, width:]), "dp", 2)
+    own = add_short(pick(second == 1, own[:, width:], own[:, :width]), got)
+    distance = 4
+    while distance < size:
+        own = add_short(own, flip(own, "dp", distance))
+        distance *= 2
+    own = jnp.concatenate(order_by(second, own, flip(own, "dp", 2)), axis=1)
+    own = jnp.concatenate(order_by(first, own, flip(own, "dp", 1)), axis=1)
+    return own.astype(jnp.float32)
+
+
+def blocks_of(total):
+    rows = total.shape[0] // 4
+    total = total.astype(jnp.bfloat16)
+    return [[total[(2 * a + b) * rows : (2 * a + b + 1) * rows] for b in range(2)] for a in range(2)]
+
+
 def forward_run(hidden, complete_weights, cosine_table, sine_table, layout):
     unitized, normalized_input, query_rows, key_rows_block = attention_inputs(
         hidden, complete_weights, cosine_table, sine_table
     )
-    gathered = lax.all_gather(key_rows_block, "fsdp", axis=0, tiled=True)
+    gathered = gather_rows(key_rows_block)
     attended_rows, row_peak, row_total = attention_forward(query_rows, gathered, layout)
     attended_rows = attended_rows.astype(jnp.bfloat16)
     middle = hidden + matrix_product(attended_rows, complete_weights[4])
@@ -252,6 +366,7 @@
         attended_rows,
         row_peak,
         row_total,
+        gathered,
     )
 
 
@@ -260,6 +375,7 @@
     attended_rows,
     row_peak,
     row_total,
+    gathered,
     grad_after,
     complete_weights,
     cosine_table,
@@ -282,32 +398,25 @@
     unitized, normalized_input, query_rows, key_rows_block = attention_inputs(
         hidden, complete_weights, cosine_table, sine_table
     )
-    gathered = lax.all_gather(key_rows_block, "fsdp", axis=0, tiled=True)
     middle = hidden + matrix_product(attended_rows, output_weight)
     unit_ffn, normed_ffn, gating, upward, sigmoid_gate, activation = feedforward_front(
         middle, complete_weights
     )
     grad_branch = grad_after.astype(jnp.bfloat16)
-    down_grad = first_trans(activation, grad_branch)
     grad_inner = second_trans(grad_branch, down_weight)
     grad_gating = (
         grad_inner * upward * (sigmoid_gate * (1.0 + gating * (1.0 - sigmoid_gate)))
     ).astype(jnp.bfloat16)
     grad_upward = (grad_inner * (gating * sigmoid_gate)).astype(jnp.bfloat16)
-    gate_grad = first_trans(normed_ffn, grad_gating)
-    up_grad = first_trans(normed_ffn, grad_upward)
     grad_normed_ffn = second_trans(grad_gating, gate_weight) + second_trans(grad_upward, up_weight)
     ffn_gain_grad = jnp.sum(grad_normed_ffn * unit_ffn, axis=0)
     grad_middle = grad_after + norm_back(grad_normed_ffn * feedforward_norm, unit_ffn, middle)
     grad_mixed = grad_middle.astype(jnp.bfloat16)
-    output_grad = first_trans(attended_rows, grad_mixed)
     attended_gradient = second_trans(grad_mixed, output_weight).astype(jnp.bfloat16)
     query_gradient, key_terms = attention_backward(
         query_rows, gathered, layout, row_peak, row_total, attended_gradient
     )
-    diagonal_terms = lax.psum_scatter(
-        key_terms.astype(jnp.bfloat16), "fsdp", scatter_dimension=0, tiled=True
-    ).astype(jnp.float32)
+    diagonal_terms = scatter_group(blocks_of(key_terms)).astype(jnp.float32)
     grad_queries = (
         apply_rotation(
             query_gradient.reshape(row_number, QUERY_HEADS, HEAD_SIZE), cosine_table, -sine_table
@@ -325,9 +434,6 @@
         .reshape(row_number, key_total_width)
     )
     value_gradient = diagonal_terms[:, key_total_width:].astype(jnp.bfloat16)
-    query_grad = first_trans(normalized_input, grad_queries)
-    key_grad = first_trans(normalized_input, key_gradient)
-    value_grad = first_trans(normalized_input, value_gradient)
     grad_normed = (
         second_trans(grad_queries, query_weight)
         + second_trans(key_gradient, key_matrix)
@@ -335,18 +441,14 @@
     )
     attn_gain_grad = jnp.sum(grad_normed * unitized, axis=0)
     grad_hidden = grad_middle + norm_back(grad_normed * attention_norm, unitized, hidden)
-    gradients = (
-        attn_gain_grad,
-        query_grad,
-        key_grad,
-        value_grad,
-        output_grad,
-        ffn_gain_grad,
-        gate_grad,
-        up_grad,
-        down_grad,
-    )
-    return (grad_hidden, gradients)
+    factors = (
+        (normalized_input, jnp.concatenate([grad_queries, key_gradient, value_gradient], axis=1)),
+        (attended_rows, grad_mixed),
+        (normed_ffn, jnp.concatenate([grad_gating, grad_upward], axis=1)),
+        (activation, grad_branch),
+        (attn_gain_grad, ffn_gain_grad),
+    )
+    return (grad_hidden, factors)
 
 
 def body(
@@ -364,16 +466,26 @@
     up_weight,
     down_weight,
 ):
+    width = output_weight.shape[1]
+    key_total_width = key_matrix.shape[1]
+    ffn_width = gate_weight.shape[1]
+    first_end = width + key_total_width
+    second_end = first_end + key_total_width
+    attention_weights = gather_shared(
+        jnp.concatenate([query_weight, key_matrix, value_matrix, output_weight], axis=1)
+    )
+    gains = gather_rows(jnp.stack([attention_norm, feedforward_norm], axis=1))
+    ffn_weights = gather_shared(jnp.concatenate([gate_weight, up_weight], axis=1))
     complete_weights = (
-        lax.all_gather(attention_norm, "fsdp", axis=0, tiled=True),
-        lax.all_gather(query_weight, "fsdp", axis=0, tiled=True),
-        lax.all_gather(key_matrix, "fsdp", axis=0, tiled=True),
-        lax.all_gather(value_matrix, "fsdp", axis=0, tiled=True),
-        lax.all_gather(output_weight, "fsdp", axis=0, tiled=True),
-        lax.all_gather(feedforward_norm, "fsdp", axis=0, tiled=True),
-        lax.all_gather(gate_weight, "fsdp", axis=0, tiled=True),
-        lax.all_gather(up_weight, "fsdp", axis=0, tiled=True),
-        lax.all_gather(down_weight, "fsdp", axis=0, tiled=True),
+        gains[:, 0],
+        attention_weights[:, :width],
+        attention_weights[:, width:first_end],
+        attention_weights[:, first_end:second_end],
+        attention_weights[:, second_end:],
+        gains[:, 1],
+        ffn_weights[:, :ffn_width],
+        ffn_weights[:, ffn_width:],
+        gather_direct(down_weight),
     )
     row_number = tokens.shape[0]
     member_count = lax.axis_size("fsdp")
@@ -396,57 +508,73 @@
     hidden = tokens.astype(jnp.float32)
     stored = []
     for repeat in range(2):
-        finish, attended_rows, row_peak, row_total = forward_run(
+        finish, attended_rows, row_peak, row_total, gathered = forward_run(
             hidden, complete_weights, cosine_table, sine_table, layout
         )
-        stored.append((hidden, attended_rows, row_peak, row_total))
+        stored.append((hidden, attended_rows, row_peak, row_total, gathered))
         hidden = finish
     activations = hidden.astype(jnp.bfloat16)
-    complete_weights = (
-        lax.all_gather(attention_norm, "fsdp", axis=0, tiled=True),
-        lax.all_gather(query_weight, "fsdp", axis=0, tiled=True),
-        lax.all_gather(key_matrix, "fsdp", axis=0, tiled=True),
-        lax.all_gather(value_matrix, "fsdp", axis=0, tiled=True),
-        lax.all_gather(output_weight, "fsdp", axis=0, tiled=True),
-        lax.all_gather(feedforward_norm, "fsdp", axis=0, tiled=True),
-        lax.all_gather(gate_weight, "fsdp", axis=0, tiled=True),
-        lax.all_gather(up_weight, "fsdp", axis=0, tiled=True),
-        lax.all_gather(down_weight, "fsdp", axis=0, tiled=True),
-    )
     grad_hidden = cotangent.astype(jnp.float32)
-    summed = None
-    shard_sums = None
+    factors = []
     for repeat in (1, 0):
-        stored_hidden, attended_rows, row_peak, row_total = stored[repeat]
-        grad_hidden, run_grads = backward_run(
+        stored_hidden, attended_rows, row_peak, row_total, gathered = stored[repeat]
+        grad_hidden, run_factors = backward_run(
             stored_hidden,
             attended_rows,
             row_peak,
             row_total,
+            gathered,
             grad_hidden,
             complete_weights,
             cosine_table,
             sine_table,
             layout,
         )
-        summed = run_grads if summed is None else jax.tree.map(jnp.add, summed, run_grads)
-    shard_sums = jax.tree.map(
-        lambda part: part.astype(jnp.float32),
-        lax.psum_scatter(as_sent(summed), "fsdp", scatter_dimension=0, tiled=True),
-    )
-    totals = lax.psum(shard_sums, "dp")
+        factors.append(run_factors)
+
+    def both(entry):
+        left = jnp.concatenate([run[entry][0] for run in factors], axis=0)
+        right = jnp.concatenate([run[entry][1] for run in factors], axis=0)
+        return first_trans(left, right)
+
+    ffn_width = gate_weight.shape[1]
+    width = output_weight.shape[1]
+    key_total_width = key_matrix.shape[1]
+    down_grad = reduce_rows(blocks_of(both(3)))
+    gate_up = both(2)
+    gate_grad = reduce_rows(blocks_of(gate_up[:, :ffn_width]))
+    up_grad = reduce_rows(blocks_of(gate_up[:, ffn_width:]))
+    shard_rows = query_weight.shape[0]
+    attention_grad = jnp.concatenate([both(0), both(1)], axis=1).astype(jnp.bfloat16)
+    gains = [factors[0][4][i] + factors[1][4][i] for i in range(2)]
+    extra = jnp.stack(gains).reshape(2, 4, shard_rows).transpose(1, 0, 2).reshape(4, 1, 2 * shard_rows)
+    extra = jnp.pad(extra, ((0, 0), (0, 15), (0, attention_grad.shape[1] - 2 * shard_rows)))
+    extra = extra.astype(jnp.bfloat16)
+    rows = attention_grad.shape[0] // 4
+    blocks = [
+        [
+            jnp.concatenate(
+                [attention_grad[(2 * a + b) * rows : (2 * a + b + 1) * rows], extra[2 * a + b]], axis=0
+            )
+            for b in range(2)
+        ]
+        for a in range(2)
+    ]
+    mixed = reduce_rows(blocks)
+    first_end = width + key_total_width
+    second_end = first_end + key_total_width
     return (
         activations,
         grad_hidden.astype(jnp.bfloat16),
-        totals[0],
-        totals[1],
-        totals[2],
-        totals[3],
-        totals[4],
-        totals[5],
-        totals[6],
-        totals[7],
-        totals[8],
+        mixed[rows, :shard_rows],
+        mixed[:rows, :width],
+        mixed[:rows, width:first_end],
+        mixed[:rows, first_end:second_end],
+        mixed[:rows, second_end:],
+        mixed[rows, shard_rows : 2 * shard_rows],
+        gate_grad,
+        up_grad,
+        down_grad,
     )
 
 

time: 1130 us -> 685 us (0.61)
  blocking collectives: 417 us -> 0 us
  waiting for transfers between devices: 425 us -> 233 us
  starting transfers between devices: 1.07 us -> 145 us
  other arithmetic: 32.9 us -> 83.5 us
  matrix products: 163 us -> 119 us
  local copies, waits for them, and re-layouts: 44 us -> 65.3 us
  between operations: 31.3 us -> 17.2 us
    psum x1 -> x0, blocking collectives: 388 us -> none  [body(): totals = lax.psum(shard_sums, 'dp')]
    ppermute x0 -> x58, waiting for transfers between devices: none -> 233 us  [flip(): lax.ppermute(value, axis_name, [(i, i ^ distance) for i in range(size)])]
    reduce_scatter x6 -> x0, waiting for transfers between devices: 179 us -> none  [the longest x4 118 us: body(): lax.psum_scatter(as_sent(summed), 'fsdp', scatter_dimension=0, tiled=True)]
    ppermute x0 -> x58, starting transfers between devices: none -> 145 us  [flip(): lax.ppermute(value, axis_name, [(i, i ^ distance) for i in range(size)])]
    all_gather x7 -> x0, waiting for transfers between devices: 140 us -> none  [the longest x1 34.6 us: body(): lax.all_gather(up_weight, 'fsdp', axis=0, tiled=True)]
    unnamed x19 -> x0, waiting for transfers between devices: 106 us -> none
    select_n x0 -> x44, other arithmetic: none -> 39.3 us  [pick(): return jnp.where(condition, when_true, when_false)]
    all_gather x2 -> x0, blocking collectives: 15.1 us -> none  [the longest x1 8.01 us: body(): lax.all_gather(value_matrix, 'fsdp', axis=0, tiled=True)]
  transfers between devices with their start and end apart: 16 -> 58, of which waited for: 14 -> 30; matrix products, arithmetic and copies ran while one was open for 9% -> 18% of each run, Pallas kernels for 0% -> 0%
where the time goes in v1:
time: 685 us; the launch traced here: 673 us
  waiting for transfers between devices  233 us (34%)
  starting transfers between devices  145 us (21%)
  matrix products  119 us (17%)
  other arithmetic  83.5 us (12%)
  local copies, waits for them, and re-layouts  65.3 us (10%)
  between operations  17.2 us (3%)
  loops' own time  10.5 us (2%)
    ppermute x58, waiting for transfers between devices, flip(): lax.ppermute(value, axis_name, [(i, i ^ distance) for i in range(size)])  233 us
    ppermute x58, starting transfers between devices, flip(): lax.ppermute(value, axis_name, [(i, i ^ distance) for i in range(size)])  145 us
    select_n x44, other arithmetic, pick(): return jnp.where(condition, when_true, when_false)  39.3 us
    dot_general x14, matrix products, second_trans(): lax.dot_general(left_side, right_side, (((1,), (1,)), ((), ())), preferre...  34.9 us
    unnamed x322, local copies, waits for them, and re-layouts  34 us
    dot_general x14, matrix products, matrix_product(): return jnp.dot(left_side, right_side, preferred_element_type=jnp.float32)  32.9 us
    dot_general x4, matrix products, first_trans(): lax.dot_general(left_side, right_side, (((0,), (0,)), ((), ())), preferre...  28.5 us
  transfers between devices with their start and end apart: 58, of which 30 were waited for; matrix products, arithmetic and copies ran while one was open for 18% of the time, Pallas kernels for 0%

profile of v1, /device:TPU:0, one launch (start us, length us, event | category | flops | bytes accessed | tf_op | source)
XLA Modules:
  0.0 673.5 jit_solution(5518957983579128027)
XLA Ops:
  35.1 6.9 %collective-permute-done.3 = bf16[240,640]{1,0:T(8,128)(2,1)} collective-permute-done((bf16[240,640]{1,0:T(8,128)(2,1)}, bf16[240,640]{1,0:T(8,128)(2,1)}, u32[]{:S(2)}, u32[]{:S(2)}) %collective-permute-start.3) | collective-permute-done | bytes 307232 | tf_op jit(solution)/shard_map/ppermute | solution.py:235
  56.0 5.9 collective-permute-done.5
  71.3 4.8 collective-permute-done.7
  82.1 7.6 %collective-permute-done.15 = bf16[240,1280]{1,0:T(8,128)(2,1)} collective-permute-done((bf16[240,1280]{1,0:T(8,128)(2,1)}, bf16[240,1280]{1,0:T(8,128)(2,1)}, u32[]{:S(2)}, u32[]{:S(2)}) %collective-permute-start.15) | collective-permute-done | bytes 614432 | tf_op jit(solution)/shard_map/ppermute | solution.py:235
  93.3 8.9 %collective-permute-done.17 = bf16[240,1280]{1,0:T(8,128)(2,1)S(1)} collective-permute-done((bf16[240,1280]{1,0:T(8,128)(2,1)S(1)}, bf16[240,1280]{1,0:T(8,128)(2,1)S(1)}, u32[]{:S(2)}, u32[]{:S(2)}) %collective-permute-start.17) | collective-permute-done | bytes 614432 | tf_op jit(solution)/shard_map/ppermute | solution.py:235
  111.3 7.1 %pad_maximum_fusion.6 = (bf16[960,960]{1,0:T(8,128)(2,1)}, bf16[960,960]{1,0:T(8,128)(2,1)S(1)}) fusion(bf16[240,2560]{1,0:T(8,128)(2,1)S(1)} %get-tuple-element.1218, bf16[240,2560]{1,0:T(8,128)(2,1)S(1)} %get-tuple-element.1217, bf16[240,2560]{1,0:T(8,128)(2,1)S(1)} %get-tuple-element.1216, bf16[240,2560]{1,0:T(8,128)(2,1)S(1)} %get-tuple-element.1215), kind=kLoop, calls=%fused_computation.439 | loop fusion | flops 14745600 | bytes 8601600 | tf_op jit(solution)/shard_map/concatenate | solution.py:296
  120.1 8.1 %collective-permute-done.10 = bf16[256,640]{0,1:T(8,128)(2,1)S(1)} collective-permute-done((bf16[256,640]{0,1:T(8,128)(2,1)S(1)}, bf16[256,640]{0,1:T(8,128)(2,1)S(1)}, u32[]{:S(2)}, u32[]{:S(2)}) %collective-permute-start.10) | collective-permute-done | bytes 327712 | tf_op jit(solution)/shard_map/ppermute | solution.py:235
  128.1 4.8 broadcast_select_fusion.21
  139.1 7.0 %conditional.36 = (f32[256,5,3,64]{0,3,2,1:T(8,128)}) conditional(s32[]{:T(128)} %bitcast.379, () %tuple.272, (pred[256,256]{0,1:T(8,128)(4,1)}, bf16[256,640]{0,1:T(8,128)(2,1)}, bf16[256,5,3,64]{0,3,2,1:T(8,128)(2,1)S(1)}, f32[5,3,256,1]{2,1,0,3:T(4,128)}, f32[5,3,256,1]{2,1,0,3:T(4,128)}) %tuple.278), branch_computations={%region_17.18_spmd, %region_18.19_spmd} | conditional | flops 256573440 | bytes 2684936 | solution.py:157
  150.6 4.5 broadcast_select_fusion.7
  155.1 4.6 pad_maximum_fusion
  163.7 6.6 multiply_convert_fusion.5
  173.6 13.9 %collective-permute-start.23 = (bf16[256,640]{0,1:T(8,128)(2,1)S(1)}, bf16[256,640]{0,1:T(8,128)(2,1)S(1)}, u32[]{:S(2)}, u32[]{:S(2)}) collective-permute-start(bf16[256,640]{0,1:T(8,128)(2,1)S(1)} %pad_maximum_fusion.28), channel_id=1, source_target_pairs={{0,2},{1,3},{2,0},{3,1},{4,6},{5,7},{6,4},{7,5},{8,10},{9,11},{10,... | collective-permute-start | bytes 983048 | tf_op jit(solution)/shard_map/ppermute | solution.py:235
  187.5 24.8 %collective-permute-start.25 = (bf16[256,640]{0,1:T(8,128)(2,1)S(1)}, bf16[256,640]{0,1:T(8,128)(2,1)S(1)}, u32[]{:S(2)}, u32[]{:S(2)}) collective-permute-start(bf16[256,640]{0,1:T(8,128)(2,1)S(1)} %pad_maximum_fusion.28), channel_id=1, source_target_pairs={{0,1},{1,0},{2,3},{3,2},{4,5},{5,4},{6,7},{7,6},{8,9},{9,8},{10,11... | collective-permute-start | bytes 983048 | tf_op jit(solution)/shard_map/ppermute | solution.py:235
  240.5 5.6 multiply_convert_fusion.3
  246.1 4.8 fusion.387
  251.0 4.6 multiply_reduce_fusion.1
  263.1 5.7 conditional.52
  281.1 21.0 %collective-permute-start.26 = (bf16[512,640]{0,1:T(8,128)(2,1)S(1)}, bf16[512,640]{0,1:T(8,128)(2,1)S(1)}, u32[]{:S(2)}, u32[]{:S(2)}) collective-permute-start(bf16[512,640]{0,1:T(8,128)(2,1)S(1)} %pad_maximum_fusion.15), channel_id=1, source_target_pairs={{0,1},{1,0},{2,3},{3,2},{4,5},{5,4},{6,7},{7,6},{8,9},{9,8},{10,11... | collective-permute-start | bytes 1966088 | tf_op jit(solution)/shard_map/ppermute | solution.py:235
  306.1 16.6 %collective-permute-start.27 = (bf16[256,640]{0,1:T(8,128)(2,1)S(1)}, bf16[256,640]{0,1:T(8,128)(2,1)S(1)}, u32[]{:S(2)}, u32[]{:S(2)}) collective-permute-start(bf16[256,640]{0,1:T(8,128)(2,1)S(1)} %get-tuple-element.1122), channel_id=1, source_target_pairs={{0,2},{1,3},{2,0},{3,1},{4,6},{5,7},{6,4},{7,5},{8,10},{9,11},{10,... | collective-permute-start | bytes 983048 | tf_op jit(solution)/shard_map/ppermute | solution.py:235
  323.0 7.7 %collective-permute-done.27 = bf16[256,640]{0,1:T(8,128)(2,1)S(1)} collective-permute-done((bf16[256,640]{0,1:T(8,128)(2,1)S(1)}, bf16[256,640]{0,1:T(8,128)(2,1)S(1)}, u32[]{:S(2)}, u32[]{:S(2)}) %collective-permute-start.27) | collective-permute-done | bytes 327712 | tf_op jit(solution)/shard_map/ppermute | solution.py:235
  337.4 4.8 multiply_convert_fusion.1
  342.2 4.8 fusion.385
  358.7 7.0 %convolution_convert_fusion.1 = bf16[2560,960]{0,1:T(8,128)(2,1)} fusion(bf16[256,2560]{1,0:T(8,128)(2,1)} %copy-done.151, bf16[256,2560]{1,0:T(8,128)(2,1)} %get-tuple-element.1201, bf16[256,960]{0,1:T(8,128)(2,1)} %copy-done.112, bf16[256,960]{0,1:T(8,128)(2,1)} %param.78), kind=kOutput, calls=%fused_computation.369 | convolution fusion | flops 2526248960 | bytes 8519680 | tf_op jit(solution)/shard_map/dot_general | solution.py:21
  365.8 15.3 %convolution_convert_fusion = bf16[960,5120]{1,0:T(8,128)(2,1)} fusion(bf16[256,2560]{1,0:T(8,128)(2,1)} %copy-done.149, bf16[256,2560]{1,0:T(8,128)(2,1)S(1)} %copy-done.147, bf16[256,2560]{1,0:T(8,128)(2,1)} %copy-done.148, bf16[256,2560]{1,0:T(8,128)(2,1)S(1)} %copy-done.145, bf16[256,960]{0,1:T(8,128)(2,1)S(1)} %copy-done.107, ...), kind=kOutput, calls=%fused_computation.365 | convolution fusion | flops 5061017600 | bytes 16056320 | tf_op jit(solution)/shard_map/dot_general | solution.py:21
  383.5 5.7 conditional.60
  391.7 4.5 conditional.63
  399.5 12.4 %collective-permute-start.28 = (bf16[512,640]{0,1:T(8,128)(2,1)S(1)}, bf16[512,640]{0,1:T(8,128)(2,1)S(1)}, u32[]{:S(2)}, u32[]{:S(2)}) collective-permute-start(bf16[512,640]{0,1:T(8,128)(2,1)S(1)} %pad_maximum_fusion.16), channel_id=1, source_target_pairs={{0,1},{1,0},{2,3},{3,2},{4,5},{5,4},{6,7},{7,6},{8,9},{9,8},{10,11... | collective-permute-start | bytes 1966088 | tf_op jit(solution)/shard_map/ppermute | solution.py:235
  419.2 9.1 %collective-permute-start.29 = (bf16[256,640]{0,1:T(8,128)(2,1)S(1)}, bf16[256,640]{0,1:T(8,128)(2,1)S(1)}, u32[]{:S(2)}, u32[]{:S(2)}) collective-permute-start(bf16[256,640]{0,1:T(8,128)(2,1)S(1)} %get-tuple-element.1115), channel_id=1, source_target_pairs={{0,2},{1,3},{2,0},{3,1},{4,6},{5,7},{6,4},{7,5},{8,10},{9,11},{10,... | collective-permute-start | bytes 983048 | tf_op jit(solution)/shard_map/ppermute | solution.py:235
  453.6 4.3 broadcast_select_fusion.30
  458.6 23.4 %collective-permute-done.52 = bf16[640,960]{0,1:T(8,128)(2,1)} collective-permute-done((bf16[640,960]{0,1:T(8,128)(2,1)}, bf16[640,960]{0,1:T(8,128)(2,1)}, u32[]{:S(2)}, u32[]{:S(2)}) %collective-permute-start.52) | collective-permute-done | bytes 1228832 | tf_op jit(solution)/shard_map/ppermute | solution.py:235
  483.9 5.0 collective-permute-start.53
  488.9 19.2 %collective-permute-done.45 = bf16[240,2560]{1,0:T(8,128)(2,1)S(1)} collective-permute-done((bf16[240,2560]{1,0:T(8,128)(2,1)}, bf16[240,2560]{1,0:T(8,128)(2,1)S(1)}, u32[]{:S(2)}, u32[]{:S(2)}) %collective-permute-start.45) | collective-permute-done | bytes 1228832 | tf_op jit(solution)/shard_map/ppermute | solution.py:235
  511.0 4.9 collective-permute-start.46
  518.1 11.6 %collective-permute-done.46 = bf16[240,1280]{1,0:T(8,128)(2,1)S(1)} collective-permute-done((bf16[240,1280]{1,0:T(8,128)(2,1)S(1)}, bf16[240,1280]{1,0:T(8,128)(2,1)S(1)}, u32[]{:S(2)}, u32[]{:S(2)}) %collective-permute-start.46) | collective-permute-done | bytes 614432 | tf_op jit(solution)/shard_map/ppermute | solution.py:235
  531.4 4.8 collective-permute-start.55
  536.1 7.5 %collective-permute-done.47 = bf16[240,640]{1,0:T(8,128)(2,1)S(1)} collective-permute-done((bf16[240,640]{1,0:T(8,128)(2,1)S(1)}, bf16[240,640]{1,0:T(8,128)(2,1)S(1)}, u32[]{:S(2)}, u32[]{:S(2)}) %collective-permute-start.47) | collective-permute-done | bytes 307232 | tf_op jit(solution)/shard_map/ppermute | solution.py:235
  548.6 8.5 %collective-permute-done.55 = bf16[640,240]{0,1:T(8,128)(2,1)S(1)} collective-permute-done((bf16[640,240]{0,1:T(8,128)(2,1)S(1)}, bf16[640,240]{0,1:T(8,128)(2,1)S(1)}, u32[]{:S(2)}, u32[]{:S(2)}) %collective-permute-start.55) | collective-permute-done | bytes 307232 | tf_op jit(solution)/shard_map/ppermute | solution.py:235
  557.2 5.0 collective-permute-done.48
  564.4 4.3 collective-permute-done.56
  569.5 5.7 collective-permute-done.49
  576.4 21.4 %collective-permute-done.50 = bf16[240,1280]{1,0:T(8,128)(2,1)S(1)} collective-permute-done((bf16[240,1280]{1,0:T(8,128)(2,1)S(1)}, bf16[240,1280]{1,0:T(8,128)(2,1)S(1)}, u32[]{:S(2)}, u32[]{:S(2)}) %collective-permute-start.50) | collective-permute-done | bytes 614432 | tf_op jit(solution)/shard_map/ppermute | solution.py:235
  601.8 12.8 %collective-permute-done.34 = bf16[256,640]{1,0:T(8,128)(2,1)S(1)} collective-permute-done((bf16[256,640]{1,0:T(8,128)(2,1)S(1)}, bf16[256,640]{1,0:T(8,128)(2,1)S(1)}, u32[]{:S(2)}, u32[]{:S(2)}) %collective-permute-start.34) | collective-permute-done | bytes 327712 | tf_op jit(solution)/shard_map/ppermute | solution.py:235
  617.1 8.2 %collective-permute-done.35 = bf16[256,640]{1,0:T(8,128)(2,1)S(1)} collective-permute-done((bf16[256,640]{1,0:T(8,128)(2,1)S(1)}, bf16[256,640]{1,0:T(8,128)(2,1)S(1)}, u32[]{:S(2)}, u32[]{:S(2)}) %collective-permute-start.35) | collective-permute-done | bytes 327712 | tf_op jit(solution)/shard_map/ppermute | solution.py:235
  626.1 4.8 collective-permute-done.40
  633.3 13.7 %collective-permute-done.41 = bf16[240,640]{1,0:T(8,128)(2,1)S(1)} collective-permute-done((bf16[240,640]{1,0:T(8,128)(2,1)S(1)}, bf16[240,640]{1,0:T(8,128)(2,1)S(1)}, u32[]{:S(2)}, u32[]{:S(2)}) %collective-permute-start.41) | collective-permute-done | bytes 307232 | tf_op jit(solution)/shard_map/ppermute | solution.py:235
  649.9 6.4 collective-permute-done.42
  659.0 12.3 %collective-permute-done.43 = bf16[240,1280]{1,0:T(8,128)(2,1)S(1)} collective-permute-done((bf16[240,1280]{1,0:T(8,128)(2,1)S(1)}, bf16[240,1280]{1,0:T(8,128)(2,1)S(1)}, u32[]{:S(2)}, u32[]{:S(2)}) %collective-permute-start.43) | collective-permute-done | bytes 614432 | tf_op jit(solution)/shard_map/ppermute | solution.py:235
  (675 shorter events, 263.9 us)
Async XLA Ops:
  2.1 31.9 %collective-permute-start.2 = (bf16[240,2]{0,1:T(2,128)(2,1)S(1)}, bf16[240,2]{0,1:T(2,128)(2,1)S(1)}, u32[]{:S(2)}, u32[]{:S(2)}) collective-permute-start(bf16[240,2]{0,1:T(2,128)(2,1)S(1)} %pad_maximum_fusion.38), channel_id=1, source_target_pairs={{0,1},{1,0},{2,3},{3,2},{4,5},{5,4},{6,7},{7,6},{8,9},{9,8},{10,11... | collective-permute-start | bytes 2888 | tf_op jit(solution)/shard_map/ppermute | solution.py:235
  2.7 26.0 %collective-permute-start = (bf16[240,2]{0,1:T(2,128)(2,1)S(1)}, bf16[240,2]{0,1:T(2,128)(2,1)S(1)}, u32[]{:S(2)}, u32[]{:S(2)}) collective-permute-start(bf16[240,2]{0,1:T(2,128)(2,1)S(1)} %pad_maximum_fusion.38), channel_id=1, source_target_pairs={{0,2},{1,3},{2,0},{3,1},{4,6},{5,7},{6,4},{7,5},{8,10},{9,11},{10,... | collective-permute-start | bytes 2888 | tf_op jit(solution)/shard_map/ppermute | solution.py:235
  5.2 88.1 %collective-permute-start.20 = (bf16[640,960]{0,1:T(8,128)(2,1)}, bf16[640,960]{0,1:T(8,128)(2,1)}, u32[]{:S(2)}, u32[]{:S(2)}) collective-permute-start(bf16[640,960]{0,1:T(8,128)(2,1)} %param.89), channel_id=1, source_target_pairs={{0,2},{1,3},{2,0},{3,1},{4,6},{5,7},{6,4},{7,5},{8,10},{9,11},{10,... | collective-permute-start | bytes 3686408 | tf_op jit(solution)/shard_map/ppermute | solution.py:235
  5.3 114.7 %collective-permute-start.22 = (bf16[640,960]{0,1:T(8,128)(2,1)}, bf16[640,960]{0,1:T(8,128)(2,1)}, u32[]{:S(2)}, u32[]{:S(2)}) collective-permute-start(bf16[640,960]{0,1:T(8,128)(2,1)} %param.89), channel_id=1, source_target_pairs={{0,1},{1,0},{2,3},{3,2},{4,5},{5,4},{6,7},{7,6},{8,9},{9,8},{10,11... | collective-permute-start | bytes 3686408 | tf_op jit(solution)/shard_map/ppermute | solution.py:235
  10.1 31.9 %collective-permute-start.3 = (bf16[240,640]{1,0:T(8,128)(2,1)}, bf16[240,640]{1,0:T(8,128)(2,1)}, u32[]{:S(2)}, u32[]{:S(2)}) collective-permute-start(bf16[240,640]{1,0:T(8,128)(2,1)} %fusion.461), channel_id=1, source_target_pairs={{0,2},{1,3},{2,0},{3,1},{4,6},{5,7},{6,4},{7,5},{8,10},{9,11},{10,... | collective-permute-start | bytes 921608 | tf_op jit(solution)/shard_map/ppermute | solution.py:235
  34.0 20.2 %collective-permute-start.13 = (bf16[240,1280]{1,0:T(8,128)(2,1)}, bf16[240,1280]{1,0:T(8,128)(2,1)S(1)}, u32[]{:S(2)}, u32[]{:S(2)}) collective-permute-start(bf16[240,1280]{1,0:T(8,128)(2,1)} %select_select_fusion), channel_id=1, source_target_pairs={{0,2},{1,3},{2,0},{3,1},{4,6},{5,7},{6,4},{7,5},{8,10},{9,11},{10,... | collective-permute-start | bytes 1843208 | tf_op jit(solution)/shard_map/ppermute | solution.py:235
  48.7 58.9 %collective-permute-start.9 = (bf16[240,2560]{1,0:T(8,128)(2,1)S(1)}, bf16[240,2560]{1,0:T(8,128)(2,1)}, u32[]{:S(2)}, u32[]{:S(2)}) collective-permute-start(bf16[240,2560]{1,0:T(8,128)(2,1)S(1)} %concatenate.230), channel_id=1, source_target_pairs={{0,1},{1,0},{2,3},{3,2},{4,5},{5,4},{6,7},{7,6},{8,9},{9,8},{10,11... | collective-permute-start | bytes 3686408 | tf_op jit(solution)/shard_map/ppermute | solution.py:235
  54.3 12.0 %collective-permute-start.16 = (bf16[240,640]{1,0:T(8,128)(2,1)S(1)}, bf16[240,640]{1,0:T(8,128)(2,1)S(1)}, u32[]{:S(2)}, u32[]{:S(2)}) collective-permute-start(bf16[240,640]{1,0:T(8,128)(2,1)S(1)} %get-tuple-element.1267), channel_id=1, source_target_pairs={{0,8},{4,12},{8,0},{12,4},{16,24},{20,28},{24,16},{28,20},{1,9},{5... | collective-permute-start | bytes 921608 | tf_op jit(solution)/shard_map/ppermute | solution.py:235
  66.4 84.2 %collective-permute-start.19 = (bf16[240,5120]{1,0:T(8,128)(2,1)}, bf16[240,5120]{1,0:T(8,128)(2,1)}, u32[]{:S(2)}, u32[]{:S(2)}) collective-permute-start(bf16[240,5120]{1,0:T(8,128)(2,1)} %constant_dynamic-update-slice_fusion), channel_id=1, source_target_pairs={{0,1},{1,0},{2,3},{3,2},{4,5},{5,4},{6,7},{7,6},{8,9},{9,8},{10,11... | collective-permute-start | bytes 7372808 | tf_op jit(solution)/shard_map/ppermute | solution.py:235
  76.0 13.7 %collective-permute-start.15 = (bf16[240,1280]{1,0:T(8,128)(2,1)}, bf16[240,1280]{1,0:T(8,128)(2,1)}, u32[]{:S(2)}, u32[]{:S(2)}) collective-permute-start(bf16[240,1280]{1,0:T(8,128)(2,1)} %pad_maximum_fusion.18), channel_id=1, source_target_pairs={{0,8},{4,12},{8,0},{12,4},{16,24},{20,28},{24,16},{28,20},{1,9},{5... | collective-permute-start | bytes 1843208 | tf_op jit(solution)/shard_map/ppermute | solution.py:235
  89.7 12.4 %collective-permute-start.17 = (bf16[240,1280]{1,0:T(8,128)(2,1)S(1)}, bf16[240,1280]{1,0:T(8,128)(2,1)S(1)}, u32[]{:S(2)}, u32[]{:S(2)}) collective-permute-start(bf16[240,1280]{1,0:T(8,128)(2,1)S(1)} %pad_maximum_fusion.19), channel_id=1, source_target_pairs={{0,4},{4,0},{8,12},{12,8},{16,20},{20,16},{24,28},{28,24},{1,5},{5... | collective-permute-start | bytes 1843208 | tf_op jit(solution)/shard_map/ppermute | solution.py:235
  93.3 14.8 %collective-permute-start.8 = (bf16[240,2560]{1,0:T(8,128)(2,1)S(1)}, bf16[240,2560]{1,0:T(8,128)(2,1)S(1)}, u32[]{:S(2)}, u32[]{:S(2)}) collective-permute-start(bf16[240,2560]{1,0:T(8,128)(2,1)S(1)} %copy-done.33), channel_id=1, source_target_pairs={{0,1},{1,0},{2,3},{3,2},{4,5},{5,4},{6,7},{7,6},{8,9},{9,8},{10,11... | collective-permute-start | bytes 3686408 | tf_op jit(solution)/shard_map/ppermute | solution.py:235
  102.2 25.9 %collective-permute-start.21 = (bf16[640,960]{0,1:T(8,128)(2,1)}, bf16[640,960]{0,1:T(8,128)(2,1)S(1)}, u32[]{:S(2)}, u32[]{:S(2)}) collective-permute-start(bf16[640,960]{0,1:T(8,128)(2,1)} %collective-permute-done.20), channel_id=1, source_target_pairs={{0,1},{1,0},{2,3},{3,2},{4,5},{5,4},{6,7},{7,6},{8,9},{9,8},{10,11... | collective-permute-start | bytes 3686408 | tf_op jit(solution)/shard_map/ppermute | solution.py:235
  107.6 43.0 %collective-permute-start.18 = (bf16[240,5120]{1,0:T(8,128)(2,1)}, bf16[240,5120]{1,0:T(8,128)(2,1)}, u32[]{:S(2)}, u32[]{:S(2)}) collective-permute-start(bf16[240,5120]{1,0:T(8,128)(2,1)} %slice_dynamic-update-slice_fusion), channel_id=1, source_target_pairs={{0,1},{1,0},{2,3},{3,2},{4,5},{5,4},{6,7},{7,6},{8,9},{9,8},{10,11... | collective-permute-start | bytes 7372808 | tf_op jit(solution)/shard_map/ppermute | solution.py:235
  120.0 12.9 %collective-permute-start.12 = (bf16[256,640]{0,1:T(8,128)(2,1)S(1)}, bf16[256,640]{0,1:T(8,128)(2,1)S(1)}, u32[]{:S(2)}, u32[]{:S(2)}) collective-permute-start(bf16[256,640]{0,1:T(8,128)(2,1)S(1)} %pad_maximum_fusion.27), channel_id=1, source_target_pairs={{0,1},{1,0},{2,3},{3,2},{4,5},{5,4},{6,7},{7,6},{8,9},{9,8},{10,11... | collective-permute-start | bytes 983048 | tf_op jit(solution)/shard_map/ppermute | solution.py:235
  173.6 39.6 %collective-permute-start.23 = (bf16[256,640]{0,1:T(8,128)(2,1)S(1)}, bf16[256,640]{0,1:T(8,128)(2,1)S(1)}, u32[]{:S(2)}, u32[]{:S(2)}) collective-permute-start(bf16[256,640]{0,1:T(8,128)(2,1)S(1)} %pad_maximum_fusion.28), channel_id=1, source_target_pairs={{0,2},{1,3},{2,0},{3,1},{4,6},{5,7},{6,4},{7,5},{8,10},{9,11},{10,... | collective-permute-start | bytes 983048 | tf_op jit(solution)/shard_map/ppermute | solution.py:235
  187.5 29.4 %collective-permute-start.25 = (bf16[256,640]{0,1:T(8,128)(2,1)S(1)}, bf16[256,640]{0,1:T(8,128)(2,1)S(1)}, u32[]{:S(2)}, u32[]{:S(2)}) collective-permute-start(bf16[256,640]{0,1:T(8,128)(2,1)S(1)} %pad_maximum_fusion.28), channel_id=1, source_target_pairs={{0,1},{1,0},{2,3},{3,2},{4,5},{5,4},{6,7},{7,6},{8,9},{9,8},{10,11... | collective-permute-start | bytes 983048 | tf_op jit(solution)/shard_map/ppermute | solution.py:235
  281.1 24.8 %collective-permute-start.26 = (bf16[512,640]{0,1:T(8,128)(2,1)S(1)}, bf16[512,640]{0,1:T(8,128)(2,1)S(1)}, u32[]{:S(2)}, u32[]{:S(2)}) collective-permute-start(bf16[512,640]{0,1:T(8,128)(2,1)S(1)} %pad_maximum_fusion.15), channel_id=1, source_target_pairs={{0,1},{1,0},{2,3},{3,2},{4,5},{5,4},{6,7},{7,6},{8,9},{9,8},{10,11... | collective-permute-start | bytes 1966088 | tf_op jit(solution)/shard_map/ppermute | solution.py:235
  306.1 24.5 %collective-permute-start.27 = (bf16[256,640]{0,1:T(8,128)(2,1)S(1)}, bf16[256,640]{0,1:T(8,128)(2,1)S(1)}, u32[]{:S(2)}, u32[]{:S(2)}) collective-permute-start(bf16[256,640]{0,1:T(8,128)(2,1)S(1)} %get-tuple-element.1122), channel_id=1, source_target_pairs={{0,2},{1,3},{2,0},{3,1},{4,6},{5,7},{6,4},{7,5},{8,10},{9,11},{10,... | collective-permute-start | bytes 983048 | tf_op jit(solution)/shard_map/ppermute | solution.py:235
  399.5 19.3 %collective-permute-start.28 = (bf16[512,640]{0,1:T(8,128)(2,1)S(1)}, bf16[512,640]{0,1:T(8,128)(2,1)S(1)}, u32[]{:S(2)}, u32[]{:S(2)}) collective-permute-start(bf16[512,640]{0,1:T(8,128)(2,1)S(1)} %pad_maximum_fusion.16), channel_id=1, source_target_pairs={{0,1},{1,0},{2,3},{3,2},{4,5},{5,4},{6,7},{7,6},{8,9},{9,8},{10,11... | collective-permute-start | bytes 1966088 | tf_op jit(solution)/shard_map/ppermute | solution.py:235
  416.2 31.3 %collective-permute-start.51 = (bf16[1280,960]{0,1:T(8,128)(2,1)}, bf16[1280,960]{0,1:T(8,128)(2,1)}, u32[]{:S(2)}, u32[]{:S(2)}) collective-permute-start(bf16[1280,960]{0,1:T(8,128)(2,1)} %pad_maximum_fusion.5), channel_id=1, source_target_pairs={{0,1},{1,0},{2,3},{3,2},{4,5},{5,4},{6,7},{7,6},{8,9},{9,8},{10,11... | collective-permute-start | bytes 7372808 | tf_op jit(solution)/shard_map/ppermute | solution.py:235
  419.2 17.5 %collective-permute-start.29 = (bf16[256,640]{0,1:T(8,128)(2,1)S(1)}, bf16[256,640]{0,1:T(8,128)(2,1)S(1)}, u32[]{:S(2)}, u32[]{:S(2)}) collective-permute-start(bf16[256,640]{0,1:T(8,128)(2,1)S(1)} %get-tuple-element.1115), channel_id=1, source_target_pairs={{0,2},{1,3},{2,0},{3,1},{4,6},{5,7},{6,4},{7,5},{8,10},{9,11},{10,... | collective-permute-start | bytes 983048 | tf_op jit(solution)/shard_map/ppermute | solution.py:235
  429.8 23.7 %collective-permute-start.44 = (bf16[480,2560]{1,0:T(8,128)(2,1)}, bf16[480,2560]{1,0:T(8,128)(2,1)}, u32[]{:S(2)}, u32[]{:S(2)}) collective-permute-start(bf16[480,2560]{1,0:T(8,128)(2,1)} %pad_maximum_fusion.4), channel_id=1, source_target_pairs={{0,1},{1,0},{2,3},{3,2},{4,5},{5,4},{6,7},{7,6},{8,9},{9,8},{10,11... | collective-permute-start | bytes 7372808 | tf_op jit(solution)/shard_map/ppermute | solution.py:235
  447.5 68.4 %collective-permute-start.30 = (bf16[512,2560]{1,0:T(8,128)(2,1)S(1)}, bf16[512,2560]{1,0:T(8,128)(2,1)S(1)}, u32[]{:S(2)}, u32[]{:S(2)}) collective-permute-start(bf16[512,2560]{1,0:T(8,128)(2,1)S(1)} %pad_maximum_fusion.2), channel_id=1, source_target_pairs={{0,1},{1,0},{2,3},{3,2},{4,5},{5,4},{6,7},{7,6},{8,9},{9,8},{10,11... | collective-permute-start | bytes 7864328 | tf_op jit(solution)/shard_map/ppermute | solution.py:235
  451.8 30.2 %collective-permute-start.52 = (bf16[640,960]{0,1:T(8,128)(2,1)}, bf16[640,960]{0,1:T(8,128)(2,1)}, u32[]{:S(2)}, u32[]{:S(2)}) collective-permute-start(bf16[640,960]{0,1:T(8,128)(2,1)} %get-tuple-element.1101), channel_id=1, source_target_pairs={{0,2},{1,3},{2,0},{3,1},{4,6},{5,7},{6,4},{7,5},{8,10},{9,11},{10,... | collective-permute-start | bytes 3686408 | tf_op jit(solution)/shard_map/ppermute | solution.py:235
  457.9 50.2 %collective-permute-start.45 = (bf16[240,2560]{1,0:T(8,128)(2,1)}, bf16[240,2560]{1,0:T(8,128)(2,1)S(1)}, u32[]{:S(2)}, u32[]{:S(2)}) collective-permute-start(bf16[240,2560]{1,0:T(8,128)(2,1)} %get-tuple-element.1104), channel_id=1, source_target_pairs={{0,2},{1,3},{2,0},{3,1},{4,6},{5,7},{6,4},{7,5},{8,10},{9,11},{10,... | collective-permute-start | bytes 3686408 | tf_op jit(solution)/shard_map/ppermute | solution.py:235
  458.4 104.0 %collective-permute-start.37 = (bf16[480,2560]{1,0:T(8,128)(2,1)S(1)}, bf16[480,2560]{1,0:T(8,128)(2,1)S(1)}, u32[]{:S(2)}, u32[]{:S(2)}) collective-permute-start(bf16[480,2560]{1,0:T(8,128)(2,1)S(1)} %pad_maximum_fusion.3), channel_id=1, source_target_pairs={{0,1},{1,0},{2,3},{3,2},{4,5},{5,4},{6,7},{7,6},{8,9},{9,8},{10,11... | collective-permute-start | bytes 7372808 | tf_op jit(solution)/shard_map/ppermute | solution.py:235
  483.9 33.8 %collective-permute-start.53 = (bf16[640,480]{0,1:T(8,128)(2,1)S(1)}, bf16[640,480]{0,1:T(8,128)(2,1)S(1)}, u32[]{:S(2)}, u32[]{:S(2)}) collective-permute-start(bf16[640,480]{0,1:T(8,128)(2,1)S(1)} %broadcast_select_fusion.41), channel_id=1, source_target_pairs={{0,4},{4,0},{8,12},{12,8},{16,20},{20,16},{24,28},{28,24},{1,5},{5... | collective-permute-start | bytes 1843208 | tf_op jit(solution)/shard_map/ppermute | solution.py:235
  511.0 18.8 %collective-permute-start.46 = (bf16[240,1280]{1,0:T(8,128)(2,1)S(1)}, bf16[240,1280]{1,0:T(8,128)(2,1)S(1)}, u32[]{:S(2)}, u32[]{:S(2)}) collective-permute-start(bf16[240,1280]{1,0:T(8,128)(2,1)S(1)} %broadcast_select_fusion.43), channel_id=1, source_target_pairs={{0,4},{4,0},{8,12},{12,8},{16,20},{20,16},{24,28},{28,24},{1,5},{5... | collective-permute-start | bytes 1843208 | tf_op jit(solution)/shard_map/ppermute | solution.py:235
  517.3 30.3 %collective-permute-start.31 = (bf16[256,2560]{1,0:T(8,128)(2,1)S(1)}, bf16[256,2560]{1,0:T(8,128)(2,1)S(1)}, u32[]{:S(2)}, u32[]{:S(2)}) collective-permute-start(bf16[256,2560]{1,0:T(8,128)(2,1)S(1)} %get-tuple-element.1110), channel_id=1, source_target_pairs={{0,2},{1,3},{2,0},{3,1},{4,6},{5,7},{6,4},{7,5},{8,10},{9,11},{10,... | collective-permute-start | bytes 3932168 | tf_op jit(solution)/shard_map/ppermute | solution.py:235
  518.1 13.2 %collective-permute-start.54 = (bf16[640,240]{0,1:T(8,128)(2,1)S(1)}, bf16[640,240]{0,1:T(8,128)(2,1)S(1)}, u32[]{:S(2)}, u32[]{:S(2)}) collective-permute-start(bf16[640,240]{0,1:T(8,128)(2,1)S(1)} %broadcast_select_fusion.79), channel_id=1, source_target_pairs={{0,8},{4,12},{8,0},{12,4},{16,24},{20,28},{24,16},{28,20},{1,9},{5... | collective-permute-start | bytes 921608 | tf_op jit(solution)/shard_map/ppermute | solution.py:235
  530.0 13.6 %collective-permute-start.47 = (bf16[240,640]{1,0:T(8,128)(2,1)S(1)}, bf16[240,640]{1,0:T(8,128)(2,1)S(1)}, u32[]{:S(2)}, u32[]{:S(2)}) collective-permute-start(bf16[240,640]{1,0:T(8,128)(2,1)S(1)} %broadcast_select_fusion.86), channel_id=1, source_target_pairs={{0,8},{4,12},{8,0},{12,4},{16,24},{20,28},{24,16},{28,20},{1,9},{5... | collective-permute-start | bytes 921608 | tf_op jit(solution)/shard_map/ppermute | solution.py:235
  531.4 25.7 %collective-permute-start.55 = (bf16[640,240]{0,1:T(8,128)(2,1)S(1)}, bf16[640,240]{0,1:T(8,128)(2,1)S(1)}, u32[]{:S(2)}, u32[]{:S(2)}) collective-permute-start(bf16[640,240]{0,1:T(8,128)(2,1)S(1)} %add_convert_fusion.25), channel_id=1, source_target_pairs={{0,16},{4,20},{8,24},{12,28},{16,0},{20,4},{24,8},{28,12},{1,17},{... | collective-permute-start | bytes 921608 | tf_op jit(solution)/shard_map/ppermute | solution.py:235
  543.8 18.4 %collective-permute-start.48 = (bf16[240,640]{1,0:T(8,128)(2,1)S(1)}, bf16[240,640]{1,0:T(8,128)(2,1)S(1)}, u32[]{:S(2)}, u32[]{:S(2)}) collective-permute-start(bf16[240,640]{1,0:T(8,128)(2,1)S(1)} %add_convert_fusion.27), channel_id=1, source_target_pairs={{0,16},{4,20},{8,24},{12,28},{16,0},{20,4},{24,8},{28,12},{1,17},{... | collective-permute-start | bytes 921608 | tf_op jit(solution)/shard_map/ppermute | solution.py:235
  548.2 27.8 %collective-permute-start.32 = (bf16[256,1280]{1,0:T(8,128)(2,1)S(1)}, bf16[256,1280]{1,0:T(8,128)(2,1)S(1)}, u32[]{:S(2)}, u32[]{:S(2)}) collective-permute-start(bf16[256,1280]{1,0:T(8,128)(2,1)S(1)} %broadcast_select_fusion.38), channel_id=1, source_target_pairs={{0,4},{4,0},{8,12},{12,8},{16,20},{20,16},{24,28},{28,24},{1,5},{5... | collective-permute-start | bytes 1966088 | tf_op jit(solution)/shard_map/ppermute | solution.py:235
  557.1 11.6 %collective-permute-start.56 = (bf16[640,240]{0,1:T(8,128)(2,1)S(1)}, bf16[640,240]{0,1:T(8,128)(2,1)S(1)}, u32[]{:S(2)}, u32[]{:S(2)}) collective-permute-start(bf16[640,240]{0,1:T(8,128)(2,1)S(1)} %add_convert_fusion.24), channel_id=1, source_target_pairs={{0,8},{4,12},{8,0},{12,4},{16,24},{20,28},{24,16},{28,20},{1,9},{5... | collective-permute-start | bytes 921608 | tf_op jit(solution)/shard_map/ppermute | solution.py:235
  562.2 13.0 %collective-permute-start.49 = (bf16[240,640]{1,0:T(8,128)(2,1)S(1)}, bf16[240,640]{1,0:T(8,128)(2,1)S(1)}, u32[]{:S(2)}, u32[]{:S(2)}) collective-permute-start(bf16[240,640]{1,0:T(8,128)(2,1)S(1)} %add_convert_fusion.26), channel_id=1, source_target_pairs={{0,8},{4,12},{8,0},{12,4},{16,24},{20,28},{24,16},{28,20},{1,9},{5... | collective-permute-start | bytes 921608 | tf_op jit(solution)/shard_map/ppermute | solution.py:235
  563.7 35.0 %collective-permute-start.38 = (bf16[240,2560]{1,0:T(8,128)(2,1)S(1)}, bf16[240,2560]{1,0:T(8,128)(2,1)S(1)}, u32[]{:S(2)}, u32[]{:S(2)}) collective-permute-start(bf16[240,2560]{1,0:T(8,128)(2,1)S(1)} %get-tuple-element.1107), channel_id=1, source_target_pairs={{0,2},{1,3},{2,0},{3,1},{4,6},{5,7},{6,4},{7,5},{8,10},{9,11},{10,... | collective-permute-start | bytes 3686408 | tf_op jit(solution)/shard_map/ppermute | solution.py:235
  568.9 31.1 %collective-permute-start.57 = (bf16[640,480]{0,1:T(8,128)(2,1)S(1)}, bf16[640,480]{0,1:T(8,128)(2,1)S(1)}, u32[]{:S(2)}, u32[]{:S(2)}) collective-permute-start(bf16[640,480]{0,1:T(8,128)(2,1)S(1)} %pad_maximum_fusion.22), channel_id=1, source_target_pairs={{0,4},{4,0},{8,12},{12,8},{16,20},{20,16},{24,28},{28,24},{1,5},{5... | collective-permute-start | bytes 1843208 | tf_op jit(solution)/shard_map/ppermute | solution.py:235
  575.4 22.4 %collective-permute-start.50 = (bf16[240,1280]{1,0:T(8,128)(2,1)S(1)}, bf16[240,1280]{1,0:T(8,128)(2,1)S(1)}, u32[]{:S(2)}, u32[]{:S(2)}) collective-permute-start(bf16[240,1280]{1,0:T(8,128)(2,1)S(1)} %pad_maximum_fusion.21), channel_id=1, source_target_pairs={{0,4},{4,0},{8,12},{12,8},{16,20},{20,16},{24,28},{28,24},{1,5},{5... | collective-permute-start | bytes 1843208 | tf_op jit(solution)/shard_map/ppermute | solution.py:235
  576.3 21.7 %collective-permute-start.33 = (bf16[256,640]{1,0:T(8,128)(2,1)S(1)}, bf16[256,640]{1,0:T(8,128)(2,1)S(1)}, u32[]{:S(2)}, u32[]{:S(2)}) collective-permute-start(bf16[256,640]{1,0:T(8,128)(2,1)S(1)} %broadcast_select_fusion.54), channel_id=1, source_target_pairs={{0,8},{4,12},{8,0},{12,4},{16,24},{20,28},{24,16},{28,20},{1,9},{5... | collective-permute-start | bytes 983048 | tf_op jit(solution)/shard_map/ppermute | solution.py:235
  598.2 16.4 %collective-permute-start.34 = (bf16[256,640]{1,0:T(8,128)(2,1)S(1)}, bf16[256,640]{1,0:T(8,128)(2,1)S(1)}, u32[]{:S(2)}, u32[]{:S(2)}) collective-permute-start(bf16[256,640]{1,0:T(8,128)(2,1)S(1)} %add_convert_fusion.17), channel_id=1, source_target_pairs={{0,16},{4,20},{8,24},{12,28},{16,0},{20,4},{24,8},{28,12},{1,17},{... | collective-permute-start | bytes 983048 | tf_op jit(solution)/shard_map/ppermute | solution.py:235
  599.3 15.5 %collective-permute-start.39 = (bf16[240,1280]{1,0:T(8,128)(2,1)S(1)}, bf16[240,1280]{1,0:T(8,128)(2,1)S(1)}, u32[]{:S(2)}, u32[]{:S(2)}) collective-permute-start(bf16[240,1280]{1,0:T(8,128)(2,1)S(1)} %broadcast_select_fusion.46), channel_id=1, source_target_pairs={{0,4},{4,0},{8,12},{12,8},{16,20},{20,16},{24,28},{28,24},{1,5},{5... | collective-permute-start | bytes 1843208 | tf_op jit(solution)/shard_map/ppermute | solution.py:235
  614.7 10.6 %collective-permute-start.35 = (bf16[256,640]{1,0:T(8,128)(2,1)S(1)}, bf16[256,640]{1,0:T(8,128)(2,1)S(1)}, u32[]{:S(2)}, u32[]{:S(2)}) collective-permute-start(bf16[256,640]{1,0:T(8,128)(2,1)S(1)} %add_convert_fusion.16), channel_id=1, source_target_pairs={{0,8},{4,12},{8,0},{12,4},{16,24},{20,28},{24,16},{28,20},{1,9},{5... | collective-permute-start | bytes 983048 | tf_op jit(solution)/shard_map/ppermute | solution.py:235
  615.0 15.9 %collective-permute-start.40 = (bf16[240,640]{1,0:T(8,128)(2,1)S(1)}, bf16[240,640]{1,0:T(8,128)(2,1)S(1)}, u32[]{:S(2)}, u32[]{:S(2)}) collective-permute-start(bf16[240,640]{1,0:T(8,128)(2,1)S(1)} %broadcast_select_fusion.89), channel_id=1, source_target_pairs={{0,8},{4,12},{8,0},{12,4},{16,24},{20,28},{24,16},{28,20},{1,9},{5... | collective-permute-start | bytes 921608 | tf_op jit(solution)/shard_map/ppermute | solution.py:235
  625.4 21.7 %collective-permute-start.36 = (bf16[256,1280]{1,0:T(8,128)(2,1)S(1)}, bf16[256,1280]{1,0:T(8,128)(2,1)S(1)}, u32[]{:S(2)}, u32[]{:S(2)}) collective-permute-start(bf16[256,1280]{1,0:T(8,128)(2,1)S(1)} %pad_maximum_fusion.17), channel_id=1, source_target_pairs={{0,4},{4,0},{8,12},{12,8},{16,20},{20,16},{24,28},{28,24},{1,5},{5... | collective-permute-start | bytes 1966088 | tf_op jit(solution)/shard_map/ppermute | solution.py:235
  631.1 15.9 %collective-permute-start.41 = (bf16[240,640]{1,0:T(8,128)(2,1)S(1)}, bf16[240,640]{1,0:T(8,128)(2,1)S(1)}, u32[]{:S(2)}, u32[]{:S(2)}) collective-permute-start(bf16[240,640]{1,0:T(8,128)(2,1)S(1)} %add_convert_fusion.29), channel_id=1, source_target_pairs={{0,16},{4,20},{8,24},{12,28},{16,0},{20,4},{24,8},{28,12},{1,17},{... | collective-permute-start | bytes 921608 | tf_op jit(solution)/shard_map/ppermute | solution.py:235
  656.4 14.9 %collective-permute-start.43 = (bf16[240,1280]{1,0:T(8,128)(2,1)S(1)}, bf16[240,1280]{1,0:T(8,128)(2,1)S(1)}, u32[]{:S(2)}, u32[]{:S(2)}) collective-permute-start(bf16[240,1280]{1,0:T(8,128)(2,1)S(1)} %pad_maximum_fusion.20), channel_id=1, source_target_pairs={{0,4},{4,0},{8,12},{12,8},{16,20},{20,16},{24,28},{28,24},{1,5},{5... | collective-permute-start | bytes 1843208 | tf_op jit(solution)/shard_map/ppermute | solution.py:235
  (161 other events, 1558.1 us)

commit v2 on v0

v2 whole, which is shorter than its diff:
```python
import functools

import jax
import jax.numpy as jnp
from jax import lax
from jax.experimental import pallas as pl
from jax.experimental.pallas import tpu as pltpu
from jax.sharding import PartitionSpec as P

QUERY_HEADS = 15
KEY_VALUE_HEADS = 5
HEAD_SIZE = 64
SHARING = QUERY_HEADS // KEY_VALUE_HEADS
HALF = HEAD_SIZE // 2

epsilon = 1e-05
rope_base = 10000.0
masked = -1e30
score_scale = HEAD_SIZE ** (-0.5)

bf16 = jnp.bfloat16
f32 = jnp.float32
VMEM_BYTES = 56 * 1024 * 1024
GAIN_ROWS = 16


def nn(left, right):
    return jnp.dot(left, right, preferred_element_type=f32)


def nt(left, right):
    return lax.dot_general(left, right, (((1,), (1,)), ((), ())), preferred_element_type=f32)


def in_vmem():
    return pl.BlockSpec(memory_space=pltpu.VMEM)


def in_smem():
    return pl.BlockSpec(memory_space=pltpu.SMEM)


def anywhere():
    return pl.BlockSpec(memory_space=pl.ANY)


def params():
    return pltpu.CompilerParams(vmem_limit_bytes=VMEM_BYTES)


def shape(dims, dtype):
    return jax.ShapeDtypeStruct(dims, dtype)


def cost(flops, bytes_accessed):
    return pl.CostEstimate(flops=int(flops), bytes_accessed=int(bytes_accessed), transcendentals=0)


def inverse_rms(hidden):
    return lax.rsqrt(jnp.mean(hidden * hidden, axis=-1, keepdims=True) + epsilon)


def pack_kernel(
    bits_ref, query_ref, key_ref, value_ref, out_ref, gate_hbm, up_hbm, packed_ref, mine_ref, gate_ref,
    up_ref, sems,
):
    half = gate_ref.shape[1]
    loads = [
        pltpu.make_async_copy(
            source.at[:, pl.ds(pl.multiple_of(bits_ref[i] * half, 128), half)], target, sems.at[i]
        )
        for i, (source, target) in enumerate(((gate_hbm, gate_ref), (up_hbm, up_ref)))
    ]
    for load in loads:
        load.start()
    packed_ref[...] = jnp.concatenate(
        [
            query_ref[...].astype(f32),
            key_ref[...].astype(f32).T,
            value_ref[...].astype(f32).T,
            out_ref[...].astype(f32),
        ],
        axis=1,
    ).astype(bf16)
    wide = mine_ref.shape[1]
    mine_ref[...] = packed_ref[:, pl.ds(pl.multiple_of(bits_ref[0] * wide, 128), wide)]
    for load in loads:
        load.wait()


def pack(bits, query, key_t, value_t, out, gate, up):
    rows, width = query.shape
    columns = 2 * width + 2 * key_t.shape[0]
    return pl.pallas_call(
        pack_kernel,
        out_shape=(
            shape((rows, columns), bf16),
            shape((rows, columns // 2), bf16),
        )
        + (shape((rows, gate.shape[1] // 2), bf16),) * 2,
        in_specs=[in_smem()] + [in_vmem()] * 4 + [anywhere()] * 2,
        out_specs=(in_vmem(),) * 4,
        scratch_shapes=[pltpu.SemaphoreType.DMA((2,))],
        compiler_params=params(),
        cost_estimate=cost(0, 8 * rows * columns),
        name="pack",
    )(bits, query, key_t, value_t, out, gate, up)


def piece_copies(plan, bits_ref, sources, target_ref, sems):
    me = bits_ref[2]
    copies = []
    for i, (which, member, column, part, bit) in enumerate(plan):
        source = sources[which]
        height, width = source.shape
        if column is None:
            turned = pl.ds(pl.multiple_of((me ^ member) * width, 128), width)
            if part is None:
                rows = pl.ds(0, height)
            else:
                rows = pl.ds(pl.multiple_of((bits_ref[bit] ^ part) * height, 16), height)
            target = target_ref.at[rows, turned]
        else:
            rows = pl.ds(pl.multiple_of((me ^ member) * height, 16), height)
            if part is None:
                columns = pl.ds(column, width)
            else:
                columns = pl.ds(
                    pl.multiple_of(column + (bits_ref[bit] ^ part) * width, 128), width
                )
            target = target_ref.at[rows, columns]
        copies.append(pltpu.make_async_copy(source, target, sems.at[i]))
    return copies


def shared_plan(first, column, bit):
    return (
        (first, 0, column, None, bit),
        (first + 1, 1, column, None, bit),
        (first + 2, 2, column, 0, bit),
        (first + 3, 2, column, 1, bit),
        (first + 4, 3, column, 0, bit),
        (first + 5, 3, column, 1, bit),
    )


def enter_body(hidden, gain_ref, cos_ref, sin_ref, ready, normed_ref, q_ref, kv_ref, w_ref):
    width = hidden.shape[1]
    key_width = kv_ref.shape[0] // 2
    mixed_width = width + key_width
    wide = width + 2 * key_width + HEAD_SIZE
    normed = (hidden * inverse_rms(hidden) * gain_ref[...]).astype(bf16)
    normed_ref[...] = normed
    cos, sin = cos_ref[...], sin_ref[...]
    ready()
    mixed = nn(normed, w_ref[:, :mixed_width]).T
    for head in range(QUERY_HEADS + KEY_VALUE_HEADS):
        low = head * HEAD_SIZE
        first = mixed[low : low + HALF]
        second = mixed[low + HALF : low + HEAD_SIZE]
        top = first * cos - second * sin
        bottom = second * cos + first * sin
        if head < QUERY_HEADS:
            q_ref[low : low + HALF, :] = (top * score_scale).astype(bf16)
            q_ref[low + HALF : low + HEAD_SIZE, :] = (bottom * score_scale).astype(bf16)
        else:
            low = low - width
            kv_ref[low : low + HALF, :] = top.astype(bf16)
            kv_ref[low + HALF : low + HEAD_SIZE, :] = bottom.astype(bf16)
    values = nn(normed, w_ref[:, mixed_width:wide]).T
    kv_ref[key_width:, :] = values[:key_width].astype(bf16)


def enter_first_kernel(plan, count, index_ref, h_ref, gain_ref, cos_ref, sin_ref, *refs):
    sources = refs[:count]
    hidden_ref, normed_ref, q_ref, kv_ref, w_hbm, w_ref, sems, out_sem = refs[count:]
    copies = piece_copies(plan, index_ref, sources, w_ref, sems)
    for copy in copies:
        copy.start()
    hidden = h_ref[...].astype(f32).T
    hidden_ref[...] = hidden
    out = pltpu.make_async_copy(w_ref, w_hbm, out_sem)

    def ready():
        for copy in copies:
            copy.wait()
        out.start()

    enter_body(hidden, gain_ref, cos_ref, sin_ref, ready, normed_ref, q_ref, kv_ref, w_ref)
    out.wait()


def enter_first(index, hidden_t, gain, cos, sin, plan, sources):
    width, rows = hidden_t.shape
    key_width = KEY_VALUE_HEADS * HEAD_SIZE
    columns = 2 * (width + key_width)
    return pl.pallas_call(
        functools.partial(enter_first_kernel, plan, len(sources)),
        out_shape=(
            shape((rows, width), f32),
            shape((rows, width), bf16),
            shape((width, rows), bf16),
            shape((2 * key_width, rows), bf16),
            shape((width, columns), bf16),
        ),
        in_specs=[in_smem()] + [in_vmem()] * 4 + [anywhere()] * len(sources),
        out_specs=(in_vmem(),) * 4 + (anywhere(),),
        scratch_shapes=[
            pltpu.VMEM((width, columns), bf16),
            pltpu.SemaphoreType.DMA((len(plan),)),
            pltpu.SemaphoreType.DMA,
        ],
        compiler_params=params(),
        cost_estimate=cost(4 * rows * width * width, width * columns * 4),
        name="enter_first",
    )(index, hidden_t, gain, cos, sin, *sources)


def enter_kernel(h_ref, gain_ref, cos_ref, sin_ref, w_hbm, normed_ref, q_ref, kv_ref, w_ref, sem):
    load = pltpu.make_async_copy(w_hbm.at[:, pl.ds(0, w_ref.shape[1])], w_ref, sem)
    load.start()
    enter_body(
        h_ref[...], gain_ref, cos_ref, sin_ref, load.wait, normed_ref, q_ref, kv_ref, w_ref
    )


def enter(hidden, gain, cos, sin, weights_a):
    rows, width = hidden.shape
    key_width = KEY_VALUE_HEADS * HEAD_SIZE
    wide = width + 2 * key_width + HEAD_SIZE
    return pl.pallas_call(
        enter_kernel,
        out_shape=(
            shape((rows, width), bf16),
            shape((width, rows), bf16),
            shape((2 * key_width, rows), bf16),
        ),
        in_specs=[in_vmem()] * 4 + [anywhere()],
        out_specs=(in_vmem(),) * 3,
        scratch_shapes=[pltpu.VMEM((width, wide), bf16), pltpu.SemaphoreType.DMA],
        compiler_params=params(),
        cost_estimate=cost(2 * rows * width * wide, width * wide * 2 + rows * width * 10),
        name="enter",
    )(hidden, gain, cos, sin, weights_a)


def stacked_heads(ref, group):
    parts = []
    for j in range(SHARING):
        low = (group * SHARING + j) * HEAD_SIZE
        parts.append(ref[low : low + HEAD_SIZE, :])
    return jnp.concatenate(parts, axis=1)


def key_block(ref, group):
    return ref[group * HEAD_SIZE : (group + 1) * HEAD_SIZE, :]


def value_block(ref, group):
    key_width = KEY_VALUE_HEADS * HEAD_SIZE
    return ref[key_width + group * HEAD_SIZE : key_width + (group + 1) * HEAD_SIZE, :]


def causal(rows):
    keys = lax.broadcasted_iota(jnp.int32, (rows, SHARING * rows), 0)
    queries = lax.broadcasted_iota(jnp.int32, (rows, SHARING * rows), 1) % rows
    return keys <= queries


def forward_kernel(plans, counts, *refs):
    (visible_ref, index_ref, h_ref, q_ref, kv0_ref, kv1_ref, kv2_ref, kv3_ref, gain_ref, a_hbm) = refs[:10]
    gu_sources = refs[10 : 10 + counts[0]]
    dn_sources = refs[10 + counts[0] : 10 + counts[0] + counts[1]]
    refs = refs[10 + counts[0] + counts[1] :]
    (out_ref, att_ref, att_t_ref, lse_ref, middle_ref, nf_ref, gating_ref, upward_ref, inner_ref) = refs[:9]
    refs = refs[9:]
    first = plans is not None
    if first:
        gu_hbm, dn_hbm = refs[:2]
        refs = refs[2:]
    (wo_ref, gu_ref, dn_ref, acc_ref, m_ref, l_ref, wo_sem, gu_sems, dn_sems) = refs
    rows, width = h_ref.shape
    ffn = inner_ref.shape[1]
    wo_wide = wo_ref.shape[1]
    wo_load = pltpu.make_async_copy(
        a_hbm.at[:, pl.ds(a_hbm.shape[1] - wo_wide, wo_wide)], wo_ref, wo_sem
    )
    if first:
        gu_loads = piece_copies(plans[0], index_ref, gu_sources, gu_ref, gu_sems)
        dn_loads = piece_copies(plans[1], index_ref, dn_sources, dn_ref, dn_sems)
    else:
        gu_loads = [pltpu.make_async_copy(gu_sources[0], gu_ref, gu_sems.at[0])]
        dn_loads = [pltpu.make_async_copy(dn_sources[0], dn_ref, dn_sems.at[0])]
    for load in [wo_load] + gu_loads + dn_loads:
        load.start()

    allowed = causal(rows)
    for group in range(KEY_VALUE_HEADS):
        scores = nn(key_block(kv0_ref, group).T, stacked_heads(q_ref, group))
        scores = jnp.where(allowed, scores, masked)
        peak = jnp.max(scores, axis=0, keepdims=True)
        raised = jnp.exp(scores - peak)
        m_ref[group : group + 1, :] = peak
        l_ref[group : group + 1, :] = jnp.sum(raised, axis=0, keepdims=True)
        acc_ref[group] = nn(value_block(kv0_ref, group), raised.astype(bf16))
    for member, kv_ref in ((1, kv1_ref), (2, kv2_ref), (3, kv3_ref)):

        @pl.when(visible_ref[member] == 1)
        def _(kv_ref=kv_ref):
            for group in range(KEY_VALUE_HEADS):
                scores = nn(key_block(kv_ref, group).T, stacked_heads(q_ref, group))
                old = m_ref[group : group + 1, :]
                peak = jnp.maximum(old, jnp.max(scores, axis=0, keepdims=True))
                raised = jnp.exp(scores - peak)
                fade = jnp.exp(old - peak)
                m_ref[group : group + 1, :] = peak
                l_ref[group : group + 1, :] = l_ref[group : group + 1, :] * fade + jnp.sum(
                    raised, axis=0, keepdims=True
                )
                acc_ref[group] = acc_ref[group] * fade + nn(
                    value_block(kv_ref, group), raised.astype(bf16)
                )

    total = l_ref[...]
    lse_ref[...] = m_ref[...] + jnp.log(total)
    for group in range(KEY_VALUE_HEADS):
        mean = acc_ref[group] / total[group : group + 1, :]
        for j in range(SHARING):
            low = (group * SHARING + j) * HEAD_SIZE
            att_t_ref[low : low + HEAD_SIZE, :] = mean[:, j * rows : (j + 1) * rows].astype(bf16)
    attended = att_t_ref[...].T
    att_ref[...] = attended
    wo_load.wait()
    middle = h_ref[...] + nn(attended, wo_ref[...])[:, wo_wide - width :]
    middle_ref[...] = middle
    normed = (middle * inverse_rms(middle) * gain_ref[...]).astype(bf16)
    nf_ref[...] = normed
    for load in gu_loads:
        load.wait()
    if first:
        gu_out = pltpu.make_async_copy(gu_ref, gu_hbm, gu_sems.at[0])
        gu_out.start()
    step = 512
    for low in range(0, ffn, step):
        gating = nn(normed, gu_ref[:, low : low + step])
        upward = nn(normed, gu_ref[:, ffn + low : ffn + low + step])
        gating_ref[:, low : low + step] = gating.astype(bf16)
        upward_ref[:, low : low + step] = upward.astype(bf16)
        inner_ref[:, low : low + step] = (gating * jax.nn.sigmoid(gating) * upward).astype(bf16)
    for load in dn_loads:
        load.wait()
    if first:
        dn_out = pltpu.make_async_copy(dn_ref, dn_hbm, dn_sems.at[0])
        dn_out.start()
    finished = middle + nt(inner_ref[...], dn_ref[...])
    if first:
        out_ref[...] = finished
        gu_out.wait()
        dn_out.wait()
    else:
        out_ref[...] = finished.T.astype(bf16)


def forward_block(visible, index, hidden, q, kvs, gain, weights_a, gu, dn, plans=None):
    rows, width = hidden.shape
    ffn = gu[0].shape[1] if plans is not None else gu[0].shape[1] // 2
    wo_wide = width + HEAD_SIZE
    lanes = SHARING * rows
    counts = (len(gu), len(dn))
    first = plans is not None
    whole = (shape((width, 2 * ffn), bf16), shape((width, ffn), bf16))
    return pl.pallas_call(
        functools.partial(forward_kernel, plans, counts),
        out_shape=(
            shape((rows, width), f32) if first else shape((width, rows), bf16),
            shape((rows, width), bf16),
            shape((width, rows), bf16),
            shape((KEY_VALUE_HEADS, lanes), f32),
            shape((rows, width), f32),
            shape((rows, width), bf16),
            shape((rows, ffn), bf16),
            shape((rows, ffn), bf16),
            shape((rows, ffn), bf16),
        )
        + (whole if first else ()),
        in_specs=[in_smem()] * 2 + [in_vmem()] * 7 + [anywhere()] * (1 + sum(counts)),
        out_specs=(in_vmem(),) * 9 + ((anywhere(),) * 2 if first else ()),
        scratch_shapes=[
            pltpu.VMEM((width, wo_wide), bf16),
            pltpu.VMEM((width, 2 * ffn), bf16),
            pltpu.VMEM((width, ffn), bf16),
            pltpu.VMEM((KEY_VALUE_HEADS, HEAD_SIZE, lanes), f32),
            pltpu.VMEM((KEY_VALUE_HEADS, lanes), f32),
            pltpu.VMEM((KEY_VALUE_HEADS, lanes), f32),
            pltpu.SemaphoreType.DMA,
            pltpu.SemaphoreType.DMA((len(plans[0]) if first else 1,)),
            pltpu.SemaphoreType.DMA((len(plans[1]) if first else 1,)),
        ],
        compiler_params=params(),
        cost_estimate=cost(2 * rows * width * (4 * ffn), 3 * width * ffn * 2 + rows * ffn * 8),
        name="forward_first" if first else "forward_last",
    )(visible, index, hidden, q, *kvs, gain, weights_a, *gu, *dn)


def feed_back_kernel(
    g_ref,
    middle_ref,
    gating_ref,
    upward_ref,
    gain_ref,
    a_hbm,
    gu_hbm,
    dn_hbm,
    gb_ref,
    dgu_ref,
    dmid_ref,
    gm_ref,
    do_ref,
    dgain_ref,
    wo_ref,
    gu_ref,
    dn_ref,
    sum_ref,
    sems,
):
    rows, width = middle_ref.shape
    ffn = gating_ref.shape[1]
    wo_wide = wo_ref.shape[1]
    loads = [
        pltpu.make_async_copy(dn_hbm, dn_ref, sems.at[0]),
        pltpu.make_async_copy(gu_hbm, gu_ref, sems.at[1]),
        pltpu.make_async_copy(
            a_hbm.at[:, pl.ds(a_hbm.shape[1] - wo_wide, wo_wide)], wo_ref, sems.at[2]
        ),
    ]
    for load in loads:
        load.start()
    grad = g_ref[...] if g_ref.shape[0] == rows else g_ref[...].astype(f32).T
    short = grad.astype(bf16)
    gb_ref[...] = short
    loads[0].wait()
    step = 512
    for low in range(0, ffn, step):
        part = slice(low, low + step)
        behind = slice(ffn + low, ffn + low + step)
        d_inner = nn(short, dn_ref[:, part])
        gating = gating_ref[:, part].astype(f32)
        upward = upward_ref[:, part].astype(f32)
        gate = jax.nn.sigmoid(gating)
        d_gating = (d_inner * upward * (gate * (1.0 + gating * (1.0 - gate)))).astype(bf16)
        d_upward = (d_inner * (gating * gate)).astype(bf16)
        dgu_ref[:, part] = d_gating
        dgu_ref[:, behind] = d_upward
        if low == 0:
            loads[1].wait()
            sum_ref[...] = nt(d_gating, gu_ref[:, part]) + nt(d_upward, gu_ref[:, behind])
        else:
            sum_ref[...] += nt(d_gating, gu_ref[:, part]) + nt(d_upward, gu_ref[:, behind])
    d_normed = sum_ref[...]
    middle = middle_ref[...]
    factor = inverse_rms(middle)
    unit = middle * factor
    dgain_ref[...] = jnp.sum(d_normed * unit, axis=0, keepdims=True)
    scaled = d_normed * gain_ref[...]
    d_middle = grad + factor * (scaled - unit * jnp.mean(scaled * unit, axis=-1, keepdims=True))
    dmid_ref[...] = d_middle
    padded = jnp.concatenate(
        [jnp.zeros((rows, wo_wide - width), f32), d_middle], axis=1
    ).astype(bf16)
    gm_ref[...] = padded
    loads[2].wait()
    do_ref[...] = nt(padded, wo_ref[...]).T.astype(bf16)


def feed_back(grad, middle, gating, upward, gain, weights):
    rows, width = middle.shape
    weights_a, weights_gu, weights_dn = weights
    ffn = weights_dn.shape[1]
    wo_wide = width + HEAD_SIZE
    return pl.pallas_call(
        feed_back_kernel,
        out_shape=(
            shape((rows, width), bf16),
            shape((rows, 2 * ffn), bf16),
            shape((rows, width), f32),
            shape((rows, wo_wide), bf16),
            shape((width, rows), bf16),
            shape((1, width), f32),
        ),
        in_specs=[in_vmem()] * 5 + [anywhere()] * 3,
        out_specs=(in_vmem(),) * 6,
        scratch_shapes=[
            pltpu.VMEM((width, wo_wide), bf16),
            pltpu.VMEM((width, 2 * ffn), bf16),
            pltpu.VMEM((width, ffn), bf16),
            pltpu.VMEM((rows, width), f32),
            pltpu.SemaphoreType.DMA((3,)),
        ],
        compiler_params=params(),
        cost_estimate=cost(2 * rows * width * (4 * ffn), 3 * width * ffn * 2 + rows * ffn * 8),
        name="feed_back",
    )(grad, middle, gating, upward, gain, weights_a, weights_gu, weights_dn)


def attend_back_kernel(
    visible_ref,
    q_ref,
    do_ref,
    att_ref,
    lse_ref,
    cos_ref,
    sin_ref,
    kv0_ref,
    kv1_ref,
    kv2_ref,
    kv3_ref,
    dq_ref,
    dkv0_ref,
    dkv1_ref,
    dkv2_ref,
    dkv3_ref,
    acc_ref,
    row_ref,
):
    rows = q_ref.shape[1]
    key_width = KEY_VALUE_HEADS * HEAD_SIZE
    allowed = causal(rows)
    for group in range(KEY_VALUE_HEADS):
        row_ref[group : group + 1, :] = jnp.sum(
            stacked_heads(do_ref, group).astype(f32) * stacked_heads(att_ref, group).astype(f32),
            axis=0,
            keepdims=True,
        )

    def one(group, kv_ref, dkv_ref, own):
        queries = stacked_heads(q_ref, group)
        d_out = stacked_heads(do_ref, group)
        keys = key_block(kv_ref, group)
        scores = nn(keys.T, queries)
        if own:
            scores = jnp.where(allowed, scores, masked)
        probs = jnp.exp(scores - lse_ref[group : group + 1, :])
        d_probs = nn(value_block(kv_ref, group).T, d_out)
        d_scores = (probs * (d_probs - row_ref[group : group + 1, :])).astype(bf16)
        dkv_ref[group * HEAD_SIZE : (group + 1) * HEAD_SIZE, :] = nt(queries, d_scores).astype(bf16)
        dkv_ref[key_width + group * HEAD_SIZE : key_width + (group + 1) * HEAD_SIZE, :] = nt(
            d_out, probs.astype(bf16)
        ).astype(bf16)
        moved = nn(keys, d_scores)
        if own:
            acc_ref[group] = moved
        else:
            acc_ref[group] += moved

    for group in range(KEY_VALUE_HEADS):
        one(group, kv0_ref, dkv0_ref, True)
    for member, kv_ref, dkv_ref in (
        (1, kv1_ref, dkv1_ref),
        (2, kv2_ref, dkv2_ref),
        (3, kv3_ref, dkv3_ref),
    ):

        @pl.when(visible_ref[member] == 1)
        def _(kv_ref=kv_ref, dkv_ref=dkv_ref):
            for group in range(KEY_VALUE_HEADS):
                one(group, kv_ref, dkv_ref, False)

        @pl.when(visible_ref[member] == 0)
        def _(dkv_ref=dkv_ref):
            dkv_ref[...] = jnp.zeros_like(dkv_ref)

    cos, sin = cos_ref[...], sin_ref[...]
    for group in range(KEY_VALUE_HEADS):
        for j in range(SHARING):
            low = (group * SHARING + j) * HEAD_SIZE
            lanes = slice(j * rows, (j + 1) * rows)
            first = acc_ref[group, :HALF, lanes] * score_scale
            second = acc_ref[group, HALF:, lanes] * score_scale
            dq_ref[low : low + HALF, :] = (first * cos + second * sin).astype(bf16)
            dq_ref[low + HALF : low + HEAD_SIZE, :] = (second * cos - first * sin).astype(bf16)


def attend_back(visible, q, d_out, att_t, lse, cos, sin, kvs):
    width, rows = q.shape
    key_rows = kvs[0].shape[0]
    lanes = SHARING * rows
    return pl.pallas_call(
        attend_back_kernel,
        out_shape=(shape((width, rows), bf16),) + (shape((key_rows, rows), bf16),) * 4,
        in_specs=[in_smem()] + [in_vmem()] * 10,
        out_specs=(in_vmem(),) * 5,
        scratch_shapes=[
            pltpu.VMEM((KEY_VALUE_HEADS, HEAD_SIZE, lanes), f32),
            pltpu.VMEM((KEY_VALUE_HEADS, lanes), f32),
        ],
        compiler_params=params(),
        cost_estimate=cost(2 * rows * width * 4 * rows * 10, 10 * width * rows * 2),
        name="attend_back",
    )(visible, q, d_out, att_t, lse, cos, sin, *kvs)


def leave_kernel(
    h_ref,
    dmid_ref,
    dq_ref,
    own_ref,
    got_ref,
    gain_ref,
    cos_ref,
    sin_ref,
    w_hbm,
    g_ref,
    dqkv_ref,
    dgain_ref,
    w_ref,
    turned_ref,
    sem,
):
    width, rows = dq_ref.shape
    key_width = own_ref.shape[0] // 2
    wide = w_ref.shape[1]
    load = pltpu.make_async_copy(w_hbm.at[:, pl.ds(0, wide)], w_ref, sem)
    load.start()
    cos, sin = cos_ref[...], sin_ref[...]
    turned_ref[:width, :] = dq_ref[...]
    summed = own_ref[...].astype(f32) + got_ref[...].astype(f32)
    for head in range(KEY_VALUE_HEADS):
        low = head * HEAD_SIZE
        first = summed[low : low + HALF]
        second = summed[low + HALF : low + HEAD_SIZE]
        base = width + low
        turned_ref[base : base + HALF, :] = (first * cos + second * sin).astype(bf16)
        turned_ref[base + HALF : base + HEAD_SIZE, :] = (second * cos - first * sin).astype(bf16)
    turned_ref[width + key_width : width + 2 * key_width, :] = summed[key_width:].astype(bf16)
    turned_ref[width + 2 * key_width :, :] = jnp.zeros((wide - width - 2 * key_width, rows), bf16)
    d_mixed = turned_ref[...].T
    dqkv_ref[...] = d_mixed
    load.wait()
    d_normed = nt(d_mixed, w_ref[...])
    hidden = h_ref[...]
    factor = inverse_rms(hidden)
    unit = hidden * factor
    dgain_ref[...] = jnp.sum(d_normed * unit, axis=0, keepdims=True)
    scaled = d_normed * gain_ref[...]
    grad = dmid_ref[...] + factor * (
        scaled - unit * jnp.mean(scaled * unit, axis=-1, keepdims=True)
    )
    g_ref[...] = grad if g_ref.dtype == f32 else grad.T.astype(bf16)


def leave(hidden, d_middle, dq, own, got, gain, cos, sin, weights_a):
    rows, width = hidden.shape
    key_width = KEY_VALUE_HEADS * HEAD_SIZE
    wide = width + 2 * key_width + HEAD_SIZE
    return pl.pallas_call(
        leave_kernel,
        out_shape=(
            shape((rows, width), f32),
            shape((rows, wide), bf16),
            shape((1, width), f32),
        ),
        in_specs=[in_vmem()] * 8 + [anywhere()],
        out_specs=(in_vmem(),) * 3,
        scratch_shapes=[
            pltpu.VMEM((width, wide), bf16),
            pltpu.VMEM((wide, rows), bf16),
            pltpu.SemaphoreType.DMA,
        ],
        compiler_params=params(),
        cost_estimate=cost(2 * rows * width * wide, width * wide * 2 + rows * width * 14),
        name="leave",
    )(hidden, d_middle, dq, own, got, gain, cos, sin, weights_a)


def grad_parts(place_ref, right, keep_ref, send_ref, xt_ref):
    block, step = keep_ref.shape[2:]
    core, chip, quarter = place_ref[0], place_ref[1], place_ref[2]
    for part in range(4):
        columns = right(part * step, (part + 1) * step)
        for away in range(2):
            for out_ref, which in ((keep_ref, core), (send_ref, 1 - core)):
                start = pl.multiple_of((2 * (chip ^ away) + which) * block, 16)
                out_ref[away, part ^ quarter] = nn(
                    xt_ref[pl.ds(start, block), :], columns
                ).astype(bf16)


def feed_back_gate_kernel(*refs):
    (place_ref, g_ref, middle_ref, gating_ref, upward_ref, gain_ref, nf2_ref, nf_ref, dgu2_ref,
     a_hbm, gu_hbm, dn_hbm, dmid_ref, gm_ref, do_ref, dgain_ref, keep_ref, send_ref, keep2_ref,
     send2_ref, gb_ref, dgu_ref, wo_ref, gu_ref, dn_ref, sum_ref, xt_ref, sems) = refs
    feed_back_kernel(
        g_ref, middle_ref, gating_ref, upward_ref, gain_ref, a_hbm, gu_hbm, dn_hbm, gb_ref, dgu_ref,
        dmid_ref, gm_ref, do_ref, dgain_ref, wo_ref, gu_ref, dn_ref, sum_ref, sems,
    )

    rows = nf_ref.shape[0]
    ffn = gating_ref.shape[1]
    xt_ref[:, :rows] = nf2_ref[...].T
    xt_ref[:, rows:] = nf_ref[...].T
    for base, out_refs in ((0, (keep_ref, send_ref)), (ffn, (keep2_ref, send2_ref))):

        def right(low, high, base=base):
            return jnp.concatenate(
                [dgu2_ref[:, base + low : base + high], dgu_ref[:, base + low : base + high]], axis=0
            )

        grad_parts(place_ref, right, *out_refs, xt_ref)


def feed_back_gate(place, grad, middle, gating, upward, gain, nf2, nf, dgu2, weights):
    rows, width = grad.shape
    weights_a, weights_gu, weights_dn = weights
    ffn = weights_dn.shape[1]
    wo_wide = width + HEAD_SIZE
    return pl.pallas_call(
        feed_back_gate_kernel,
        out_shape=(
            shape((rows, width), f32),
            shape((rows, wo_wide), bf16),
            shape((width, rows), bf16),
            shape((1, width), f32),
        )
        + (shape((2, 4, width // 4, ffn // 4), bf16),) * 4,
        in_specs=[in_smem()] + [in_vmem()] * 8 + [anywhere()] * 3,
        out_specs=(in_vmem(),) * 8,
        scratch_shapes=[
            pltpu.VMEM((rows, width), bf16),
            pltpu.VMEM((rows, 2 * ffn), bf16),
            pltpu.VMEM((width, wo_wide), bf16),
            pltpu.VMEM((width, 2 * ffn), bf16),
            pltpu.VMEM((width, ffn), bf16),
            pltpu.VMEM((rows, width), f32),
            pltpu.VMEM((width, 2 * rows), bf16),
            pltpu.SemaphoreType.DMA((3,)),
        ],
        compiler_params=params(),
        cost_estimate=cost(2 * rows * width * (8 * ffn), 3 * width * ffn * 2 + rows * ffn * 8),
        name="feed_back_gate",
    )(place, grad, middle, gating, upward, gain, nf2, nf, dgu2, weights_a, weights_gu, weights_dn)


def leave_mixed_kernel(*refs):
    (place_ref, h_ref, dmid_ref, dq_ref, own_ref, got_ref, gain_ref, cos_ref, sin_ref, n1_ref, n2_ref,
     d1_ref, a1_ref, a2_ref, m1_ref, m2_ref, attention_gain_ref, ffn_gain_ref, ffn_gain2_ref, w_hbm,
     g_ref, keep_ref, send_ref, d2_ref, dgain_ref, w_ref, turned_ref, nt_ref, at_ref, gains_ref,
     sem) = refs
    leave_kernel(
        h_ref, dmid_ref, dq_ref, own_ref, got_ref, gain_ref, cos_ref, sin_ref, w_hbm, g_ref, d2_ref,
        dgain_ref, w_ref, turned_ref, sem,
    )
    gains = (attention_gain_ref[...] + dgain_ref[...], ffn_gain_ref[...] + ffn_gain2_ref[...])
    attention_grad_kernel(
        place_ref, n1_ref, n2_ref, d1_ref, d2_ref, a1_ref, a2_ref, m1_ref, m2_ref, gains, keep_ref,
        send_ref, nt_ref, at_ref, gains_ref,
    )


def leave_mixed(
    place, hidden, d_middle, dq, own, got, gain, cos, sin, normed, dqkv2, att, gm, gain_grads, weights_a
):
    rows, width = hidden.shape
    key_width = KEY_VALUE_HEADS * HEAD_SIZE
    wide = width + 2 * key_width + HEAD_SIZE
    block = width // 4 + GAIN_ROWS
    columns = 2 * width + 2 * key_width
    return pl.pallas_call(
        leave_mixed_kernel,
        out_shape=(shape((width, rows), bf16),)
        + (shape((2, 4, block, columns // 4), bf16),) * 2,
        in_specs=[in_smem()] + [in_vmem()] * 18 + [anywhere()],
        out_specs=(in_vmem(),) * 3,
        scratch_shapes=[
            pltpu.VMEM((rows, wide), bf16),
            pltpu.VMEM((1, width), f32),
            pltpu.VMEM((width, wide), bf16),
            pltpu.VMEM((wide, rows), bf16),
            pltpu.VMEM((width, 2 * rows), bf16),
            pltpu.VMEM((width, 2 * rows), bf16),
            pltpu.VMEM((GAIN_ROWS, columns), f32),
            pltpu.SemaphoreType.DMA,
        ],
        compiler_params=params(),
        cost_estimate=cost(6 * rows * width * wide, width * wide * 2 + rows * width * 14),
        name="leave_mixed",
    )(place, hidden, d_middle, dq, own, got, gain, cos, sin, *normed, dqkv2, *att, *gm, *gain_grads,
      weights_a)


def down_grad_kernel(place_ref, g2_ref, g_ref, inner2_ref, inner_ref, keep_ref, send_ref, gt_ref):
    rows = g2_ref.shape[0]
    height, step = keep_ref.shape[2:]
    gt_ref[:, :rows] = g2_ref[...].T
    gt_ref[:, rows:] = g_ref[...].astype(bf16).T
    core, chip, quarter = place_ref[0], place_ref[1], place_ref[2]
    for away in range(2):
        for out_ref, which in ((keep_ref, core), (send_ref, 1 - core)):
            columns = pl.ds(pl.multiple_of((2 * (chip ^ away) + which) * step, 128), step)
            right = jnp.concatenate([inner2_ref[:, columns], inner_ref[:, columns]], axis=0)
            for part in range(4):
                out_ref[away, part ^ quarter] = nn(
                    gt_ref[part * height : (part + 1) * height, :], right
                ).astype(bf16)


def down_grad_parts(place, g2, g, inner2, inner):
    rows, width = g.shape
    ffn = inner.shape[1]
    return pl.pallas_call(
        down_grad_kernel,
        out_shape=(shape((2, 4, width // 4, ffn // 4), bf16),) * 2,
        in_specs=[in_smem()] + [in_vmem()] * 4,
        out_specs=(in_vmem(),) * 2,
        scratch_shapes=[pltpu.VMEM((width, 2 * rows), bf16)],
        compiler_params=params(),
        cost_estimate=cost(4 * rows * width * ffn, width * ffn * 2),
        name="down_grad",
    )(place, g2, g, inner2, inner)


def attention_grad_kernel(
    place_ref, n1_ref, n2_ref, d1_ref, d2_ref, a1_ref, a2_ref, m1_ref, m2_ref, gains,
    keep_ref, send_ref, nt_ref, at_ref, gains_ref,
):
    rows = n1_ref.shape[0]
    block = n1_ref.shape[1] // 4
    wide = d1_ref.shape[1]
    edge = wide - 128
    step = keep_ref.shape[3]
    nt_ref[:, :rows] = n1_ref[...].T
    nt_ref[:, rows:] = n2_ref[...].T
    at_ref[:, :rows] = a1_ref[...].T
    at_ref[:, rows:] = a2_ref[...].T
    half = GAIN_ROWS // 2
    gains_ref[...] = jnp.zeros_like(gains_ref)
    for i, gain in enumerate(gains):
        gains_ref[i * half : (i + 1) * half, : gain.shape[1]] = jnp.broadcast_to(
            gain, (half, gain.shape[1])
        )
    core, chip, quarter = place_ref[0], place_ref[1], place_ref[2]
    d_mixed = jnp.concatenate([d1_ref[...], d2_ref[...]], axis=0)
    d_out = jnp.concatenate([m1_ref[...], m2_ref[...]], axis=0)
    for away in range(2):
        for out_ref, which in ((keep_ref, core), (send_ref, 1 - core)):
            member = 2 * (chip ^ away) + which
            start = pl.multiple_of(member * block, 16)
            normed = nt_ref[pl.ds(start, block), :]
            attended = at_ref[pl.ds(start, block), :]
            for part in range(4):
                low, high = part * step, (part + 1) * step
                pieces = []
                if low < edge:
                    pieces.append(nn(normed, d_mixed[:, low : min(high, edge)]))
                if low <= edge < high:
                    pieces.append(nn(normed, d_mixed[:, edge:]) + nn(attended, d_out[:, :128]))
                if high > wide:
                    base = wide - 128
                    pieces.append(nn(attended, d_out[:, max(low, wide) - base : high - base]))
                piece = pieces[0] if len(pieces) == 1 else jnp.concatenate(pieces, axis=1)
                out_ref[away, part ^ quarter, :block, :] = piece.astype(bf16)
                out_ref[away, part ^ quarter, block:, :] = gains_ref[:, low:high].astype(bf16)


def finish_kernel(place_ref, p0_ref, p1_ref, p2_ref, p3_ref, out_ref):
    part = pl.program_id(0)
    for i, ref in enumerate((p0_ref, p1_ref, p2_ref, p3_ref)):

        @pl.when(part == i)
        def _(ref=ref):
            out_ref[...] = ref[...].astype(f32)


def finish(place, pieces, by_rows):
    height, step = pieces[0].shape
    whole = pl.BlockSpec((height, step), lambda i, place: (0, 0))
    if by_rows:
        dims, index = (4 * height, step), lambda i, place: (i ^ place[2], 0)
    else:
        dims, index = (height, 4 * step), lambda i, place: (0, i ^ place[2])
    return pl.pallas_call(
        finish_kernel,
        grid_spec=pltpu.PrefetchScalarGridSpec(
            num_scalar_prefetch=1,
            grid=(4,),
            in_specs=[whole] * 4,
            out_specs=pl.BlockSpec((height, step), index),
        ),
        out_shape=shape(dims, f32),
        compiler_params=params(),
        cost_estimate=cost(0, 24 * height * step),
        name="finish",
    )(place, *pieces)


def finish_mixed_kernel(
    place_ref, p0_ref, p1_ref, p2_ref, p3_ref, query_ref, key_ref, value_ref, out_ref, gain_ref,
    mixed_ref,
):
    quarter = place_ref[2]
    block, width = query_ref.shape
    key_width = key_ref.shape[0]
    step = p0_ref.shape[1]
    for i, ref in enumerate((p0_ref, p1_ref, p2_ref, p3_ref)):
        start = pl.multiple_of((quarter ^ i) * step, 128)
        mixed_ref[:, pl.ds(start, step)] = ref[...].astype(f32)
    first_end = width + key_width
    second_end = first_end + key_width
    query_ref[...] = mixed_ref[:block, :width]
    key_ref[...] = mixed_ref[:block, width:first_end].T
    value_ref[...] = mixed_ref[:block, first_end:second_end].T
    out_ref[...] = mixed_ref[:block, second_end:]
    gain_ref[...] = mixed_ref[block:, : gain_ref.shape[1]]


def finish_mixed(place, pieces, width, key_width):
    height, step = pieces[0].shape
    block = height - GAIN_ROWS
    return pl.pallas_call(
        finish_mixed_kernel,
        out_shape=(
            shape((block, width), f32),
            shape((key_width, block), f32),
            shape((key_width, block), f32),
            shape((block, width), f32),
            shape((GAIN_ROWS, width + HEAD_SIZE), f32),
        ),
        in_specs=[in_smem()] + [in_vmem()] * 4,
        out_specs=(in_vmem(),) * 5,
        scratch_shapes=[pltpu.VMEM((height, 4 * step), f32)],
        compiler_params=params(),
        cost_estimate=cost(0, 24 * height * step),
        name="finish_mixed",
    )(place, *pieces)


def flip(value, axis_name, distance):
    size = lax.axis_size(axis_name)
    return lax.ppermute(value, axis_name, [(i, i ^ distance) for i in range(size)])


def pick(condition, when_true, when_false):
    return jnp.where(condition, when_true, when_false)


def order_by(bit, own, other):
    return (pick(bit == 1, other, own), pick(bit == 1, own, other))


def exchange_kv(block):
    beside = flip(block, "fsdp", 1)
    across = flip(block, "fsdp", 2)
    diagonal = flip(across, "fsdp", 1)
    return (block, beside, across, diagonal)


def fold_kv(pieces):
    rows = pieces[0].shape[0]
    got = flip(jnp.concatenate([pieces[1], pieces[3]], axis=0), "fsdp", 1)
    return total(pieces[0], got[:rows]), total(pieces[2], got[rows:])


def return_kv(pieces):
    own, across = fold_kv(pieces)
    return own, flip(across, "fsdp", 2)


def total(*terms):
    result = terms[0].astype(f32)
    for term in terms[1:]:
        result = result + term.astype(f32)
    return result.astype(bf16)


class Order:
    def __init__(self, *token):
        self.token = token

    def tie(self, *values):
        tied = lax.optimization_barrier(self.token + values)[len(self.token) :]
        return tied[0] if len(tied) == 1 else tied

    def done(self, value):
        self.token = (value,)
        return value

    def done_all(self, *values):
        self.token = values
        return values


class Reduction:
    def __init__(self, order, keep, send):
        self.order = order
        self.keep = keep
        self.core = flip(order.tie(send), "fsdp", 1)

    def chip(self):
        self.core = self.order.tie(self.core)
        high = total(self.keep[1, 2:], self.core[1, 2:])
        low = total(self.keep[1, :2], self.core[1, :2])
        high, low = self.order.done_all(high, low)
        self.high = flip(high, "fsdp", 2)
        self.low = flip(low, "fsdp", 2)

    def first(self, both=False):
        if both:
            self.high, self.low = self.order.tie(self.high, self.low)
        else:
            self.high = self.order.tie(self.high)
        out = total(self.keep[0, 2:], self.core[0, 2:], self.high)
        self.got = flip(self.order.done(out), "dp", 1)

    def rest(self):
        self.low = self.order.done(self.order.tie(self.low))

    def second(self):
        self.got, self.low = self.order.tie(self.got, self.low)
        self.terms = (self.keep[0, :2], self.core[0, :2], self.low, self.got)
        self.got = flip(self.order.done(total(*[term[1] for term in self.terms])), "dp", 2)

    def third(self):
        size = lax.axis_size("dp")
        own = total(*[term[0] for term in self.terms], self.order.tie(self.got))
        distance = 4
        while 2 * distance < size:
            own = total(own, flip(own, "dp", distance))
            distance *= 2
        self.own = self.order.done(own)
        self.got = flip(own, "dp", distance) if distance < size else jnp.zeros_like(own)

    def back(self):
        self.own = self.order.done(total(self.own, self.order.tie(self.got)))
        self.beside = flip(self.own, "dp", 2)
        self.pieces = [self.own, self.beside, flip(self.own, "dp", 1)]

    def back_again(self):
        self.beside = self.order.done(self.order.tie(self.beside))
        self.pieces.append(flip(self.beside, "dp", 1))

    def end(self):
        return self.order.tie(*self.pieces)


def rotation(token_positions):
    frequency = rope_base ** (-jnp.arange(HALF, dtype=f32) / HALF)
    angles = frequency[:, None] * token_positions.astype(f32)[None, :]
    return jnp.cos(angles), jnp.sin(angles)


def body(
    tokens,
    cotangent,
    sequence_ids,
    span_position,
    attention_norm,
    query_weight,
    key_matrix,
    value_matrix,
    output_weight,
    feedforward_norm,
    gate_weight,
    up_weight,
    down_weight,
):
    rows, width = tokens.shape
    key_width = key_matrix.shape[1]
    ffn = gate_weight.shape[1]
    itself = lax.axis_index("fsdp")
    outer = lax.axis_index("dp")
    quarter = 2 * (outer % 2) + (outer // 2) % 2
    place = jnp.stack([itself % 2, itself // 2, quarter]).astype(jnp.int32)

    outer = lax.axis_index("dp")
    bits = jnp.stack([outer % 2, (outer // 2) % 2, itself]).astype(jnp.int32)
    packed, *mine = pack(
        bits, query_weight, key_matrix.T, value_matrix.T, output_weight, gate_weight, up_weight
    )
    down_t = down_weight.T
    half = width // 2
    mine.append(pick(outer % 2 == 1, down_t[half:], down_t[:half]))
    gains = jnp.stack([attention_norm, feedforward_norm], axis=0)
    gains = [flip(gains, "fsdp", distance) if distance else gains for distance in range(4)]
    mine = Order(*gains).tie(*mine)
    far = [flip(piece, "fsdp", 2) for piece in mine]
    shards = (packed, gate_weight, up_weight, down_t)
    near = [flip(shard, "fsdp", 1) for shard in shards]
    sequence_ids, span_position = Order(*mine).tie(sequence_ids, span_position)
    places = jnp.arange(rows, dtype=jnp.int32) + span_position[itself] * rows
    cos, sin = rotation(places)
    others = itself ^ jnp.arange(4)
    visible = (
        (sequence_ids[others] == sequence_ids[itself])
        & (span_position[others] <= span_position[itself])
    ).astype(jnp.int32)

    beside = order_by(itself % 2, gains[0], gains[1])
    away = order_by(itself % 2, gains[2], gains[3])
    chip = itself // 2 == 1
    gains = jnp.concatenate(
        [pick(chip, a, n) for a, n in zip(away, beside)]
        + [pick(chip, n, a) for a, n in zip(away, beside)],
        axis=1,
    ).astype(f32)
    attention_gain, ffn_gain = gains[:1], gains[1:]
    order = Order(cos, sin, visible, attention_gain, ffn_gain)
    share = ((1, 0), (1, 0), (2, 1), (1, 0))

    def shared(i):
        got = order.done(order.tie(far[i]))
        return got, flip(got, "dp", share[i][0])

    def gathered(i, got, other):
        return [shards[i], near[i], got, other, flip(got, "fsdp", 1), flip(other, "fsdp", 1)]

    shared_a = shared(0)
    order.done_all(*order.tie(*shared_a))
    shared_gate = shared(1)
    sources_a = gathered(0, *shared_a)
    order.done_all(*order.tie(*near), *sources_a)
    tokens_t = order.tie(tokens.T)
    hidden, normed, q, kv, weights_a = enter_first(
        bits, tokens_t, attention_gain, cos, sin, shared_plan(0, 0, 0), tuple(sources_a)
    )
    order.done(kv)
    shared_up = shared(2)
    shared_gate = order.done_all(*order.tie(*shared_gate))
    kvs = exchange_kv(kv)
    shared_down = shared(3)
    order.done_all(*order.tie(*shared_up))
    sources_gu = gathered(1, *shared_gate) + gathered(2, *shared_up)
    sources_dn = gathered(3, *order.tie(*shared_down))
    plan_gu = shared_plan(0, 0, 0) + shared_plan(6, ffn, 1)
    plan_dn = shared_plan(0, None, 0)
    finished, att, att_t, lse, middle, nf, gating, upward, inner, weights_gu, weights_dn = forward_block(
        visible, bits, hidden, q, kvs, ffn_gain, weights_a, tuple(sources_gu), tuple(sources_dn),
        (plan_gu, plan_dn),
    )
    weights = (weights_a, weights_gu, weights_dn)
    saved = [(hidden, normed, q, kvs, att, att_t, lse, middle, nf, gating, upward, inner)]
    hidden = finished
    normed, q, kv = enter(hidden, attention_gain, cos, sin, weights_a)
    kvs = exchange_kv(kv)
    activations, att, att_t, lse, middle, nf, gating, upward, inner = forward_block(
        visible, bits, hidden, q, kvs, ffn_gain, weights_a, (weights_gu,), (weights_dn,)
    )
    saved.append((hidden, normed, q, kvs, att, att_t, lse, middle, nf, gating, upward, inner))

    hidden, normed2, q, kvs, att2, att_t, lse, middle, nf2, gating, upward, inner2 = saved[1]
    gb2, dgu2, d_middle, gm2, d_out, ffn_gain_grad2 = feed_back(
        cotangent.T, middle, gating, upward, ffn_gain, weights
    )
    dq, *dkvs = attend_back(visible, q, d_out, att_t, lse, cos, sin, kvs)
    own, got = return_kv(dkvs)
    grad, dqkv2, attention_gain_grad2 = leave(
        hidden, d_middle, dq, own, got, attention_gain, cos, sin, weights_a
    )

    hidden, normed, q, kvs, att, att_t, lse, middle, nf, gating, upward, inner = saved[0]
    order = Order(grad)
    down = Reduction(order, *down_grad_parts(place, gb2, grad, inner2, inner))
    down.chip()
    d_middle, gm, d_out, ffn_gain_grad, *rest = feed_back_gate(
        place, order.tie(grad), middle, gating, upward, ffn_gain, nf2, nf, dgu2, weights
    )
    order.done(d_middle)
    down.first(both=True)
    gate = Reduction(order, *rest[:2])
    gate.chip()
    up = Reduction(order, *rest[2:])
    dq, *dkvs = attend_back(visible, order.tie(q), d_out, att_t, lse, cos, sin, kvs)
    order.done(dq)
    gate.first()
    down.second()
    own, across = fold_kv(order.tie(*dkvs))
    order.done(across)
    gate.rest()
    across = order.tie(across)
    got = flip(across, "fsdp", 2)
    order.done(across)
    up.chip()
    d_middle, got = order.tie(d_middle, got)
    grad, *mixed = leave_mixed(
        place,
        hidden,
        d_middle,
        dq,
        own,
        got,
        attention_gain,
        cos,
        sin,
        (normed2, normed),
        dqkv2,
        (att2, att),
        (gm2, gm),
        (attention_gain_grad2, ffn_gain_grad2, ffn_gain_grad),
        weights_a,
    )
    order.done(grad)
    up.first()
    mixed = Reduction(order, *mixed)
    gate.second()
    down.third()
    mixed.chip()
    up.second()
    gate.third()
    down.back()
    mixed.first()
    down.back_again()
    gate.back()
    up.third()
    gate.back_again()
    down_grad = order.done(finish(place, down.end(), True))
    up.back()
    mixed.second()
    up.back_again()
    gate_grad = order.done(finish(place, gate.end(), False))
    mixed.third()
    up_grad = order.done(finish(place, up.end(), False))
    mixed.back()
    mixed.back_again()
    query_grad, key_grad, value_grad, output_grad, gain_grads = finish_mixed(
        place, mixed.end(), width, key_width
    )
    shard_rows = attention_norm.shape[0]
    gain_grads = lax.dynamic_slice_in_dim(gain_grads, itself * shard_rows, shard_rows, axis=1)
    return (
        activations.T,
        grad.T,
        gain_grads[0],
        query_grad,
        key_grad.T,
        value_grad.T,
        output_grad,
        gain_grads[GAIN_ROWS // 2],
        gate_grad,
        up_grad,
        down_grad.T,
    )


def solution(mesh):
    return jax.shard_map(
        body,
        mesh=mesh,
        in_specs=(
            P(("dp", "fsdp"), None),
            P(("dp", "fsdp"), None),
            P("dp"),
            P("dp"),
            P("fsdp"),
            P("fsdp", None),
            P("fsdp", None),
            P("fsdp", None),
            P("fsdp", None),
            P("fsdp"),
            P("fsdp", None),
            P("fsdp", None),
            P("fsdp", None),
        ),
        out_specs=(
            P(("dp", "fsdp"), None),
            P(("dp", "fsdp"), None),
            P("fsdp"),
            P("fsdp", None),
            P("fsdp", None),
            P("fsdp", None),
            P("fsdp", None),
            P("fsdp"),
            P("fsdp", None),
            P("fsdp", None),
            P("fsdp", None),
        ),
        check_vma=False,
    )
```

time: 1130 us -> 487 us (0.43)
  blocking collectives: 417 us -> 0 us
  waiting for transfers between devices: 425 us -> 190 us
  matrix products: 163 us -> 0 us
  Pallas kernels: 0 us -> 153 us
  starting transfers between devices: 1.07 us -> 86.5 us
  between operations: 31.3 us -> 2.42 us
  local copies, waits for them, and re-layouts: 44 us -> 15.5 us
    psum x1 -> x0, blocking collectives: 388 us -> none  [body(): totals = lax.psum(shard_sums, 'dp')]
    ppermute x0 -> x69, waiting for transfers between devices: none -> 190 us  [flip(): lax.ppermute(value, axis_name, [(i, i ^ distance) for i in range(size)])]
    reduce_scatter x6 -> x0, waiting for transfers between devices: 179 us -> none  [the longest x4 118 us: body(): lax.psum_scatter(as_sent(summed), 'fsdp', scatter_dimension=0, tiled=True)]
    dot_general x96 -> x0, matrix products: 163 us -> none  [the longest x14 39.9 us: matrix_product(): return jnp.dot(left_side, right_side, preferred_element_type=jnp.float32)]
    pallas_call x0 -> x16, Pallas kernels: none -> 153 us  [the longest x2 36.2 us: forward_block(): pl.pallas_call(functools.partial(forward_kernel, plans, counts), out_shap...]
    all_gather x7 -> x0, waiting for transfers between devices: 140 us -> none  [the longest x1 34.6 us: body(): lax.all_gather(up_weight, 'fsdp', axis=0, tiled=True)]
    unnamed x19 -> x0, waiting for transfers between devices: 106 us -> none
    ppermute x0 -> x69, starting transfers between devices: none -> 86.5 us  [flip(): lax.ppermute(value, axis_name, [(i, i ^ distance) for i in range(size)])]
  transfers between devices with their start and end apart: 16 -> 69, of which waited for: 14 -> 35; matrix products, arithmetic and copies ran while one was open for 9% -> 5% of each run, Pallas kernels for 0% -> 14%
where the time goes in v2:
time: 487 us; the launch traced here: 479 us
  waiting for transfers between devices  190 us (39%)
  Pallas kernels  153 us (31%)
  starting transfers between devices  86.5 us (18%)
  other arithmetic  31.7 us (7%)
  local copies, waits for them, and re-layouts  15.5 us (3%)
    ppermute x69, waiting for transfers between devices, flip(): lax.ppermute(value, axis_name, [(i, i ^ distance) for i in range(size)])  190 us
    ppermute x69, starting transfers between devices, flip(): lax.ppermute(value, axis_name, [(i, i ^ distance) for i in range(size)])  86.5 us
    pallas_call x2, Pallas kernels, forward_block(): pl.pallas_call(functools.partial(forward_kernel, plans, counts), out_shap...  36.2 us
    pallas_call x1, Pallas kernels, feed_back_gate(): pl.pallas_call(feed_back_gate_kernel, out_shape=(shape((rows, width), f32...  25 us
    convert_element_type x22, other arithmetic, total(): return result.astype(bf16)  24.1 us
    pallas_call x2, Pallas kernels, attend_back(): pl.pallas_call(attend_back_kernel, out_shape=(shape((width, rows), bf16),...  20.2 us
    pallas_call x1, Pallas kernels, feed_back(): pl.pallas_call(feed_back_kernel, out_shape=(shape((rows, width), bf16), s...  14.9 us
    pallas_call x3, Pallas kernels, finish(): pl.pallas_call(finish_kernel, grid_spec=pltpu.PrefetchScalarGridSpec(num_...  11.9 us
  transfers between devices with their start and end apart: 69, of which 35 were waited for; matrix products, arithmetic and copies ran while one was open for 5% of the time, Pallas kernels for 14%

profile of v2, /device:TPU:0, one launch (start us, length us, event | category | flops | bytes accessed | tf_op | source)
XLA Modules:
  0.0 478.6 jit_solution(7183638316740176229)
XLA Ops:
  2.5 2.6 collective-permute-start.1
  5.7 4.2 pack.1
  21.1 7.8 %collective-permute-done.4.refs_2_ = bf16[240,1280]{1,0:T(8,128)(2,1)} collective-permute-done((bf16[240,1280]{1,0:T(8,128)(2,1)S(1)}, bf16[240,1280]{1,0:T(8,128)(2,1)}, u32[]{:S(2)}, u32[]{:S(2)}) %collective-permute-start.4) | collective-permute-done | bytes 614432 | tf_op jit(solution)/shard_map/ppermute | solution.py:938
  32.7 11.7 %collective-permute-done.5.refs_3_ = bf16[240,1280]{1,0:T(8,128)(2,1)S(1)} collective-permute-done((bf16[240,1280]{1,0:T(8,128)(2,1)}, bf16[240,1280]{1,0:T(8,128)(2,1)S(1)}, u32[]{:S(2)}, u32[]{:S(2)}) %collective-permute-start.5) | collective-permute-done | bytes 614432 | tf_op jit(solution)/shard_map/ppermute | solution.py:938
  44.4 3.2 collective-permute-done.13.refs_12_
  47.6 11.2 %collective-permute-done.12.refs_18_ = bf16[240,1280]{1,0:T(8,128)(2,1)S(1)} collective-permute-done((bf16[240,1280]{1,0:T(8,128)(2,1)}, bf16[240,1280]{1,0:T(8,128)(2,1)S(1)}, u32[]{:S(2)}, u32[]{:S(2)}) %collective-permute-start.12) | collective-permute-done | bytes 614432 | tf_op jit(solution)/shard_map/ppermute | solution.py:938
  62.5 7.1 %enter_first.1 = (f32[256,960]{1,0:T(8,128)}, bf16[256,960]{1,0:T(8,128)(2,1)}, bf16[960,256]{1,0:T(8,128)(2,1)}, bf16[640,256]{1,0:T(8,128)(2,1)}, bf16[960,2560]{1,0:T(8,128)(2,1)}) custom-call(s32[3]{0:T(128)} %pad_add_fusion.bits_ref.index_ref.refs_1_, bf16[960,256]{1,0:T(8,128)(2,1)} %bitcast.122, f32[1,960]{1,0:T(1,128)} %get-tuple-element.310.gain_ref.refs_6_, ...), custom_call_target="tpu_custom_call" | custom-call | flops 943718400 | bytes 9830400 | tf_op jit(solution)/shard_map/enter_first/pallas_call | solution.py:197
  69.6 3.3 collective-permute-done.14.refs_13_
  78.0 8.6 %collective-permute-done.23.refs_25_ = bf16[480,640]{1,0:T(8,128)(2,1)S(1)} collective-permute-done((bf16[480,640]{1,0:T(8,128)(2,1)}, bf16[480,640]{1,0:T(8,128)(2,1)S(1)}, u32[]{:S(2)}, u32[]{:S(2)}) %collective-permute-start.23) | collective-permute-done | bytes 614432 | tf_op jit(solution)/shard_map/ppermute | solution.py:938
  87.7 3.4 collective-permute-done.18.refs_19_
  95.0 16.7 %forward_first.1 = (f32[256,960]{1,0:T(8,128)}, bf16[256,960]{1,0:T(8,128)(2,1)}, bf16[960,256]{1,0:T(8,128)(2,1)}, f32[5,768]{1,0:T(8,128)}, f32[256,960]{1,0:T...) custom-call(s32[4]{0:T(128)} %and_convert_fusion.refs_0_.visible_ref, ...), custom_call_target="tpu_custom_call" | custom-call | flops 5033164800 | bytes 19988480 | tf_op jit(solution)/shard_map/forward_first/pallas_call | solution.py:372
  111.8 5.2 %enter.1 = (bf16[256,960]{1,0:T(8,128)(2,1)}, bf16[960,256]{1,0:T(8,128)(2,1)}, bf16[640,256]{1,0:T(8,128)(2,1)}) custom-call(f32[256,960]{1,0:T(8,128)} %get-tuple-element.175.h_ref.refs_2_, f32[1,960]{1,0:T(1,128)} %get-tuple-element.310.gain_ref.refs_6_, f32[32,256]{1,0:T(8,128)} %get-tuple-element.316.cos_ref.refs_7_, ...), custom_call_target="tpu_custom_call" | custom-call | flops 817889280 | bytes 5652480 | tf_op jit(solution)/shard_map/enter/pallas_call | solution.py:231
  118.5 8.5 %collective-permute-done.27.refs_6_.kv2_ref = bf16[640,256]{1,0:T(8,128)(2,1)S(1)} collective-permute-done((bf16[640,256]{1,0:T(8,128)(2,1)}, bf16[640,256]{1,0:T(8,128)(2,1)S(1)}, u32[]{:S(2)}, u32[]{:S(2)}) %collective-permute-start.27) | collective-permute-done | bytes 327712 | tf_op jit(solution)/shard_map/ppermute | solution.py:938
  129.3 19.5 %forward_last.1 = (bf16[960,256]{1,0:T(8,128)(2,1)}, bf16[256,960]{1,0:T(8,128)(2,1)}, bf16[960,256]{1,0:T(8,128)(2,1)}, f32[5,768]{1,0:T(8,128)}, f32[256,960]{...) custom-call(s32[4]{0:T(128)} %and_convert_fusion.refs_0_.visible_ref, ...), custom_call_target="tpu_custom_call" | custom-call | flops 5033164800 | bytes 19988480 | tf_op jit(solution)/shard_map/forward_last/pallas_call | solution.py:372
  148.8 14.9 %feed_back.1 = (bf16[256,960]{1,0:T(8,128)(2,1)}, bf16[256,5120]{1,0:T(8,128)(2,1)}, f32[256,960]{1,0:T(8,128)}, bf16[256,1024]{1,0:T(8,128)(2,1)}, bf16[960,256]{1,0:T(8,128)(2,1)}, /*index=5*/f32[1,960]{1,0:T(1,128)}) custom-call(bf16[960,256]{1,0:T(8,128)(2,1)} %bitcast.123, f32[256,960]{1,0:T(8,128)} %get-tuple-element.181.middle_ref, ...), custom_call_target="tpu_custom_call" | custom-call | flops 5033164800 | bytes 19988480 | tf_op jit(solution)/shard_map/feed_back/pallas_call | solution.py:480
  163.7 14.0 %attend_back.2 = (bf16[960,256]{1,0:T(8,128)(2,1)}, bf16[640,256]{1,0:T(8,128)(2,1)}, bf16[640,256]{1,0:T(8,128)(2,1)}, bf16[640,256]{1,0:T(8,128)(2,1)}, bf16[640,256]{1,0:T(8,128)(2,1)}) custom-call(s32[4]{0:T(128)} %and_convert_fusion.refs_0_.visible_ref, bf16[960,256]{1,0:T(8,128)(2,1)} %get-tuple-element.176.refs_3_.q_ref, ...), custom_call_target="tpu_custom_call" | custom-call | flops 5033164800 | bytes 4915200 | tf_op jit(solution)/shard_map/attend_back/pallas_call | solution.py:587
  184.2 7.6 %collective-permute-done.30.got_ref = bf16[640,256]{1,0:T(8,128)(2,1)S(1)} collective-permute-done((bf16[640,256]{1,0:T(8,128)(2,1)S(1)}, bf16[640,256]{1,0:T(8,128)(2,1)S(1)}, u32[]{:S(2)}, u32[]{:S(2)}) %collective-permute-start.30) | collective-permute-done | bytes 327712 | tf_op jit(solution)/shard_map/ppermute | solution.py:938
  192.5 6.2 %leave.1 = (f32[256,960]{1,0:T(8,128)}, bf16[256,1664]{1,0:T(8,128)(2,1)}, f32[1,960]{1,0:T(1,128)}) custom-call(f32[256,960]{1,0:T(8,128)} %get-tuple-element.175.h_ref.refs_2_, f32[256,960]{1,0:T(8,128)} %get-tuple-element.185.dmid_ref, bf16[960,256]{1,0:T(8,128)(2,1)} %get-tuple-element.189.dq_ref, bf16[640,256]{1,0:T(8,128)(2,1)} %get-tuple-element.306.own_ref, ...), custom_call_target="tpu_custom_call" | custom-call | flops 817889280 | bytes 6635520 | tf_op jit(solution)/shard_map/leave/pallas_call | solution.py:655
  198.7 7.0 %down_grad.1 = (bf16[2,4,240,640]{3,2,1,0:T(8,128)(2,1)}, bf16[2,4,240,640]{3,2,1,0:T(8,128)(2,1)}) custom-call(s32[3]{0:T(128)} %pad_add_fusion.1.place_ref.refs_0_, bf16[256,960]{1,0:T(8,128)(2,1)} %get-tuple-element.184.g2_ref, f32[256,960]{1,0:T(8,128)} %get-tuple-element.201.g_ref.refs_1_, bf16[256,2560]{1,0:T(8,128)(2,1)} %get-tuple-element.195.inner2_ref, ...), custom_call_target="tpu_custom_call" | custom-call | flops 2516582400 | bytes 4915200 | tf_op jit(solution)/shard_map/down_grad/pallas_call | solution.py:809
  205.7 4.9 %collective-permute-done.31 = bf16[2,4,240,640]{3,2,1,0:T(8,128)(2,1)S(1)} collective-permute-done((bf16[2,4,240,640]{3,2,1,0:T(8,128)(2,1)}, bf16[2,4,240,640]{3,2,1,0:T(8,128)(2,1)S(1)}, u32[]{:S(2)}, u32[]{:S(2)}) %collective-permute-start.31) | collective-permute-done | bytes 2457632 | tf_op jit(solution)/shard_map/ppermute | solution.py:938
  210.6 2.4 fusion.10
  215.1 25.0 %feed_back_gate.1 = (f32[256,960]{1,0:T(8,128)}, bf16[256,1024]{1,0:T(8,128)(2,1)}, bf16[960,256]{1,0:T(8,128)(2,1)}, f32[1,960]{1,0:T(1,128)}, bf16[2,4,240,640...) custom-call(s32[3]{0:T(128)} %pad_add_fusion.1.place_ref.refs_0_, ...), custom_call_target="tpu_custom_call" | custom-call | flops 10066329600 | bytes 19988480 | tf_op jit(solution)/shard_map/feed_back_gate/pallas_call | solution.py:716
  242.2 2.4 fusion.3
  244.6 4.9 %collective-permute-done.34 = bf16[2,4,240,640]{3,2,1,0:T(8,128)(2,1)S(1)} collective-permute-done((bf16[2,4,240,640]{3,2,1,0:T(8,128)(2,1)}, bf16[2,4,240,640]{3,2,1,0:T(8,128)(2,1)S(1)}, u32[]{:S(2)}, u32[]{:S(2)}) %collective-permute-start.34) | collective-permute-done | bytes 2457632 | tf_op jit(solution)/shard_map/ppermute | solution.py:938
  253.3 6.2 %attend_back.3 = (bf16[960,256]{1,0:T(8,128)(2,1)}, bf16[640,256]{1,0:T(8,128)(2,1)}, bf16[640,256]{1,0:T(8,128)(2,1)}, bf16[640,256]{1,0:T(8,128)(2,1)}, bf16[640,256]{1,0:T(8,128)(2,1)}) custom-call(s32[4]{0:T(128)} %and_convert_fusion.refs_0_.visible_ref, bf16[960,256]{1,0:T(8,128)(2,1)} %get-tuple-element.215.refs_3_.q_ref, ...), custom_call_target="tpu_custom_call" | custom-call | flops 5033164800 | bytes 4915200 | tf_op jit(solution)/shard_map/attend_back/pallas_call | solution.py:587
  259.4 8.2 %collective-permute-done.35 = bf16[2,240,640]{2,1,0:T(8,128)(2,1)} collective-permute-done((bf16[2,240,640]{2,1,0:T(8,128)(2,1)}, bf16[2,240,640]{2,1,0:T(8,128)(2,1)}, u32[]{:S(2)}, u32[]{:S(2)}) %collective-permute-start.35) | collective-permute-done | bytes 614432 | tf_op jit(solution)/shard_map/ppermute | solution.py:938
  275.2 13.3 %collective-permute-done.38 = bf16[2,240,640]{2,1,0:T(8,128)(2,1)S(1)} collective-permute-done((bf16[2,240,640]{2,1,0:T(8,128)(2,1)S(1)}, bf16[2,240,640]{2,1,0:T(8,128)(2,1)S(1)}, u32[]{:S(2)}, u32[]{:S(2)}) %collective-permute-start.38) | collective-permute-done | bytes 614432 | tf_op jit(solution)/shard_map/ppermute | solution.py:938
  291.7 20.4 %collective-permute-done.40.refs_5_ = bf16[640,256]{1,0:T(8,128)(2,1)S(1)} collective-permute-done((bf16[640,256]{1,0:T(8,128)(2,1)S(1)}, bf16[640,256]{1,0:T(8,128)(2,1)S(1)}, u32[]{:S(2)}, u32[]{:S(2)}) %collective-permute-start.40) | collective-permute-done | bytes 327712 | tf_op jit(solution)/shard_map/ppermute | solution.py:938
  312.8 11.6 %leave_mixed.1 = (bf16[960,256]{1,0:T(8,128)(2,1)}, bf16[2,4,256,640]{3,2,1,0:T(8,128)(2,1)}, bf16[2,4,256,640]{3,2,1,0:T(8,128)(2,1)}) custom-call(s32[3]{0:T(128)} %pad_add_fusion.1.place_ref.refs_0_, f32[256,960]{1,0:T(8,128)} %get-tuple-element.165.refs_2_.refs_1_, f32[256,960]{1,0:T(8,128)} %get-tuple-element.236.refs_2_, ...), custom_call_target="tpu_custom_call" | custom-call | flops 2453667840 | bytes 6635520 | tf_op jit(solution)/shard_map/leave_mixed/pallas_call | solution.py:767
  326.3 10.8 %collective-permute-start.43 = (bf16[240,640]{1,0:T(8,128)(2,1)S(1)}, bf16[240,640]{1,0:T(8,128)(2,1)S(1)}, u32[]{:S(2)}, u32[]{:S(2)}) collective-permute-start(bf16[240,640]{1,0:T(8,128)(2,1)S(1)} %copy-done.52), channel_id=1, source_target_pairs={{0,8},{4,12},{8,0},{12,4},{16,24},{20,28},{24,16},{28,20},{1,9},{5... | collective-permute-start | bytes 921608 | tf_op jit(solution)/shard_map/ppermute | solution.py:938
  343.1 11.4 %collective-permute-start.47 = (bf16[240,640]{1,0:T(8,128)(2,1)S(1)}, bf16[240,640]{1,0:T(8,128)(2,1)S(1)}, u32[]{:S(2)}, u32[]{:S(2)}) collective-permute-start(bf16[240,640]{1,0:T(8,128)(2,1)S(1)} %fusion.20), channel_id=1, source_target_pairs={{0,8},{4,12},{8,0},{12,4},{16,24},{20,28},{24,16},{28,20},{1,9},{5... | collective-permute-start | bytes 921608 | tf_op jit(solution)/shard_map/ppermute | solution.py:938
  355.9 2.6 collective-permute-start.48
  365.9 4.5 collective-permute-done.48
  370.6 3.1 collective-permute-start.51
  374.8 10.7 %collective-permute-done.50.p1_ref = bf16[240,640]{1,0:T(8,128)(2,1)S(1)} collective-permute-done((bf16[240,640]{1,0:T(8,128)(2,1)S(1)}, bf16[240,640]{1,0:T(8,128)(2,1)S(1)}, u32[]{:S(2)}, u32[]{:S(2)}) %collective-permute-start.50) | collective-permute-done | bytes 307232 | tf_op jit(solution)/shard_map/ppermute | solution.py:938
  385.6 3.0 collective-permute-start.53
  399.6 5.9 %collective-permute-done.55.p3_ref = bf16[240,640]{1,0:T(8,128)(2,1)} collective-permute-done((bf16[240,640]{1,0:T(8,128)(2,1)S(1)}, bf16[240,640]{1,0:T(8,128)(2,1)}, u32[]{:S(2)}, u32[]{:S(2)}) %collective-permute-start.55) | collective-permute-done | bytes 307232 | tf_op jit(solution)/shard_map/ppermute | solution.py:938
  405.5 4.1 finish.3
  418.2 9.7 %collective-permute-done.59.p1_ref = bf16[240,640]{1,0:T(8,128)(2,1)S(1)} collective-permute-done((bf16[240,640]{1,0:T(8,128)(2,1)S(1)}, bf16[240,640]{1,0:T(8,128)(2,1)S(1)}, u32[]{:S(2)}, u32[]{:S(2)}) %collective-permute-start.59) | collective-permute-done | bytes 307232 | tf_op jit(solution)/shard_map/ppermute | solution.py:938
  429.7 3.9 finish.4
  434.9 2.9 collective-permute-start.65
  439.8 8.2 %collective-permute-done.63.p2_ref = bf16[240,640]{1,0:T(8,128)(2,1)S(1)} collective-permute-done((bf16[240,640]{1,0:T(8,128)(2,1)S(1)}, bf16[240,640]{1,0:T(8,128)(2,1)S(1)}, u32[]{:S(2)}, u32[]{:S(2)}) %collective-permute-start.63) | collective-permute-done | bytes 307232 | tf_op jit(solution)/shard_map/ppermute | solution.py:938
  448.0 3.3 collective-permute-done.64.p3_ref
  452.1 3.9 finish.5
  456.0 2.5 collective-permute-start.66
  460.0 4.1 collective-permute-done.66.p1_ref
  467.5 5.2 %collective-permute-done.68.p3_ref = bf16[256,640]{1,0:T(8,128)(2,1)S(1)} collective-permute-done((bf16[256,640]{1,0:T(8,128)(2,1)S(1)}, bf16[256,640]{1,0:T(8,128)(2,1)S(1)}, u32[]{:S(2)}, u32[]{:S(2)}) %collective-permute-start.68) | collective-permute-done | bytes 327712 | tf_op jit(solution)/shard_map/ppermute | solution.py:938
  473.4 3.4 finish_mixed.1
  (276 shorter events, 110.7 us)
Async XLA Ops:
  2.0 10.6 %collective-permute-start = (bf16[2,240]{1,0:T(2,128)(2,1)S(1)}, bf16[2,240]{1,0:T(2,128)(2,1)S(1)}, u32[]{:S(2)}, u32[]{:S(2)}) collective-permute-start(bf16[2,240]{1,0:T(2,128)(2,1)S(1)} %pad_maximum_fusion.2), channel_id=1, source_target_pairs={{0,1},{1,0},{2,3},{3,2},{4,5},{5,4},{6,7},{7,6},{8,9},{9,8},{10,11... | collective-permute-start | bytes 2888 | tf_op jit(solution)/shard_map/ppermute | solution.py:938
  10.0 49.3 %collective-permute-start.3 = (bf16[240,2560]{1,0:T(8,128)(2,1)}, bf16[240,2560]{1,0:T(8,128)(2,1)}, u32[]{:S(2)}, u32[]{:S(2)}) collective-permute-start(bf16[240,2560]{1,0:T(8,128)(2,1)} %get-tuple-element.162.refs_0_), channel_id=1, source_target_pairs={{0,1},{1,0},{2,3},{3,2},{4,5},{5,4},{6,7},{7,6},{8,9},{9,8},{10,11... | collective-permute-start | bytes 3686408 | tf_op jit(solution)/shard_map/ppermute | solution.py:938
  12.6 16.3 %collective-permute-start.4 = (bf16[240,1280]{1,0:T(8,128)(2,1)S(1)}, bf16[240,1280]{1,0:T(8,128)(2,1)}, u32[]{:S(2)}, u32[]{:S(2)}) collective-permute-start(bf16[240,1280]{1,0:T(8,128)(2,1)S(1)} %copy-done.62), channel_id=1, source_target_pairs={{0,2},{1,3},{2,0},{3,1},{4,6},{5,7},{6,4},{7,5},{8,10},{9,11},{10,... | collective-permute-start | bytes 1843208 | tf_op jit(solution)/shard_map/ppermute | solution.py:938
  28.9 15.5 %collective-permute-start.5 = (bf16[240,1280]{1,0:T(8,128)(2,1)}, bf16[240,1280]{1,0:T(8,128)(2,1)S(1)}, u32[]{:S(2)}, u32[]{:S(2)}) collective-permute-start(bf16[240,1280]{1,0:T(8,128)(2,1)} %collective-permute-done.4.refs_2_), channel_id=1, source_target_pairs={{0,4},{4,0},{8,12},{12,8},{16,20},{20,16},{24,28},{28,24},{1,5},{5... | collective-permute-start | bytes 1843208 | tf_op jit(solution)/shard_map/ppermute | solution.py:938
  30.6 17.0 %collective-permute-start.13 = (bf16[240,1280]{1,0:T(8,128)(2,1)}, bf16[240,1280]{1,0:T(8,128)(2,1)S(1)}, u32[]{:S(2)}, u32[]{:S(2)}) collective-permute-start(bf16[240,1280]{1,0:T(8,128)(2,1)} %get-tuple-element.157), channel_id=1, source_target_pairs={{0,2},{1,3},{2,0},{3,1},{4,6},{5,7},{6,4},{7,5},{8,10},{9,11},{10,... | collective-permute-start | bytes 1843208 | tf_op jit(solution)/shard_map/ppermute | solution.py:938
  32.1 26.7 %collective-permute-start.12 = (bf16[240,1280]{1,0:T(8,128)(2,1)}, bf16[240,1280]{1,0:T(8,128)(2,1)S(1)}, u32[]{:S(2)}, u32[]{:S(2)}) collective-permute-start(bf16[240,1280]{1,0:T(8,128)(2,1)} %get-tuple-element.158), channel_id=1, source_target_pairs={{0,2},{1,3},{2,0},{3,1},{4,6},{5,7},{6,4},{7,5},{8,10},{9,11},{10,... | collective-permute-start | bytes 1843208 | tf_op jit(solution)/shard_map/ppermute | solution.py:938
  32.7 28.2 %collective-permute-start.6 = (bf16[240,1280]{1,0:T(8,128)(2,1)}, bf16[240,1280]{1,0:T(8,128)(2,1)S(1)}, u32[]{:S(2)}, u32[]{:S(2)}) collective-permute-start(bf16[240,1280]{1,0:T(8,128)(2,1)} %collective-permute-done.4.refs_2_), channel_id=1, source_target_pairs={{0,1},{1,0},{2,3},{3,2},{4,5},{5,4},{6,7},{7,6},{8,9},{9,8},{10,11... | collective-permute-start | bytes 1843208 | tf_op jit(solution)/shard_map/ppermute | solution.py:938
  44.4 17.3 %collective-permute-start.7 = (bf16[240,1280]{1,0:T(8,128)(2,1)S(1)}, bf16[240,1280]{1,0:T(8,128)(2,1)S(1)}, u32[]{:S(2)}, u32[]{:S(2)}) collective-permute-start(bf16[240,1280]{1,0:T(8,128)(2,1)S(1)} %collective-permute-done.5.refs_3_), channel_id=1, source_target_pairs={{0,1},{1,0},{2,3},{3,2},{4,5},{5,4},{6,7},{7,6},{8,9},{9,8},{10,11... | collective-permute-start | bytes 1843208 | tf_op jit(solution)/shard_map/ppermute | solution.py:938
  47.6 27.2 %collective-permute-start.21 = (bf16[960,640]{1,0:T(8,128)(2,1)}, bf16[960,640]{1,0:T(8,128)(2,1)S(1)}, u32[]{:S(2)}, u32[]{:S(2)}) collective-permute-start(bf16[960,640]{1,0:T(8,128)(2,1)} %bitcast.119), channel_id=1, source_target_pairs={{0,1},{1,0},{2,3},{3,2},{4,5},{5,4},{6,7},{7,6},{8,9},{9,8},{10,11... | collective-permute-start | bytes 3686408 | tf_op jit(solution)/shard_map/ppermute | solution.py:938
  58.8 14.0 %collective-permute-start.14 = (bf16[240,1280]{1,0:T(8,128)(2,1)S(1)}, bf16[240,1280]{1,0:T(8,128)(2,1)}, u32[]{:S(2)}, u32[]{:S(2)}) collective-permute-start(bf16[240,1280]{1,0:T(8,128)(2,1)S(1)} %collective-permute-done.13.refs_12_), channel_id=1, source_target_pairs={{0,4},{4,0},{8,12},{12,8},{16,20},{20,16},{24,28},{28,24},{1,5},{5... | collective-permute-start | bytes 1843208 | tf_op jit(solution)/shard_map/ppermute | solution.py:938
  59.3 14.2 %collective-permute-start.22 = (bf16[480,640]{1,0:T(8,128)(2,1)}, bf16[480,640]{1,0:T(8,128)(2,1)}, u32[]{:S(2)}, u32[]{:S(2)}) collective-permute-start(bf16[480,640]{1,0:T(8,128)(2,1)} %slice_select_fusion), channel_id=1, source_target_pairs={{0,2},{1,3},{2,0},{3,1},{4,6},{5,7},{6,4},{7,5},{8,10},{9,11},{10,... | collective-permute-start | bytes 1843208 | tf_op jit(solution)/shard_map/ppermute | solution.py:938
  60.8 15.6 %collective-permute-start.11 = (bf16[240,2560]{1,0:T(8,128)(2,1)S(1)}, bf16[240,2560]{1,0:T(8,128)(2,1)S(1)}, u32[]{:S(2)}, u32[]{:S(2)}) collective-permute-start(bf16[240,2560]{1,0:T(8,128)(2,1)S(1)} %copy-done.2), channel_id=1, source_target_pairs={{0,1},{1,0},{2,3},{3,2},{4,5},{5,4},{6,7},{7,6},{8,9},{9,8},{10,11... | collective-permute-start | bytes 3686408 | tf_op jit(solution)/shard_map/ppermute | solution.py:938
  61.7 16.3 %collective-permute-start.17 = (bf16[240,2560]{1,0:T(8,128)(2,1)S(1)}, bf16[240,2560]{1,0:T(8,128)(2,1)S(1)}, u32[]{:S(2)}, u32[]{:S(2)}) collective-permute-start(bf16[240,2560]{1,0:T(8,128)(2,1)S(1)} %copy-done.3), channel_id=1, source_target_pairs={{0,1},{1,0},{2,3},{3,2},{4,5},{5,4},{6,7},{7,6},{8,9},{9,8},{10,11... | collective-permute-start | bytes 3686408 | tf_op jit(solution)/shard_map/ppermute | solution.py:938
  73.5 13.1 %collective-permute-start.23 = (bf16[480,640]{1,0:T(8,128)(2,1)}, bf16[480,640]{1,0:T(8,128)(2,1)S(1)}, u32[]{:S(2)}, u32[]{:S(2)}) collective-permute-start(bf16[480,640]{1,0:T(8,128)(2,1)} %collective-permute-done.22.refs_24_), channel_id=1, source_target_pairs={{0,4},{4,0},{8,12},{12,8},{16,20},{20,16},{24,28},{28,24},{1,5},{5... | collective-permute-start | bytes 1843208 | tf_op jit(solution)/shard_map/ppermute | solution.py:938
  74.8 12.5 %collective-permute-start.15 = (bf16[240,1280]{1,0:T(8,128)(2,1)S(1)}, bf16[240,1280]{1,0:T(8,128)(2,1)S(1)}, u32[]{:S(2)}, u32[]{:S(2)}) collective-permute-start(bf16[240,1280]{1,0:T(8,128)(2,1)S(1)} %collective-permute-done.13.refs_12_), channel_id=1, source_target_pairs={{0,1},{1,0},{2,3},{3,2},{4,5},{5,4},{6,7},{7,6},{8,9},{9,8},{10,11... | collective-permute-start | bytes 1843208 | tf_op jit(solution)/shard_map/ppermute | solution.py:938
  74.8 16.3 %collective-permute-start.18 = (bf16[240,1280]{1,0:T(8,128)(2,1)S(1)}, bf16[240,1280]{1,0:T(8,128)(2,1)S(1)}, u32[]{:S(2)}, u32[]{:S(2)}) collective-permute-start(bf16[240,1280]{1,0:T(8,128)(2,1)S(1)} %collective-permute-done.12.refs_18_), channel_id=1, source_target_pairs={{0,8},{4,12},{8,0},{12,4},{16,24},{20,28},{24,16},{28,20},{1,9},{5... | collective-permute-start | bytes 1843208 | tf_op jit(solution)/shard_map/ppermute | solution.py:938
  213.0 27.1 %collective-permute-start.32 = (bf16[2,240,640]{2,1,0:T(8,128)(2,1)S(1)}, bf16[2,240,640]{2,1,0:T(8,128)(2,1)S(1)}, u32[]{:S(2)}, u32[]{:S(2)}) collective-permute-start(bf16[2,240,640]{2,1,0:T(8,128)(2,1)S(1)} %get-tuple-element.302), channel_id=1, source_target_pairs={{0,2},{1,3},{2,0},{3,1},{4,6},{5,7},{6,4},{7,5},{8,10},{9,11},{10,... | collective-permute-start | bytes 1843208 | tf_op jit(solution)/shard_map/ppermute | solution.py:938
  214.6 27.5 %collective-permute-start.33 = (bf16[2,240,640]{2,1,0:T(8,128)(2,1)S(1)}, bf16[2,240,640]{2,1,0:T(8,128)(2,1)S(1)}, u32[]{:S(2)}, u32[]{:S(2)}) collective-permute-start(bf16[2,240,640]{2,1,0:T(8,128)(2,1)S(1)} %get-tuple-element.301), channel_id=1, source_target_pairs={{0,2},{1,3},{2,0},{3,1},{4,6},{5,7},{6,4},{7,5},{8,10},{9,11},{10,... | collective-permute-start | bytes 1843208 | tf_op jit(solution)/shard_map/ppermute | solution.py:938
  251.1 37.4 %collective-permute-start.39 = (bf16[2,4,240,640]{3,2,1,0:T(8,128)(2,1)}, bf16[2,4,240,640]{3,2,1,0:T(8,128)(2,1)S(1)}, u32[]{:S(2)}, u32[]{:S(2)}) collective-permute-start(bf16[2,4,240,640]{3,2,1,0:T(8,128)(2,1)} %get-tuple-element.234), channel_id=1, source_target_pairs={{0,1},{1,0},{2,3},{3,2},{4,5},{5,4},{6,7},{7,6},{8,9},{9,8},{10,11... | collective-permute-start | bytes 7372808 | tf_op jit(solution)/shard_map/ppermute | solution.py:938
  251.2 16.4 %collective-permute-start.35 = (bf16[2,240,640]{2,1,0:T(8,128)(2,1)}, bf16[2,240,640]{2,1,0:T(8,128)(2,1)}, u32[]{:S(2)}, u32[]{:S(2)}) collective-permute-start(bf16[2,240,640]{2,1,0:T(8,128)(2,1)} %get-tuple-element.300), channel_id=1, source_target_pairs={{0,2},{1,3},{2,0},{3,1},{4,6},{5,7},{6,4},{7,5},{8,10},{9,11},{10,... | collective-permute-start | bytes 1843208 | tf_op jit(solution)/shard_map/ppermute | solution.py:938
  252.7 17.3 %collective-permute-start.36 = (bf16[2,240,640]{2,1,0:T(8,128)(2,1)}, bf16[2,240,640]{2,1,0:T(8,128)(2,1)}, u32[]{:S(2)}, u32[]{:S(2)}) collective-permute-start(bf16[2,240,640]{2,1,0:T(8,128)(2,1)} %fusion.3), channel_id=1, source_target_pairs={{0,4},{4,0},{8,12},{12,8},{16,20},{20,16},{24,28},{28,24},{1,5},{5... | collective-permute-start | bytes 1843208 | tf_op jit(solution)/shard_map/ppermute | solution.py:938
  272.2 16.3 %collective-permute-start.38 = (bf16[2,240,640]{2,1,0:T(8,128)(2,1)S(1)}, bf16[2,240,640]{2,1,0:T(8,128)(2,1)S(1)}, u32[]{:S(2)}, u32[]{:S(2)}) collective-permute-start(bf16[2,240,640]{2,1,0:T(8,128)(2,1)S(1)} %get-tuple-element.299), channel_id=1, source_target_pairs={{0,2},{1,3},{2,0},{3,1},{4,6},{5,7},{6,4},{7,5},{8,10},{9,11},{10,... | collective-permute-start | bytes 1843208 | tf_op jit(solution)/shard_map/ppermute | solution.py:938
  289.6 34.9 %collective-permute-start.41 = (bf16[2,240,640]{2,1,0:T(8,128)(2,1)S(1)}, bf16[2,240,640]{2,1,0:T(8,128)(2,1)S(1)}, u32[]{:S(2)}, u32[]{:S(2)}) collective-permute-start(bf16[2,240,640]{2,1,0:T(8,128)(2,1)S(1)} %get-tuple-element.298), channel_id=1, source_target_pairs={{0,2},{1,3},{2,0},{3,1},{4,6},{5,7},{6,4},{7,5},{8,10},{9,11},{10,... | collective-permute-start | bytes 1843208 | tf_op jit(solution)/shard_map/ppermute | solution.py:938
  291.2 20.9 %collective-permute-start.40 = (bf16[640,256]{1,0:T(8,128)(2,1)S(1)}, bf16[640,256]{1,0:T(8,128)(2,1)S(1)}, u32[]{:S(2)}, u32[]{:S(2)}) collective-permute-start(bf16[640,256]{1,0:T(8,128)(2,1)S(1)} %get-tuple-element.232), channel_id=1, source_target_pairs={{0,2},{1,3},{2,0},{3,1},{4,6},{5,7},{6,4},{7,5},{8,10},{9,11},{10,... | collective-permute-start | bytes 983048 | tf_op jit(solution)/shard_map/ppermute | solution.py:938
  324.9 33.7 %collective-permute-start.44 = (bf16[2,4,256,640]{3,2,1,0:T(8,128)(2,1)}, bf16[2,4,256,640]{3,2,1,0:T(8,128)(2,1)S(1)}, u32[]{:S(2)}, u32[]{:S(2)}) collective-permute-start(bf16[2,4,256,640]{3,2,1,0:T(8,128)(2,1)} %get-tuple-element.256), channel_id=1, source_target_pairs={{0,1},{1,0},{2,3},{3,2},{4,5},{5,4},{6,7},{7,6},{8,9},{9,8},{10,11... | collective-permute-start | bytes 7864328 | tf_op jit(solution)/shard_map/ppermute | solution.py:938
  325.6 16.3 %collective-permute-start.42 = (bf16[2,240,640]{2,1,0:T(8,128)(2,1)S(1)}, bf16[2,240,640]{2,1,0:T(8,128)(2,1)S(1)}, u32[]{:S(2)}, u32[]{:S(2)}) collective-permute-start(bf16[2,240,640]{2,1,0:T(8,128)(2,1)S(1)} %copy-done.32), channel_id=1, source_target_pairs={{0,4},{4,0},{8,12},{12,8},{16,20},{20,16},{24,28},{28,24},{1,5},{5... | collective-permute-start | bytes 1843208 | tf_op jit(solution)/shard_map/ppermute | solution.py:938
  326.3 28.3 %collective-permute-start.43 = (bf16[240,640]{1,0:T(8,128)(2,1)S(1)}, bf16[240,640]{1,0:T(8,128)(2,1)S(1)}, u32[]{:S(2)}, u32[]{:S(2)}) collective-permute-start(bf16[240,640]{1,0:T(8,128)(2,1)S(1)} %copy-done.52), channel_id=1, source_target_pairs={{0,8},{4,12},{8,0},{12,4},{16,24},{20,28},{24,16},{28,20},{1,9},{5... | collective-permute-start | bytes 921608 | tf_op jit(solution)/shard_map/ppermute | solution.py:938
  337.0 24.4 %collective-permute-start.46 = (bf16[2,240,640]{2,1,0:T(8,128)(2,1)S(1)}, bf16[2,240,640]{2,1,0:T(8,128)(2,1)S(1)}, u32[]{:S(2)}, u32[]{:S(2)}) collective-permute-start(bf16[2,240,640]{2,1,0:T(8,128)(2,1)S(1)} %get-tuple-element.297), channel_id=1, source_target_pairs={{0,2},{1,3},{2,0},{3,1},{4,6},{5,7},{6,4},{7,5},{8,10},{9,11},{10,... | collective-permute-start | bytes 1843208 | tf_op jit(solution)/shard_map/ppermute | solution.py:938
  338.8 22.7 %collective-permute-start.45 = (bf16[2,240,640]{2,1,0:T(8,128)(2,1)S(1)}, bf16[2,240,640]{2,1,0:T(8,128)(2,1)S(1)}, u32[]{:S(2)}, u32[]{:S(2)}) collective-permute-start(bf16[2,240,640]{2,1,0:T(8,128)(2,1)S(1)} %fusion.1), channel_id=1, source_target_pairs={{0,4},{4,0},{8,12},{12,8},{16,20},{20,16},{24,28},{28,24},{1,5},{5... | collective-permute-start | bytes 1843208 | tf_op jit(solution)/shard_map/ppermute | solution.py:938
  343.1 21.5 %collective-permute-start.47 = (bf16[240,640]{1,0:T(8,128)(2,1)S(1)}, bf16[240,640]{1,0:T(8,128)(2,1)S(1)}, u32[]{:S(2)}, u32[]{:S(2)}) collective-permute-start(bf16[240,640]{1,0:T(8,128)(2,1)S(1)} %fusion.20), channel_id=1, source_target_pairs={{0,8},{4,12},{8,0},{12,4},{16,24},{20,28},{24,16},{28,20},{1,9},{5... | collective-permute-start | bytes 921608 | tf_op jit(solution)/shard_map/ppermute | solution.py:938
  355.9 14.5 %collective-permute-start.48 = (bf16[240,640]{1,0:T(8,128)(2,1)S(1)}, bf16[240,640]{1,0:T(8,128)(2,1)S(1)}, u32[]{:S(2)}, u32[]{:S(2)}) collective-permute-start(bf16[240,640]{1,0:T(8,128)(2,1)S(1)} %fusion.22), channel_id=1, source_target_pairs={{0,16},{4,20},{8,24},{12,28},{16,0},{20,4},{24,8},{28,12},{1,17},{... | collective-permute-start | bytes 921608 | tf_op jit(solution)/shard_map/ppermute | solution.py:938
  359.7 14.0 %collective-permute-start.49 = (bf16[2,256,640]{2,1,0:T(8,128)(2,1)S(1)}, bf16[2,256,640]{2,1,0:T(8,128)(2,1)S(1)}, u32[]{:S(2)}, u32[]{:S(2)}) collective-permute-start(bf16[2,256,640]{2,1,0:T(8,128)(2,1)S(1)} %get-tuple-element.296), channel_id=1, source_target_pairs={{0,2},{1,3},{2,0},{3,1},{4,6},{5,7},{6,4},{7,5},{8,10},{9,11},{10,... | collective-permute-start | bytes 1966088 | tf_op jit(solution)/shard_map/ppermute | solution.py:938
  370.5 15.0 %collective-permute-start.50 = (bf16[240,640]{1,0:T(8,128)(2,1)S(1)}, bf16[240,640]{1,0:T(8,128)(2,1)S(1)}, u32[]{:S(2)}, u32[]{:S(2)}) collective-permute-start(bf16[240,640]{1,0:T(8,128)(2,1)S(1)} %add_convert_fusion.15.p0_ref), channel_id=1, source_target_pairs={{0,8},{4,12},{8,0},{12,4},{16,24},{20,28},{24,16},{28,20},{1,9},{5... | collective-permute-start | bytes 921608 | tf_op jit(solution)/shard_map/ppermute | solution.py:938
  370.6 15.0 %collective-permute-start.51 = (bf16[240,640]{1,0:T(8,128)(2,1)S(1)}, bf16[240,640]{1,0:T(8,128)(2,1)S(1)}, u32[]{:S(2)}, u32[]{:S(2)}) collective-permute-start(bf16[240,640]{1,0:T(8,128)(2,1)S(1)} %fusion.17), channel_id=1, source_target_pairs={{0,16},{4,20},{8,24},{12,28},{16,0},{20,4},{24,8},{28,12},{1,17},{... | collective-permute-start | bytes 921608 | tf_op jit(solution)/shard_map/ppermute | solution.py:938
  373.6 18.8 %collective-permute-start.52 = (bf16[240,640]{1,0:T(8,128)(2,1)S(1)}, bf16[240,640]{1,0:T(8,128)(2,1)S(1)}, u32[]{:S(2)}, u32[]{:S(2)}) collective-permute-start(bf16[240,640]{1,0:T(8,128)(2,1)S(1)} %fusion.15), channel_id=1, source_target_pairs={{0,8},{4,12},{8,0},{12,4},{16,24},{20,28},{24,16},{28,20},{1,9},{5... | collective-permute-start | bytes 921608 | tf_op jit(solution)/shard_map/ppermute | solution.py:938
  385.6 11.0 %collective-permute-start.53 = (bf16[240,640]{1,0:T(8,128)(2,1)S(1)}, bf16[240,640]{1,0:T(8,128)(2,1)S(1)}, u32[]{:S(2)}, u32[]{:S(2)}) collective-permute-start(bf16[240,640]{1,0:T(8,128)(2,1)S(1)} %add_convert_fusion.14.p0_ref), channel_id=1, source_target_pairs={{0,8},{4,12},{8,0},{12,4},{16,24},{20,28},{24,16},{28,20},{1,9},{5... | collective-permute-start | bytes 921608 | tf_op jit(solution)/shard_map/ppermute | solution.py:938
  388.6 10.2 %collective-permute-start.54 = (bf16[240,640]{1,0:T(8,128)(2,1)S(1)}, bf16[240,640]{1,0:T(8,128)(2,1)S(1)}, u32[]{:S(2)}, u32[]{:S(2)}) collective-permute-start(bf16[240,640]{1,0:T(8,128)(2,1)S(1)} %add_convert_fusion.15.p0_ref), channel_id=1, source_target_pairs={{0,4},{4,0},{8,12},{12,8},{16,20},{20,16},{24,28},{28,24},{1,5},{5... | collective-permute-start | bytes 921608 | tf_op jit(solution)/shard_map/ppermute | solution.py:938
  389.2 22.3 %collective-permute-start.58 = (bf16[2,256,640]{2,1,0:T(8,128)(2,1)}, bf16[2,256,640]{2,1,0:T(8,128)(2,1)}, u32[]{:S(2)}, u32[]{:S(2)}) collective-permute-start(bf16[2,256,640]{2,1,0:T(8,128)(2,1)} %get-tuple-element.295), channel_id=1, source_target_pairs={{0,2},{1,3},{2,0},{3,1},{4,6},{5,7},{6,4},{7,5},{8,10},{9,11},{10,... | collective-permute-start | bytes 1966088 | tf_op jit(solution)/shard_map/ppermute | solution.py:938
  391.0 14.6 %collective-permute-start.55 = (bf16[240,640]{1,0:T(8,128)(2,1)S(1)}, bf16[240,640]{1,0:T(8,128)(2,1)}, u32[]{:S(2)}, u32[]{:S(2)}) collective-permute-start(bf16[240,640]{1,0:T(8,128)(2,1)S(1)} %collective-permute-done.50.p1_ref), channel_id=1, source_target_pairs={{0,4},{4,0},{8,12},{12,8},{16,20},{20,16},{24,28},{28,24},{1,5},{5... | collective-permute-start | bytes 921608 | tf_op jit(solution)/shard_map/ppermute | solution.py:938
  392.4 20.4 %collective-permute-start.57 = (bf16[2,256,640]{2,1,0:T(8,128)(2,1)}, bf16[2,256,640]{2,1,0:T(8,128)(2,1)}, u32[]{:S(2)}, u32[]{:S(2)}) collective-permute-start(bf16[2,256,640]{2,1,0:T(8,128)(2,1)} %fusion), channel_id=1, source_target_pairs={{0,4},{4,0},{8,12},{12,8},{16,20},{20,16},{24,28},{28,24},{1,5},{5... | collective-permute-start | bytes 1966088 | tf_op jit(solution)/shard_map/ppermute | solution.py:938
  396.6 14.8 %collective-permute-start.56 = (bf16[240,640]{1,0:T(8,128)(2,1)S(1)}, bf16[240,640]{1,0:T(8,128)(2,1)S(1)}, u32[]{:S(2)}, u32[]{:S(2)}) collective-permute-start(bf16[240,640]{1,0:T(8,128)(2,1)S(1)} %fusion.19), channel_id=1, source_target_pairs={{0,16},{4,20},{8,24},{12,28},{16,0},{20,4},{24,8},{28,12},{1,17},{... | collective-permute-start | bytes 921608 | tf_op jit(solution)/shard_map/ppermute | solution.py:938
  414.1 19.5 %collective-permute-start.62 = (bf16[256,640]{1,0:T(8,128)(2,1)S(1)}, bf16[256,640]{1,0:T(8,128)(2,1)S(1)}, u32[]{:S(2)}, u32[]{:S(2)}) collective-permute-start(bf16[256,640]{1,0:T(8,128)(2,1)S(1)} %fusion.6), channel_id=1, source_target_pairs={{0,8},{4,12},{8,0},{12,4},{16,24},{20,28},{24,16},{28,20},{1,9},{5... | collective-permute-start | bytes 983048 | tf_op jit(solution)/shard_map/ppermute | solution.py:938
  414.5 13.4 %collective-permute-start.59 = (bf16[240,640]{1,0:T(8,128)(2,1)S(1)}, bf16[240,640]{1,0:T(8,128)(2,1)S(1)}, u32[]{:S(2)}, u32[]{:S(2)}) collective-permute-start(bf16[240,640]{1,0:T(8,128)(2,1)S(1)} %add_convert_fusion.13.p0_ref), channel_id=1, source_target_pairs={{0,8},{4,12},{8,0},{12,4},{16,24},{20,28},{24,16},{28,20},{1,9},{5... | collective-permute-start | bytes 921608 | tf_op jit(solution)/shard_map/ppermute | solution.py:938
  416.2 11.7 %collective-permute-start.60 = (bf16[240,640]{1,0:T(8,128)(2,1)S(1)}, bf16[240,640]{1,0:T(8,128)(2,1)S(1)}, u32[]{:S(2)}, u32[]{:S(2)}) collective-permute-start(bf16[240,640]{1,0:T(8,128)(2,1)S(1)} %add_convert_fusion.14.p0_ref), channel_id=1, source_target_pairs={{0,4},{4,0},{8,12},{12,8},{16,20},{20,16},{24,28},{28,24},{1,5},{5... | collective-permute-start | bytes 921608 | tf_op jit(solution)/shard_map/ppermute | solution.py:938
  417.5 11.4 %collective-permute-start.61 = (bf16[240,640]{1,0:T(8,128)(2,1)S(1)}, bf16[240,640]{1,0:T(8,128)(2,1)S(1)}, u32[]{:S(2)}, u32[]{:S(2)}) collective-permute-start(bf16[240,640]{1,0:T(8,128)(2,1)S(1)} %copy-done.54), channel_id=1, source_target_pairs={{0,4},{4,0},{8,12},{12,8},{16,20},{20,16},{24,28},{28,24},{1,5},{5... | collective-permute-start | bytes 921608 | tf_op jit(solution)/shard_map/ppermute | solution.py:938
  434.9 21.1 %collective-permute-start.65 = (bf16[256,640]{1,0:T(8,128)(2,1)S(1)}, bf16[256,640]{1,0:T(8,128)(2,1)S(1)}, u32[]{:S(2)}, u32[]{:S(2)}) collective-permute-start(bf16[256,640]{1,0:T(8,128)(2,1)S(1)} %fusion.8), channel_id=1, source_target_pairs={{0,16},{4,20},{8,24},{12,28},{16,0},{20,4},{24,8},{28,12},{1,17},{... | collective-permute-start | bytes 983048 | tf_op jit(solution)/shard_map/ppermute | solution.py:938
  437.8 10.2 %collective-permute-start.63 = (bf16[240,640]{1,0:T(8,128)(2,1)S(1)}, bf16[240,640]{1,0:T(8,128)(2,1)S(1)}, u32[]{:S(2)}, u32[]{:S(2)}) collective-permute-start(bf16[240,640]{1,0:T(8,128)(2,1)S(1)} %add_convert_fusion.13.p0_ref), channel_id=1, source_target_pairs={{0,4},{4,0},{8,12},{12,8},{16,20},{20,16},{24,28},{28,24},{1,5},{5... | collective-permute-start | bytes 921608 | tf_op jit(solution)/shard_map/ppermute | solution.py:938
  439.2 12.1 %collective-permute-start.64 = (bf16[240,640]{1,0:T(8,128)(2,1)S(1)}, bf16[240,640]{1,0:T(8,128)(2,1)S(1)}, u32[]{:S(2)}, u32[]{:S(2)}) collective-permute-start(bf16[240,640]{1,0:T(8,128)(2,1)S(1)} %collective-permute-done.59.p1_ref), channel_id=1, source_target_pairs={{0,4},{4,0},{8,12},{12,8},{16,20},{20,16},{24,28},{28,24},{1,5},{5... | collective-permute-start | bytes 921608 | tf_op jit(solution)/shard_map/ppermute | solution.py:938
  (84 other events, 791.0 us)

commit v3 on v2

--- a/solution.py
+++ b/solution.py
@@ -20,8 +20,8 @@
 
 bf16 = jnp.bfloat16
 f32 = jnp.float32
-VMEM_BYTES = 56 * 1024 * 1024
 GAIN_ROWS = 16
+FFN_MEBIBYTES = 30
 
 
 def nn(left, right):
@@ -44,14 +44,22 @@
     return pl.BlockSpec(memory_space=pl.ANY)
 
 
-def params():
-    return pltpu.CompilerParams(vmem_limit_bytes=VMEM_BYTES)
+def params(mebibytes=20):
+    return pltpu.CompilerParams(vmem_limit_bytes=mebibytes * 1024 * 1024)
 
 
 def shape(dims, dtype):
     return jax.ShapeDtypeStruct(dims, dtype)
 
 
+def kept(array):
+    return pltpu.with_memory_space_constraint(array, pltpu.VMEM)
+
+
+def in_hbm(array):
+    return pltpu.with_memory_space_constraint(array, pltpu.HBM)
+
+
 def cost(flops, bytes_accessed):
     return pl.CostEstimate(flops=int(flops), bytes_accessed=int(bytes_accessed), transcendentals=0)
 
@@ -61,18 +69,28 @@
 
 
 def pack_kernel(
-    bits_ref, query_ref, key_ref, value_ref, out_ref, gate_hbm, up_hbm, packed_ref, mine_ref, gate_ref,
-    up_ref, sems,
+    bits_ref, query_hbm, key_hbm, value_hbm, out_hbm, gate_hbm, up_hbm, packed_hbm, mine_hbm,
+    mine_gate_hbm, mine_up_hbm, query_ref, key_ref, value_ref, out_ref, gate_ref, up_ref, packed_ref,
+    mine_ref, sems,
 ):
     half = gate_ref.shape[1]
     loads = [
-        pltpu.make_async_copy(
-            source.at[:, pl.ds(pl.multiple_of(bits_ref[i] * half, 128), half)], target, sems.at[i]
+        pltpu.make_async_copy(source, target, sems.at[i])
+        for i, (source, target) in enumerate(
+            (
+                (query_hbm, query_ref),
+                (key_hbm, key_ref),
+                (value_hbm, value_ref),
+                (out_hbm, out_ref),
+                (gate_hbm.at[:, pl.ds(pl.multiple_of(bits_ref[0] * half, 128), half)], gate_ref),
+                (up_hbm.at[:, pl.ds(pl.multiple_of(bits_ref[1] * half, 128), half)], up_ref),
+            )
         )
-        for i, (source, target) in enumerate(((gate_hbm, gate_ref), (up_hbm, up_ref)))
     ]
     for load in loads:
         load.start()
+    for load in loads[:4]:
+        load.wait()
     packed_ref[...] = jnp.concatenate(
         [
             query_ref[...].astype(f32),
@@ -84,27 +102,54 @@
     ).astype(bf16)
     wide = mine_ref.shape[1]
     mine_ref[...] = packed_ref[:, pl.ds(pl.multiple_of(bits_ref[0] * wide, 128), wide)]
-    for load in loads:
+    for load in loads[4:]:
         load.wait()
+    stores = [
+        pltpu.make_async_copy(source, target, sems.at[i])
+        for i, (source, target) in enumerate(
+            (
+                (mine_ref, mine_hbm),
+                (gate_ref, mine_gate_hbm),
+                (up_ref, mine_up_hbm),
+                (packed_ref, packed_hbm),
+            )
+        )
+    ]
+    for store in stores:
+        store.start()
+    for store in stores:
+        store.wait()
 
 
 def pack(bits, query, key_t, value_t, out, gate, up):
     rows, width = query.shape
     columns = 2 * width + 2 * key_t.shape[0]
+    ffn = gate.shape[1]
     return pl.pallas_call(
         pack_kernel,
         out_shape=(
-            shape((rows, columns), bf16),
-            shape((rows, columns // 2), bf16),
-        )
-        + (shape((rows, gate.shape[1] // 2), bf16),) * 2,
-        in_specs=[in_smem()] + [in_vmem()] * 4 + [anywhere()] * 2,
-        out_specs=(in_vmem(),) * 4,
-        scratch_shapes=[pltpu.SemaphoreType.DMA((2,))],
+            pltpu.HBM((rows, columns), bf16),
+            pltpu.HBM((rows, columns // 2), bf16),
+            pltpu.HBM((rows, ffn // 2), bf16),
+            pltpu.HBM((rows, ffn // 2), bf16),
+        ),
+        in_specs=[in_smem()] + [anywhere()] * 6,
+        out_specs=(anywhere(),) * 4,
+        scratch_shapes=[
+            pltpu.VMEM((rows, width), bf16),
+            pltpu.VMEM(key_t.shape, bf16),
+            pltpu.VMEM(value_t.shape, bf16),
+            pltpu.VMEM((rows, width), bf16),
+            pltpu.VMEM((rows, ffn // 2), bf16),
+            pltpu.VMEM((rows, ffn // 2), bf16),
+            pltpu.VMEM((rows, columns), bf16),
+            pltpu.VMEM((rows, columns // 2), bf16),
+            pltpu.SemaphoreType.DMA((6,)),
+        ],
         compiler_params=params(),
         cost_estimate=cost(0, 8 * rows * columns),
         name="pack",
-    )(bits, query, key_t, value_t, out, gate, up)
+    )(bits, *[in_hbm(part) for part in (query, key_t, value_t, out, gate, up)])
 
 
 def piece_copies(plan, bits_ref, sources, target_ref, sems):
@@ -173,21 +218,18 @@
 
 def enter_first_kernel(plan, count, index_ref, h_ref, gain_ref, cos_ref, sin_ref, *refs):
     sources = refs[:count]
-    hidden_ref, normed_ref, q_ref, kv_ref, w_hbm, w_ref, sems, out_sem = refs[count:]
+    hidden_ref, normed_ref, q_ref, kv_ref, w_ref, sems = refs[count:]
     copies = piece_copies(plan, index_ref, sources, w_ref, sems)
     for copy in copies:
         copy.start()
     hidden = h_ref[...].astype(f32).T
     hidden_ref[...] = hidden
-    out = pltpu.make_async_copy(w_ref, w_hbm, out_sem)
 
     def ready():
         for copy in copies:
             copy.wait()
-        out.start()
 
     enter_body(hidden, gain_ref, cos_ref, sin_ref, ready, normed_ref, q_ref, kv_ref, w_ref)
-    out.wait()
 
 
 def enter_first(index, hidden_t, gain, cos, sin, plan, sources):
@@ -201,26 +243,20 @@
             shape((rows, width), bf16),
             shape((width, rows), bf16),
             shape((2 * key_width, rows), bf16),
-            shape((width, columns), bf16),
+            pltpu.VMEM((width, columns), bf16),
         ),
         in_specs=[in_smem()] + [in_vmem()] * 4 + [anywhere()] * len(sources),
-        out_specs=(in_vmem(),) * 4 + (anywhere(),),
-        scratch_shapes=[
-            pltpu.VMEM((width, columns), bf16),
-            pltpu.SemaphoreType.DMA((len(plan),)),
-            pltpu.SemaphoreType.DMA,
-        ],
+        out_specs=(in_vmem(),) * 5,
+        scratch_shapes=[pltpu.SemaphoreType.DMA((len(plan),))],
         compiler_params=params(),
         cost_estimate=cost(4 * rows * width * width, width * columns * 4),
         name="enter_first",
     )(index, hidden_t, gain, cos, sin, *sources)
 
 
-def enter_kernel(h_ref, gain_ref, cos_ref, sin_ref, w_hbm, normed_ref, q_ref, kv_ref, w_ref, sem):
-    load = pltpu.make_async_copy(w_hbm.at[:, pl.ds(0, w_ref.shape[1])], w_ref, sem)
-    load.start()
+def enter_kernel(h_ref, gain_ref, cos_ref, sin_ref, w_ref, normed_ref, q_ref, kv_ref):
     enter_body(
-        h_ref[...], gain_ref, cos_ref, sin_ref, load.wait, normed_ref, q_ref, kv_ref, w_ref
+        h_ref[...], gain_ref, cos_ref, sin_ref, lambda: None, normed_ref, q_ref, kv_ref, w_ref
     )
 
 
@@ -235,13 +271,16 @@
             shape((width, rows), bf16),
             shape((2 * key_width, rows), bf16),
         ),
-        in_specs=[in_vmem()] * 4 + [anywhere()],
+        in_specs=[in_vmem()] * 5,
         out_specs=(in_vmem(),) * 3,
-        scratch_shapes=[pltpu.VMEM((width, wide), bf16), pltpu.SemaphoreType.DMA],
         compiler_params=params(),
         cost_estimate=cost(2 * rows * width * wide, width * wide * 2 + rows * width * 10),
         name="enter",
-    )(hidden, gain, cos, sin, weights_a)
+    )(hidden, gain, cos, sin, kept(weights_a))
+
+
+def out_weight(a_ref):
+    return a_ref[:, a_ref.shape[1] - a_ref.shape[0] - HEAD_SIZE :]
 
 
 def stacked_heads(ref, group):
@@ -267,31 +306,39 @@
     return keys <= queries
 
 
+def whole_copies(source_ref, target_ref, sems):
+    parts = 4
+    height = source_ref.shape[0] // parts
+    return [
+        pltpu.make_async_copy(
+            source_ref.at[pl.ds(i * height, height), :],
+            target_ref.at[pl.ds(i * height, height), :],
+            sems.at[i],
+        )
+        for i in range(parts)
+    ]
+
+
 def forward_kernel(plans, counts, *refs):
-    (visible_ref, index_ref, h_ref, q_ref, kv0_ref, kv1_ref, kv2_ref, kv3_ref, gain_ref, a_hbm) = refs[:10]
+    (visible_ref, bits_ref, h_ref, q_ref, kv0_ref, kv1_ref, kv2_ref, kv3_ref, gain_ref, a_ref) = refs[:10]
     gu_sources = refs[10 : 10 + counts[0]]
     dn_sources = refs[10 + counts[0] : 10 + counts[0] + counts[1]]
     refs = refs[10 + counts[0] + counts[1] :]
     (out_ref, att_ref, att_t_ref, lse_ref, middle_ref, nf_ref, gating_ref, upward_ref, inner_ref) = refs[:9]
     refs = refs[9:]
-    first = plans is not None
-    if first:
-        gu_hbm, dn_hbm = refs[:2]
+    gu_ref, gu_sems, dn_sems = refs[-3:]
+    if plans is not None:
+        gu_hbm, dn_ref = refs[:2]
         refs = refs[2:]
-    (wo_ref, gu_ref, dn_ref, acc_ref, m_ref, l_ref, wo_sem, gu_sems, dn_sems) = refs
+        gu_loads = piece_copies(plans[0], bits_ref, gu_sources, gu_ref, gu_sems)
+        dn_loads = piece_copies(plans[1], bits_ref, dn_sources, dn_ref, dn_sems)
+    else:
+        (dn_ref,) = dn_sources
+        gu_loads, dn_loads = whole_copies(gu_sources[0], gu_ref, gu_sems), []
+    acc_ref, m_ref, l_ref = refs[:3]
     rows, width = h_ref.shape
     ffn = inner_ref.shape[1]
-    wo_wide = wo_ref.shape[1]
-    wo_load = pltpu.make_async_copy(
-        a_hbm.at[:, pl.ds(a_hbm.shape[1] - wo_wide, wo_wide)], wo_ref, wo_sem
-    )
-    if first:
-        gu_loads = piece_copies(plans[0], index_ref, gu_sources, gu_ref, gu_sems)
-        dn_loads = piece_copies(plans[1], index_ref, dn_sources, dn_ref, dn_sems)
-    else:
-        gu_loads = [pltpu.make_async_copy(gu_sources[0], gu_ref, gu_sems.at[0])]
-        dn_loads = [pltpu.make_async_copy(dn_sources[0], dn_ref, dn_sems.at[0])]
-    for load in [wo_load] + gu_loads + dn_loads:
+    for load in gu_loads + dn_loads:
         load.start()
 
     allowed = causal(rows)
@@ -330,16 +377,15 @@
             att_t_ref[low : low + HEAD_SIZE, :] = mean[:, j * rows : (j + 1) * rows].astype(bf16)
     attended = att_t_ref[...].T
     att_ref[...] = attended
-    wo_load.wait()
-    middle = h_ref[...] + nn(attended, wo_ref[...])[:, wo_wide - width :]
+    middle = h_ref[...] + nn(attended, out_weight(a_ref))[:, HEAD_SIZE:]
     middle_ref[...] = middle
     normed = (middle * inverse_rms(middle) * gain_ref[...]).astype(bf16)
     nf_ref[...] = normed
     for load in gu_loads:
         load.wait()
-    if first:
-        gu_out = pltpu.make_async_copy(gu_ref, gu_hbm, gu_sems.at[0])
-        gu_out.start()
+    gu_stores = whole_copies(gu_ref, gu_hbm, gu_sems) if plans is not None else []
+    for store in gu_stores:
+        store.start()
     step = 512
     for low in range(0, ffn, step):
         gating = nn(normed, gu_ref[:, low : low + step])
@@ -349,26 +395,19 @@
         inner_ref[:, low : low + step] = (gating * jax.nn.sigmoid(gating) * upward).astype(bf16)
     for load in dn_loads:
         load.wait()
-    if first:
-        dn_out = pltpu.make_async_copy(dn_ref, dn_hbm, dn_sems.at[0])
-        dn_out.start()
     finished = middle + nt(inner_ref[...], dn_ref[...])
-    if first:
-        out_ref[...] = finished
-        gu_out.wait()
-        dn_out.wait()
-    else:
-        out_ref[...] = finished.T.astype(bf16)
+    out_ref[...] = finished if plans is not None else finished.T.astype(bf16)
+    for store in gu_stores:
+        store.wait()
 
 
 def forward_block(visible, index, hidden, q, kvs, gain, weights_a, gu, dn, plans=None):
     rows, width = hidden.shape
     ffn = gu[0].shape[1] if plans is not None else gu[0].shape[1] // 2
-    wo_wide = width + HEAD_SIZE
     lanes = SHARING * rows
     counts = (len(gu), len(dn))
     first = plans is not None
-    whole = (shape((width, 2 * ffn), bf16), shape((width, ffn), bf16))
+    whole = (pltpu.HBM((width, 2 * ffn), bf16), pltpu.VMEM((width, ffn), bf16))
     return pl.pallas_call(
         functools.partial(forward_kernel, plans, counts),
         out_shape=(
@@ -383,23 +422,26 @@
             shape((rows, ffn), bf16),
         )
         + (whole if first else ()),
-        in_specs=[in_smem()] * 2 + [in_vmem()] * 7 + [anywhere()] * (1 + sum(counts)),
-        out_specs=(in_vmem(),) * 9 + ((anywhere(),) * 2 if first else ()),
+        in_specs=[in_smem()] * 2
+        + [in_vmem()] * 8
+        + [anywhere()] * counts[0]
+        + [anywhere() if first else in_vmem()] * counts[1],
+        out_specs=(in_vmem(),) * 9 + ((anywhere(), in_vmem()) if first else ()),
         scratch_shapes=[
-            pltpu.VMEM((width, wo_wide), bf16),
-            pltpu.VMEM((width, 2 * ffn), bf16),
-            pltpu.VMEM((width, ffn), bf16),
             pltpu.VMEM((KEY_VALUE_HEADS, HEAD_SIZE, lanes), f32),
             pltpu.VMEM((KEY_VALUE_HEADS, lanes), f32),
             pltpu.VMEM((KEY_VALUE_HEADS, lanes), f32),
-            pltpu.SemaphoreType.DMA,
-            pltpu.SemaphoreType.DMA((len(plans[0]) if first else 1,)),
+            pltpu.VMEM((width, 2 * ffn), bf16),
+            pltpu.SemaphoreType.DMA((len(plans[0]) if first else 4,)),
             pltpu.SemaphoreType.DMA((len(plans[1]) if first else 1,)),
         ],
-        compiler_params=params(),
+        compiler_params=params(FFN_MEBIBYTES),
         cost_estimate=cost(2 * rows * width * (4 * ffn), 3 * width * ffn * 2 + rows * ffn * 8),
         name="forward_first" if first else "forward_last",
-    )(visible, index, hidden, q, *kvs, gain, weights_a, *gu, *dn)
+    )(
+        visible, index, hidden, q, *kvs, gain, kept(weights_a),
+        *([*gu, *dn] if first else [in_hbm(gu[0]), kept(dn[0])]),
+    )
 
 
 def feed_back_kernel(
@@ -408,37 +450,27 @@
     gating_ref,
     upward_ref,
     gain_ref,
-    a_hbm,
+    a_ref,
     gu_hbm,
-    dn_hbm,
+    dn_ref,
     gb_ref,
     dgu_ref,
     dmid_ref,
     gm_ref,
     do_ref,
     dgain_ref,
-    wo_ref,
+    sum_ref,
     gu_ref,
-    dn_ref,
-    sum_ref,
-    sems,
+    gu_sems,
 ):
     rows, width = middle_ref.shape
     ffn = gating_ref.shape[1]
-    wo_wide = wo_ref.shape[1]
-    loads = [
-        pltpu.make_async_copy(dn_hbm, dn_ref, sems.at[0]),
-        pltpu.make_async_copy(gu_hbm, gu_ref, sems.at[1]),
-        pltpu.make_async_copy(
-            a_hbm.at[:, pl.ds(a_hbm.shape[1] - wo_wide, wo_wide)], wo_ref, sems.at[2]
-        ),
-    ]
+    loads = whole_copies(gu_hbm, gu_ref, gu_sems)
     for load in loads:
         load.start()
     grad = g_ref[...] if g_ref.shape[0] == rows else g_ref[...].astype(f32).T
     short = grad.astype(bf16)
     gb_ref[...] = short
-    loads[0].wait()
     step = 512
     for low in range(0, ffn, step):
         part = slice(low, low + step)
@@ -451,11 +483,9 @@
         d_upward = (d_inner * (gating * gate)).astype(bf16)
         dgu_ref[:, part] = d_gating
         dgu_ref[:, behind] = d_upward
-        if low == 0:
-            loads[1].wait()
-            sum_ref[...] = nt(d_gating, gu_ref[:, part]) + nt(d_upward, gu_ref[:, behind])
-        else:
-            sum_ref[...] += nt(d_gating, gu_ref[:, part]) + nt(d_upward, gu_ref[:, behind])
+    for load in loads:
+        load.wait()
+    sum_ref[...] = nt(dgu_ref[...], gu_ref[...])
     d_normed = sum_ref[...]
     middle = middle_ref[...]
     factor = inverse_rms(middle)
@@ -465,11 +495,10 @@
     d_middle = grad + factor * (scaled - unit * jnp.mean(scaled * unit, axis=-1, keepdims=True))
     dmid_ref[...] = d_middle
     padded = jnp.concatenate(
-        [jnp.zeros((rows, wo_wide - width), f32), d_middle], axis=1
+        [jnp.zeros((rows, HEAD_SIZE), f32), d_middle], axis=1
     ).astype(bf16)
     gm_ref[...] = padded
-    loads[2].wait()
-    do_ref[...] = nt(padded, wo_ref[...]).T.astype(bf16)
+    do_ref[...] = nt(padded, out_weight(a_ref)).T.astype(bf16)
 
 
 def feed_back(grad, middle, gating, upward, gain, weights):
@@ -487,19 +516,17 @@
             shape((width, rows), bf16),
             shape((1, width), f32),
         ),
-        in_specs=[in_vmem()] * 5 + [anywhere()] * 3,
+        in_specs=[in_vmem()] * 6 + [anywhere(), in_vmem()],
         out_specs=(in_vmem(),) * 6,
         scratch_shapes=[
-            pltpu.VMEM((width, wo_wide), bf16),
+            pltpu.VMEM((rows, width), f32),
             pltpu.VMEM((width, 2 * ffn), bf16),
-            pltpu.VMEM((width, ffn), bf16),
-            pltpu.VMEM((rows, width), f32),
-            pltpu.SemaphoreType.DMA((3,)),
+            pltpu.SemaphoreType.DMA((4,)),
         ],
-        compiler_params=params(),
+        compiler_params=params(FFN_MEBIBYTES),
         cost_estimate=cost(2 * rows * width * (4 * ffn), 3 * width * ffn * 2 + rows * ffn * 8),
         name="feed_back",
-    )(grad, middle, gating, upward, gain, weights_a, weights_gu, weights_dn)
+    )(grad, middle, gating, upward, gain, kept(weights_a), in_hbm(weights_gu), kept(weights_dn))
 
 
 def attend_back_kernel(
@@ -608,19 +635,15 @@
     gain_ref,
     cos_ref,
     sin_ref,
-    w_hbm,
+    w_ref,
     g_ref,
     dqkv_ref,
     dgain_ref,
-    w_ref,
     turned_ref,
-    sem,
 ):
     width, rows = dq_ref.shape
     key_width = own_ref.shape[0] // 2
-    wide = w_ref.shape[1]
-    load = pltpu.make_async_copy(w_hbm.at[:, pl.ds(0, wide)], w_ref, sem)
-    load.start()
+    wide = turned_ref.shape[0]
     cos, sin = cos_ref[...], sin_ref[...]
     turned_ref[:width, :] = dq_ref[...]
     summed = own_ref[...].astype(f32) + got_ref[...].astype(f32)
@@ -635,8 +658,7 @@
     turned_ref[width + 2 * key_width :, :] = jnp.zeros((wide - width - 2 * key_width, rows), bf16)
     d_mixed = turned_ref[...].T
     dqkv_ref[...] = d_mixed
-    load.wait()
-    d_normed = nt(d_mixed, w_ref[...])
+    d_normed = nt(d_mixed, w_ref[:, :wide])
     hidden = h_ref[...]
     factor = inverse_rms(hidden)
     unit = hidden * factor
@@ -659,17 +681,13 @@
             shape((rows, wide), bf16),
             shape((1, width), f32),
         ),
-        in_specs=[in_vmem()] * 8 + [anywhere()],
+        in_specs=[in_vmem()] * 9,
         out_specs=(in_vmem(),) * 3,
-        scratch_shapes=[
-            pltpu.VMEM((width, wide), bf16),
-            pltpu.VMEM((wide, rows), bf16),
-            pltpu.SemaphoreType.DMA,
-        ],
+        scratch_shapes=[pltpu.VMEM((wide, rows), bf16)],
         compiler_params=params(),
         cost_estimate=cost(2 * rows * width * wide, width * wide * 2 + rows * width * 14),
         name="leave",
-    )(hidden, d_middle, dq, own, got, gain, cos, sin, weights_a)
+    )(hidden, d_middle, dq, own, got, gain, cos, sin, kept(weights_a))
 
 
 def grad_parts(place_ref, right, keep_ref, send_ref, xt_ref):
@@ -687,11 +705,11 @@
 
 def feed_back_gate_kernel(*refs):
     (place_ref, g_ref, middle_ref, gating_ref, upward_ref, gain_ref, nf2_ref, nf_ref, dgu2_ref,
-     a_hbm, gu_hbm, dn_hbm, dmid_ref, gm_ref, do_ref, dgain_ref, keep_ref, send_ref, keep2_ref,
-     send2_ref, gb_ref, dgu_ref, wo_ref, gu_ref, dn_ref, sum_ref, xt_ref, sems) = refs
+     a_ref, gu_hbm, dn_ref, dmid_ref, gm_ref, do_ref, dgain_ref, keep_ref, send_ref, keep2_ref,
+     send2_ref, gb_ref, dgu_ref, sum_ref, xt_ref, gu_ref, gu_sems) = refs
     feed_back_kernel(
-        g_ref, middle_ref, gating_ref, upward_ref, gain_ref, a_hbm, gu_hbm, dn_hbm, gb_ref, dgu_ref,
-        dmid_ref, gm_ref, do_ref, dgain_ref, wo_ref, gu_ref, dn_ref, sum_ref, sems,
+        g_ref, middle_ref, gating_ref, upward_ref, gain_ref, a_ref, gu_hbm, dn_ref, gb_ref, dgu_ref,
+        dmid_ref, gm_ref, do_ref, dgain_ref, sum_ref, gu_ref, gu_sems,
     )
 
     rows = nf_ref.shape[0]
@@ -722,32 +740,30 @@
             shape((1, width), f32),
         )
         + (shape((2, 4, width // 4, ffn // 4), bf16),) * 4,
-        in_specs=[in_smem()] + [in_vmem()] * 8 + [anywhere()] * 3,
+        in_specs=[in_smem()] + [in_vmem()] * 9 + [anywhere(), in_vmem()],
         out_specs=(in_vmem(),) * 8,
         scratch_shapes=[
             pltpu.VMEM((rows, width), bf16),
             pltpu.VMEM((rows, 2 * ffn), bf16),
-            pltpu.VMEM((width, wo_wide), bf16),
-            pltpu.VMEM((width, 2 * ffn), bf16),
-            pltpu.VMEM((width, ffn), bf16),
             pltpu.VMEM((rows, width), f32),
             pltpu.VMEM((width, 2 * rows), bf16),
-            pltpu.SemaphoreType.DMA((3,)),
+            pltpu.VMEM((width, 2 * ffn), bf16),
+            pltpu.SemaphoreType.DMA((4,)),
         ],
-        compiler_params=params(),
+        compiler_params=params(FFN_MEBIBYTES),
         cost_estimate=cost(2 * rows * width * (8 * ffn), 3 * width * ffn * 2 + rows * ffn * 8),
         name="feed_back_gate",
-    )(place, grad, middle, gating, upward, gain, nf2, nf, dgu2, weights_a, weights_gu, weights_dn)
+    )(place, grad, middle, gating, upward, gain, nf2, nf, dgu2, kept(weights_a), in_hbm(weights_gu),
+      kept(weights_dn))
 
 
 def leave_mixed_kernel(*refs):
     (place_ref, h_ref, dmid_ref, dq_ref, own_ref, got_ref, gain_ref, cos_ref, sin_ref, n1_ref, n2_ref,
-     d1_ref, a1_ref, a2_ref, m1_ref, m2_ref, attention_gain_ref, ffn_gain_ref, ffn_gain2_ref, w_hbm,
-     g_ref, keep_ref, send_ref, d2_ref, dgain_ref, w_ref, turned_ref, nt_ref, at_ref, gains_ref,
-     sem) = refs
+     d1_ref, a1_ref, a2_ref, m1_ref, m2_ref, attention_gain_ref, ffn_gain_ref, ffn_gain2_ref, w_ref,
+     g_ref, keep_ref, send_ref, d2_ref, dgain_ref, turned_ref, nt_ref, at_ref, gains_ref) = refs
     leave_kernel(
-        h_ref, dmid_ref, dq_ref, own_ref, got_ref, gain_ref, cos_ref, sin_ref, w_hbm, g_ref, d2_ref,
-        dgain_ref, w_ref, turned_ref, sem,
+        h_ref, dmid_ref, dq_ref, own_ref, got_ref, gain_ref, cos_ref, sin_ref, w_ref, g_ref, d2_ref,
+        dgain_ref, turned_ref,
     )
     gains = (attention_gain_ref[...] + dgain_ref[...], ffn_gain_ref[...] + ffn_gain2_ref[...])
     attention_grad_kernel(
@@ -768,23 +784,21 @@
         leave_mixed_kernel,
         out_shape=(shape((width, rows), bf16),)
         + (shape((2, 4, block, columns // 4), bf16),) * 2,
-        in_specs=[in_smem()] + [in_vmem()] * 18 + [anywhere()],
+        in_specs=[in_smem()] + [in_vmem()] * 19,
         out_specs=(in_vmem(),) * 3,
         scratch_shapes=[
             pltpu.VMEM((rows, wide), bf16),
             pltpu.VMEM((1, width), f32),
-            pltpu.VMEM((width, wide), bf16),
             pltpu.VMEM((wide, rows), bf16),
             pltpu.VMEM((width, 2 * rows), bf16),
             pltpu.VMEM((width, 2 * rows), bf16),
             pltpu.VMEM((GAIN_ROWS, columns), f32),
-            pltpu.SemaphoreType.DMA,
         ],
         compiler_params=params(),
         cost_estimate=cost(6 * rows * width * wide, width * wide * 2 + rows * width * 14),
         name="leave_mixed",
     )(place, hidden, d_middle, dq, own, got, gain, cos, sin, *normed, dqkv2, *att, *gm, *gain_grads,
-      weights_a)
+      kept(weights_a))
 
 
 def down_grad_kernel(place_ref, g2_ref, g_ref, inner2_ref, inner_ref, keep_ref, send_ref, gt_ref):
@@ -1174,11 +1188,12 @@
     own, across = fold_kv(order.tie(*dkvs))
     order.done(across)
     gate.rest()
+    down.third()
     across = order.tie(across)
-    got = flip(across, "fsdp", 2)
-    order.done(across)
+    got = order.done(order.tie(flip(across, "fsdp", 2)))
+    gate.second()
     up.chip()
-    d_middle, got = order.tie(d_middle, got)
+    d_middle = order.tie(d_middle)
     grad, *mixed = leave_mixed(
         place,
         hidden,
@@ -1198,26 +1213,25 @@
     )
     order.done(grad)
     up.first()
+    down.back()
+    gate.third()
     mixed = Reduction(order, *mixed)
-    gate.second()
-    down.third()
     mixed.chip()
     up.second()
-    gate.third()
-    down.back()
+    gate.back()
     mixed.first()
+    up.third()
     down.back_again()
-    gate.back()
-    up.third()
+    mixed.rest()
+    mixed.second()
     gate.back_again()
+    up.back()
     down_grad = order.done(finish(place, down.end(), True))
-    up.back()
-    mixed.second()
+    mixed.third()
     up.back_again()
     gate_grad = order.done(finish(place, gate.end(), False))
-    mixed.third()
+    mixed.back()
     up_grad = order.done(finish(place, up.end(), False))
-    mixed.back()
     mixed.back_again()
     query_grad, key_grad, value_grad, output_grad, gain_grads = finish_mixed(
         place, mixed.end(), width, key_width

time: 487 us -> 428 us (0.88)
  Pallas kernels: 153 us -> 94.4 us
  other arithmetic: 31.7 us -> 9.81 us
  waiting for transfers between devices: 190 us -> 205 us
  local copies, waits for them, and re-layouts: 15.5 us -> 23.9 us
    convert_element_type x22, other arithmetic: 24.1 us -> 5.69 us  [total(): return result.astype(bf16)]
    ppermute x69, waiting for transfers between devices: 190 us -> 205 us  [flip(): lax.ppermute(value, axis_name, [(i, i ^ distance) for i in range(size)])]
    pallas_call x2, Pallas kernels: 20.2 us -> 7.95 us  [attend_back(): pl.pallas_call(attend_back_kernel, out_shape=(shape((width, rows), bf16),...]
    unnamed x126, local copies, waits for them, and re-layouts: 9.79 us -> 19.5 us
    pallas_call x2, Pallas kernels: 36.2 us -> 28.7 us  [forward_block(): pl.pallas_call(functools.partial(forward_kernel, plans, counts), out_shap...]
    pallas_call x1, Pallas kernels: 25 us -> 18.4 us  [feed_back_gate(): pl.pallas_call(feed_back_gate_kernel, out_shape=(shape((rows, width), f32...]
    pallas_call x1, Pallas kernels: 14.9 us -> 9.16 us  [feed_back(): pl.pallas_call(feed_back_kernel, out_shape=(shape((rows, width), bf16), s...]
    pallas_call x1, Pallas kernels: 11.6 us -> 6.38 us  [leave_mixed(): pl.pallas_call(leave_mixed_kernel, out_shape=(shape((width, rows), bf16),...]
  transfers between devices with their start and end apart: 69 -> 69, of which waited for: 35 -> 38; matrix products, arithmetic and copies ran while one was open for 5% -> 2% of each run, Pallas kernels for 14% -> 10%
where the time goes in v3:
time: 428 us; the launch traced here: 420 us
  waiting for transfers between devices  205 us (48%)
  Pallas kernels  94.4 us (22%)
  starting transfers between devices  84.2 us (20%)
  local copies, waits for them, and re-layouts  23.9 us (6%)
  other arithmetic  9.81 us (2%)
    ppermute x69, waiting for transfers between devices, flip(): lax.ppermute(value, axis_name, [(i, i ^ distance) for i in range(size)])  205 us
    ppermute x69, starting transfers between devices, flip(): lax.ppermute(value, axis_name, [(i, i ^ distance) for i in range(size)])  84.2 us
    pallas_call x2, Pallas kernels, forward_block(): pl.pallas_call(functools.partial(forward_kernel, plans, counts), out_shap...  28.7 us
    unnamed x126, local copies, waits for them, and re-layouts  19.5 us
    pallas_call x1, Pallas kernels, feed_back_gate(): pl.pallas_call(feed_back_gate_kernel, out_shape=(shape((rows, width), f32...  18.4 us
    pallas_call x1, Pallas kernels, feed_back(): pl.pallas_call(feed_back_kernel, out_shape=(shape((rows, width), bf16), s...  9.16 us
  transfers between devices with their start and end apart: 69, of which 38 were waited for; matrix products, arithmetic and copies ran while one was open for 2% of the time, Pallas kernels for 10%

profile of v3, /device:TPU:0, one launch (start us, length us, event | category | flops | bytes accessed | tf_op | source)
XLA Modules:
  0.0 419.6 jit_solution(2695576939937599494)
XLA Ops:
  2.5 2.6 collective-permute-start.1
  5.2 4.0 pack.1
  18.4 9.7 %collective-permute-done.4.refs_2_ = bf16[240,1280]{1,0:T(8,128)(2,1)S(1)} collective-permute-done((bf16[240,1280]{1,0:T(8,128)(2,1)}, bf16[240,1280]{1,0:T(8,128)(2,1)S(1)}, u32[]{:S(2)}, u32[]{:S(2)}) %collective-permute-start.4) | collective-permute-done | bytes 614432 | tf_op jit(solution)/shard_map/ppermute | solution.py:952
  31.9 11.5 %collective-permute-done.5.refs_3_ = bf16[240,1280]{1,0:T(8,128)(2,1)S(1)} collective-permute-done((bf16[240,1280]{1,0:T(8,128)(2,1)S(1)}, bf16[240,1280]{1,0:T(8,128)(2,1)S(1)}, u32[]{:S(2)}, u32[]{:S(2)}) %collective-permute-start.5) | collective-permute-done | bytes 614432 | tf_op jit(solution)/shard_map/ppermute | solution.py:952
  43.4 3.4 collective-permute-done.13.refs_12_
  46.9 11.2 %collective-permute-done.12.refs_18_ = bf16[240,1280]{1,0:T(8,128)(2,1)S(1)} collective-permute-done((bf16[240,1280]{1,0:T(8,128)(2,1)}, bf16[240,1280]{1,0:T(8,128)(2,1)S(1)}, u32[]{:S(2)}, u32[]{:S(2)}) %collective-permute-start.12) | collective-permute-done | bytes 614432 | tf_op jit(solution)/shard_map/ppermute | solution.py:952
  65.2 3.0 enter_first.1
  69.0 2.9 collective-permute-done.14.refs_13_
  78.1 8.4 %collective-permute-done.23.refs_25_ = bf16[480,640]{1,0:T(8,128)(2,1)S(1)} collective-permute-done((bf16[480,640]{1,0:T(8,128)(2,1)S(1)}, bf16[480,640]{1,0:T(8,128)(2,1)S(1)}, u32[]{:S(2)}, u32[]{:S(2)}) %collective-permute-start.23) | collective-permute-done | bytes 614432 | tf_op jit(solution)/shard_map/ppermute | solution.py:952
  87.6 3.6 collective-permute-done.18.refs_19_
  93.8 11.2 %forward_first.1 = (f32[256,960]{1,0:T(8,128)S(1)}, bf16[256,960]{1,0:T(8,128)(2,1)S(1)}, bf16[960,256]{1,0:T(8,128)(2,1)S(1)}, f32[5,768]{1,0:T(8,128)S(1)}, f3...) custom-call(s32[4]{0:T(128)S(1)} %and_convert_fusion.refs_0_.visible, ...), custom_call_target="tpu_custom_call" | custom-call | flops 5033164800 | bytes 19988480 | tf_op jit(solution)/shard_map/forward_first/pallas_call | solution.py:411
  109.8 8.3 %collective-permute-done.27.refs_6_.kv2_ref = bf16[640,256]{1,0:T(8,128)(2,1)S(1)} collective-permute-done((bf16[640,256]{1,0:T(8,128)(2,1)S(1)}, bf16[640,256]{1,0:T(8,128)(2,1)S(1)}, u32[]{:S(2)}, u32[]{:S(2)}) %collective-permute-start.27) | collective-permute-done | bytes 327712 | tf_op jit(solution)/shard_map/ppermute | solution.py:952
  119.7 17.4 %forward_last.1 = (bf16[960,256]{1,0:T(8,128)(2,1)}, bf16[256,960]{1,0:T(8,128)(2,1)S(1)}, bf16[960,256]{1,0:T(8,128)(2,1)S(1)}, f32[5,768]{1,0:T(8,128)S(1)}, f...) custom-call(s32[4]{0:T(128)S(1)} %and_convert_fusion.refs_0_.visible, ...), custom_call_target="tpu_custom_call" | custom-call | flops 5033164800 | bytes 19988480 | tf_op jit(solution)/shard_map/forward_last/pallas_call | solution.py:411
  137.2 9.2 %feed_back.1 = (bf16[256,960]{1,0:T(8,128)(2,1)S(1)}, bf16[256,5120]{1,0:T(8,128)(2,1)S(1)}, f32[256,960]{1,0:T(8,128)S(1)}, bf16[256,1024]{1,0:T(8,128)(2,1)S(1...) custom-call(bf16[960,256]{1,0:T(8,128)(2,1)S(1)} %bitcast.123, f32[256,960]{1,0:T(8,128)S(1)} %get-tuple-element.182.middle_ref, ...), custom_call_target="tpu_custom_call" | custom-call | flops 5033164800 | bytes 19988480 | tf_op jit(solution)/shard_map/feed_back/pallas_call | solution.py:509
  147.2 4.1 attend_back.2
  155.9 8.2 %collective-permute-done.30.got_ref = bf16[640,256]{1,0:T(8,128)(2,1)S(1)} collective-permute-done((bf16[640,256]{1,0:T(8,128)(2,1)S(1)}, bf16[640,256]{1,0:T(8,128)(2,1)S(1)}, u32[]{:S(2)}, u32[]{:S(2)}) %collective-permute-start.30) | collective-permute-done | bytes 327712 | tf_op jit(solution)/shard_map/ppermute | solution.py:952
  164.8 2.4 copy-done.1
  176.4 3.9 down_grad.1
  180.3 4.7 %collective-permute-done.31 = bf16[2,4,240,640]{3,2,1,0:T(8,128)(2,1)S(1)} collective-permute-done((bf16[2,4,240,640]{3,2,1,0:T(8,128)(2,1)S(1)}, bf16[2,4,240,640]{3,2,1,0:T(8,128)(2,1)S(1)}, u32[]{:S(2)}, u32[]{:S(2)}) %collective-permute-start.31) | collective-permute-done | bytes 2457632 | tf_op jit(solution)/shard_map/ppermute | solution.py:952
  187.5 18.4 %feed_back_gate.1 = (f32[256,960]{1,0:T(8,128)S(1)}, bf16[256,1024]{1,0:T(8,128)(2,1)S(1)}, bf16[960,256]{1,0:T(8,128)(2,1)S(1)}, f32[1,960]{1,0:T(1,128)S(1)}, ...) custom-call(s32[3]{0:T(128)S(1)} %pad_add_fusion.1.place_ref.refs_0_, ...), custom_call_target="tpu_custom_call" | custom-call | flops 10066329600 | bytes 19988480 | tf_op jit(solution)/shard_map/feed_back_gate/pallas_call | solution.py:734
  205.9 8.5 %collective-permute-done.33 = bf16[2,240,640]{2,1,0:T(8,128)(2,1)S(1)} collective-permute-done((bf16[2,240,640]{2,1,0:T(8,128)(2,1)S(1)}, bf16[2,240,640]{2,1,0:T(8,128)(2,1)S(1)}, u32[]{:S(2)}, u32[]{:S(2)}) %collective-permute-start.33) | collective-permute-done | bytes 614432 | tf_op jit(solution)/shard_map/ppermute | solution.py:952
  216.0 4.7 %collective-permute-done.34 = bf16[2,4,240,640]{3,2,1,0:T(8,128)(2,1)S(1)} collective-permute-done((bf16[2,4,240,640]{3,2,1,0:T(8,128)(2,1)S(1)}, bf16[2,4,240,640]{3,2,1,0:T(8,128)(2,1)S(1)}, u32[]{:S(2)}, u32[]{:S(2)}) %collective-permute-start.34) | collective-permute-done | bytes 2457632 | tf_op jit(solution)/shard_map/ppermute | solution.py:952
  223.1 3.9 attend_back.3
  227.1 10.0 %collective-permute-done.35 = bf16[2,240,640]{2,1,0:T(8,128)(2,1)S(1)} collective-permute-done((bf16[2,240,640]{2,1,0:T(8,128)(2,1)S(1)}, bf16[2,240,640]{2,1,0:T(8,128)(2,1)S(1)}, u32[]{:S(2)}, u32[]{:S(2)}) %collective-permute-start.35) | collective-permute-done | bytes 614432 | tf_op jit(solution)/shard_map/ppermute | solution.py:952
  239.1 20.9 %collective-permute-start.39 = (bf16[240,640]{1,0:T(8,128)(2,1)S(1)}, bf16[240,640]{1,0:T(8,128)(2,1)S(1)}, u32[]{:S(2)}, u32[]{:S(2)}) collective-permute-start(bf16[240,640]{1,0:T(8,128)(2,1)S(1)} %fusion.21), channel_id=1, source_target_pairs={{0,8},{4,12},{8,0},{12,4},{16,24},{20,28},{24,16},{28,20},{1,9},{5... | collective-permute-start | bytes 921608 | tf_op jit(solution)/shard_map/ppermute | solution.py:952
  261.9 5.7 %collective-permute-done.39 = bf16[240,640]{1,0:T(8,128)(2,1)S(1)} collective-permute-done((bf16[240,640]{1,0:T(8,128)(2,1)S(1)}, bf16[240,640]{1,0:T(8,128)(2,1)S(1)}, u32[]{:S(2)}, u32[]{:S(2)}) %collective-permute-start.39) | collective-permute-done | bytes 307232 | tf_op jit(solution)/shard_map/ppermute | solution.py:952
  268.2 8.9 %collective-permute-done.40.refs_5_ = bf16[640,256]{1,0:T(8,128)(2,1)S(1)} collective-permute-done((bf16[640,256]{1,0:T(8,128)(2,1)S(1)}, bf16[640,256]{1,0:T(8,128)(2,1)S(1)}, u32[]{:S(2)}, u32[]{:S(2)}) %collective-permute-start.40) | collective-permute-done | bytes 327712 | tf_op jit(solution)/shard_map/ppermute | solution.py:952
  278.1 10.5 %collective-permute-start.44 = (bf16[240,640]{1,0:T(8,128)(2,1)S(1)}, bf16[240,640]{1,0:T(8,128)(2,1)S(1)}, u32[]{:S(2)}, u32[]{:S(2)}) collective-permute-start(bf16[240,640]{1,0:T(8,128)(2,1)S(1)} %fusion.23), channel_id=1, source_target_pairs={{0,16},{4,20},{8,24},{12,28},{16,0},{20,4},{24,8},{28,12},{1,17},{... | collective-permute-start | bytes 921608 | tf_op jit(solution)/shard_map/ppermute | solution.py:952
  290.0 6.4 %leave_mixed.1 = (bf16[960,256]{1,0:T(8,128)(2,1)}, bf16[2,4,256,640]{3,2,1,0:T(8,128)(2,1)S(1)}, bf16[2,4,256,640]{3,2,1,0:T(8,128)(2,1)S(1)}) custom-call(s32[3]{0:T(128)S(1)} %pad_add_fusion.1.place_ref.refs_0_, f32[256,960]{1,0:T(8,128)S(1)} %get-tuple-element.166.refs_2_.refs_1_, f32[256,960]{1,0:T(8,128)S(1)} %get-tuple-element.241.refs_2_, ...), custom_call_target="tpu_custom_call" | custom-call | flops 2453667840 | bytes 6635520 | tf_op jit(solution)/shard_map/leave_mixed/pallas_call | solution.py:783
  296.6 4.6 %collective-permute-done.44 = bf16[240,640]{1,0:T(8,128)(2,1)S(1)} collective-permute-done((bf16[240,640]{1,0:T(8,128)(2,1)S(1)}, bf16[240,640]{1,0:T(8,128)(2,1)S(1)}, u32[]{:S(2)}, u32[]{:S(2)}) %collective-permute-start.44) | collective-permute-done | bytes 307232 | tf_op jit(solution)/shard_map/ppermute | solution.py:952
  303.8 3.1 collective-permute-done.46
  310.5 8.1 %collective-permute-done.48 = bf16[2,240,640]{2,1,0:T(8,128)(2,1)S(1)} collective-permute-done((bf16[2,240,640]{2,1,0:T(8,128)(2,1)S(1)}, bf16[2,240,640]{2,1,0:T(8,128)(2,1)S(1)}, u32[]{:S(2)}, u32[]{:S(2)}) %collective-permute-start.48) | collective-permute-done | bytes 614432 | tf_op jit(solution)/shard_map/ppermute | solution.py:952
  319.6 5.7 %collective-permute-done.49 = bf16[240,640]{1,0:T(8,128)(2,1)S(1)} collective-permute-done((bf16[240,640]{1,0:T(8,128)(2,1)S(1)}, bf16[240,640]{1,0:T(8,128)(2,1)S(1)}, u32[]{:S(2)}, u32[]{:S(2)}) %collective-permute-start.49) | collective-permute-done | bytes 307232 | tf_op jit(solution)/shard_map/ppermute | solution.py:952
  325.3 7.4 %collective-permute-done.50 = bf16[2,256,640]{2,1,0:T(8,128)(2,1)S(1)} collective-permute-done((bf16[2,256,640]{2,1,0:T(8,128)(2,1)S(1)}, bf16[2,256,640]{2,1,0:T(8,128)(2,1)S(1)}, u32[]{:S(2)}, u32[]{:S(2)}) %collective-permute-start.50) | collective-permute-done | bytes 655392 | tf_op jit(solution)/shard_map/ppermute | solution.py:952
  336.6 6.7 %collective-permute-done.52 = bf16[240,640]{1,0:T(8,128)(2,1)S(1)} collective-permute-done((bf16[240,640]{1,0:T(8,128)(2,1)S(1)}, bf16[240,640]{1,0:T(8,128)(2,1)S(1)}, u32[]{:S(2)}, u32[]{:S(2)}) %collective-permute-start.52) | collective-permute-done | bytes 307232 | tf_op jit(solution)/shard_map/ppermute | solution.py:952
  345.2 11.3 %collective-permute-done.53.p1_ref = bf16[240,640]{1,0:T(8,128)(2,1)S(1)} collective-permute-done((bf16[240,640]{1,0:T(8,128)(2,1)S(1)}, bf16[240,640]{1,0:T(8,128)(2,1)S(1)}, u32[]{:S(2)}, u32[]{:S(2)}) %collective-permute-start.53) | collective-permute-done | bytes 307232 | tf_op jit(solution)/shard_map/ppermute | solution.py:952
  358.8 4.2 %collective-permute-done.55.p1_ref = bf16[240,640]{1,0:T(8,128)(2,1)S(1)} collective-permute-done((bf16[240,640]{1,0:T(8,128)(2,1)S(1)}, bf16[240,640]{1,0:T(8,128)(2,1)S(1)}, u32[]{:S(2)}, u32[]{:S(2)}) %collective-permute-start.55) | collective-permute-done | bytes 307232 | tf_op jit(solution)/shard_map/ppermute | solution.py:952
  363.1 2.6 collective-permute-done.57.p2_ref
  365.7 3.3 collective-permute-done.58.p3_ref
  369.0 2.5 finish.3
  371.8 3.3 collective-permute-start.63
  377.4 8.1 %collective-permute-done.60.p1_ref = bf16[240,640]{1,0:T(8,128)(2,1)S(1)} collective-permute-done((bf16[240,640]{1,0:T(8,128)(2,1)S(1)}, bf16[240,640]{1,0:T(8,128)(2,1)S(1)}, u32[]{:S(2)}, u32[]{:S(2)}) %collective-permute-start.60) | collective-permute-done | bytes 307232 | tf_op jit(solution)/shard_map/ppermute | solution.py:952
  386.1 2.5 finish.4
  392.4 7.9 %collective-permute-done.64.p2_ref = bf16[240,640]{1,0:T(8,128)(2,1)S(1)} collective-permute-done((bf16[240,640]{1,0:T(8,128)(2,1)S(1)}, bf16[240,640]{1,0:T(8,128)(2,1)S(1)}, u32[]{:S(2)}, u32[]{:S(2)}) %collective-permute-start.64) | collective-permute-done | bytes 307232 | tf_op jit(solution)/shard_map/ppermute | solution.py:952
  400.3 6.0 %collective-permute-done.65.p3_ref = bf16[240,640]{1,0:T(8,128)(2,1)S(1)} collective-permute-done((bf16[240,640]{1,0:T(8,128)(2,1)S(1)}, bf16[240,640]{1,0:T(8,128)(2,1)S(1)}, u32[]{:S(2)}, u32[]{:S(2)}) %collective-permute-start.65) | collective-permute-done | bytes 307232 | tf_op jit(solution)/shard_map/ppermute | solution.py:952
  406.4 2.5 finish.5
  409.9 6.1 %collective-permute-done.68.p3_ref = bf16[256,640]{1,0:T(8,128)(2,1)S(1)} collective-permute-done((bf16[256,640]{1,0:T(8,128)(2,1)S(1)}, bf16[256,640]{1,0:T(8,128)(2,1)S(1)}, u32[]{:S(2)}, u32[]{:S(2)}) %collective-permute-start.68) | collective-permute-done | bytes 327712 | tf_op jit(solution)/shard_map/ppermute | solution.py:952
  416.0 2.6 finish_mixed.1
  (278 shorter events, 91.2 us)
Async XLA Ops:
  9.2 49.4 %collective-permute-start.3 = (bf16[240,2560]{1,0:T(8,128)(2,1)}, bf16[240,2560]{1,0:T(8,128)(2,1)S(1)}, u32[]{:S(2)}, u32[]{:S(2)}) collective-permute-start(bf16[240,2560]{1,0:T(8,128)(2,1)} %get-tuple-element.163.refs_0_), channel_id=1, source_target_pairs={{0,1},{1,0},{2,3},{3,2},{4,5},{5,4},{6,7},{7,6},{8,9},{9,8},{10,11... | collective-permute-start | bytes 3686408 | tf_op jit(solution)/shard_map/ppermute | solution.py:952
  11.7 16.4 %collective-permute-start.4 = (bf16[240,1280]{1,0:T(8,128)(2,1)}, bf16[240,1280]{1,0:T(8,128)(2,1)S(1)}, u32[]{:S(2)}, u32[]{:S(2)}) collective-permute-start(bf16[240,1280]{1,0:T(8,128)(2,1)} %get-tuple-element.157), channel_id=1, source_target_pairs={{0,2},{1,3},{2,0},{3,1},{4,6},{5,7},{6,4},{7,5},{8,10},{9,11},{10,... | collective-permute-start | bytes 1843208 | tf_op jit(solution)/shard_map/ppermute | solution.py:952
  28.1 15.3 %collective-permute-start.5 = (bf16[240,1280]{1,0:T(8,128)(2,1)S(1)}, bf16[240,1280]{1,0:T(8,128)(2,1)S(1)}, u32[]{:S(2)}, u32[]{:S(2)}) collective-permute-start(bf16[240,1280]{1,0:T(8,128)(2,1)S(1)} %collective-permute-done.4.refs_2_), channel_id=1, source_target_pairs={{0,4},{4,0},{8,12},{12,8},{16,20},{20,16},{24,28},{28,24},{1,5},{5... | collective-permute-start | bytes 1843208 | tf_op jit(solution)/shard_map/ppermute | solution.py:952
  29.9 17.0 %collective-permute-start.13 = (bf16[240,1280]{1,0:T(8,128)(2,1)}, bf16[240,1280]{1,0:T(8,128)(2,1)S(1)}, u32[]{:S(2)}, u32[]{:S(2)}) collective-permute-start(bf16[240,1280]{1,0:T(8,128)(2,1)} %get-tuple-element.158), channel_id=1, source_target_pairs={{0,2},{1,3},{2,0},{3,1},{4,6},{5,7},{6,4},{7,5},{8,10},{9,11},{10,... | collective-permute-start | bytes 1843208 | tf_op jit(solution)/shard_map/ppermute | solution.py:952
  31.4 26.7 %collective-permute-start.12 = (bf16[240,1280]{1,0:T(8,128)(2,1)}, bf16[240,1280]{1,0:T(8,128)(2,1)S(1)}, u32[]{:S(2)}, u32[]{:S(2)}) collective-permute-start(bf16[240,1280]{1,0:T(8,128)(2,1)} %get-tuple-element.159), channel_id=1, source_target_pairs={{0,2},{1,3},{2,0},{3,1},{4,6},{5,7},{6,4},{7,5},{8,10},{9,11},{10,... | collective-permute-start | bytes 1843208 | tf_op jit(solution)/shard_map/ppermute | solution.py:952
  31.9 29.2 %collective-permute-start.6 = (bf16[240,1280]{1,0:T(8,128)(2,1)S(1)}, bf16[240,1280]{1,0:T(8,128)(2,1)S(1)}, u32[]{:S(2)}, u32[]{:S(2)}) collective-permute-start(bf16[240,1280]{1,0:T(8,128)(2,1)S(1)} %collective-permute-done.4.refs_2_), channel_id=1, source_target_pairs={{0,1},{1,0},{2,3},{3,2},{4,5},{5,4},{6,7},{7,6},{8,9},{9,8},{10,11... | collective-permute-start | bytes 1843208 | tf_op jit(solution)/shard_map/ppermute | solution.py:952
  43.4 17.7 %collective-permute-start.7 = (bf16[240,1280]{1,0:T(8,128)(2,1)S(1)}, bf16[240,1280]{1,0:T(8,128)(2,1)S(1)}, u32[]{:S(2)}, u32[]{:S(2)}) collective-permute-start(bf16[240,1280]{1,0:T(8,128)(2,1)S(1)} %collective-permute-done.5.refs_3_), channel_id=1, source_target_pairs={{0,1},{1,0},{2,3},{3,2},{4,5},{5,4},{6,7},{7,6},{8,9},{9,8},{10,11... | collective-permute-start | bytes 1843208 | tf_op jit(solution)/shard_map/ppermute | solution.py:952
  46.9 28.1 %collective-permute-start.21 = (bf16[960,640]{1,0:T(8,128)(2,1)}, bf16[960,640]{1,0:T(8,128)(2,1)S(1)}, u32[]{:S(2)}, u32[]{:S(2)}) collective-permute-start(bf16[960,640]{1,0:T(8,128)(2,1)} %bitcast.125), channel_id=1, source_target_pairs={{0,1},{1,0},{2,3},{3,2},{4,5},{5,4},{6,7},{7,6},{8,9},{9,8},{10,11... | collective-permute-start | bytes 3686408 | tf_op jit(solution)/shard_map/ppermute | solution.py:952
  58.1 13.9 %collective-permute-start.14 = (bf16[240,1280]{1,0:T(8,128)(2,1)S(1)}, bf16[240,1280]{1,0:T(8,128)(2,1)S(1)}, u32[]{:S(2)}, u32[]{:S(2)}) collective-permute-start(bf16[240,1280]{1,0:T(8,128)(2,1)S(1)} %collective-permute-done.13.refs_12_), channel_id=1, source_target_pairs={{0,4},{4,0},{8,12},{12,8},{16,20},{20,16},{24,28},{28,24},{1,5},{5... | collective-permute-start | bytes 1843208 | tf_op jit(solution)/shard_map/ppermute | solution.py:952
  59.6 14.0 %collective-permute-start.22 = (bf16[480,640]{1,0:T(8,128)(2,1)}, bf16[480,640]{1,0:T(8,128)(2,1)S(1)}, u32[]{:S(2)}, u32[]{:S(2)}) collective-permute-start(bf16[480,640]{1,0:T(8,128)(2,1)} %slice_select_fusion), channel_id=1, source_target_pairs={{0,2},{1,3},{2,0},{3,1},{4,6},{5,7},{6,4},{7,5},{8,10},{9,11},{10,... | collective-permute-start | bytes 1843208 | tf_op jit(solution)/shard_map/ppermute | solution.py:952
  61.1 15.5 %collective-permute-start.11 = (bf16[240,2560]{1,0:T(8,128)(2,1)S(1)}, bf16[240,2560]{1,0:T(8,128)(2,1)S(1)}, u32[]{:S(2)}, u32[]{:S(2)}) collective-permute-start(bf16[240,2560]{1,0:T(8,128)(2,1)S(1)} %copy-done.3), channel_id=1, source_target_pairs={{0,1},{1,0},{2,3},{3,2},{4,5},{5,4},{6,7},{7,6},{8,9},{9,8},{10,11... | collective-permute-start | bytes 3686408 | tf_op jit(solution)/shard_map/ppermute | solution.py:952
  61.1 17.0 %collective-permute-start.17 = (bf16[240,2560]{1,0:T(8,128)(2,1)}, bf16[240,2560]{1,0:T(8,128)(2,1)S(1)}, u32[]{:S(2)}, u32[]{:S(2)}) collective-permute-start(bf16[240,2560]{1,0:T(8,128)(2,1)} %refs_16_.1), channel_id=1, source_target_pairs={{0,1},{1,0},{2,3},{3,2},{4,5},{5,4},{6,7},{7,6},{8,9},{9,8},{10,11... | collective-permute-start | bytes 3686408 | tf_op jit(solution)/shard_map/ppermute | solution.py:952
  73.6 12.9 %collective-permute-start.23 = (bf16[480,640]{1,0:T(8,128)(2,1)S(1)}, bf16[480,640]{1,0:T(8,128)(2,1)S(1)}, u32[]{:S(2)}, u32[]{:S(2)}) collective-permute-start(bf16[480,640]{1,0:T(8,128)(2,1)S(1)} %collective-permute-done.22.refs_24_), channel_id=1, source_target_pairs={{0,4},{4,0},{8,12},{12,8},{16,20},{20,16},{24,28},{28,24},{1,5},{5... | collective-permute-start | bytes 1843208 | tf_op jit(solution)/shard_map/ppermute | solution.py:952
  75.0 12.2 %collective-permute-start.15 = (bf16[240,1280]{1,0:T(8,128)(2,1)S(1)}, bf16[240,1280]{1,0:T(8,128)(2,1)S(1)}, u32[]{:S(2)}, u32[]{:S(2)}) collective-permute-start(bf16[240,1280]{1,0:T(8,128)(2,1)S(1)} %collective-permute-done.13.refs_12_), channel_id=1, source_target_pairs={{0,1},{1,0},{2,3},{3,2},{4,5},{5,4},{6,7},{7,6},{8,9},{9,8},{10,11... | collective-permute-start | bytes 1843208 | tf_op jit(solution)/shard_map/ppermute | solution.py:952
  75.0 16.3 %collective-permute-start.18 = (bf16[240,1280]{1,0:T(8,128)(2,1)S(1)}, bf16[240,1280]{1,0:T(8,128)(2,1)S(1)}, u32[]{:S(2)}, u32[]{:S(2)}) collective-permute-start(bf16[240,1280]{1,0:T(8,128)(2,1)S(1)} %collective-permute-done.12.refs_18_), channel_id=1, source_target_pairs={{0,8},{4,12},{8,0},{12,4},{16,24},{20,28},{24,16},{28,20},{1,9},{5... | collective-permute-start | bytes 1843208 | tf_op jit(solution)/shard_map/ppermute | solution.py:952
  76.6 9.9 %collective-permute-start.9 = (bf16[640,256]{1,0:T(8,128)(2,1)S(1)}, bf16[640,256]{1,0:T(8,128)(2,1)S(1)}, u32[]{:S(2)}, u32[]{:S(2)}) collective-permute-start(bf16[640,256]{1,0:T(8,128)(2,1)S(1)} %get-tuple-element.168.refs_4_.kv0_ref), channel_id=1, source_target_pairs={{0,2},{1,3},{2,0},{3,1},{4,6},{5,7},{6,4},{7,5},{8,10},{9,11},{10,... | collective-permute-start | bytes 983048 | tf_op jit(solution)/shard_map/ppermute | solution.py:952
  185.3 20.6 %collective-permute-start.32 = (bf16[2,240,640]{2,1,0:T(8,128)(2,1)S(1)}, bf16[2,240,640]{2,1,0:T(8,128)(2,1)}, u32[]{:S(2)}, u32[]{:S(2)}) collective-permute-start(bf16[2,240,640]{2,1,0:T(8,128)(2,1)S(1)} %get-tuple-element.304), channel_id=1, source_target_pairs={{0,2},{1,3},{2,0},{3,1},{4,6},{5,7},{6,4},{7,5},{8,10},{9,11},{10,... | collective-permute-start | bytes 1843208 | tf_op jit(solution)/shard_map/ppermute | solution.py:952
  186.8 27.6 %collective-permute-start.33 = (bf16[2,240,640]{2,1,0:T(8,128)(2,1)S(1)}, bf16[2,240,640]{2,1,0:T(8,128)(2,1)S(1)}, u32[]{:S(2)}, u32[]{:S(2)}) collective-permute-start(bf16[2,240,640]{2,1,0:T(8,128)(2,1)S(1)} %get-tuple-element.303), channel_id=1, source_target_pairs={{0,2},{1,3},{2,0},{3,1},{4,6},{5,7},{6,4},{7,5},{8,10},{9,11},{10,... | collective-permute-start | bytes 1843208 | tf_op jit(solution)/shard_map/ppermute | solution.py:952
  221.1 16.0 %collective-permute-start.35 = (bf16[2,240,640]{2,1,0:T(8,128)(2,1)S(1)}, bf16[2,240,640]{2,1,0:T(8,128)(2,1)S(1)}, u32[]{:S(2)}, u32[]{:S(2)}) collective-permute-start(bf16[2,240,640]{2,1,0:T(8,128)(2,1)S(1)} %get-tuple-element.302), channel_id=1, source_target_pairs={{0,2},{1,3},{2,0},{3,1},{4,6},{5,7},{6,4},{7,5},{8,10},{9,11},{10,... | collective-permute-start | bytes 1843208 | tf_op jit(solution)/shard_map/ppermute | solution.py:952
  222.6 15.6 %collective-permute-start.36 = (bf16[2,240,640]{2,1,0:T(8,128)(2,1)S(1)}, bf16[2,240,640]{2,1,0:T(8,128)(2,1)S(1)}, u32[]{:S(2)}, u32[]{:S(2)}) collective-permute-start(bf16[2,240,640]{2,1,0:T(8,128)(2,1)S(1)} %fusion.3), channel_id=1, source_target_pairs={{0,4},{4,0},{8,12},{12,8},{16,20},{20,16},{24,28},{28,24},{1,5},{5... | collective-permute-start | bytes 1843208 | tf_op jit(solution)/shard_map/ppermute | solution.py:952
  223.1 54.2 %collective-permute-start.42 = (bf16[2,4,240,640]{3,2,1,0:T(8,128)(2,1)S(1)}, bf16[2,4,240,640]{3,2,1,0:T(8,128)(2,1)S(1)}, u32[]{:S(2)}, u32[]{:S(2)}) collective-permute-start(bf16[2,4,240,640]{3,2,1,0:T(8,128)(2,1)S(1)} %copy-done.58), channel_id=1, source_target_pairs={{0,1},{1,0},{2,3},{3,2},{4,5},{5,4},{6,7},{7,6},{8,9},{9,8},{10,11... | collective-permute-start | bytes 7372808 | tf_op jit(solution)/shard_map/ppermute | solution.py:952
  238.4 23.3 %collective-permute-start.37 = (bf16[1280,256]{1,0:T(8,128)(2,1)S(1)}, bf16[1280,256]{1,0:T(8,128)(2,1)S(1)}, u32[]{:S(2)}, u32[]{:S(2)}) collective-permute-start(bf16[1280,256]{1,0:T(8,128)(2,1)S(1)} %pad_maximum_fusion.1), channel_id=1, source_target_pairs={{0,1},{1,0},{2,3},{3,2},{4,5},{5,4},{6,7},{7,6},{8,9},{9,8},{10,11... | collective-permute-start | bytes 1966088 | tf_op jit(solution)/shard_map/ppermute | solution.py:952
  238.5 23.4 %collective-permute-start.38 = (bf16[2,240,640]{2,1,0:T(8,128)(2,1)S(1)}, bf16[2,240,640]{2,1,0:T(8,128)(2,1)S(1)}, u32[]{:S(2)}, u32[]{:S(2)}) collective-permute-start(bf16[2,240,640]{2,1,0:T(8,128)(2,1)S(1)} %get-tuple-element.301), channel_id=1, source_target_pairs={{0,2},{1,3},{2,0},{3,1},{4,6},{5,7},{6,4},{7,5},{8,10},{9,11},{10,... | collective-permute-start | bytes 1843208 | tf_op jit(solution)/shard_map/ppermute | solution.py:952
  239.1 28.5 %collective-permute-start.39 = (bf16[240,640]{1,0:T(8,128)(2,1)S(1)}, bf16[240,640]{1,0:T(8,128)(2,1)S(1)}, u32[]{:S(2)}, u32[]{:S(2)}) collective-permute-start(bf16[240,640]{1,0:T(8,128)(2,1)S(1)} %fusion.21), channel_id=1, source_target_pairs={{0,8},{4,12},{8,0},{12,4},{16,24},{20,28},{24,16},{28,20},{1,9},{5... | collective-permute-start | bytes 921608 | tf_op jit(solution)/shard_map/ppermute | solution.py:952
  260.0 17.1 %collective-permute-start.41 = (bf16[2,240,640]{2,1,0:T(8,128)(2,1)S(1)}, bf16[2,240,640]{2,1,0:T(8,128)(2,1)S(1)}, u32[]{:S(2)}, u32[]{:S(2)}) collective-permute-start(bf16[2,240,640]{2,1,0:T(8,128)(2,1)S(1)} %fusion.2), channel_id=1, source_target_pairs={{0,4},{4,0},{8,12},{12,8},{16,20},{20,16},{24,28},{28,24},{1,5},{5... | collective-permute-start | bytes 1843208 | tf_op jit(solution)/shard_map/ppermute | solution.py:952
  277.7 18.7 %collective-permute-start.43 = (bf16[2,240,640]{2,1,0:T(8,128)(2,1)S(1)}, bf16[2,240,640]{2,1,0:T(8,128)(2,1)S(1)}, u32[]{:S(2)}, u32[]{:S(2)}) collective-permute-start(bf16[2,240,640]{2,1,0:T(8,128)(2,1)S(1)} %get-tuple-element.300), channel_id=1, source_target_pairs={{0,2},{1,3},{2,0},{3,1},{4,6},{5,7},{6,4},{7,5},{8,10},{9,11},{10,... | collective-permute-start | bytes 1843208 | tf_op jit(solution)/shard_map/ppermute | solution.py:952
  278.1 23.1 %collective-permute-start.44 = (bf16[240,640]{1,0:T(8,128)(2,1)S(1)}, bf16[240,640]{1,0:T(8,128)(2,1)S(1)}, u32[]{:S(2)}, u32[]{:S(2)}) collective-permute-start(bf16[240,640]{1,0:T(8,128)(2,1)S(1)} %fusion.23), channel_id=1, source_target_pairs={{0,16},{4,20},{8,24},{12,28},{16,0},{20,4},{24,8},{28,12},{1,17},{... | collective-permute-start | bytes 921608 | tf_op jit(solution)/shard_map/ppermute | solution.py:952
  288.6 13.0 %collective-permute-start.45 = (bf16[240,640]{1,0:T(8,128)(2,1)S(1)}, bf16[240,640]{1,0:T(8,128)(2,1)S(1)}, u32[]{:S(2)}, u32[]{:S(2)}) collective-permute-start(bf16[240,640]{1,0:T(8,128)(2,1)S(1)} %fusion.20), channel_id=1, source_target_pairs={{0,8},{4,12},{8,0},{12,4},{16,24},{20,28},{24,16},{28,20},{1,9},{5... | collective-permute-start | bytes 921608 | tf_op jit(solution)/shard_map/ppermute | solution.py:952
  301.9 16.7 %collective-permute-start.48 = (bf16[2,240,640]{2,1,0:T(8,128)(2,1)S(1)}, bf16[2,240,640]{2,1,0:T(8,128)(2,1)S(1)}, u32[]{:S(2)}, u32[]{:S(2)}) collective-permute-start(bf16[2,240,640]{2,1,0:T(8,128)(2,1)S(1)} %get-tuple-element.299), channel_id=1, source_target_pairs={{0,2},{1,3},{2,0},{3,1},{4,6},{5,7},{6,4},{7,5},{8,10},{9,11},{10,... | collective-permute-start | bytes 1843208 | tf_op jit(solution)/shard_map/ppermute | solution.py:952
  303.5 15.9 %collective-permute-start.47 = (bf16[2,240,640]{2,1,0:T(8,128)(2,1)S(1)}, bf16[2,240,640]{2,1,0:T(8,128)(2,1)S(1)}, u32[]{:S(2)}, u32[]{:S(2)}) collective-permute-start(bf16[2,240,640]{2,1,0:T(8,128)(2,1)S(1)} %fusion.1), channel_id=1, source_target_pairs={{0,4},{4,0},{8,12},{12,8},{16,20},{20,16},{24,28},{28,24},{1,5},{5... | collective-permute-start | bytes 1843208 | tf_op jit(solution)/shard_map/ppermute | solution.py:952
  307.2 25.5 %collective-permute-start.50 = (bf16[2,256,640]{2,1,0:T(8,128)(2,1)S(1)}, bf16[2,256,640]{2,1,0:T(8,128)(2,1)S(1)}, u32[]{:S(2)}, u32[]{:S(2)}) collective-permute-start(bf16[2,256,640]{2,1,0:T(8,128)(2,1)S(1)} %get-tuple-element.298), channel_id=1, source_target_pairs={{0,2},{1,3},{2,0},{3,1},{4,6},{5,7},{6,4},{7,5},{8,10},{9,11},{10,... | collective-permute-start | bytes 1966088 | tf_op jit(solution)/shard_map/ppermute | solution.py:952
  308.7 16.5 %collective-permute-start.49 = (bf16[240,640]{1,0:T(8,128)(2,1)S(1)}, bf16[240,640]{1,0:T(8,128)(2,1)S(1)}, u32[]{:S(2)}, u32[]{:S(2)}) collective-permute-start(bf16[240,640]{1,0:T(8,128)(2,1)S(1)} %fusion.19), channel_id=1, source_target_pairs={{0,16},{4,20},{8,24},{12,28},{16,0},{20,4},{24,8},{28,12},{1,17},{... | collective-permute-start | bytes 921608 | tf_op jit(solution)/shard_map/ppermute | solution.py:952
  309.6 46.9 %collective-permute-start.54 = (bf16[2,256,640]{2,1,0:T(8,128)(2,1)S(1)}, bf16[2,256,640]{2,1,0:T(8,128)(2,1)S(1)}, u32[]{:S(2)}, u32[]{:S(2)}) collective-permute-start(bf16[2,256,640]{2,1,0:T(8,128)(2,1)S(1)} %get-tuple-element.297), channel_id=1, source_target_pairs={{0,2},{1,3},{2,0},{3,1},{4,6},{5,7},{6,4},{7,5},{8,10},{9,11},{10,... | collective-permute-start | bytes 1966088 | tf_op jit(solution)/shard_map/ppermute | solution.py:952
  332.9 23.5 %collective-permute-start.51 = (bf16[2,256,640]{2,1,0:T(8,128)(2,1)S(1)}, bf16[2,256,640]{2,1,0:T(8,128)(2,1)S(1)}, u32[]{:S(2)}, u32[]{:S(2)}) collective-permute-start(bf16[2,256,640]{2,1,0:T(8,128)(2,1)S(1)} %fusion), channel_id=1, source_target_pairs={{0,4},{4,0},{8,12},{12,8},{16,20},{20,16},{24,28},{28,24},{1,5},{5... | collective-permute-start | bytes 1966088 | tf_op jit(solution)/shard_map/ppermute | solution.py:952
  333.0 10.3 %collective-permute-start.52 = (bf16[240,640]{1,0:T(8,128)(2,1)S(1)}, bf16[240,640]{1,0:T(8,128)(2,1)S(1)}, u32[]{:S(2)}, u32[]{:S(2)}) collective-permute-start(bf16[240,640]{1,0:T(8,128)(2,1)S(1)} %fusion.17), channel_id=1, source_target_pairs={{0,8},{4,12},{8,0},{12,4},{16,24},{20,28},{24,16},{28,20},{1,9},{5... | collective-permute-start | bytes 921608 | tf_op jit(solution)/shard_map/ppermute | solution.py:952
  334.6 21.9 %collective-permute-start.53 = (bf16[240,640]{1,0:T(8,128)(2,1)S(1)}, bf16[240,640]{1,0:T(8,128)(2,1)S(1)}, u32[]{:S(2)}, u32[]{:S(2)}) collective-permute-start(bf16[240,640]{1,0:T(8,128)(2,1)S(1)} %add_convert_fusion.15.p0_ref), channel_id=1, source_target_pairs={{0,8},{4,12},{8,0},{12,4},{16,24},{20,28},{24,16},{28,20},{1,9},{5... | collective-permute-start | bytes 921608 | tf_op jit(solution)/shard_map/ppermute | solution.py:952
  335.1 27.9 %collective-permute-start.55 = (bf16[240,640]{1,0:T(8,128)(2,1)S(1)}, bf16[240,640]{1,0:T(8,128)(2,1)S(1)}, u32[]{:S(2)}, u32[]{:S(2)}) collective-permute-start(bf16[240,640]{1,0:T(8,128)(2,1)S(1)} %add_convert_fusion.14.p0_ref), channel_id=1, source_target_pairs={{0,8},{4,12},{8,0},{12,4},{16,24},{20,28},{24,16},{28,20},{1,9},{5... | collective-permute-start | bytes 921608 | tf_op jit(solution)/shard_map/ppermute | solution.py:952
  343.5 19.6 %collective-permute-start.56 = (bf16[240,640]{1,0:T(8,128)(2,1)S(1)}, bf16[240,640]{1,0:T(8,128)(2,1)S(1)}, u32[]{:S(2)}, u32[]{:S(2)}) collective-permute-start(bf16[240,640]{1,0:T(8,128)(2,1)S(1)} %fusion.16), channel_id=1, source_target_pairs={{0,16},{4,20},{8,24},{12,28},{16,0},{20,4},{24,8},{28,12},{1,17},{... | collective-permute-start | bytes 921608 | tf_op jit(solution)/shard_map/ppermute | solution.py:952
  356.6 14.9 %collective-permute-start.59 = (bf16[256,640]{1,0:T(8,128)(2,1)S(1)}, bf16[256,640]{1,0:T(8,128)(2,1)S(1)}, u32[]{:S(2)}, u32[]{:S(2)}) collective-permute-start(bf16[256,640]{1,0:T(8,128)(2,1)S(1)} %fusion.6), channel_id=1, source_target_pairs={{0,8},{4,12},{8,0},{12,4},{16,24},{20,28},{24,16},{28,20},{1,9},{5... | collective-permute-start | bytes 983048 | tf_op jit(solution)/shard_map/ppermute | solution.py:952
  358.7 10.3 %collective-permute-start.58 = (bf16[240,640]{1,0:T(8,128)(2,1)S(1)}, bf16[240,640]{1,0:T(8,128)(2,1)S(1)}, u32[]{:S(2)}, u32[]{:S(2)}) collective-permute-start(bf16[240,640]{1,0:T(8,128)(2,1)S(1)} %collective-permute-done.53.p1_ref), channel_id=1, source_target_pairs={{0,4},{4,0},{8,12},{12,8},{16,20},{20,16},{24,28},{28,24},{1,5},{5... | collective-permute-start | bytes 921608 | tf_op jit(solution)/shard_map/ppermute | solution.py:952
  371.8 16.8 %collective-permute-start.63 = (bf16[256,640]{1,0:T(8,128)(2,1)S(1)}, bf16[256,640]{1,0:T(8,128)(2,1)S(1)}, u32[]{:S(2)}, u32[]{:S(2)}) collective-permute-start(bf16[256,640]{1,0:T(8,128)(2,1)S(1)} %fusion.8), channel_id=1, source_target_pairs={{0,16},{4,20},{8,24},{12,28},{16,0},{20,4},{24,8},{28,12},{1,17},{... | collective-permute-start | bytes 983048 | tf_op jit(solution)/shard_map/ppermute | solution.py:952
  375.0 10.5 %collective-permute-start.60 = (bf16[240,640]{1,0:T(8,128)(2,1)S(1)}, bf16[240,640]{1,0:T(8,128)(2,1)S(1)}, u32[]{:S(2)}, u32[]{:S(2)}) collective-permute-start(bf16[240,640]{1,0:T(8,128)(2,1)S(1)} %add_convert_fusion.13.p0_ref), channel_id=1, source_target_pairs={{0,8},{4,12},{8,0},{12,4},{16,24},{20,28},{24,16},{28,20},{1,9},{5... | collective-permute-start | bytes 921608 | tf_op jit(solution)/shard_map/ppermute | solution.py:952
  375.4 10.1 %collective-permute-start.61 = (bf16[240,640]{1,0:T(8,128)(2,1)S(1)}, bf16[240,640]{1,0:T(8,128)(2,1)S(1)}, u32[]{:S(2)}, u32[]{:S(2)}) collective-permute-start(bf16[240,640]{1,0:T(8,128)(2,1)S(1)} %add_convert_fusion.14.p0_ref), channel_id=1, source_target_pairs={{0,4},{4,0},{8,12},{12,8},{16,20},{20,16},{24,28},{28,24},{1,5},{5... | collective-permute-start | bytes 921608 | tf_op jit(solution)/shard_map/ppermute | solution.py:952
  375.7 10.4 %collective-permute-start.62 = (bf16[240,640]{1,0:T(8,128)(2,1)S(1)}, bf16[240,640]{1,0:T(8,128)(2,1)S(1)}, u32[]{:S(2)}, u32[]{:S(2)}) collective-permute-start(bf16[240,640]{1,0:T(8,128)(2,1)S(1)} %collective-permute-done.55.p1_ref), channel_id=1, source_target_pairs={{0,4},{4,0},{8,12},{12,8},{16,20},{20,16},{24,28},{28,24},{1,5},{5... | collective-permute-start | bytes 921608 | tf_op jit(solution)/shard_map/ppermute | solution.py:952
  388.7 20.2 %collective-permute-start.66 = (bf16[256,640]{1,0:T(8,128)(2,1)S(1)}, bf16[256,640]{1,0:T(8,128)(2,1)S(1)}, u32[]{:S(2)}, u32[]{:S(2)}) collective-permute-start(bf16[256,640]{1,0:T(8,128)(2,1)S(1)} %add_convert_fusion.8.p0_ref), channel_id=1, source_target_pairs={{0,8},{4,12},{8,0},{12,4},{16,24},{20,28},{24,16},{28,20},{1,9},{5... | collective-permute-start | bytes 983048 | tf_op jit(solution)/shard_map/ppermute | solution.py:952
  390.1 10.2 %collective-permute-start.64 = (bf16[240,640]{1,0:T(8,128)(2,1)S(1)}, bf16[240,640]{1,0:T(8,128)(2,1)S(1)}, u32[]{:S(2)}, u32[]{:S(2)}) collective-permute-start(bf16[240,640]{1,0:T(8,128)(2,1)S(1)} %add_convert_fusion.13.p0_ref), channel_id=1, source_target_pairs={{0,4},{4,0},{8,12},{12,8},{16,20},{20,16},{24,28},{28,24},{1,5},{5... | collective-permute-start | bytes 921608 | tf_op jit(solution)/shard_map/ppermute | solution.py:952
  390.4 15.9 %collective-permute-start.65 = (bf16[240,640]{1,0:T(8,128)(2,1)S(1)}, bf16[240,640]{1,0:T(8,128)(2,1)S(1)}, u32[]{:S(2)}, u32[]{:S(2)}) collective-permute-start(bf16[240,640]{1,0:T(8,128)(2,1)S(1)} %collective-permute-done.60.p1_ref), channel_id=1, source_target_pairs={{0,4},{4,0},{8,12},{12,8},{16,20},{20,16},{24,28},{28,24},{1,5},{5... | collective-permute-start | bytes 921608 | tf_op jit(solution)/shard_map/ppermute | solution.py:952
  392.2 17.7 %collective-permute-start.67 = (bf16[256,640]{1,0:T(8,128)(2,1)S(1)}, bf16[256,640]{1,0:T(8,128)(2,1)S(1)}, u32[]{:S(2)}, u32[]{:S(2)}) collective-permute-start(bf16[256,640]{1,0:T(8,128)(2,1)S(1)} %add_convert_fusion.8.p0_ref), channel_id=1, source_target_pairs={{0,4},{4,0},{8,12},{12,8},{16,20},{20,16},{24,28},{28,24},{1,5},{5... | collective-permute-start | bytes 983048 | tf_op jit(solution)/shard_map/ppermute | solution.py:952
  (84 other events, 761.2 us)

commit v4 on v3

--- a/solution.py
+++ b/solution.py
@@ -21,7 +21,7 @@
 bf16 = jnp.bfloat16
 f32 = jnp.float32
 GAIN_ROWS = 16
-FFN_MEBIBYTES = 30
+FFN_MEBIBYTES = 26
 
 
 def nn(left, right):
@@ -44,7 +44,7 @@
     return pl.BlockSpec(memory_space=pl.ANY)
 
 
-def params(mebibytes=20):
+def params(mebibytes=14):
     return pltpu.CompilerParams(vmem_limit_bytes=mebibytes * 1024 * 1024)
 
 
@@ -335,7 +335,7 @@
     else:
         (dn_ref,) = dn_sources
         gu_loads, dn_loads = whole_copies(gu_sources[0], gu_ref, gu_sems), []
-    acc_ref, m_ref, l_ref = refs[:3]
+    acc_ref, m_ref, l_ref, kvs_ref = refs[:4]
     rows, width = h_ref.shape
     ffn = inner_ref.shape[1]
     for load in gu_loads + dn_loads:
@@ -350,10 +350,15 @@
         m_ref[group : group + 1, :] = peak
         l_ref[group : group + 1, :] = jnp.sum(raised, axis=0, keepdims=True)
         acc_ref[group] = nn(value_block(kv0_ref, group), raised.astype(bf16))
-    for member, kv_ref in ((1, kv1_ref), (2, kv2_ref), (3, kv3_ref)):
-
-        @pl.when(visible_ref[member] == 1)
-        def _(kv_ref=kv_ref):
+    for i, kv_ref in enumerate((kv1_ref, kv2_ref, kv3_ref)):
+        kvs_ref[i] = kv_ref[...]
+
+    @pl.loop(0, 3)
+    def _(member):
+        kv_ref = kvs_ref.at[member]
+
+        @pl.when(visible_ref[member + 1] == 1)
+        def _():
             for group in range(KEY_VALUE_HEADS):
                 scores = nn(key_block(kv_ref, group).T, stacked_heads(q_ref, group))
                 old = m_ref[group : group + 1, :]
@@ -431,6 +436,7 @@
             pltpu.VMEM((KEY_VALUE_HEADS, HEAD_SIZE, lanes), f32),
             pltpu.VMEM((KEY_VALUE_HEADS, lanes), f32),
             pltpu.VMEM((KEY_VALUE_HEADS, lanes), f32),
+            pltpu.VMEM((3, *kvs[0].shape), bf16),
             pltpu.VMEM((width, 2 * ffn), bf16),
             pltpu.SemaphoreType.DMA((len(plans[0]) if first else 4,)),
             pltpu.SemaphoreType.DMA((len(plans[1]) if first else 1,)),
@@ -542,12 +548,12 @@
     kv2_ref,
     kv3_ref,
     dq_ref,
-    dkv0_ref,
-    dkv1_ref,
-    dkv2_ref,
-    dkv3_ref,
+    keep_ref,
+    send_ref,
     acc_ref,
     row_ref,
+    kvs_ref,
+    dkvs_ref,
 ):
     rows = q_ref.shape[1]
     key_width = KEY_VALUE_HEADS * HEAD_SIZE
@@ -580,22 +586,26 @@
             acc_ref[group] += moved
 
     for group in range(KEY_VALUE_HEADS):
-        one(group, kv0_ref, dkv0_ref, True)
-    for member, kv_ref, dkv_ref in (
-        (1, kv1_ref, dkv1_ref),
-        (2, kv2_ref, dkv2_ref),
-        (3, kv3_ref, dkv3_ref),
-    ):
-
-        @pl.when(visible_ref[member] == 1)
-        def _(kv_ref=kv_ref, dkv_ref=dkv_ref):
+        one(group, kv0_ref, keep_ref.at[0], True)
+    for i, kv_ref in enumerate((kv1_ref, kv2_ref, kv3_ref)):
+        kvs_ref[i] = kv_ref[...]
+
+    @pl.loop(0, 3)
+    def _(member):
+        kv_ref, dkv_ref = kvs_ref.at[member], dkvs_ref.at[member]
+
+        @pl.when(visible_ref[member + 1] == 1)
+        def _():
             for group in range(KEY_VALUE_HEADS):
                 one(group, kv_ref, dkv_ref, False)
 
-        @pl.when(visible_ref[member] == 0)
-        def _(dkv_ref=dkv_ref):
-            dkv_ref[...] = jnp.zeros_like(dkv_ref)
-
+        @pl.when(visible_ref[member + 1] == 0)
+        def _():
+            dkv_ref[...] = jnp.zeros(dkv_ref.shape, bf16)
+
+    send_ref[0] = dkvs_ref[0]
+    keep_ref[1] = dkvs_ref[1]
+    send_ref[1] = dkvs_ref[2]
     cos, sin = cos_ref[...], sin_ref[...]
     for group in range(KEY_VALUE_HEADS):
         for j in range(SHARING):
@@ -613,12 +623,14 @@
     lanes = SHARING * rows
     return pl.pallas_call(
         attend_back_kernel,
-        out_shape=(shape((width, rows), bf16),) + (shape((key_rows, rows), bf16),) * 4,
+        out_shape=(shape((width, rows), bf16),) + (shape((2, key_rows, rows), bf16),) * 2,
         in_specs=[in_smem()] + [in_vmem()] * 10,
-        out_specs=(in_vmem(),) * 5,
+        out_specs=(in_vmem(),) * 3,
         scratch_shapes=[
             pltpu.VMEM((KEY_VALUE_HEADS, HEAD_SIZE, lanes), f32),
             pltpu.VMEM((KEY_VALUE_HEADS, lanes), f32),
+            pltpu.VMEM((3, key_rows, rows), bf16),
+            pltpu.VMEM((3, key_rows, rows), bf16),
         ],
         compiler_params=params(),
         cost_estimate=cost(2 * rows * width * 4 * rows * 10, 10 * width * rows * 2),
@@ -967,14 +979,13 @@
     return (block, beside, across, diagonal)
 
 
-def fold_kv(pieces):
-    rows = pieces[0].shape[0]
-    got = flip(jnp.concatenate([pieces[1], pieces[3]], axis=0), "fsdp", 1)
-    return total(pieces[0], got[:rows]), total(pieces[2], got[rows:])
-
-
-def return_kv(pieces):
-    own, across = fold_kv(pieces)
+def fold_kv(keep, send):
+    got = flip(send, "fsdp", 1)
+    return total(keep[0], got[0]), total(keep[1], got[1])
+
+
+def return_kv(keep, send):
+    own, across = fold_kv(keep, send)
     return own, flip(across, "fsdp", 2)
 
 
@@ -1164,7 +1175,7 @@
         cotangent.T, middle, gating, upward, ffn_gain, weights
     )
     dq, *dkvs = attend_back(visible, q, d_out, att_t, lse, cos, sin, kvs)
-    own, got = return_kv(dkvs)
+    own, got = return_kv(*dkvs)
     grad, dqkv2, attention_gain_grad2 = leave(
         hidden, d_middle, dq, own, got, attention_gain, cos, sin, weights_a
     )
@@ -1185,7 +1196,7 @@
     order.done(dq)
     gate.first()
     down.second()
-    own, across = fold_kv(order.tie(*dkvs))
+    own, across = fold_kv(*order.tie(*dkvs))
     order.done(across)
     gate.rest()
     down.third()

time: 428 us -> 412 us (0.963)
  starting transfers between devices: 84.2 us -> 72.4 us
  local copies, waits for them, and re-layouts: 23.9 us -> 16.6 us
    ppermute x69, starting transfers between devices: 84.2 us -> 72.4 us  [flip(): lax.ppermute(value, axis_name, [(i, i ^ distance) for i in range(size)])]
    unnamed x126 -> x114, local copies, waits for them, and re-layouts: 19.5 us -> 12.1 us
    pallas_call x2, Pallas kernels: 7.95 us -> 13.4 us  [attend_back(): pl.pallas_call(attend_back_kernel, out_shape=(shape((width, rows), bf16),...]
  transfers between devices with their start and end apart: 69 -> 69, of which waited for: 38 -> 38; matrix products, arithmetic and copies ran while one was open for 2% -> 2% of each run, Pallas kernels for 10% -> 11%
where the time goes in v4:
time: 412 us; the launch traced here: 405 us
  waiting for transfers between devices  207 us (50%)
  Pallas kernels  96.8 us (23%)
  starting transfers between devices  72.4 us (18%)
  local copies, waits for them, and re-layouts  16.6 us (4%)
  other arithmetic  9.36 us (2%)
    ppermute x69, waiting for transfers between devices, flip(): lax.ppermute(value, axis_name, [(i, i ^ distance) for i in range(size)])  207 us
    ppermute x69, starting transfers between devices, flip(): lax.ppermute(value, axis_name, [(i, i ^ distance) for i in range(size)])  72.4 us
    pallas_call x2, Pallas kernels, forward_block(): pl.pallas_call(functools.partial(forward_kernel, plans, counts), out_shap...  25.7 us
    pallas_call x1, Pallas kernels, feed_back_gate(): pl.pallas_call(feed_back_gate_kernel, out_shape=(shape((rows, width), f32...  17 us
    pallas_call x2, Pallas kernels, attend_back(): pl.pallas_call(attend_back_kernel, out_shape=(shape((width, rows), bf16),...  13.4 us
    unnamed x114, local copies, waits for them, and re-layouts  12.1 us
    pallas_call x1, Pallas kernels, feed_back(): pl.pallas_call(feed_back_kernel, out_shape=(shape((rows, width), bf16), s...  9.03 us
  transfers between devices with their start and end apart: 69, of which 38 were waited for; matrix products, arithmetic and copies ran while one was open for 2% of the time, Pallas kernels for 11%

profile of v4, /device:TPU:0, one launch (start us, length us, event | category | flops | bytes accessed | tf_op | source)
XLA Modules:
  0.0 405.2 jit_solution(15766385859236431357)
XLA Ops:
  2.5 2.6 collective-permute-start.1
  5.2 4.0 pack.1
  18.5 9.7 %collective-permute-done.4.refs_2_ = bf16[240,1280]{1,0:T(8,128)(2,1)S(1)} collective-permute-done((bf16[240,1280]{1,0:T(8,128)(2,1)}, bf16[240,1280]{1,0:T(8,128)(2,1)S(1)}, u32[]{:S(2)}, u32[]{:S(2)}) %collective-permute-start.4) | collective-permute-done | bytes 614432 | tf_op jit(solution)/shard_map/ppermute | solution.py:964
  32.0 11.5 %collective-permute-done.5.refs_3_ = bf16[240,1280]{1,0:T(8,128)(2,1)S(1)} collective-permute-done((bf16[240,1280]{1,0:T(8,128)(2,1)S(1)}, bf16[240,1280]{1,0:T(8,128)(2,1)S(1)}, u32[]{:S(2)}, u32[]{:S(2)}) %collective-permute-start.5) | collective-permute-done | bytes 614432 | tf_op jit(solution)/shard_map/ppermute | solution.py:964
  43.5 3.4 collective-permute-done.13.refs_12_
  46.9 11.2 %collective-permute-done.12.refs_18_ = bf16[240,1280]{1,0:T(8,128)(2,1)S(1)} collective-permute-done((bf16[240,1280]{1,0:T(8,128)(2,1)}, bf16[240,1280]{1,0:T(8,128)(2,1)S(1)}, u32[]{:S(2)}, u32[]{:S(2)}) %collective-permute-start.12) | collective-permute-done | bytes 614432 | tf_op jit(solution)/shard_map/ppermute | solution.py:964
  63.0 3.4 enter_first.1
  67.2 4.8 %collective-permute-done.14.refs_13_ = bf16[240,1280]{1,0:T(8,128)(2,1)S(1)} collective-permute-done((bf16[240,1280]{1,0:T(8,128)(2,1)S(1)}, bf16[240,1280]{1,0:T(8,128)(2,1)S(1)}, u32[]{:S(2)}, u32[]{:S(2)}) %collective-permute-start.14) | collective-permute-done | bytes 614432 | tf_op jit(solution)/shard_map/ppermute | solution.py:964
  77.1 8.4 %collective-permute-done.23.refs_25_ = bf16[480,640]{1,0:T(8,128)(2,1)S(1)} collective-permute-done((bf16[480,640]{1,0:T(8,128)(2,1)S(1)}, bf16[480,640]{1,0:T(8,128)(2,1)S(1)}, u32[]{:S(2)}, u32[]{:S(2)}) %collective-permute-start.23) | collective-permute-done | bytes 614432 | tf_op jit(solution)/shard_map/ppermute | solution.py:964
  86.6 3.6 collective-permute-done.18.refs_19_
  92.8 14.0 %forward_first.1 = (f32[256,960]{1,0:T(8,128)S(1)}, bf16[256,960]{1,0:T(8,128)(2,1)S(1)}, bf16[960,256]{1,0:T(8,128)(2,1)S(1)}, f32[5,768]{1,0:T(8,128)S(1)}, f3...) custom-call(s32[4]{0:T(128)S(1)} %and_convert_fusion.refs_0_.visible, ...), custom_call_target="tpu_custom_call" | custom-call | flops 5033164800 | bytes 19988480 | tf_op jit(solution)/shard_map/forward_first/pallas_call | solution.py:416
  110.0 6.5 %collective-permute-start.27 = (bf16[640,256]{1,0:T(8,128)(2,1)S(1)}, bf16[640,256]{1,0:T(8,128)(2,1)S(1)}, u32[]{:S(2)}, u32[]{:S(2)}) collective-permute-start(bf16[640,256]{1,0:T(8,128)(2,1)S(1)} %get-tuple-element.172.refs_4_.kv0_ref), channel_id=1, source_target_pairs={{0,2},{1,3},{2,0},{3,1},{4,6},{5,7},{6,4},{7,5},{8,10},{9,11},{10,... | collective-permute-start | bytes 983048 | tf_op jit(solution)/shard_map/ppermute | solution.py:964
  116.5 5.8 %collective-permute-done.27.refs_6_.kv2_ref = bf16[640,256]{1,0:T(8,128)(2,1)S(1)} collective-permute-done((bf16[640,256]{1,0:T(8,128)(2,1)S(1)}, bf16[640,256]{1,0:T(8,128)(2,1)S(1)}, u32[]{:S(2)}, u32[]{:S(2)}) %collective-permute-start.27) | collective-permute-done | bytes 327712 | tf_op jit(solution)/shard_map/ppermute | solution.py:964
  123.9 11.7 %forward_last.1 = (bf16[960,256]{1,0:T(8,128)(2,1)}, bf16[256,960]{1,0:T(8,128)(2,1)S(1)}, bf16[960,256]{1,0:T(8,128)(2,1)S(1)}, f32[5,768]{1,0:T(8,128)S(1)}, f...) custom-call(s32[4]{0:T(128)S(1)} %and_convert_fusion.refs_0_.visible, ...), custom_call_target="tpu_custom_call" | custom-call | flops 5033164800 | bytes 19988480 | tf_op jit(solution)/shard_map/forward_last/pallas_call | solution.py:416
  135.6 9.0 %feed_back.1 = (bf16[256,960]{1,0:T(8,128)(2,1)S(1)}, bf16[256,5120]{1,0:T(8,128)(2,1)S(1)}, f32[256,960]{1,0:T(8,128)S(1)}, bf16[256,1024]{1,0:T(8,128)(2,1)S(1...) custom-call(bf16[960,256]{1,0:T(8,128)(2,1)S(1)} %bitcast.131, f32[256,960]{1,0:T(8,128)S(1)} %get-tuple-element.176.middle_ref, ...), custom_call_target="tpu_custom_call" | custom-call | flops 5033164800 | bytes 19988480 | tf_op jit(solution)/shard_map/feed_back/pallas_call | solution.py:515
  144.7 6.6 %attend_back.2 = (bf16[960,256]{1,0:T(8,128)(2,1)S(1)}, bf16[2,640,256]{2,1,0:T(8,128)(2,1)S(1)}, bf16[2,640,256]{2,1,0:T(8,128)(2,1)S(1)}) custom-call(s32[4]{0:T(128)S(1)} %and_convert_fusion.refs_0_.visible_ref, bf16[960,256]{1,0:T(8,128)(2,1)S(1)} %get-tuple-element.171.refs_3_.q_ref, bf16[960,256]{1,0:T(8,128)(2,1)S(1)} %get-tuple-element.181.do_ref, ...), custom_call_target="tpu_custom_call" | custom-call | flops 5033164800 | bytes 4915200 | tf_op jit(solution)/shard_map/attend_back/pallas_call | solution.py:624
  151.5 5.4 %collective-permute-start.29 = (bf16[2,640,256]{2,1,0:T(8,128)(2,1)S(1)}, bf16[2,640,256]{2,1,0:T(8,128)(2,1)S(1)}, u32[]{:S(2)}, u32[]{:S(2)}) collective-permute-start(bf16[2,640,256]{2,1,0:T(8,128)(2,1)S(1)} %get-tuple-element.186), channel_id=1, source_target_pairs={{0,1},{1,0},{2,3},{3,2},{4,5},{5,4},{6,7},{7,6},{8,9},{9,8},{10,11... | collective-permute-start | bytes 1966088 | tf_op jit(solution)/shard_map/ppermute | solution.py:964
  159.5 6.7 %collective-permute-start.30 = (bf16[640,256]{1,0:T(8,128)(2,1)}, bf16[640,256]{1,0:T(8,128)(2,1)}, u32[]{:S(2)}, u32[]{:S(2)}) collective-permute-start(bf16[640,256]{1,0:T(8,128)(2,1)} %get-tuple-element.295), channel_id=1, source_target_pairs={{0,2},{1,3},{2,0},{3,1},{4,6},{5,7},{6,4},{7,5},{8,10},{9,11},{10,... | collective-permute-start | bytes 983048 | tf_op jit(solution)/shard_map/ppermute | solution.py:964
  166.3 8.2 %collective-permute-done.30.got_ref = bf16[640,256]{1,0:T(8,128)(2,1)} collective-permute-done((bf16[640,256]{1,0:T(8,128)(2,1)}, bf16[640,256]{1,0:T(8,128)(2,1)}, u32[]{:S(2)}, u32[]{:S(2)}) %collective-permute-start.30) | collective-permute-done | bytes 327712 | tf_op jit(solution)/shard_map/ppermute | solution.py:964
  177.9 2.6 leave.1
  184.2 3.9 down_grad.1
  188.2 4.7 %collective-permute-done.31 = bf16[2,4,240,640]{3,2,1,0:T(8,128)(2,1)S(1)} collective-permute-done((bf16[2,4,240,640]{3,2,1,0:T(8,128)(2,1)S(1)}, bf16[2,4,240,640]{3,2,1,0:T(8,128)(2,1)S(1)}, u32[]{:S(2)}, u32[]{:S(2)}) %collective-permute-start.31) | collective-permute-done | bytes 2457632 | tf_op jit(solution)/shard_map/ppermute | solution.py:964
  195.4 17.0 %feed_back_gate.1 = (f32[256,960]{1,0:T(8,128)S(1)}, bf16[256,1024]{1,0:T(8,128)(2,1)S(1)}, bf16[960,256]{1,0:T(8,128)(2,1)S(1)}, f32[1,960]{1,0:T(1,128)S(1)}, ...) custom-call(s32[3]{0:T(128)S(1)} %pad_add_fusion.1.place_ref.refs_0_, ...), custom_call_target="tpu_custom_call" | custom-call | flops 10066329600 | bytes 19988480 | tf_op jit(solution)/shard_map/feed_back_gate/pallas_call | solution.py:746
  212.4 9.9 %collective-permute-done.33 = bf16[2,240,640]{2,1,0:T(8,128)(2,1)S(1)} collective-permute-done((bf16[2,240,640]{2,1,0:T(8,128)(2,1)S(1)}, bf16[2,240,640]{2,1,0:T(8,128)(2,1)S(1)}, u32[]{:S(2)}, u32[]{:S(2)}) %collective-permute-start.33) | collective-permute-done | bytes 614432 | tf_op jit(solution)/shard_map/ppermute | solution.py:964
  222.7 4.7 %collective-permute-done.34 = bf16[2,4,240,640]{3,2,1,0:T(8,128)(2,1)S(1)} collective-permute-done((bf16[2,4,240,640]{3,2,1,0:T(8,128)(2,1)S(1)}, bf16[2,4,240,640]{3,2,1,0:T(8,128)(2,1)S(1)}, u32[]{:S(2)}, u32[]{:S(2)}) %collective-permute-start.34) | collective-permute-done | bytes 2457632 | tf_op jit(solution)/shard_map/ppermute | solution.py:964
  229.5 6.7 %attend_back.3 = (bf16[960,256]{1,0:T(8,128)(2,1)S(1)}, bf16[2,640,256]{2,1,0:T(8,128)(2,1)S(1)}, bf16[2,640,256]{2,1,0:T(8,128)(2,1)S(1)}) custom-call(s32[4]{0:T(128)S(1)} %and_convert_fusion.refs_0_.visible_ref, bf16[960,256]{1,0:T(8,128)(2,1)S(1)} %copy-done.19, bf16[960,256]{1,0:T(8,128)(2,1)S(1)} %get-tuple-element.209.do_ref, ...), custom_call_target="tpu_custom_call" | custom-call | flops 5033164800 | bytes 4915200 | tf_op jit(solution)/shard_map/attend_back/pallas_call | solution.py:624
  236.2 7.4 %collective-permute-done.35 = bf16[2,240,640]{2,1,0:T(8,128)(2,1)S(1)} collective-permute-done((bf16[2,240,640]{2,1,0:T(8,128)(2,1)S(1)}, bf16[2,240,640]{2,1,0:T(8,128)(2,1)S(1)}, u32[]{:S(2)}, u32[]{:S(2)}) %collective-permute-start.35) | collective-permute-done | bytes 614432 | tf_op jit(solution)/shard_map/ppermute | solution.py:964
  248.2 13.4 %collective-permute-done.38 = bf16[2,240,640]{2,1,0:T(8,128)(2,1)S(1)} collective-permute-done((bf16[2,240,640]{2,1,0:T(8,128)(2,1)S(1)}, bf16[2,240,640]{2,1,0:T(8,128)(2,1)S(1)}, u32[]{:S(2)}, u32[]{:S(2)}) %collective-permute-start.38) | collective-permute-done | bytes 614432 | tf_op jit(solution)/shard_map/ppermute | solution.py:964
  262.4 8.7 %collective-permute-done.40.refs_5_ = bf16[640,256]{1,0:T(8,128)(2,1)S(1)} collective-permute-done((bf16[640,256]{1,0:T(8,128)(2,1)S(1)}, bf16[640,256]{1,0:T(8,128)(2,1)S(1)}, u32[]{:S(2)}, u32[]{:S(2)}) %collective-permute-start.40) | collective-permute-done | bytes 327712 | tf_op jit(solution)/shard_map/ppermute | solution.py:964
  272.3 2.6 collective-permute-start.44
  277.2 6.4 %leave_mixed.1 = (bf16[960,256]{1,0:T(8,128)(2,1)}, bf16[2,4,256,640]{3,2,1,0:T(8,128)(2,1)S(1)}, bf16[2,4,256,640]{3,2,1,0:T(8,128)(2,1)S(1)}) custom-call(s32[3]{0:T(128)S(1)} %pad_add_fusion.1.place_ref.refs_0_, f32[256,960]{1,0:T(8,128)S(1)} %copy-done.6, f32[256,960]{1,0:T(8,128)S(1)} %get-tuple-element.230.refs_2_, ...), custom_call_target="tpu_custom_call" | custom-call | flops 2453667840 | bytes 6635520 | tf_op jit(solution)/shard_map/leave_mixed/pallas_call | solution.py:795
  283.7 2.6 collective-permute-done.43
  289.9 2.9 collective-permute-done.46
  297.4 7.3 %collective-permute-done.48 = bf16[2,240,640]{2,1,0:T(8,128)(2,1)S(1)} collective-permute-done((bf16[2,240,640]{2,1,0:T(8,128)(2,1)S(1)}, bf16[2,240,640]{2,1,0:T(8,128)(2,1)S(1)}, u32[]{:S(2)}, u32[]{:S(2)}) %collective-permute-start.48) | collective-permute-done | bytes 614432 | tf_op jit(solution)/shard_map/ppermute | solution.py:964
  305.8 5.7 %collective-permute-done.49 = bf16[240,640]{1,0:T(8,128)(2,1)S(1)} collective-permute-done((bf16[240,640]{1,0:T(8,128)(2,1)S(1)}, bf16[240,640]{1,0:T(8,128)(2,1)S(1)}, u32[]{:S(2)}, u32[]{:S(2)}) %collective-permute-start.49) | collective-permute-done | bytes 307232 | tf_op jit(solution)/shard_map/ppermute | solution.py:964
  311.6 7.1 %collective-permute-done.50 = bf16[2,256,640]{2,1,0:T(8,128)(2,1)S(1)} collective-permute-done((bf16[2,256,640]{2,1,0:T(8,128)(2,1)S(1)}, bf16[2,256,640]{2,1,0:T(8,128)(2,1)S(1)}, u32[]{:S(2)}, u32[]{:S(2)}) %collective-permute-start.50) | collective-permute-done | bytes 655392 | tf_op jit(solution)/shard_map/ppermute | solution.py:964
  323.1 10.2 %collective-permute-done.52 = bf16[240,640]{1,0:T(8,128)(2,1)S(1)} collective-permute-done((bf16[240,640]{1,0:T(8,128)(2,1)S(1)}, bf16[240,640]{1,0:T(8,128)(2,1)S(1)}, u32[]{:S(2)}, u32[]{:S(2)}) %collective-permute-start.52) | collective-permute-done | bytes 307232 | tf_op jit(solution)/shard_map/ppermute | solution.py:964
  333.5 9.6 %collective-permute-done.53.p1_ref = bf16[240,640]{1,0:T(8,128)(2,1)S(1)} collective-permute-done((bf16[240,640]{1,0:T(8,128)(2,1)S(1)}, bf16[240,640]{1,0:T(8,128)(2,1)S(1)}, u32[]{:S(2)}, u32[]{:S(2)}) %collective-permute-start.53) | collective-permute-done | bytes 307232 | tf_op jit(solution)/shard_map/ppermute | solution.py:964
  345.5 4.2 %collective-permute-done.55.p1_ref = bf16[240,640]{1,0:T(8,128)(2,1)S(1)} collective-permute-done((bf16[240,640]{1,0:T(8,128)(2,1)S(1)}, bf16[240,640]{1,0:T(8,128)(2,1)S(1)}, u32[]{:S(2)}, u32[]{:S(2)}) %collective-permute-start.55) | collective-permute-done | bytes 307232 | tf_op jit(solution)/shard_map/ppermute | solution.py:964
  350.3 3.3 collective-permute-done.58.p3_ref
  353.6 2.5 finish.3
  356.3 3.1 collective-permute-start.63
  361.6 9.0 %collective-permute-done.60.p1_ref = bf16[240,640]{1,0:T(8,128)(2,1)S(1)} collective-permute-done((bf16[240,640]{1,0:T(8,128)(2,1)S(1)}, bf16[240,640]{1,0:T(8,128)(2,1)S(1)}, u32[]{:S(2)}, u32[]{:S(2)}) %collective-permute-start.60) | collective-permute-done | bytes 307232 | tf_op jit(solution)/shard_map/ppermute | solution.py:964
  371.9 2.5 finish.4
  378.5 6.8 %collective-permute-done.64.p2_ref = bf16[240,640]{1,0:T(8,128)(2,1)S(1)} collective-permute-done((bf16[240,640]{1,0:T(8,128)(2,1)S(1)}, bf16[240,640]{1,0:T(8,128)(2,1)S(1)}, u32[]{:S(2)}, u32[]{:S(2)}) %collective-permute-start.64) | collective-permute-done | bytes 307232 | tf_op jit(solution)/shard_map/ppermute | solution.py:964
  385.3 6.6 %collective-permute-done.65.p3_ref = bf16[240,640]{1,0:T(8,128)(2,1)S(1)} collective-permute-done((bf16[240,640]{1,0:T(8,128)(2,1)S(1)}, bf16[240,640]{1,0:T(8,128)(2,1)S(1)}, u32[]{:S(2)}, u32[]{:S(2)}) %collective-permute-start.65) | collective-permute-done | bytes 307232 | tf_op jit(solution)/shard_map/ppermute | solution.py:964
  396.7 4.8 %collective-permute-done.68.p3_ref = bf16[256,640]{1,0:T(8,128)(2,1)S(1)} collective-permute-done((bf16[256,640]{1,0:T(8,128)(2,1)S(1)}, bf16[256,640]{1,0:T(8,128)(2,1)S(1)}, u32[]{:S(2)}, u32[]{:S(2)}) %collective-permute-start.68) | collective-permute-done | bytes 327712 | tf_op jit(solution)/shard_map/ppermute | solution.py:964
  401.5 2.6 finish_mixed.1
  (264 shorter events, 87.1 us)
Async XLA Ops:
  9.2 49.4 %collective-permute-start.3 = (bf16[240,2560]{1,0:T(8,128)(2,1)}, bf16[240,2560]{1,0:T(8,128)(2,1)}, u32[]{:S(2)}, u32[]{:S(2)}) collective-permute-start(bf16[240,2560]{1,0:T(8,128)(2,1)} %get-tuple-element.157.refs_0_), channel_id=1, source_target_pairs={{0,1},{1,0},{2,3},{3,2},{4,5},{5,4},{6,7},{7,6},{8,9},{9,8},{10,11... | collective-permute-start | bytes 3686408 | tf_op jit(solution)/shard_map/ppermute | solution.py:964
  11.8 16.4 %collective-permute-start.4 = (bf16[240,1280]{1,0:T(8,128)(2,1)}, bf16[240,1280]{1,0:T(8,128)(2,1)S(1)}, u32[]{:S(2)}, u32[]{:S(2)}) collective-permute-start(bf16[240,1280]{1,0:T(8,128)(2,1)} %get-tuple-element.151), channel_id=1, source_target_pairs={{0,2},{1,3},{2,0},{3,1},{4,6},{5,7},{6,4},{7,5},{8,10},{9,11},{10,... | collective-permute-start | bytes 1843208 | tf_op jit(solution)/shard_map/ppermute | solution.py:964
  28.2 15.3 %collective-permute-start.5 = (bf16[240,1280]{1,0:T(8,128)(2,1)S(1)}, bf16[240,1280]{1,0:T(8,128)(2,1)S(1)}, u32[]{:S(2)}, u32[]{:S(2)}) collective-permute-start(bf16[240,1280]{1,0:T(8,128)(2,1)S(1)} %collective-permute-done.4.refs_2_), channel_id=1, source_target_pairs={{0,4},{4,0},{8,12},{12,8},{16,20},{20,16},{24,28},{28,24},{1,5},{5... | collective-permute-start | bytes 1843208 | tf_op jit(solution)/shard_map/ppermute | solution.py:964
  29.9 17.0 %collective-permute-start.13 = (bf16[240,1280]{1,0:T(8,128)(2,1)}, bf16[240,1280]{1,0:T(8,128)(2,1)S(1)}, u32[]{:S(2)}, u32[]{:S(2)}) collective-permute-start(bf16[240,1280]{1,0:T(8,128)(2,1)} %get-tuple-element.152), channel_id=1, source_target_pairs={{0,2},{1,3},{2,0},{3,1},{4,6},{5,7},{6,4},{7,5},{8,10},{9,11},{10,... | collective-permute-start | bytes 1843208 | tf_op jit(solution)/shard_map/ppermute | solution.py:964
  31.4 26.7 %collective-permute-start.12 = (bf16[240,1280]{1,0:T(8,128)(2,1)}, bf16[240,1280]{1,0:T(8,128)(2,1)S(1)}, u32[]{:S(2)}, u32[]{:S(2)}) collective-permute-start(bf16[240,1280]{1,0:T(8,128)(2,1)} %get-tuple-element.153), channel_id=1, source_target_pairs={{0,2},{1,3},{2,0},{3,1},{4,6},{5,7},{6,4},{7,5},{8,10},{9,11},{10,... | collective-permute-start | bytes 1843208 | tf_op jit(solution)/shard_map/ppermute | solution.py:964
  32.0 28.2 %collective-permute-start.6 = (bf16[240,1280]{1,0:T(8,128)(2,1)S(1)}, bf16[240,1280]{1,0:T(8,128)(2,1)S(1)}, u32[]{:S(2)}, u32[]{:S(2)}) collective-permute-start(bf16[240,1280]{1,0:T(8,128)(2,1)S(1)} %collective-permute-done.4.refs_2_), channel_id=1, source_target_pairs={{0,1},{1,0},{2,3},{3,2},{4,5},{5,4},{6,7},{7,6},{8,9},{9,8},{10,11... | collective-permute-start | bytes 1843208 | tf_op jit(solution)/shard_map/ppermute | solution.py:964
  43.5 16.6 %collective-permute-start.7 = (bf16[240,1280]{1,0:T(8,128)(2,1)S(1)}, bf16[240,1280]{1,0:T(8,128)(2,1)S(1)}, u32[]{:S(2)}, u32[]{:S(2)}) collective-permute-start(bf16[240,1280]{1,0:T(8,128)(2,1)S(1)} %collective-permute-done.5.refs_3_), channel_id=1, source_target_pairs={{0,1},{1,0},{2,3},{3,2},{4,5},{5,4},{6,7},{7,6},{8,9},{9,8},{10,11... | collective-permute-start | bytes 1843208 | tf_op jit(solution)/shard_map/ppermute | solution.py:964
  46.9 27.1 %collective-permute-start.21 = (bf16[960,640]{1,0:T(8,128)(2,1)}, bf16[960,640]{1,0:T(8,128)(2,1)S(1)}, u32[]{:S(2)}, u32[]{:S(2)}) collective-permute-start(bf16[960,640]{1,0:T(8,128)(2,1)} %bitcast.133), channel_id=1, source_target_pairs={{0,1},{1,0},{2,3},{3,2},{4,5},{5,4},{6,7},{7,6},{8,9},{9,8},{10,11... | collective-permute-start | bytes 3686408 | tf_op jit(solution)/shard_map/ppermute | solution.py:964
  58.1 13.9 %collective-permute-start.14 = (bf16[240,1280]{1,0:T(8,128)(2,1)S(1)}, bf16[240,1280]{1,0:T(8,128)(2,1)S(1)}, u32[]{:S(2)}, u32[]{:S(2)}) collective-permute-start(bf16[240,1280]{1,0:T(8,128)(2,1)S(1)} %collective-permute-done.13.refs_12_), channel_id=1, source_target_pairs={{0,4},{4,0},{8,12},{12,8},{16,20},{20,16},{24,28},{28,24},{1,5},{5... | collective-permute-start | bytes 1843208 | tf_op jit(solution)/shard_map/ppermute | solution.py:964
  58.6 14.0 %collective-permute-start.22 = (bf16[480,640]{1,0:T(8,128)(2,1)}, bf16[480,640]{1,0:T(8,128)(2,1)S(1)}, u32[]{:S(2)}, u32[]{:S(2)}) collective-permute-start(bf16[480,640]{1,0:T(8,128)(2,1)} %slice_select_fusion), channel_id=1, source_target_pairs={{0,2},{1,3},{2,0},{3,1},{4,6},{5,7},{6,4},{7,5},{8,10},{9,11},{10,... | collective-permute-start | bytes 1843208 | tf_op jit(solution)/shard_map/ppermute | solution.py:964
  60.1 15.5 %collective-permute-start.11 = (bf16[240,2560]{1,0:T(8,128)(2,1)S(1)}, bf16[240,2560]{1,0:T(8,128)(2,1)S(1)}, u32[]{:S(2)}, u32[]{:S(2)}) collective-permute-start(bf16[240,2560]{1,0:T(8,128)(2,1)S(1)} %copy-done.3), channel_id=1, source_target_pairs={{0,1},{1,0},{2,3},{3,2},{4,5},{5,4},{6,7},{7,6},{8,9},{9,8},{10,11... | collective-permute-start | bytes 3686408 | tf_op jit(solution)/shard_map/ppermute | solution.py:964
  60.2 17.0 %collective-permute-start.17 = (bf16[240,2560]{1,0:T(8,128)(2,1)S(1)}, bf16[240,2560]{1,0:T(8,128)(2,1)S(1)}, u32[]{:S(2)}, u32[]{:S(2)}) collective-permute-start(bf16[240,2560]{1,0:T(8,128)(2,1)S(1)} %copy-done.4), channel_id=1, source_target_pairs={{0,1},{1,0},{2,3},{3,2},{4,5},{5,4},{6,7},{7,6},{8,9},{9,8},{10,11... | collective-permute-start | bytes 3686408 | tf_op jit(solution)/shard_map/ppermute | solution.py:964
  72.7 12.9 %collective-permute-start.23 = (bf16[480,640]{1,0:T(8,128)(2,1)S(1)}, bf16[480,640]{1,0:T(8,128)(2,1)S(1)}, u32[]{:S(2)}, u32[]{:S(2)}) collective-permute-start(bf16[480,640]{1,0:T(8,128)(2,1)S(1)} %collective-permute-done.22.refs_24_), channel_id=1, source_target_pairs={{0,4},{4,0},{8,12},{12,8},{16,20},{20,16},{24,28},{28,24},{1,5},{5... | collective-permute-start | bytes 1843208 | tf_op jit(solution)/shard_map/ppermute | solution.py:964
  74.0 12.2 %collective-permute-start.15 = (bf16[240,1280]{1,0:T(8,128)(2,1)S(1)}, bf16[240,1280]{1,0:T(8,128)(2,1)S(1)}, u32[]{:S(2)}, u32[]{:S(2)}) collective-permute-start(bf16[240,1280]{1,0:T(8,128)(2,1)S(1)} %collective-permute-done.13.refs_12_), channel_id=1, source_target_pairs={{0,1},{1,0},{2,3},{3,2},{4,5},{5,4},{6,7},{7,6},{8,9},{9,8},{10,11... | collective-permute-start | bytes 1843208 | tf_op jit(solution)/shard_map/ppermute | solution.py:964
  74.0 16.3 %collective-permute-start.18 = (bf16[240,1280]{1,0:T(8,128)(2,1)S(1)}, bf16[240,1280]{1,0:T(8,128)(2,1)S(1)}, u32[]{:S(2)}, u32[]{:S(2)}) collective-permute-start(bf16[240,1280]{1,0:T(8,128)(2,1)S(1)} %collective-permute-done.12.refs_18_), channel_id=1, source_target_pairs={{0,8},{4,12},{8,0},{12,4},{16,24},{20,28},{24,16},{28,20},{1,9},{5... | collective-permute-start | bytes 1843208 | tf_op jit(solution)/shard_map/ppermute | solution.py:964
  75.6 9.9 %collective-permute-start.9 = (bf16[640,256]{1,0:T(8,128)(2,1)S(1)}, bf16[640,256]{1,0:T(8,128)(2,1)S(1)}, u32[]{:S(2)}, u32[]{:S(2)}) collective-permute-start(bf16[640,256]{1,0:T(8,128)(2,1)S(1)} %get-tuple-element.162.refs_4_.kv0_ref), channel_id=1, source_target_pairs={{0,2},{1,3},{2,0},{3,1},{4,6},{5,7},{6,4},{7,5},{8,10},{9,11},{10,... | collective-permute-start | bytes 983048 | tf_op jit(solution)/shard_map/ppermute | solution.py:964
  110.0 12.3 %collective-permute-start.27 = (bf16[640,256]{1,0:T(8,128)(2,1)S(1)}, bf16[640,256]{1,0:T(8,128)(2,1)S(1)}, u32[]{:S(2)}, u32[]{:S(2)}) collective-permute-start(bf16[640,256]{1,0:T(8,128)(2,1)S(1)} %get-tuple-element.172.refs_4_.kv0_ref), channel_id=1, source_target_pairs={{0,2},{1,3},{2,0},{3,1},{4,6},{5,7},{6,4},{7,5},{8,10},{9,11},{10,... | collective-permute-start | bytes 983048 | tf_op jit(solution)/shard_map/ppermute | solution.py:964
  159.5 15.0 %collective-permute-start.30 = (bf16[640,256]{1,0:T(8,128)(2,1)}, bf16[640,256]{1,0:T(8,128)(2,1)}, u32[]{:S(2)}, u32[]{:S(2)}) collective-permute-start(bf16[640,256]{1,0:T(8,128)(2,1)} %get-tuple-element.295), channel_id=1, source_target_pairs={{0,2},{1,3},{2,0},{3,1},{4,6},{5,7},{6,4},{7,5},{8,10},{9,11},{10,... | collective-permute-start | bytes 983048 | tf_op jit(solution)/shard_map/ppermute | solution.py:964
  193.2 19.2 %collective-permute-start.32 = (bf16[2,240,640]{2,1,0:T(8,128)(2,1)S(1)}, bf16[2,240,640]{2,1,0:T(8,128)(2,1)S(1)}, u32[]{:S(2)}, u32[]{:S(2)}) collective-permute-start(bf16[2,240,640]{2,1,0:T(8,128)(2,1)S(1)} %get-tuple-element.292), channel_id=1, source_target_pairs={{0,2},{1,3},{2,0},{3,1},{4,6},{5,7},{6,4},{7,5},{8,10},{9,11},{10,... | collective-permute-start | bytes 1843208 | tf_op jit(solution)/shard_map/ppermute | solution.py:964
  195.0 27.4 %collective-permute-start.33 = (bf16[2,240,640]{2,1,0:T(8,128)(2,1)S(1)}, bf16[2,240,640]{2,1,0:T(8,128)(2,1)S(1)}, u32[]{:S(2)}, u32[]{:S(2)}) collective-permute-start(bf16[2,240,640]{2,1,0:T(8,128)(2,1)S(1)} %get-tuple-element.291), channel_id=1, source_target_pairs={{0,2},{1,3},{2,0},{3,1},{4,6},{5,7},{6,4},{7,5},{8,10},{9,11},{10,... | collective-permute-start | bytes 1843208 | tf_op jit(solution)/shard_map/ppermute | solution.py:964
  227.7 16.0 %collective-permute-start.35 = (bf16[2,240,640]{2,1,0:T(8,128)(2,1)S(1)}, bf16[2,240,640]{2,1,0:T(8,128)(2,1)S(1)}, u32[]{:S(2)}, u32[]{:S(2)}) collective-permute-start(bf16[2,240,640]{2,1,0:T(8,128)(2,1)S(1)} %get-tuple-element.290), channel_id=1, source_target_pairs={{0,2},{1,3},{2,0},{3,1},{4,6},{5,7},{6,4},{7,5},{8,10},{9,11},{10,... | collective-permute-start | bytes 1843208 | tf_op jit(solution)/shard_map/ppermute | solution.py:964
  229.4 15.6 %collective-permute-start.36 = (bf16[2,240,640]{2,1,0:T(8,128)(2,1)S(1)}, bf16[2,240,640]{2,1,0:T(8,128)(2,1)S(1)}, u32[]{:S(2)}, u32[]{:S(2)}) collective-permute-start(bf16[2,240,640]{2,1,0:T(8,128)(2,1)S(1)} %fusion.3), channel_id=1, source_target_pairs={{0,4},{4,0},{8,12},{12,8},{16,20},{20,16},{24,28},{28,24},{1,5},{5... | collective-permute-start | bytes 1843208 | tf_op jit(solution)/shard_map/ppermute | solution.py:964
  229.4 41.8 %collective-permute-start.42 = (bf16[2,4,240,640]{3,2,1,0:T(8,128)(2,1)S(1)}, bf16[2,4,240,640]{3,2,1,0:T(8,128)(2,1)S(1)}, u32[]{:S(2)}, u32[]{:S(2)}) collective-permute-start(bf16[2,4,240,640]{3,2,1,0:T(8,128)(2,1)S(1)} %get-tuple-element.228), channel_id=1, source_target_pairs={{0,1},{1,0},{2,3},{3,2},{4,5},{5,4},{6,7},{7,6},{8,9},{9,8},{10,11... | collective-permute-start | bytes 7372808 | tf_op jit(solution)/shard_map/ppermute | solution.py:964
  245.3 16.3 %collective-permute-start.38 = (bf16[2,240,640]{2,1,0:T(8,128)(2,1)S(1)}, bf16[2,240,640]{2,1,0:T(8,128)(2,1)S(1)}, u32[]{:S(2)}, u32[]{:S(2)}) collective-permute-start(bf16[2,240,640]{2,1,0:T(8,128)(2,1)S(1)} %get-tuple-element.289), channel_id=1, source_target_pairs={{0,2},{1,3},{2,0},{3,1},{4,6},{5,7},{6,4},{7,5},{8,10},{9,11},{10,... | collective-permute-start | bytes 1843208 | tf_op jit(solution)/shard_map/ppermute | solution.py:964
  245.9 15.6 %collective-permute-start.39 = (bf16[240,640]{1,0:T(8,128)(2,1)S(1)}, bf16[240,640]{1,0:T(8,128)(2,1)S(1)}, u32[]{:S(2)}, u32[]{:S(2)}) collective-permute-start(bf16[240,640]{1,0:T(8,128)(2,1)S(1)} %fusion.21), channel_id=1, source_target_pairs={{0,8},{4,12},{8,0},{12,4},{16,24},{20,28},{24,16},{28,20},{1,9},{5... | collective-permute-start | bytes 921608 | tf_op jit(solution)/shard_map/ppermute | solution.py:964
  246.1 25.1 %collective-permute-start.41 = (bf16[2,240,640]{2,1,0:T(8,128)(2,1)S(1)}, bf16[2,240,640]{2,1,0:T(8,128)(2,1)S(1)}, u32[]{:S(2)}, u32[]{:S(2)}) collective-permute-start(bf16[2,240,640]{2,1,0:T(8,128)(2,1)S(1)} %fusion.2), channel_id=1, source_target_pairs={{0,4},{4,0},{8,12},{12,8},{16,20},{20,16},{24,28},{28,24},{1,5},{5... | collective-permute-start | bytes 1843208 | tf_op jit(solution)/shard_map/ppermute | solution.py:964
  271.7 14.6 %collective-permute-start.43 = (bf16[2,240,640]{2,1,0:T(8,128)(2,1)S(1)}, bf16[2,240,640]{2,1,0:T(8,128)(2,1)S(1)}, u32[]{:S(2)}, u32[]{:S(2)}) collective-permute-start(bf16[2,240,640]{2,1,0:T(8,128)(2,1)S(1)} %get-tuple-element.288), channel_id=1, source_target_pairs={{0,2},{1,3},{2,0},{3,1},{4,6},{5,7},{6,4},{7,5},{8,10},{9,11},{10,... | collective-permute-start | bytes 1843208 | tf_op jit(solution)/shard_map/ppermute | solution.py:964
  272.3 15.2 %collective-permute-start.44 = (bf16[240,640]{1,0:T(8,128)(2,1)S(1)}, bf16[240,640]{1,0:T(8,128)(2,1)S(1)}, u32[]{:S(2)}, u32[]{:S(2)}) collective-permute-start(bf16[240,640]{1,0:T(8,128)(2,1)S(1)} %fusion.23), channel_id=1, source_target_pairs={{0,16},{4,20},{8,24},{12,28},{16,0},{20,4},{24,8},{28,12},{1,17},{... | collective-permute-start | bytes 921608 | tf_op jit(solution)/shard_map/ppermute | solution.py:964
  274.9 12.8 %collective-permute-start.45 = (bf16[240,640]{1,0:T(8,128)(2,1)S(1)}, bf16[240,640]{1,0:T(8,128)(2,1)S(1)}, u32[]{:S(2)}, u32[]{:S(2)}) collective-permute-start(bf16[240,640]{1,0:T(8,128)(2,1)S(1)} %fusion.20), channel_id=1, source_target_pairs={{0,8},{4,12},{8,0},{12,4},{16,24},{20,28},{24,16},{28,20},{1,9},{5... | collective-permute-start | bytes 921608 | tf_op jit(solution)/shard_map/ppermute | solution.py:964
  287.9 16.7 %collective-permute-start.48 = (bf16[2,240,640]{2,1,0:T(8,128)(2,1)S(1)}, bf16[2,240,640]{2,1,0:T(8,128)(2,1)S(1)}, u32[]{:S(2)}, u32[]{:S(2)}) collective-permute-start(bf16[2,240,640]{2,1,0:T(8,128)(2,1)S(1)} %get-tuple-element.287), channel_id=1, source_target_pairs={{0,2},{1,3},{2,0},{3,1},{4,6},{5,7},{6,4},{7,5},{8,10},{9,11},{10,... | collective-permute-start | bytes 1843208 | tf_op jit(solution)/shard_map/ppermute | solution.py:964
  289.7 15.9 %collective-permute-start.47 = (bf16[2,240,640]{2,1,0:T(8,128)(2,1)S(1)}, bf16[2,240,640]{2,1,0:T(8,128)(2,1)S(1)}, u32[]{:S(2)}, u32[]{:S(2)}) collective-permute-start(bf16[2,240,640]{2,1,0:T(8,128)(2,1)S(1)} %fusion.1), channel_id=1, source_target_pairs={{0,4},{4,0},{8,12},{12,8},{16,20},{20,16},{24,28},{28,24},{1,5},{5... | collective-permute-start | bytes 1843208 | tf_op jit(solution)/shard_map/ppermute | solution.py:964
  293.2 25.5 %collective-permute-start.50 = (bf16[2,256,640]{2,1,0:T(8,128)(2,1)S(1)}, bf16[2,256,640]{2,1,0:T(8,128)(2,1)S(1)}, u32[]{:S(2)}, u32[]{:S(2)}) collective-permute-start(bf16[2,256,640]{2,1,0:T(8,128)(2,1)S(1)} %get-tuple-element.286), channel_id=1, source_target_pairs={{0,2},{1,3},{2,0},{3,1},{4,6},{5,7},{6,4},{7,5},{8,10},{9,11},{10,... | collective-permute-start | bytes 1966088 | tf_op jit(solution)/shard_map/ppermute | solution.py:964
  295.0 16.5 %collective-permute-start.49 = (bf16[240,640]{1,0:T(8,128)(2,1)S(1)}, bf16[240,640]{1,0:T(8,128)(2,1)S(1)}, u32[]{:S(2)}, u32[]{:S(2)}) collective-permute-start(bf16[240,640]{1,0:T(8,128)(2,1)S(1)} %fusion.19), channel_id=1, source_target_pairs={{0,16},{4,20},{8,24},{12,28},{16,0},{20,4},{24,8},{28,12},{1,17},{... | collective-permute-start | bytes 921608 | tf_op jit(solution)/shard_map/ppermute | solution.py:964
  295.9 47.2 %collective-permute-start.54 = (bf16[2,256,640]{2,1,0:T(8,128)(2,1)S(1)}, bf16[2,256,640]{2,1,0:T(8,128)(2,1)S(1)}, u32[]{:S(2)}, u32[]{:S(2)}) collective-permute-start(bf16[2,256,640]{2,1,0:T(8,128)(2,1)S(1)} %get-tuple-element.285), channel_id=1, source_target_pairs={{0,2},{1,3},{2,0},{3,1},{4,6},{5,7},{6,4},{7,5},{8,10},{9,11},{10,... | collective-permute-start | bytes 1966088 | tf_op jit(solution)/shard_map/ppermute | solution.py:964
  319.0 24.2 %collective-permute-start.51 = (bf16[2,256,640]{2,1,0:T(8,128)(2,1)S(1)}, bf16[2,256,640]{2,1,0:T(8,128)(2,1)S(1)}, u32[]{:S(2)}, u32[]{:S(2)}) collective-permute-start(bf16[2,256,640]{2,1,0:T(8,128)(2,1)S(1)} %fusion), channel_id=1, source_target_pairs={{0,4},{4,0},{8,12},{12,8},{16,20},{20,16},{24,28},{28,24},{1,5},{5... | collective-permute-start | bytes 1966088 | tf_op jit(solution)/shard_map/ppermute | solution.py:964
  319.7 13.5 %collective-permute-start.52 = (bf16[240,640]{1,0:T(8,128)(2,1)S(1)}, bf16[240,640]{1,0:T(8,128)(2,1)S(1)}, u32[]{:S(2)}, u32[]{:S(2)}) collective-permute-start(bf16[240,640]{1,0:T(8,128)(2,1)S(1)} %fusion.17), channel_id=1, source_target_pairs={{0,8},{4,12},{8,0},{12,4},{16,24},{20,28},{24,16},{28,20},{1,9},{5... | collective-permute-start | bytes 921608 | tf_op jit(solution)/shard_map/ppermute | solution.py:964
  321.1 22.1 %collective-permute-start.53 = (bf16[240,640]{1,0:T(8,128)(2,1)S(1)}, bf16[240,640]{1,0:T(8,128)(2,1)S(1)}, u32[]{:S(2)}, u32[]{:S(2)}) collective-permute-start(bf16[240,640]{1,0:T(8,128)(2,1)S(1)} %add_convert_fusion.15.p0_ref), channel_id=1, source_target_pairs={{0,8},{4,12},{8,0},{12,4},{16,24},{20,28},{24,16},{28,20},{1,9},{5... | collective-permute-start | bytes 921608 | tf_op jit(solution)/shard_map/ppermute | solution.py:964
  321.8 27.9 %collective-permute-start.55 = (bf16[240,640]{1,0:T(8,128)(2,1)S(1)}, bf16[240,640]{1,0:T(8,128)(2,1)S(1)}, u32[]{:S(2)}, u32[]{:S(2)}) collective-permute-start(bf16[240,640]{1,0:T(8,128)(2,1)S(1)} %add_convert_fusion.14.p0_ref), channel_id=1, source_target_pairs={{0,8},{4,12},{8,0},{12,4},{16,24},{20,28},{24,16},{28,20},{1,9},{5... | collective-permute-start | bytes 921608 | tf_op jit(solution)/shard_map/ppermute | solution.py:964
  333.5 16.3 %collective-permute-start.56 = (bf16[240,640]{1,0:T(8,128)(2,1)S(1)}, bf16[240,640]{1,0:T(8,128)(2,1)S(1)}, u32[]{:S(2)}, u32[]{:S(2)}) collective-permute-start(bf16[240,640]{1,0:T(8,128)(2,1)S(1)} %fusion.16), channel_id=1, source_target_pairs={{0,16},{4,20},{8,24},{12,28},{16,0},{20,4},{24,8},{28,12},{1,17},{... | collective-permute-start | bytes 921608 | tf_op jit(solution)/shard_map/ppermute | solution.py:964
  343.3 12.8 %collective-permute-start.59 = (bf16[256,640]{1,0:T(8,128)(2,1)S(1)}, bf16[256,640]{1,0:T(8,128)(2,1)S(1)}, u32[]{:S(2)}, u32[]{:S(2)}) collective-permute-start(bf16[256,640]{1,0:T(8,128)(2,1)S(1)} %fusion.6), channel_id=1, source_target_pairs={{0,8},{4,12},{8,0},{12,4},{16,24},{20,28},{24,16},{28,20},{1,9},{5... | collective-permute-start | bytes 983048 | tf_op jit(solution)/shard_map/ppermute | solution.py:964
  356.3 18.0 %collective-permute-start.63 = (bf16[256,640]{1,0:T(8,128)(2,1)S(1)}, bf16[256,640]{1,0:T(8,128)(2,1)S(1)}, u32[]{:S(2)}, u32[]{:S(2)}) collective-permute-start(bf16[256,640]{1,0:T(8,128)(2,1)S(1)} %fusion.8), channel_id=1, source_target_pairs={{0,16},{4,20},{8,24},{12,28},{16,0},{20,4},{24,8},{28,12},{1,17},{... | collective-permute-start | bytes 983048 | tf_op jit(solution)/shard_map/ppermute | solution.py:964
  359.5 11.1 %collective-permute-start.60 = (bf16[240,640]{1,0:T(8,128)(2,1)S(1)}, bf16[240,640]{1,0:T(8,128)(2,1)S(1)}, u32[]{:S(2)}, u32[]{:S(2)}) collective-permute-start(bf16[240,640]{1,0:T(8,128)(2,1)S(1)} %add_convert_fusion.13.p0_ref), channel_id=1, source_target_pairs={{0,8},{4,12},{8,0},{12,4},{16,24},{20,28},{24,16},{28,20},{1,9},{5... | collective-permute-start | bytes 921608 | tf_op jit(solution)/shard_map/ppermute | solution.py:964
  359.6 11.0 %collective-permute-start.61 = (bf16[240,640]{1,0:T(8,128)(2,1)S(1)}, bf16[240,640]{1,0:T(8,128)(2,1)S(1)}, u32[]{:S(2)}, u32[]{:S(2)}) collective-permute-start(bf16[240,640]{1,0:T(8,128)(2,1)S(1)} %add_convert_fusion.14.p0_ref), channel_id=1, source_target_pairs={{0,4},{4,0},{8,12},{12,8},{16,20},{20,16},{24,28},{28,24},{1,5},{5... | collective-permute-start | bytes 921608 | tf_op jit(solution)/shard_map/ppermute | solution.py:964
  361.1 10.8 %collective-permute-start.62 = (bf16[240,640]{1,0:T(8,128)(2,1)S(1)}, bf16[240,640]{1,0:T(8,128)(2,1)S(1)}, u32[]{:S(2)}, u32[]{:S(2)}) collective-permute-start(bf16[240,640]{1,0:T(8,128)(2,1)S(1)} %collective-permute-done.55.p1_ref), channel_id=1, source_target_pairs={{0,4},{4,0},{8,12},{12,8},{16,20},{20,16},{24,28},{28,24},{1,5},{5... | collective-permute-start | bytes 921608 | tf_op jit(solution)/shard_map/ppermute | solution.py:964
  374.5 19.9 %collective-permute-start.66 = (bf16[256,640]{1,0:T(8,128)(2,1)S(1)}, bf16[256,640]{1,0:T(8,128)(2,1)S(1)}, u32[]{:S(2)}, u32[]{:S(2)}) collective-permute-start(bf16[256,640]{1,0:T(8,128)(2,1)S(1)} %add_convert_fusion.8.p0_ref), channel_id=1, source_target_pairs={{0,8},{4,12},{8,0},{12,4},{16,24},{20,28},{24,16},{28,20},{1,9},{5... | collective-permute-start | bytes 983048 | tf_op jit(solution)/shard_map/ppermute | solution.py:964
  375.1 10.2 %collective-permute-start.64 = (bf16[240,640]{1,0:T(8,128)(2,1)S(1)}, bf16[240,640]{1,0:T(8,128)(2,1)S(1)}, u32[]{:S(2)}, u32[]{:S(2)}) collective-permute-start(bf16[240,640]{1,0:T(8,128)(2,1)S(1)} %add_convert_fusion.13.p0_ref), channel_id=1, source_target_pairs={{0,4},{4,0},{8,12},{12,8},{16,20},{20,16},{24,28},{28,24},{1,5},{5... | collective-permute-start | bytes 921608 | tf_op jit(solution)/shard_map/ppermute | solution.py:964
  376.4 15.4 %collective-permute-start.65 = (bf16[240,640]{1,0:T(8,128)(2,1)S(1)}, bf16[240,640]{1,0:T(8,128)(2,1)S(1)}, u32[]{:S(2)}, u32[]{:S(2)}) collective-permute-start(bf16[240,640]{1,0:T(8,128)(2,1)S(1)} %collective-permute-done.60.p1_ref), channel_id=1, source_target_pairs={{0,4},{4,0},{8,12},{12,8},{16,20},{20,16},{24,28},{28,24},{1,5},{5... | collective-permute-start | bytes 921608 | tf_op jit(solution)/shard_map/ppermute | solution.py:964
  377.1 19.5 %collective-permute-start.67 = (bf16[256,640]{1,0:T(8,128)(2,1)S(1)}, bf16[256,640]{1,0:T(8,128)(2,1)S(1)}, u32[]{:S(2)}, u32[]{:S(2)}) collective-permute-start(bf16[256,640]{1,0:T(8,128)(2,1)S(1)} %add_convert_fusion.8.p0_ref), channel_id=1, source_target_pairs={{0,4},{4,0},{8,12},{12,8},{16,20},{20,16},{24,28},{28,24},{1,5},{5... | collective-permute-start | bytes 983048 | tf_op jit(solution)/shard_map/ppermute | solution.py:964
  (78 other events, 888.4 us)

commit v5 on v4

--- a/solution.py
+++ b/solution.py
@@ -841,7 +841,7 @@
         compiler_params=params(),
         cost_estimate=cost(4 * rows * width * ffn, width * ffn * 2),
         name="down_grad",
-    )(place, g2, g, inner2, inner)
+    )(place, in_hbm(g2), g, in_hbm(inner2), in_hbm(inner))
 
 
 def attention_grad_kernel(
@@ -1188,9 +1188,10 @@
         place, order.tie(grad), middle, gating, upward, ffn_gain, nf2, nf, dgu2, weights
     )
     order.done(d_middle)
-    down.first(both=True)
+    down.first()
     gate = Reduction(order, *rest[:2])
     gate.chip()
+    down.rest()
     up = Reduction(order, *rest[2:])
     dq, *dkvs = attend_back(visible, order.tie(q), d_out, att_t, lse, cos, sin, kvs)
     order.done(dq)
@@ -1229,20 +1230,20 @@
     mixed = Reduction(order, *mixed)
     mixed.chip()
     up.second()
+    down.back_again()
+    down_grad = order.done(finish(place, down.end(), True))
+    mixed.first()
     gate.back()
-    mixed.first()
     up.third()
-    down.back_again()
     mixed.rest()
     mixed.second()
     gate.back_again()
+    gate_grad = order.done(finish(place, gate.end(), False))
     up.back()
-    down_grad = order.done(finish(place, down.end(), True))
     mixed.third()
     up.back_again()
-    gate_grad = order.done(finish(place, gate.end(), False))
+    up_grad = order.done(finish(place, up.end(), False))
     mixed.back()
-    up_grad = order.done(finish(place, up.end(), False))
     mixed.back_again()
     query_grad, key_grad, value_grad, output_grad, gain_grads = finish_mixed(
         place, mixed.end(), width, key_width

time: 412 us -> 398 us (0.966)
  starting transfers between devices: 72.4 us -> 56 us
  Pallas kernels: 96.8 us -> 109 us
  waiting for transfers between devices: 207 us -> 201 us
    ppermute x69, starting transfers between devices: 72.4 us -> 56 us  [flip(): lax.ppermute(value, axis_name, [(i, i ^ distance) for i in range(size)])]
    ppermute x69, waiting for transfers between devices: 207 us -> 201 us  [flip(): lax.ppermute(value, axis_name, [(i, i ^ distance) for i in range(size)])]
    pallas_call x2, Pallas kernels: 13.4 us -> 18.8 us  [attend_back(): pl.pallas_call(attend_back_kernel, out_shape=(shape((width, rows), bf16),...]
    pallas_call x2, Pallas kernels: 25.7 us -> 30.6 us  [forward_block(): pl.pallas_call(functools.partial(forward_kernel, plans, counts), out_shap...]
    unnamed x114 -> x108, local copies, waits for them, and re-layouts: 12.1 us -> 9.77 us
  transfers between devices with their start and end apart: 69 -> 69, of which waited for: 38 -> 36; matrix products, arithmetic and copies ran while one was open for 2% -> 2% of each run, Pallas kernels for 11% -> 12%
where the time goes in v5:
time: 398 us; the launch traced here: 392 us
  waiting for transfers between devices  201 us (51%)
  Pallas kernels  109 us (27%)
  starting transfers between devices  56 us (14%)
  local copies, waits for them, and re-layouts  14.2 us (4%)
  other arithmetic  9.41 us (2%)
    ppermute x69, waiting for transfers between devices, flip(): lax.ppermute(value, axis_name, [(i, i ^ distance) for i in range(size)])  201 us
    ppermute x69, starting transfers between devices, flip(): lax.ppermute(value, axis_name, [(i, i ^ distance) for i in range(size)])  56 us
    pallas_call x2, Pallas kernels, forward_block(): pl.pallas_call(functools.partial(forward_kernel, plans, counts), out_shap...  30.6 us
    pallas_call x2, Pallas kernels, attend_back(): pl.pallas_call(attend_back_kernel, out_shape=(shape((width, rows), bf16),...  18.8 us
    pallas_call x1, Pallas kernels, feed_back_gate(): pl.pallas_call(feed_back_gate_kernel, out_shape=(shape((rows, width), f32...  17 us
    unnamed x108, local copies, waits for them, and re-layouts  9.77 us
    pallas_call x1, Pallas kernels, feed_back(): pl.pallas_call(feed_back_kernel, out_shape=(shape((rows, width), bf16), s...  9.03 us
  transfers between devices with their start and end apart: 69, of which 36 were waited for; matrix products, arithmetic and copies ran while one was open for 2% of the time, Pallas kernels for 12%

profile of v5, /device:TPU:0, one launch (start us, length us, event | category | flops | bytes accessed | tf_op | source)
XLA Modules:
  0.0 391.7 jit_solution(4843853518315412990)
XLA Ops:
  2.5 2.6 collective-permute-start.1
  5.2 4.0 %pack.1 = (bf16[240,2560]{1,0:T(8,128)(2,1)}, bf16[240,1280]{1,0:T(8,128)(2,1)}, bf16[240,1280]{1,0:T(8,128)(2,1)}, bf16[240,1280]{1,0:T(8,128)(2,1)}) custom-call(s32[3]{0:T(128)S(1)} %pad_add_fusion.bits_ref.index_ref.refs_1_, bf16[240,960]{1,0:T(8,128)(2,1)} %query_hbm.1, bf16[320,240]{1,0:T(8,128)(2,1)} %bitcast.136, bf16[320,240]{1,0:T(8,128)(2,1)} %bitcast.137, ...), custom_call_target="tpu_custom_call" | custom-call | bytes 4915200 | tf_op jit(solution)/shard_map/pack/pallas_call | solution.py:128
  9.5 2.3 slice_select_fusion
  18.5 9.7 %collective-permute-done.4.refs_2_ = bf16[240,1280]{1,0:T(8,128)(2,1)S(1)} collective-permute-done((bf16[240,1280]{1,0:T(8,128)(2,1)}, bf16[240,1280]{1,0:T(8,128)(2,1)S(1)}, u32[]{:S(2)}, u32[]{:S(2)}) %collective-permute-start.4) | collective-permute-done | bytes 614432 | tf_op jit(solution)/shard_map/ppermute | solution.py:964
  32.0 11.5 %collective-permute-done.5.refs_3_ = bf16[240,1280]{1,0:T(8,128)(2,1)S(1)} collective-permute-done((bf16[240,1280]{1,0:T(8,128)(2,1)S(1)}, bf16[240,1280]{1,0:T(8,128)(2,1)S(1)}, u32[]{:S(2)}, u32[]{:S(2)}) %collective-permute-start.5) | collective-permute-done | bytes 614432 | tf_op jit(solution)/shard_map/ppermute | solution.py:964
  43.5 3.4 collective-permute-done.13.refs_12_
  46.9 11.2 %collective-permute-done.12.refs_18_ = bf16[240,1280]{1,0:T(8,128)(2,1)S(1)} collective-permute-done((bf16[240,1280]{1,0:T(8,128)(2,1)}, bf16[240,1280]{1,0:T(8,128)(2,1)S(1)}, u32[]{:S(2)}, u32[]{:S(2)}) %collective-permute-start.12) | collective-permute-done | bytes 614432 | tf_op jit(solution)/shard_map/ppermute | solution.py:964
  63.0 3.4 enter_first.1
  67.2 4.8 %collective-permute-done.14.refs_13_ = bf16[240,1280]{1,0:T(8,128)(2,1)S(1)} collective-permute-done((bf16[240,1280]{1,0:T(8,128)(2,1)S(1)}, bf16[240,1280]{1,0:T(8,128)(2,1)S(1)}, u32[]{:S(2)}, u32[]{:S(2)}) %collective-permute-start.14) | collective-permute-done | bytes 614432 | tf_op jit(solution)/shard_map/ppermute | solution.py:964
  77.1 8.4 %collective-permute-done.23.refs_25_ = bf16[480,640]{1,0:T(8,128)(2,1)S(1)} collective-permute-done((bf16[480,640]{1,0:T(8,128)(2,1)S(1)}, bf16[480,640]{1,0:T(8,128)(2,1)S(1)}, u32[]{:S(2)}, u32[]{:S(2)}) %collective-permute-start.23) | collective-permute-done | bytes 614432 | tf_op jit(solution)/shard_map/ppermute | solution.py:964
  86.6 3.6 collective-permute-done.18.refs_19_
  92.8 16.5 %forward_first.1 = (f32[256,960]{1,0:T(8,128)S(1)}, bf16[256,960]{1,0:T(8,128)(2,1)S(1)}, bf16[960,256]{1,0:T(8,128)(2,1)S(1)}, f32[5,768]{1,0:T(8,128)S(1)}, f3...) custom-call(s32[4]{0:T(128)S(1)} %and_convert_fusion.refs_0_.visible, ...), custom_call_target="tpu_custom_call" | custom-call | flops 5033164800 | bytes 19988480 | tf_op jit(solution)/shard_map/forward_first/pallas_call | solution.py:416
  112.6 2.7 collective-permute-start.26
  115.2 6.2 %collective-permute-done.27.refs_6_.kv2_ref = bf16[640,256]{1,0:T(8,128)(2,1)S(1)} collective-permute-done((bf16[640,256]{1,0:T(8,128)(2,1)S(1)}, bf16[640,256]{1,0:T(8,128)(2,1)S(1)}, u32[]{:S(2)}, u32[]{:S(2)}) %collective-permute-start.27) | collective-permute-done | bytes 327712 | tf_op jit(solution)/shard_map/ppermute | solution.py:964
  124.2 14.1 %forward_last.1 = (bf16[960,256]{1,0:T(8,128)(2,1)}, bf16[256,960]{1,0:T(8,128)(2,1)S(1)}, bf16[960,256]{1,0:T(8,128)(2,1)S(1)}, f32[5,768]{1,0:T(8,128)S(1)}, f...) custom-call(s32[4]{0:T(128)S(1)} %and_convert_fusion.refs_0_.visible, ...), custom_call_target="tpu_custom_call" | custom-call | flops 5033164800 | bytes 19988480 | tf_op jit(solution)/shard_map/forward_last/pallas_call | solution.py:416
  138.4 9.0 %feed_back.1 = (bf16[256,960]{1,0:T(8,128)(2,1)S(1)}, bf16[256,5120]{1,0:T(8,128)(2,1)S(1)}, f32[256,960]{1,0:T(8,128)S(1)}, bf16[256,1024]{1,0:T(8,128)(2,1)S(1...) custom-call(bf16[960,256]{1,0:T(8,128)(2,1)S(1)} %bitcast.131, f32[256,960]{1,0:T(8,128)S(1)} %get-tuple-element.176.middle_ref, ...), custom_call_target="tpu_custom_call" | custom-call | flops 5033164800 | bytes 19988480 | tf_op jit(solution)/shard_map/feed_back/pallas_call | solution.py:515
  147.5 9.3 %attend_back.2 = (bf16[960,256]{1,0:T(8,128)(2,1)S(1)}, bf16[2,640,256]{2,1,0:T(8,128)(2,1)S(1)}, bf16[2,640,256]{2,1,0:T(8,128)(2,1)S(1)}) custom-call(s32[4]{0:T(128)S(1)} %and_convert_fusion.refs_0_.visible_ref, bf16[960,256]{1,0:T(8,128)(2,1)S(1)} %get-tuple-element.171.refs_3_.q_ref, bf16[960,256]{1,0:T(8,128)(2,1)S(1)} %get-tuple-element.181.do_ref, ...), custom_call_target="tpu_custom_call" | custom-call | flops 5033164800 | bytes 4915200 | tf_op jit(solution)/shard_map/attend_back/pallas_call | solution.py:624
  156.9 5.6 %collective-permute-start.29 = (bf16[2,640,256]{2,1,0:T(8,128)(2,1)S(1)}, bf16[2,640,256]{2,1,0:T(8,128)(2,1)S(1)}, u32[]{:S(2)}, u32[]{:S(2)}) collective-permute-start(bf16[2,640,256]{2,1,0:T(8,128)(2,1)S(1)} %get-tuple-element.186), channel_id=1, source_target_pairs={{0,1},{1,0},{2,3},{3,2},{4,5},{5,4},{6,7},{7,6},{8,9},{9,8},{10,11... | collective-permute-start | bytes 1966088 | tf_op jit(solution)/shard_map/ppermute | solution.py:964
  165.3 10.2 %collective-permute-done.30.got_ref = bf16[640,256]{1,0:T(8,128)(2,1)} collective-permute-done((bf16[640,256]{1,0:T(8,128)(2,1)}, bf16[640,256]{1,0:T(8,128)(2,1)}, u32[]{:S(2)}, u32[]{:S(2)}) %collective-permute-start.30) | collective-permute-done | bytes 327712 | tf_op jit(solution)/shard_map/ppermute | solution.py:964
  175.5 2.4 copy-done.1
  178.9 2.6 leave.1
  181.6 5.3 %down_grad.1 = (bf16[2,4,240,640]{3,2,1,0:T(8,128)(2,1)S(1)}, bf16[2,4,240,640]{3,2,1,0:T(8,128)(2,1)S(1)}) custom-call(s32[3]{0:T(128)S(1)} %pad_add_fusion.1.place_ref.refs_0_, bf16[256,960]{1,0:T(8,128)(2,1)} %copy-done.42, f32[256,960]{1,0:T(8,128)S(1)} %get-tuple-element.194.g_ref.refs_1_, bf16[256,2560]{1,0:T(8,128)(2,1)} %copy-done.35, ...), custom_call_target="tpu_custom_call" | custom-call | flops 2516582400 | bytes 4915200 | tf_op jit(solution)/shard_map/down_grad/pallas_call | solution.py:835
  187.0 4.7 %collective-permute-done.31 = bf16[2,4,240,640]{3,2,1,0:T(8,128)(2,1)S(1)} collective-permute-done((bf16[2,4,240,640]{3,2,1,0:T(8,128)(2,1)S(1)}, bf16[2,4,240,640]{3,2,1,0:T(8,128)(2,1)S(1)}, u32[]{:S(2)}, u32[]{:S(2)}) %collective-permute-start.31) | collective-permute-done | bytes 2457632 | tf_op jit(solution)/shard_map/ppermute | solution.py:964
  193.7 17.0 %feed_back_gate.1 = (f32[256,960]{1,0:T(8,128)S(1)}, bf16[256,1024]{1,0:T(8,128)(2,1)S(1)}, bf16[960,256]{1,0:T(8,128)(2,1)S(1)}, f32[1,960]{1,0:T(1,128)S(1)}, ...) custom-call(s32[3]{0:T(128)S(1)} %pad_add_fusion.1.place_ref.refs_0_, ...), custom_call_target="tpu_custom_call" | custom-call | flops 10066329600 | bytes 19988480 | tf_op jit(solution)/shard_map/feed_back_gate/pallas_call | solution.py:746
  211.6 4.1 %collective-permute-done.33 = bf16[2,4,240,640]{3,2,1,0:T(8,128)(2,1)S(1)} collective-permute-done((bf16[2,4,240,640]{3,2,1,0:T(8,128)(2,1)S(1)}, bf16[2,4,240,640]{3,2,1,0:T(8,128)(2,1)S(1)}, u32[]{:S(2)}, u32[]{:S(2)}) %collective-permute-start.33) | collective-permute-done | bytes 2457632 | tf_op jit(solution)/shard_map/ppermute | solution.py:964
  216.7 11.2 %collective-permute-done.34 = bf16[2,240,640]{2,1,0:T(8,128)(2,1)S(1)} collective-permute-done((bf16[2,240,640]{2,1,0:T(8,128)(2,1)S(1)}, bf16[2,240,640]{2,1,0:T(8,128)(2,1)S(1)}, u32[]{:S(2)}, u32[]{:S(2)}) %collective-permute-start.34) | collective-permute-done | bytes 614432 | tf_op jit(solution)/shard_map/ppermute | solution.py:964
  227.9 9.4 %attend_back.3 = (bf16[960,256]{1,0:T(8,128)(2,1)S(1)}, bf16[2,640,256]{2,1,0:T(8,128)(2,1)S(1)}, bf16[2,640,256]{2,1,0:T(8,128)(2,1)S(1)}) custom-call(s32[4]{0:T(128)S(1)} %and_convert_fusion.refs_0_.visible_ref, bf16[960,256]{1,0:T(8,128)(2,1)S(1)} %copy-done.19, bf16[960,256]{1,0:T(8,128)(2,1)S(1)} %get-tuple-element.210.do_ref, ...), custom_call_target="tpu_custom_call" | custom-call | flops 5033164800 | bytes 4915200 | tf_op jit(solution)/shard_map/attend_back/pallas_call | solution.py:624
  237.4 3.1 collective-permute-done.35
  244.1 13.2 %collective-permute-done.38 = bf16[2,240,640]{2,1,0:T(8,128)(2,1)S(1)} collective-permute-done((bf16[2,240,640]{2,1,0:T(8,128)(2,1)S(1)}, bf16[2,240,640]{2,1,0:T(8,128)(2,1)S(1)}, u32[]{:S(2)}, u32[]{:S(2)}) %collective-permute-start.38) | collective-permute-done | bytes 614432 | tf_op jit(solution)/shard_map/ppermute | solution.py:964
  258.1 8.7 %collective-permute-done.40.refs_5_ = bf16[640,256]{1,0:T(8,128)(2,1)S(1)} collective-permute-done((bf16[640,256]{1,0:T(8,128)(2,1)S(1)}, bf16[640,256]{1,0:T(8,128)(2,1)S(1)}, u32[]{:S(2)}, u32[]{:S(2)}) %collective-permute-start.40) | collective-permute-done | bytes 327712 | tf_op jit(solution)/shard_map/ppermute | solution.py:964
  271.6 6.5 %leave_mixed.1 = (bf16[960,256]{1,0:T(8,128)(2,1)}, bf16[2,4,256,640]{3,2,1,0:T(8,128)(2,1)S(1)}, bf16[2,4,256,640]{3,2,1,0:T(8,128)(2,1)S(1)}) custom-call(s32[3]{0:T(128)S(1)} %pad_add_fusion.1.place_ref.refs_0_, f32[256,960]{1,0:T(8,128)S(1)} %copy-done.6, f32[256,960]{1,0:T(8,128)S(1)} %get-tuple-element.230.refs_2_, ...), custom_call_target="tpu_custom_call" | custom-call | flops 2453667840 | bytes 6635520 | tf_op jit(solution)/shard_map/leave_mixed/pallas_call | solution.py:795
  278.1 3.9 collective-permute-done.43
  285.8 2.9 collective-permute-done.46
  291.5 9.1 %collective-permute-done.48 = bf16[2,240,640]{2,1,0:T(8,128)(2,1)S(1)} collective-permute-done((bf16[2,240,640]{2,1,0:T(8,128)(2,1)S(1)}, bf16[2,240,640]{2,1,0:T(8,128)(2,1)S(1)}, u32[]{:S(2)}, u32[]{:S(2)}) %collective-permute-start.48) | collective-permute-done | bytes 614432 | tf_op jit(solution)/shard_map/ppermute | solution.py:964
  304.8 4.3 %collective-permute-done.50.p2_ref = bf16[240,640]{1,0:T(8,128)(2,1)S(1)} collective-permute-done((bf16[240,640]{1,0:T(8,128)(2,1)S(1)}, bf16[240,640]{1,0:T(8,128)(2,1)S(1)}, u32[]{:S(2)}, u32[]{:S(2)}) %collective-permute-start.50) | collective-permute-done | bytes 307232 | tf_op jit(solution)/shard_map/ppermute | solution.py:964
  309.1 5.8 %collective-permute-done.51.p3_ref = bf16[240,640]{1,0:T(8,128)(2,1)S(1)} collective-permute-done((bf16[240,640]{1,0:T(8,128)(2,1)S(1)}, bf16[240,640]{1,0:T(8,128)(2,1)S(1)}, u32[]{:S(2)}, u32[]{:S(2)}) %collective-permute-start.51) | collective-permute-done | bytes 307232 | tf_op jit(solution)/shard_map/ppermute | solution.py:964
  314.9 2.5 finish.3
  322.0 6.3 %collective-permute-done.55 = bf16[240,640]{1,0:T(8,128)(2,1)S(1)} collective-permute-done((bf16[240,640]{1,0:T(8,128)(2,1)S(1)}, bf16[240,640]{1,0:T(8,128)(2,1)S(1)}, u32[]{:S(2)}, u32[]{:S(2)}) %collective-permute-start.55) | collective-permute-done | bytes 307232 | tf_op jit(solution)/shard_map/ppermute | solution.py:964
  328.4 7.0 %collective-permute-done.53 = bf16[2,256,640]{2,1,0:T(8,128)(2,1)S(1)} collective-permute-done((bf16[2,256,640]{2,1,0:T(8,128)(2,1)S(1)}, bf16[2,256,640]{2,1,0:T(8,128)(2,1)S(1)}, u32[]{:S(2)}, u32[]{:S(2)}) %collective-permute-start.53) | collective-permute-done | bytes 655392 | tf_op jit(solution)/shard_map/ppermute | solution.py:964
  337.9 4.1 %collective-permute-done.58.p2_ref = bf16[240,640]{1,0:T(8,128)(2,1)S(1)} collective-permute-done((bf16[240,640]{1,0:T(8,128)(2,1)S(1)}, bf16[240,640]{1,0:T(8,128)(2,1)S(1)}, u32[]{:S(2)}, u32[]{:S(2)}) %collective-permute-start.58) | collective-permute-done | bytes 307232 | tf_op jit(solution)/shard_map/ppermute | solution.py:964
  342.0 4.9 %collective-permute-done.59.p3_ref = bf16[240,640]{1,0:T(8,128)(2,1)S(1)} collective-permute-done((bf16[240,640]{1,0:T(8,128)(2,1)S(1)}, bf16[240,640]{1,0:T(8,128)(2,1)S(1)}, u32[]{:S(2)}, u32[]{:S(2)}) %collective-permute-start.59) | collective-permute-done | bytes 307232 | tf_op jit(solution)/shard_map/ppermute | solution.py:964
  346.9 2.5 finish.4
  353.1 9.8 %collective-permute-done.62.p1_ref = bf16[240,640]{1,0:T(8,128)(2,1)S(1)} collective-permute-done((bf16[240,640]{1,0:T(8,128)(2,1)S(1)}, bf16[240,640]{1,0:T(8,128)(2,1)S(1)}, u32[]{:S(2)}, u32[]{:S(2)}) %collective-permute-start.62) | collective-permute-done | bytes 307232 | tf_op jit(solution)/shard_map/ppermute | solution.py:964
  363.9 7.0 %collective-permute-done.64.p3_ref = bf16[240,640]{1,0:T(8,128)(2,1)S(1)} collective-permute-done((bf16[240,640]{1,0:T(8,128)(2,1)S(1)}, bf16[240,640]{1,0:T(8,128)(2,1)S(1)}, u32[]{:S(2)}, u32[]{:S(2)}) %collective-permute-start.64) | collective-permute-done | bytes 307232 | tf_op jit(solution)/shard_map/ppermute | solution.py:964
  370.8 2.5 finish.5
  374.5 6.4 %collective-permute-done.66.p1_ref = bf16[256,640]{1,0:T(8,128)(2,1)S(1)} collective-permute-done((bf16[256,640]{1,0:T(8,128)(2,1)S(1)}, bf16[256,640]{1,0:T(8,128)(2,1)S(1)}, u32[]{:S(2)}, u32[]{:S(2)}) %collective-permute-start.66) | collective-permute-done | bytes 327712 | tf_op jit(solution)/shard_map/ppermute | solution.py:964
  381.9 6.1 %collective-permute-done.68.p3_ref = bf16[256,640]{1,0:T(8,128)(2,1)S(1)} collective-permute-done((bf16[256,640]{1,0:T(8,128)(2,1)S(1)}, bf16[256,640]{1,0:T(8,128)(2,1)S(1)}, u32[]{:S(2)}, u32[]{:S(2)}) %collective-permute-start.68) | collective-permute-done | bytes 327712 | tf_op jit(solution)/shard_map/ppermute | solution.py:964
  388.0 2.6 finish_mixed.1
  (258 shorter events, 74.5 us)
Async XLA Ops:
  2.0 9.8 %collective-permute-start = (bf16[2,240]{1,0:T(2,128)(2,1)S(1)}, bf16[2,240]{1,0:T(2,128)(2,1)S(1)}, u32[]{:S(2)}, u32[]{:S(2)}) collective-permute-start(bf16[2,240]{1,0:T(2,128)(2,1)S(1)} %pad_maximum_fusion), channel_id=1, source_target_pairs={{0,1},{1,0},{2,3},{3,2},{4,5},{5,4},{6,7},{7,6},{8,9},{9,8},{10,11... | collective-permute-start | bytes 2888 | tf_op jit(solution)/shard_map/ppermute | solution.py:964
  9.2 49.4 %collective-permute-start.3 = (bf16[240,2560]{1,0:T(8,128)(2,1)}, bf16[240,2560]{1,0:T(8,128)(2,1)}, u32[]{:S(2)}, u32[]{:S(2)}) collective-permute-start(bf16[240,2560]{1,0:T(8,128)(2,1)} %get-tuple-element.157.refs_0_), channel_id=1, source_target_pairs={{0,1},{1,0},{2,3},{3,2},{4,5},{5,4},{6,7},{7,6},{8,9},{9,8},{10,11... | collective-permute-start | bytes 3686408 | tf_op jit(solution)/shard_map/ppermute | solution.py:964
  11.8 16.4 %collective-permute-start.4 = (bf16[240,1280]{1,0:T(8,128)(2,1)}, bf16[240,1280]{1,0:T(8,128)(2,1)S(1)}, u32[]{:S(2)}, u32[]{:S(2)}) collective-permute-start(bf16[240,1280]{1,0:T(8,128)(2,1)} %get-tuple-element.151), channel_id=1, source_target_pairs={{0,2},{1,3},{2,0},{3,1},{4,6},{5,7},{6,4},{7,5},{8,10},{9,11},{10,... | collective-permute-start | bytes 1843208 | tf_op jit(solution)/shard_map/ppermute | solution.py:964
  28.2 15.3 %collective-permute-start.5 = (bf16[240,1280]{1,0:T(8,128)(2,1)S(1)}, bf16[240,1280]{1,0:T(8,128)(2,1)S(1)}, u32[]{:S(2)}, u32[]{:S(2)}) collective-permute-start(bf16[240,1280]{1,0:T(8,128)(2,1)S(1)} %collective-permute-done.4.refs_2_), channel_id=1, source_target_pairs={{0,4},{4,0},{8,12},{12,8},{16,20},{20,16},{24,28},{28,24},{1,5},{5... | collective-permute-start | bytes 1843208 | tf_op jit(solution)/shard_map/ppermute | solution.py:964
  29.9 17.0 %collective-permute-start.13 = (bf16[240,1280]{1,0:T(8,128)(2,1)}, bf16[240,1280]{1,0:T(8,128)(2,1)S(1)}, u32[]{:S(2)}, u32[]{:S(2)}) collective-permute-start(bf16[240,1280]{1,0:T(8,128)(2,1)} %get-tuple-element.152), channel_id=1, source_target_pairs={{0,2},{1,3},{2,0},{3,1},{4,6},{5,7},{6,4},{7,5},{8,10},{9,11},{10,... | collective-permute-start | bytes 1843208 | tf_op jit(solution)/shard_map/ppermute | solution.py:964
  31.4 26.7 %collective-permute-start.12 = (bf16[240,1280]{1,0:T(8,128)(2,1)}, bf16[240,1280]{1,0:T(8,128)(2,1)S(1)}, u32[]{:S(2)}, u32[]{:S(2)}) collective-permute-start(bf16[240,1280]{1,0:T(8,128)(2,1)} %get-tuple-element.153), channel_id=1, source_target_pairs={{0,2},{1,3},{2,0},{3,1},{4,6},{5,7},{6,4},{7,5},{8,10},{9,11},{10,... | collective-permute-start | bytes 1843208 | tf_op jit(solution)/shard_map/ppermute | solution.py:964
  32.0 28.2 %collective-permute-start.6 = (bf16[240,1280]{1,0:T(8,128)(2,1)S(1)}, bf16[240,1280]{1,0:T(8,128)(2,1)S(1)}, u32[]{:S(2)}, u32[]{:S(2)}) collective-permute-start(bf16[240,1280]{1,0:T(8,128)(2,1)S(1)} %collective-permute-done.4.refs_2_), channel_id=1, source_target_pairs={{0,1},{1,0},{2,3},{3,2},{4,5},{5,4},{6,7},{7,6},{8,9},{9,8},{10,11... | collective-permute-start | bytes 1843208 | tf_op jit(solution)/shard_map/ppermute | solution.py:964
  43.5 16.6 %collective-permute-start.7 = (bf16[240,1280]{1,0:T(8,128)(2,1)S(1)}, bf16[240,1280]{1,0:T(8,128)(2,1)S(1)}, u32[]{:S(2)}, u32[]{:S(2)}) collective-permute-start(bf16[240,1280]{1,0:T(8,128)(2,1)S(1)} %collective-permute-done.5.refs_3_), channel_id=1, source_target_pairs={{0,1},{1,0},{2,3},{3,2},{4,5},{5,4},{6,7},{7,6},{8,9},{9,8},{10,11... | collective-permute-start | bytes 1843208 | tf_op jit(solution)/shard_map/ppermute | solution.py:964
  46.9 27.1 %collective-permute-start.21 = (bf16[960,640]{1,0:T(8,128)(2,1)}, bf16[960,640]{1,0:T(8,128)(2,1)S(1)}, u32[]{:S(2)}, u32[]{:S(2)}) collective-permute-start(bf16[960,640]{1,0:T(8,128)(2,1)} %bitcast.133), channel_id=1, source_target_pairs={{0,1},{1,0},{2,3},{3,2},{4,5},{5,4},{6,7},{7,6},{8,9},{9,8},{10,11... | collective-permute-start | bytes 3686408 | tf_op jit(solution)/shard_map/ppermute | solution.py:964
  58.1 13.9 %collective-permute-start.14 = (bf16[240,1280]{1,0:T(8,128)(2,1)S(1)}, bf16[240,1280]{1,0:T(8,128)(2,1)S(1)}, u32[]{:S(2)}, u32[]{:S(2)}) collective-permute-start(bf16[240,1280]{1,0:T(8,128)(2,1)S(1)} %collective-permute-done.13.refs_12_), channel_id=1, source_target_pairs={{0,4},{4,0},{8,12},{12,8},{16,20},{20,16},{24,28},{28,24},{1,5},{5... | collective-permute-start | bytes 1843208 | tf_op jit(solution)/shard_map/ppermute | solution.py:964
  58.6 14.0 %collective-permute-start.22 = (bf16[480,640]{1,0:T(8,128)(2,1)}, bf16[480,640]{1,0:T(8,128)(2,1)S(1)}, u32[]{:S(2)}, u32[]{:S(2)}) collective-permute-start(bf16[480,640]{1,0:T(8,128)(2,1)} %slice_select_fusion), channel_id=1, source_target_pairs={{0,2},{1,3},{2,0},{3,1},{4,6},{5,7},{6,4},{7,5},{8,10},{9,11},{10,... | collective-permute-start | bytes 1843208 | tf_op jit(solution)/shard_map/ppermute | solution.py:964
  60.1 15.5 %collective-permute-start.11 = (bf16[240,2560]{1,0:T(8,128)(2,1)S(1)}, bf16[240,2560]{1,0:T(8,128)(2,1)S(1)}, u32[]{:S(2)}, u32[]{:S(2)}) collective-permute-start(bf16[240,2560]{1,0:T(8,128)(2,1)S(1)} %copy-done.3), channel_id=1, source_target_pairs={{0,1},{1,0},{2,3},{3,2},{4,5},{5,4},{6,7},{7,6},{8,9},{9,8},{10,11... | collective-permute-start | bytes 3686408 | tf_op jit(solution)/shard_map/ppermute | solution.py:964
  60.2 17.0 %collective-permute-start.17 = (bf16[240,2560]{1,0:T(8,128)(2,1)S(1)}, bf16[240,2560]{1,0:T(8,128)(2,1)S(1)}, u32[]{:S(2)}, u32[]{:S(2)}) collective-permute-start(bf16[240,2560]{1,0:T(8,128)(2,1)S(1)} %copy-done.4), channel_id=1, source_target_pairs={{0,1},{1,0},{2,3},{3,2},{4,5},{5,4},{6,7},{7,6},{8,9},{9,8},{10,11... | collective-permute-start | bytes 3686408 | tf_op jit(solution)/shard_map/ppermute | solution.py:964
  72.7 12.9 %collective-permute-start.23 = (bf16[480,640]{1,0:T(8,128)(2,1)S(1)}, bf16[480,640]{1,0:T(8,128)(2,1)S(1)}, u32[]{:S(2)}, u32[]{:S(2)}) collective-permute-start(bf16[480,640]{1,0:T(8,128)(2,1)S(1)} %collective-permute-done.22.refs_24_), channel_id=1, source_target_pairs={{0,4},{4,0},{8,12},{12,8},{16,20},{20,16},{24,28},{28,24},{1,5},{5... | collective-permute-start | bytes 1843208 | tf_op jit(solution)/shard_map/ppermute | solution.py:964
  74.0 12.2 %collective-permute-start.15 = (bf16[240,1280]{1,0:T(8,128)(2,1)S(1)}, bf16[240,1280]{1,0:T(8,128)(2,1)S(1)}, u32[]{:S(2)}, u32[]{:S(2)}) collective-permute-start(bf16[240,1280]{1,0:T(8,128)(2,1)S(1)} %collective-permute-done.13.refs_12_), channel_id=1, source_target_pairs={{0,1},{1,0},{2,3},{3,2},{4,5},{5,4},{6,7},{7,6},{8,9},{9,8},{10,11... | collective-permute-start | bytes 1843208 | tf_op jit(solution)/shard_map/ppermute | solution.py:964
  74.0 16.3 %collective-permute-start.18 = (bf16[240,1280]{1,0:T(8,128)(2,1)S(1)}, bf16[240,1280]{1,0:T(8,128)(2,1)S(1)}, u32[]{:S(2)}, u32[]{:S(2)}) collective-permute-start(bf16[240,1280]{1,0:T(8,128)(2,1)S(1)} %collective-permute-done.12.refs_18_), channel_id=1, source_target_pairs={{0,8},{4,12},{8,0},{12,4},{16,24},{20,28},{24,16},{28,20},{1,9},{5... | collective-permute-start | bytes 1843208 | tf_op jit(solution)/shard_map/ppermute | solution.py:964
  75.6 9.9 %collective-permute-start.9 = (bf16[640,256]{1,0:T(8,128)(2,1)S(1)}, bf16[640,256]{1,0:T(8,128)(2,1)S(1)}, u32[]{:S(2)}, u32[]{:S(2)}) collective-permute-start(bf16[640,256]{1,0:T(8,128)(2,1)S(1)} %get-tuple-element.162.refs_4_.kv0_ref), channel_id=1, source_target_pairs={{0,2},{1,3},{2,0},{3,1},{4,6},{5,7},{6,4},{7,5},{8,10},{9,11},{10,... | collective-permute-start | bytes 983048 | tf_op jit(solution)/shard_map/ppermute | solution.py:964
  112.6 10.4 %collective-permute-start.26 = (bf16[640,256]{1,0:T(8,128)(2,1)S(1)}, bf16[640,256]{1,0:T(8,128)(2,1)S(1)}, u32[]{:S(2)}, u32[]{:S(2)}) collective-permute-start(bf16[640,256]{1,0:T(8,128)(2,1)S(1)} %get-tuple-element.172.refs_4_.kv0_ref), channel_id=1, source_target_pairs={{0,1},{1,0},{2,3},{3,2},{4,5},{5,4},{6,7},{7,6},{8,9},{9,8},{10,11... | collective-permute-start | bytes 983048 | tf_op jit(solution)/shard_map/ppermute | solution.py:964
  165.2 10.3 %collective-permute-start.30 = (bf16[640,256]{1,0:T(8,128)(2,1)}, bf16[640,256]{1,0:T(8,128)(2,1)}, u32[]{:S(2)}, u32[]{:S(2)}) collective-permute-start(bf16[640,256]{1,0:T(8,128)(2,1)} %get-tuple-element.295), channel_id=1, source_target_pairs={{0,2},{1,3},{2,0},{3,1},{4,6},{5,7},{6,4},{7,5},{8,10},{9,11},{10,... | collective-permute-start | bytes 983048 | tf_op jit(solution)/shard_map/ppermute | solution.py:964
  192.0 18.7 %collective-permute-start.32 = (bf16[2,240,640]{2,1,0:T(8,128)(2,1)S(1)}, bf16[2,240,640]{2,1,0:T(8,128)(2,1)S(1)}, u32[]{:S(2)}, u32[]{:S(2)}) collective-permute-start(bf16[2,240,640]{2,1,0:T(8,128)(2,1)S(1)} %get-tuple-element.292), channel_id=1, source_target_pairs={{0,2},{1,3},{2,0},{3,1},{4,6},{5,7},{6,4},{7,5},{8,10},{9,11},{10,... | collective-permute-start | bytes 1843208 | tf_op jit(solution)/shard_map/ppermute | solution.py:964
  211.2 16.7 %collective-permute-start.34 = (bf16[2,240,640]{2,1,0:T(8,128)(2,1)S(1)}, bf16[2,240,640]{2,1,0:T(8,128)(2,1)S(1)}, u32[]{:S(2)}, u32[]{:S(2)}) collective-permute-start(bf16[2,240,640]{2,1,0:T(8,128)(2,1)S(1)} %get-tuple-element.291), channel_id=1, source_target_pairs={{0,2},{1,3},{2,0},{3,1},{4,6},{5,7},{6,4},{7,5},{8,10},{9,11},{10,... | collective-permute-start | bytes 1843208 | tf_op jit(solution)/shard_map/ppermute | solution.py:964
  216.1 24.4 %collective-permute-start.35 = (bf16[2,240,640]{2,1,0:T(8,128)(2,1)S(1)}, bf16[2,240,640]{2,1,0:T(8,128)(2,1)S(1)}, u32[]{:S(2)}, u32[]{:S(2)}) collective-permute-start(bf16[2,240,640]{2,1,0:T(8,128)(2,1)S(1)} %get-tuple-element.290), channel_id=1, source_target_pairs={{0,2},{1,3},{2,0},{3,1},{4,6},{5,7},{6,4},{7,5},{8,10},{9,11},{10,... | collective-permute-start | bytes 1843208 | tf_op jit(solution)/shard_map/ppermute | solution.py:964
  216.7 24.1 %collective-permute-start.36 = (bf16[2,240,640]{2,1,0:T(8,128)(2,1)S(1)}, bf16[2,240,640]{2,1,0:T(8,128)(2,1)S(1)}, u32[]{:S(2)}, u32[]{:S(2)}) collective-permute-start(bf16[2,240,640]{2,1,0:T(8,128)(2,1)S(1)} %fusion.3), channel_id=1, source_target_pairs={{0,4},{4,0},{8,12},{12,8},{16,20},{20,16},{24,28},{28,24},{1,5},{5... | collective-permute-start | bytes 1843208 | tf_op jit(solution)/shard_map/ppermute | solution.py:964
  227.9 39.1 %collective-permute-start.42 = (bf16[2,4,240,640]{3,2,1,0:T(8,128)(2,1)S(1)}, bf16[2,4,240,640]{3,2,1,0:T(8,128)(2,1)S(1)}, u32[]{:S(2)}, u32[]{:S(2)}) collective-permute-start(bf16[2,4,240,640]{3,2,1,0:T(8,128)(2,1)S(1)} %get-tuple-element.228), channel_id=1, source_target_pairs={{0,1},{1,0},{2,3},{3,2},{4,5},{5,4},{6,7},{7,6},{8,9},{9,8},{10,11... | collective-permute-start | bytes 7372808 | tf_op jit(solution)/shard_map/ppermute | solution.py:964
  241.1 16.2 %collective-permute-start.38 = (bf16[2,240,640]{2,1,0:T(8,128)(2,1)S(1)}, bf16[2,240,640]{2,1,0:T(8,128)(2,1)S(1)}, u32[]{:S(2)}, u32[]{:S(2)}) collective-permute-start(bf16[2,240,640]{2,1,0:T(8,128)(2,1)S(1)} %get-tuple-element.289), channel_id=1, source_target_pairs={{0,2},{1,3},{2,0},{3,1},{4,6},{5,7},{6,4},{7,5},{8,10},{9,11},{10,... | collective-permute-start | bytes 1843208 | tf_op jit(solution)/shard_map/ppermute | solution.py:964
  241.6 15.7 %collective-permute-start.39 = (bf16[240,640]{1,0:T(8,128)(2,1)S(1)}, bf16[240,640]{1,0:T(8,128)(2,1)S(1)}, u32[]{:S(2)}, u32[]{:S(2)}) collective-permute-start(bf16[240,640]{1,0:T(8,128)(2,1)S(1)} %fusion.21), channel_id=1, source_target_pairs={{0,8},{4,12},{8,0},{12,4},{16,24},{20,28},{24,16},{28,20},{1,9},{5... | collective-permute-start | bytes 921608 | tf_op jit(solution)/shard_map/ppermute | solution.py:964
  242.3 24.5 %collective-permute-start.41 = (bf16[2,240,640]{2,1,0:T(8,128)(2,1)S(1)}, bf16[2,240,640]{2,1,0:T(8,128)(2,1)S(1)}, u32[]{:S(2)}, u32[]{:S(2)}) collective-permute-start(bf16[2,240,640]{2,1,0:T(8,128)(2,1)S(1)} %fusion.2), channel_id=1, source_target_pairs={{0,4},{4,0},{8,12},{12,8},{16,20},{20,16},{24,28},{28,24},{1,5},{5... | collective-permute-start | bytes 1843208 | tf_op jit(solution)/shard_map/ppermute | solution.py:964
  267.4 14.6 %collective-permute-start.43 = (bf16[2,240,640]{2,1,0:T(8,128)(2,1)S(1)}, bf16[2,240,640]{2,1,0:T(8,128)(2,1)S(1)}, u32[]{:S(2)}, u32[]{:S(2)}) collective-permute-start(bf16[2,240,640]{2,1,0:T(8,128)(2,1)S(1)} %get-tuple-element.288), channel_id=1, source_target_pairs={{0,2},{1,3},{2,0},{3,1},{4,6},{5,7},{6,4},{7,5},{8,10},{9,11},{10,... | collective-permute-start | bytes 1843208 | tf_op jit(solution)/shard_map/ppermute | solution.py:964
  268.0 15.3 %collective-permute-start.44 = (bf16[240,640]{1,0:T(8,128)(2,1)S(1)}, bf16[240,640]{1,0:T(8,128)(2,1)S(1)}, u32[]{:S(2)}, u32[]{:S(2)}) collective-permute-start(bf16[240,640]{1,0:T(8,128)(2,1)S(1)} %fusion.23), channel_id=1, source_target_pairs={{0,16},{4,20},{8,24},{12,28},{16,0},{20,4},{24,8},{28,12},{1,17},{... | collective-permute-start | bytes 921608 | tf_op jit(solution)/shard_map/ppermute | solution.py:964
  270.1 13.5 %collective-permute-start.45 = (bf16[240,640]{1,0:T(8,128)(2,1)S(1)}, bf16[240,640]{1,0:T(8,128)(2,1)S(1)}, u32[]{:S(2)}, u32[]{:S(2)}) collective-permute-start(bf16[240,640]{1,0:T(8,128)(2,1)S(1)} %fusion.20), channel_id=1, source_target_pairs={{0,8},{4,12},{8,0},{12,4},{16,24},{20,28},{24,16},{28,20},{1,9},{5... | collective-permute-start | bytes 921608 | tf_op jit(solution)/shard_map/ppermute | solution.py:964
  283.8 16.7 %collective-permute-start.48 = (bf16[2,240,640]{2,1,0:T(8,128)(2,1)S(1)}, bf16[2,240,640]{2,1,0:T(8,128)(2,1)S(1)}, u32[]{:S(2)}, u32[]{:S(2)}) collective-permute-start(bf16[2,240,640]{2,1,0:T(8,128)(2,1)S(1)} %get-tuple-element.287), channel_id=1, source_target_pairs={{0,2},{1,3},{2,0},{3,1},{4,6},{5,7},{6,4},{7,5},{8,10},{9,11},{10,... | collective-permute-start | bytes 1843208 | tf_op jit(solution)/shard_map/ppermute | solution.py:964
  285.8 16.7 %collective-permute-start.47 = (bf16[2,240,640]{2,1,0:T(8,128)(2,1)S(1)}, bf16[2,240,640]{2,1,0:T(8,128)(2,1)S(1)}, u32[]{:S(2)}, u32[]{:S(2)}) collective-permute-start(bf16[2,240,640]{2,1,0:T(8,128)(2,1)S(1)} %fusion.1), channel_id=1, source_target_pairs={{0,4},{4,0},{8,12},{12,8},{16,20},{20,16},{24,28},{28,24},{1,5},{5... | collective-permute-start | bytes 1843208 | tf_op jit(solution)/shard_map/ppermute | solution.py:964
  289.1 28.3 %collective-permute-start.52 = (bf16[2,256,640]{2,1,0:T(8,128)(2,1)S(1)}, bf16[2,256,640]{2,1,0:T(8,128)(2,1)S(1)}, u32[]{:S(2)}, u32[]{:S(2)}) collective-permute-start(bf16[2,256,640]{2,1,0:T(8,128)(2,1)S(1)} %get-tuple-element.286), channel_id=1, source_target_pairs={{0,2},{1,3},{2,0},{3,1},{4,6},{5,7},{6,4},{7,5},{8,10},{9,11},{10,... | collective-permute-start | bytes 1966088 | tf_op jit(solution)/shard_map/ppermute | solution.py:964
  291.0 11.6 %collective-permute-start.49 = (bf16[240,640]{1,0:T(8,128)(2,1)S(1)}, bf16[240,640]{1,0:T(8,128)(2,1)S(1)}, u32[]{:S(2)}, u32[]{:S(2)}) collective-permute-start(bf16[240,640]{1,0:T(8,128)(2,1)S(1)} %add_convert_fusion.15.p0_ref), channel_id=1, source_target_pairs={{0,8},{4,12},{8,0},{12,4},{16,24},{20,28},{24,16},{28,20},{1,9},{5... | collective-permute-start | bytes 921608 | tf_op jit(solution)/shard_map/ppermute | solution.py:964
  291.5 17.6 %collective-permute-start.50 = (bf16[240,640]{1,0:T(8,128)(2,1)S(1)}, bf16[240,640]{1,0:T(8,128)(2,1)S(1)}, u32[]{:S(2)}, u32[]{:S(2)}) collective-permute-start(bf16[240,640]{1,0:T(8,128)(2,1)S(1)} %add_convert_fusion.15.p0_ref), channel_id=1, source_target_pairs={{0,4},{4,0},{8,12},{12,8},{16,20},{20,16},{24,28},{28,24},{1,5},{5... | collective-permute-start | bytes 921608 | tf_op jit(solution)/shard_map/ppermute | solution.py:964
  302.7 12.2 %collective-permute-start.51 = (bf16[240,640]{1,0:T(8,128)(2,1)S(1)}, bf16[240,640]{1,0:T(8,128)(2,1)S(1)}, u32[]{:S(2)}, u32[]{:S(2)}) collective-permute-start(bf16[240,640]{1,0:T(8,128)(2,1)S(1)} %collective-permute-done.49.p1_ref), channel_id=1, source_target_pairs={{0,4},{4,0},{8,12},{12,8},{16,20},{20,16},{24,28},{28,24},{1,5},{5... | collective-permute-start | bytes 921608 | tf_op jit(solution)/shard_map/ppermute | solution.py:964
  302.8 15.7 %collective-permute-start.54 = (bf16[240,640]{1,0:T(8,128)(2,1)S(1)}, bf16[240,640]{1,0:T(8,128)(2,1)S(1)}, u32[]{:S(2)}, u32[]{:S(2)}) collective-permute-start(bf16[240,640]{1,0:T(8,128)(2,1)S(1)} %fusion.19), channel_id=1, source_target_pairs={{0,16},{4,20},{8,24},{12,28},{16,0},{20,4},{24,8},{28,12},{1,17},{... | collective-permute-start | bytes 921608 | tf_op jit(solution)/shard_map/ppermute | solution.py:964
  303.3 25.1 %collective-permute-start.56 = (bf16[2,256,640]{2,1,0:T(8,128)(2,1)S(1)}, bf16[2,256,640]{2,1,0:T(8,128)(2,1)S(1)}, u32[]{:S(2)}, u32[]{:S(2)}) collective-permute-start(bf16[2,256,640]{2,1,0:T(8,128)(2,1)S(1)} %get-tuple-element.285), channel_id=1, source_target_pairs={{0,2},{1,3},{2,0},{3,1},{4,6},{5,7},{6,4},{7,5},{8,10},{9,11},{10,... | collective-permute-start | bytes 1966088 | tf_op jit(solution)/shard_map/ppermute | solution.py:964
  317.7 17.7 %collective-permute-start.53 = (bf16[2,256,640]{2,1,0:T(8,128)(2,1)S(1)}, bf16[2,256,640]{2,1,0:T(8,128)(2,1)S(1)}, u32[]{:S(2)}, u32[]{:S(2)}) collective-permute-start(bf16[2,256,640]{2,1,0:T(8,128)(2,1)S(1)} %fusion), channel_id=1, source_target_pairs={{0,4},{4,0},{8,12},{12,8},{16,20},{20,16},{24,28},{28,24},{1,5},{5... | collective-permute-start | bytes 1966088 | tf_op jit(solution)/shard_map/ppermute | solution.py:964
  318.0 10.2 %collective-permute-start.55 = (bf16[240,640]{1,0:T(8,128)(2,1)S(1)}, bf16[240,640]{1,0:T(8,128)(2,1)S(1)}, u32[]{:S(2)}, u32[]{:S(2)}) collective-permute-start(bf16[240,640]{1,0:T(8,128)(2,1)S(1)} %fusion.17), channel_id=1, source_target_pairs={{0,8},{4,12},{8,0},{12,4},{16,24},{20,28},{24,16},{28,20},{1,9},{5... | collective-permute-start | bytes 921608 | tf_op jit(solution)/shard_map/ppermute | solution.py:964
  318.5 17.1 %collective-permute-start.57 = (bf16[240,640]{1,0:T(8,128)(2,1)S(1)}, bf16[240,640]{1,0:T(8,128)(2,1)S(1)}, u32[]{:S(2)}, u32[]{:S(2)}) collective-permute-start(bf16[240,640]{1,0:T(8,128)(2,1)S(1)} %add_convert_fusion.14.p0_ref), channel_id=1, source_target_pairs={{0,8},{4,12},{8,0},{12,4},{16,24},{20,28},{24,16},{28,20},{1,9},{5... | collective-permute-start | bytes 921608 | tf_op jit(solution)/shard_map/ppermute | solution.py:964
  320.2 21.8 %collective-permute-start.58 = (bf16[240,640]{1,0:T(8,128)(2,1)S(1)}, bf16[240,640]{1,0:T(8,128)(2,1)S(1)}, u32[]{:S(2)}, u32[]{:S(2)}) collective-permute-start(bf16[240,640]{1,0:T(8,128)(2,1)S(1)} %add_convert_fusion.14.p0_ref), channel_id=1, source_target_pairs={{0,4},{4,0},{8,12},{12,8},{16,20},{20,16},{24,28},{28,24},{1,5},{5... | collective-permute-start | bytes 921608 | tf_op jit(solution)/shard_map/ppermute | solution.py:964
  335.6 11.3 %collective-permute-start.59 = (bf16[240,640]{1,0:T(8,128)(2,1)S(1)}, bf16[240,640]{1,0:T(8,128)(2,1)S(1)}, u32[]{:S(2)}, u32[]{:S(2)}) collective-permute-start(bf16[240,640]{1,0:T(8,128)(2,1)S(1)} %collective-permute-done.57.p1_ref), channel_id=1, source_target_pairs={{0,4},{4,0},{8,12},{12,8},{16,20},{20,16},{24,28},{28,24},{1,5},{5... | collective-permute-start | bytes 921608 | tf_op jit(solution)/shard_map/ppermute | solution.py:964
  335.9 13.7 %collective-permute-start.60 = (bf16[240,640]{1,0:T(8,128)(2,1)S(1)}, bf16[240,640]{1,0:T(8,128)(2,1)S(1)}, u32[]{:S(2)}, u32[]{:S(2)}) collective-permute-start(bf16[240,640]{1,0:T(8,128)(2,1)S(1)} %fusion.16), channel_id=1, source_target_pairs={{0,16},{4,20},{8,24},{12,28},{16,0},{20,4},{24,8},{28,12},{1,17},{... | collective-permute-start | bytes 921608 | tf_op jit(solution)/shard_map/ppermute | solution.py:964
  336.2 13.7 %collective-permute-start.61 = (bf16[256,640]{1,0:T(8,128)(2,1)S(1)}, bf16[256,640]{1,0:T(8,128)(2,1)S(1)}, u32[]{:S(2)}, u32[]{:S(2)}) collective-permute-start(bf16[256,640]{1,0:T(8,128)(2,1)S(1)} %fusion.6), channel_id=1, source_target_pairs={{0,8},{4,12},{8,0},{12,4},{16,24},{20,28},{24,16},{28,20},{1,9},{5... | collective-permute-start | bytes 983048 | tf_op jit(solution)/shard_map/ppermute | solution.py:964
  349.7 13.2 %collective-permute-start.62 = (bf16[240,640]{1,0:T(8,128)(2,1)S(1)}, bf16[240,640]{1,0:T(8,128)(2,1)S(1)}, u32[]{:S(2)}, u32[]{:S(2)}) collective-permute-start(bf16[240,640]{1,0:T(8,128)(2,1)S(1)} %add_convert_fusion.13.p0_ref), channel_id=1, source_target_pairs={{0,8},{4,12},{8,0},{12,4},{16,24},{20,28},{24,16},{28,20},{1,9},{5... | collective-permute-start | bytes 921608 | tf_op jit(solution)/shard_map/ppermute | solution.py:964
  350.2 23.1 %collective-permute-start.65 = (bf16[256,640]{1,0:T(8,128)(2,1)S(1)}, bf16[256,640]{1,0:T(8,128)(2,1)S(1)}, u32[]{:S(2)}, u32[]{:S(2)}) collective-permute-start(bf16[256,640]{1,0:T(8,128)(2,1)S(1)} %fusion.8), channel_id=1, source_target_pairs={{0,16},{4,20},{8,24},{12,28},{16,0},{20,4},{24,8},{28,12},{1,17},{... | collective-permute-start | bytes 983048 | tf_op jit(solution)/shard_map/ppermute | solution.py:964
  351.8 12.1 %collective-permute-start.63 = (bf16[240,640]{1,0:T(8,128)(2,1)S(1)}, bf16[240,640]{1,0:T(8,128)(2,1)S(1)}, u32[]{:S(2)}, u32[]{:S(2)}) collective-permute-start(bf16[240,640]{1,0:T(8,128)(2,1)S(1)} %add_convert_fusion.13.p0_ref), channel_id=1, source_target_pairs={{0,4},{4,0},{8,12},{12,8},{16,20},{20,16},{24,28},{28,24},{1,5},{5... | collective-permute-start | bytes 921608 | tf_op jit(solution)/shard_map/ppermute | solution.py:964
  (75 other events, 969.5 us)

commit v6 on v5

--- a/solution.py
+++ b/solution.py
@@ -1238,9 +1238,9 @@
     mixed.rest()
     mixed.second()
     gate.back_again()
-    gate_grad = order.done(finish(place, gate.end(), False))
     up.back()
     mixed.third()
+    gate_grad = order.done(finish(place, gate.end(), False))
     up.back_again()
     up_grad = order.done(finish(place, up.end(), False))
     mixed.back()

time: 398 us -> 393 us (0.987)
  waiting for transfers between devices: 201 us -> 176 us
  starting transfers between devices: 56 us -> 75.9 us
    ppermute x69, waiting for transfers between devices: 201 us -> 176 us  [flip(): lax.ppermute(value, axis_name, [(i, i ^ distance) for i in range(size)])]
    ppermute x69, starting transfers between devices: 56 us -> 75.9 us  [flip(): lax.ppermute(value, axis_name, [(i, i ^ distance) for i in range(size)])]
  transfers between devices with their start and end apart: 69 -> 69, of which waited for: 36 -> 36; matrix products, arithmetic and copies ran while one was open for 2% -> 3% of each run, Pallas kernels for 12% -> 12%
where the time goes in v6:
time: 393 us; the launch traced here: 386 us
  waiting for transfers between devices  176 us (45%)
  Pallas kernels  109 us (28%)
  starting transfers between devices  75.9 us (19%)
  local copies, waits for them, and re-layouts  12.9 us (3%)
  other arithmetic  9.42 us (2%)
    ppermute x69, waiting for transfers between devices, flip(): lax.ppermute(value, axis_name, [(i, i ^ distance) for i in range(size)])  176 us
    ppermute x69, starting transfers between devices, flip(): lax.ppermute(value, axis_name, [(i, i ^ distance) for i in range(size)])  75.9 us
    pallas_call x2, Pallas kernels, forward_block(): pl.pallas_call(functools.partial(forward_kernel, plans, counts), out_shap...  30.6 us
    pallas_call x2, Pallas kernels, attend_back(): pl.pallas_call(attend_back_kernel, out_shape=(shape((width, rows), bf16),...  18.8 us
    pallas_call x1, Pallas kernels, feed_back_gate(): pl.pallas_call(feed_back_gate_kernel, out_shape=(shape((rows, width), f32...  17 us
    pallas_call x1, Pallas kernels, feed_back(): pl.pallas_call(feed_back_kernel, out_shape=(shape((rows, width), bf16), s...  9.03 us
    unnamed x108, local copies, waits for them, and re-layouts  8.47 us
  transfers between devices with their start and end apart: 69, of which 36 were waited for; matrix products, arithmetic and copies ran while one was open for 3% of the time, Pallas kernels for 12%

profile of v6, /device:TPU:0, one launch (start us, length us, event | category | flops | bytes accessed | tf_op | source)
XLA Modules:
  0.0 385.9 jit_solution(1277759503214207507)
XLA Ops:
  2.5 2.6 collective-permute-start.1
  5.2 4.0 %pack.1 = (bf16[240,2560]{1,0:T(8,128)(2,1)}, bf16[240,1280]{1,0:T(8,128)(2,1)}, bf16[240,1280]{1,0:T(8,128)(2,1)}, bf16[240,1280]{1,0:T(8,128)(2,1)}) custom-call(s32[3]{0:T(128)S(1)} %pad_add_fusion.bits_ref.index_ref.refs_1_, bf16[240,960]{1,0:T(8,128)(2,1)} %query_hbm.1, bf16[320,240]{1,0:T(8,128)(2,1)} %bitcast.136, bf16[320,240]{1,0:T(8,128)(2,1)} %bitcast.137, ...), custom_call_target="tpu_custom_call" | custom-call | bytes 4915200 | tf_op jit(solution)/shard_map/pack/pallas_call | solution.py:128
  9.5 2.3 slice_select_fusion
  18.5 9.7 %collective-permute-done.4.refs_2_ = bf16[240,1280]{1,0:T(8,128)(2,1)S(1)} collective-permute-done((bf16[240,1280]{1,0:T(8,128)(2,1)}, bf16[240,1280]{1,0:T(8,128)(2,1)S(1)}, u32[]{:S(2)}, u32[]{:S(2)}) %collective-permute-start.4) | collective-permute-done | bytes 614432 | tf_op jit(solution)/shard_map/ppermute | solution.py:964
  32.0 11.5 %collective-permute-done.5.refs_3_ = bf16[240,1280]{1,0:T(8,128)(2,1)S(1)} collective-permute-done((bf16[240,1280]{1,0:T(8,128)(2,1)S(1)}, bf16[240,1280]{1,0:T(8,128)(2,1)S(1)}, u32[]{:S(2)}, u32[]{:S(2)}) %collective-permute-start.5) | collective-permute-done | bytes 614432 | tf_op jit(solution)/shard_map/ppermute | solution.py:964
  43.5 3.4 collective-permute-done.13.refs_12_
  46.9 11.2 %collective-permute-done.12.refs_18_ = bf16[240,1280]{1,0:T(8,128)(2,1)S(1)} collective-permute-done((bf16[240,1280]{1,0:T(8,128)(2,1)}, bf16[240,1280]{1,0:T(8,128)(2,1)S(1)}, u32[]{:S(2)}, u32[]{:S(2)}) %collective-permute-start.12) | collective-permute-done | bytes 614432 | tf_op jit(solution)/shard_map/ppermute | solution.py:964
  63.0 3.4 enter_first.1
  67.2 4.8 %collective-permute-done.14.refs_13_ = bf16[240,1280]{1,0:T(8,128)(2,1)S(1)} collective-permute-done((bf16[240,1280]{1,0:T(8,128)(2,1)S(1)}, bf16[240,1280]{1,0:T(8,128)(2,1)S(1)}, u32[]{:S(2)}, u32[]{:S(2)}) %collective-permute-start.14) | collective-permute-done | bytes 614432 | tf_op jit(solution)/shard_map/ppermute | solution.py:964
  77.1 8.4 %collective-permute-done.23.refs_25_ = bf16[480,640]{1,0:T(8,128)(2,1)S(1)} collective-permute-done((bf16[480,640]{1,0:T(8,128)(2,1)S(1)}, bf16[480,640]{1,0:T(8,128)(2,1)S(1)}, u32[]{:S(2)}, u32[]{:S(2)}) %collective-permute-start.23) | collective-permute-done | bytes 614432 | tf_op jit(solution)/shard_map/ppermute | solution.py:964
  86.6 3.6 collective-permute-done.18.refs_19_
  92.8 16.5 %forward_first.1 = (f32[256,960]{1,0:T(8,128)S(1)}, bf16[256,960]{1,0:T(8,128)(2,1)S(1)}, bf16[960,256]{1,0:T(8,128)(2,1)S(1)}, f32[5,768]{1,0:T(8,128)S(1)}, f3...) custom-call(s32[4]{0:T(128)S(1)} %and_convert_fusion.refs_0_.visible, ...), custom_call_target="tpu_custom_call" | custom-call | flops 5033164800 | bytes 19988480 | tf_op jit(solution)/shard_map/forward_first/pallas_call | solution.py:416
  112.6 3.8 collective-permute-start.26
  116.4 5.3 %collective-permute-done.27.refs_6_.kv2_ref = bf16[640,256]{1,0:T(8,128)(2,1)S(1)} collective-permute-done((bf16[640,256]{1,0:T(8,128)(2,1)S(1)}, bf16[640,256]{1,0:T(8,128)(2,1)S(1)}, u32[]{:S(2)}, u32[]{:S(2)}) %collective-permute-start.27) | collective-permute-done | bytes 327712 | tf_op jit(solution)/shard_map/ppermute | solution.py:964
  124.2 14.1 %forward_last.1 = (bf16[960,256]{1,0:T(8,128)(2,1)}, bf16[256,960]{1,0:T(8,128)(2,1)S(1)}, bf16[960,256]{1,0:T(8,128)(2,1)S(1)}, f32[5,768]{1,0:T(8,128)S(1)}, f...) custom-call(s32[4]{0:T(128)S(1)} %and_convert_fusion.refs_0_.visible, ...), custom_call_target="tpu_custom_call" | custom-call | flops 5033164800 | bytes 19988480 | tf_op jit(solution)/shard_map/forward_last/pallas_call | solution.py:416
  138.4 9.0 %feed_back.1 = (bf16[256,960]{1,0:T(8,128)(2,1)S(1)}, bf16[256,5120]{1,0:T(8,128)(2,1)S(1)}, f32[256,960]{1,0:T(8,128)S(1)}, bf16[256,1024]{1,0:T(8,128)(2,1)S(1...) custom-call(bf16[960,256]{1,0:T(8,128)(2,1)S(1)} %bitcast.131, f32[256,960]{1,0:T(8,128)S(1)} %get-tuple-element.176.middle_ref, ...), custom_call_target="tpu_custom_call" | custom-call | flops 5033164800 | bytes 19988480 | tf_op jit(solution)/shard_map/feed_back/pallas_call | solution.py:515
  147.5 9.3 %attend_back.2 = (bf16[960,256]{1,0:T(8,128)(2,1)S(1)}, bf16[2,640,256]{2,1,0:T(8,128)(2,1)S(1)}, bf16[2,640,256]{2,1,0:T(8,128)(2,1)S(1)}) custom-call(s32[4]{0:T(128)S(1)} %and_convert_fusion.refs_0_.visible_ref, bf16[960,256]{1,0:T(8,128)(2,1)S(1)} %get-tuple-element.171.refs_3_.q_ref, bf16[960,256]{1,0:T(8,128)(2,1)S(1)} %get-tuple-element.181.do_ref, ...), custom_call_target="tpu_custom_call" | custom-call | flops 5033164800 | bytes 4915200 | tf_op jit(solution)/shard_map/attend_back/pallas_call | solution.py:624
  160.0 5.2 %collective-permute-start.30 = (bf16[640,256]{1,0:T(8,128)(2,1)}, bf16[640,256]{1,0:T(8,128)(2,1)}, u32[]{:S(2)}, u32[]{:S(2)}) collective-permute-start(bf16[640,256]{1,0:T(8,128)(2,1)} %get-tuple-element.295), channel_id=1, source_target_pairs={{0,2},{1,3},{2,0},{3,1},{4,6},{5,7},{6,4},{7,5},{8,10},{9,11},{10,... | collective-permute-start | bytes 983048 | tf_op jit(solution)/shard_map/ppermute | solution.py:964
  165.3 8.5 %collective-permute-done.30.got_ref = bf16[640,256]{1,0:T(8,128)(2,1)} collective-permute-done((bf16[640,256]{1,0:T(8,128)(2,1)}, bf16[640,256]{1,0:T(8,128)(2,1)}, u32[]{:S(2)}, u32[]{:S(2)}) %collective-permute-start.30) | collective-permute-done | bytes 327712 | tf_op jit(solution)/shard_map/ppermute | solution.py:964
  173.8 2.4 copy-done.1
  177.2 2.6 leave.1
  179.8 5.3 %down_grad.1 = (bf16[2,4,240,640]{3,2,1,0:T(8,128)(2,1)S(1)}, bf16[2,4,240,640]{3,2,1,0:T(8,128)(2,1)S(1)}) custom-call(s32[3]{0:T(128)S(1)} %pad_add_fusion.1.place_ref.refs_0_, bf16[256,960]{1,0:T(8,128)(2,1)} %copy-done.42, f32[256,960]{1,0:T(8,128)S(1)} %get-tuple-element.194.g_ref.refs_1_, bf16[256,2560]{1,0:T(8,128)(2,1)} %copy-done.35, ...), custom_call_target="tpu_custom_call" | custom-call | flops 2516582400 | bytes 4915200 | tf_op jit(solution)/shard_map/down_grad/pallas_call | solution.py:835
  185.3 4.7 %collective-permute-done.31 = bf16[2,4,240,640]{3,2,1,0:T(8,128)(2,1)S(1)} collective-permute-done((bf16[2,4,240,640]{3,2,1,0:T(8,128)(2,1)S(1)}, bf16[2,4,240,640]{3,2,1,0:T(8,128)(2,1)S(1)}, u32[]{:S(2)}, u32[]{:S(2)}) %collective-permute-start.31) | collective-permute-done | bytes 2457632 | tf_op jit(solution)/shard_map/ppermute | solution.py:964
  192.1 17.0 %feed_back_gate.1 = (f32[256,960]{1,0:T(8,128)S(1)}, bf16[256,1024]{1,0:T(8,128)(2,1)S(1)}, bf16[960,256]{1,0:T(8,128)(2,1)S(1)}, f32[1,960]{1,0:T(1,128)S(1)}, ...) custom-call(s32[3]{0:T(128)S(1)} %pad_add_fusion.1.place_ref.refs_0_, ...), custom_call_target="tpu_custom_call" | custom-call | flops 10066329600 | bytes 19988480 | tf_op jit(solution)/shard_map/feed_back_gate/pallas_call | solution.py:746
  211.2 3.0 collective-permute-done.33
  216.1 10.1 %collective-permute-done.34 = bf16[2,240,640]{2,1,0:T(8,128)(2,1)S(1)} collective-permute-done((bf16[2,240,640]{2,1,0:T(8,128)(2,1)S(1)}, bf16[2,240,640]{2,1,0:T(8,128)(2,1)S(1)}, u32[]{:S(2)}, u32[]{:S(2)}) %collective-permute-start.34) | collective-permute-done | bytes 614432 | tf_op jit(solution)/shard_map/ppermute | solution.py:964
  226.3 9.4 %attend_back.3 = (bf16[960,256]{1,0:T(8,128)(2,1)S(1)}, bf16[2,640,256]{2,1,0:T(8,128)(2,1)S(1)}, bf16[2,640,256]{2,1,0:T(8,128)(2,1)S(1)}) custom-call(s32[4]{0:T(128)S(1)} %and_convert_fusion.refs_0_.visible_ref, bf16[960,256]{1,0:T(8,128)(2,1)S(1)} %copy-done.19, bf16[960,256]{1,0:T(8,128)(2,1)S(1)} %get-tuple-element.210.do_ref, ...), custom_call_target="tpu_custom_call" | custom-call | flops 5033164800 | bytes 4915200 | tf_op jit(solution)/shard_map/attend_back/pallas_call | solution.py:624
  235.7 3.2 collective-permute-done.35
  241.1 3.1 collective-permute-start.39
  244.3 11.4 %collective-permute-done.38 = bf16[2,240,640]{2,1,0:T(8,128)(2,1)S(1)} collective-permute-done((bf16[2,240,640]{2,1,0:T(8,128)(2,1)S(1)}, bf16[2,240,640]{2,1,0:T(8,128)(2,1)S(1)}, u32[]{:S(2)}, u32[]{:S(2)}) %collective-permute-start.38) | collective-permute-done | bytes 614432 | tf_op jit(solution)/shard_map/ppermute | solution.py:964
  257.5 7.8 %collective-permute-done.40.refs_5_ = bf16[640,256]{1,0:T(8,128)(2,1)S(1)} collective-permute-done((bf16[640,256]{1,0:T(8,128)(2,1)S(1)}, bf16[640,256]{1,0:T(8,128)(2,1)S(1)}, u32[]{:S(2)}, u32[]{:S(2)}) %collective-permute-start.40) | collective-permute-done | bytes 327712 | tf_op jit(solution)/shard_map/ppermute | solution.py:964
  269.6 3.0 collective-permute-start.45
  272.6 6.4 %leave_mixed.1 = (bf16[960,256]{1,0:T(8,128)(2,1)}, bf16[2,4,256,640]{3,2,1,0:T(8,128)(2,1)S(1)}, bf16[2,4,256,640]{3,2,1,0:T(8,128)(2,1)S(1)}) custom-call(s32[3]{0:T(128)S(1)} %pad_add_fusion.1.place_ref.refs_0_, f32[256,960]{1,0:T(8,128)S(1)} %copy-done.6, f32[256,960]{1,0:T(8,128)S(1)} %get-tuple-element.230.refs_2_, ...), custom_call_target="tpu_custom_call" | custom-call | flops 2453667840 | bytes 6635520 | tf_op jit(solution)/shard_map/leave_mixed/pallas_call | solution.py:795
  285.3 2.5 collective-permute-done.46
  291.9 7.8 %collective-permute-done.48 = bf16[2,240,640]{2,1,0:T(8,128)(2,1)S(1)} collective-permute-done((bf16[2,240,640]{2,1,0:T(8,128)(2,1)S(1)}, bf16[2,240,640]{2,1,0:T(8,128)(2,1)S(1)}, u32[]{:S(2)}, u32[]{:S(2)}) %collective-permute-start.48) | collective-permute-done | bytes 614432 | tf_op jit(solution)/shard_map/ppermute | solution.py:964
  306.8 5.8 %collective-permute-done.51.p3_ref = bf16[240,640]{1,0:T(8,128)(2,1)S(1)} collective-permute-done((bf16[240,640]{1,0:T(8,128)(2,1)S(1)}, bf16[240,640]{1,0:T(8,128)(2,1)S(1)}, u32[]{:S(2)}, u32[]{:S(2)}) %collective-permute-start.51) | collective-permute-done | bytes 307232 | tf_op jit(solution)/shard_map/ppermute | solution.py:964
  312.7 2.5 finish.3
  319.4 8.0 %collective-permute-done.55 = bf16[240,640]{1,0:T(8,128)(2,1)S(1)} collective-permute-done((bf16[240,640]{1,0:T(8,128)(2,1)S(1)}, bf16[240,640]{1,0:T(8,128)(2,1)S(1)}, u32[]{:S(2)}, u32[]{:S(2)}) %collective-permute-start.55) | collective-permute-done | bytes 307232 | tf_op jit(solution)/shard_map/ppermute | solution.py:964
  331.7 2.2 collective-permute-start.59
  334.8 4.5 %collective-permute-done.57.p1_ref = bf16[240,640]{1,0:T(8,128)(2,1)S(1)} collective-permute-done((bf16[240,640]{1,0:T(8,128)(2,1)S(1)}, bf16[240,640]{1,0:T(8,128)(2,1)S(1)}, u32[]{:S(2)}, u32[]{:S(2)}) %collective-permute-start.57) | collective-permute-done | bytes 307232 | tf_op jit(solution)/shard_map/ppermute | solution.py:964
  342.5 5.2 %collective-permute-done.59 = bf16[256,640]{1,0:T(8,128)(2,1)S(1)} collective-permute-done((bf16[256,640]{1,0:T(8,128)(2,1)S(1)}, bf16[256,640]{1,0:T(8,128)(2,1)S(1)}, u32[]{:S(2)}, u32[]{:S(2)}) %collective-permute-start.59) | collective-permute-done | bytes 327712 | tf_op jit(solution)/shard_map/ppermute | solution.py:964
  351.3 2.5 finish.4
  353.8 3.6 collective-permute-done.62.p1_ref
  358.8 5.7 %collective-permute-done.64.p3_ref = bf16[240,640]{1,0:T(8,128)(2,1)S(1)} collective-permute-done((bf16[240,640]{1,0:T(8,128)(2,1)S(1)}, bf16[240,640]{1,0:T(8,128)(2,1)S(1)}, u32[]{:S(2)}, u32[]{:S(2)}) %collective-permute-start.64) | collective-permute-done | bytes 307232 | tf_op jit(solution)/shard_map/ppermute | solution.py:964
  364.5 2.5 finish.5
  369.1 5.2 %collective-permute-done.66.p1_ref = bf16[256,640]{1,0:T(8,128)(2,1)S(1)} collective-permute-done((bf16[256,640]{1,0:T(8,128)(2,1)S(1)}, bf16[256,640]{1,0:T(8,128)(2,1)S(1)}, u32[]{:S(2)}, u32[]{:S(2)}) %collective-permute-start.66) | collective-permute-done | bytes 327712 | tf_op jit(solution)/shard_map/ppermute | solution.py:964
  377.2 5.0 %collective-permute-done.68.p3_ref = bf16[256,640]{1,0:T(8,128)(2,1)S(1)} collective-permute-done((bf16[256,640]{1,0:T(8,128)(2,1)S(1)}, bf16[256,640]{1,0:T(8,128)(2,1)S(1)}, u32[]{:S(2)}, u32[]{:S(2)}) %collective-permute-start.68) | collective-permute-done | bytes 327712 | tf_op jit(solution)/shard_map/ppermute | solution.py:964
  382.2 2.6 finish_mixed.1
  (258 shorter events, 91.5 us)
Async XLA Ops:
  2.0 9.8 %collective-permute-start = (bf16[2,240]{1,0:T(2,128)(2,1)S(1)}, bf16[2,240]{1,0:T(2,128)(2,1)S(1)}, u32[]{:S(2)}, u32[]{:S(2)}) collective-permute-start(bf16[2,240]{1,0:T(2,128)(2,1)S(1)} %pad_maximum_fusion), channel_id=1, source_target_pairs={{0,1},{1,0},{2,3},{3,2},{4,5},{5,4},{6,7},{7,6},{8,9},{9,8},{10,11... | collective-permute-start | bytes 2888 | tf_op jit(solution)/shard_map/ppermute | solution.py:964
  9.2 49.4 %collective-permute-start.3 = (bf16[240,2560]{1,0:T(8,128)(2,1)}, bf16[240,2560]{1,0:T(8,128)(2,1)}, u32[]{:S(2)}, u32[]{:S(2)}) collective-permute-start(bf16[240,2560]{1,0:T(8,128)(2,1)} %get-tuple-element.157.refs_0_), channel_id=1, source_target_pairs={{0,1},{1,0},{2,3},{3,2},{4,5},{5,4},{6,7},{7,6},{8,9},{9,8},{10,11... | collective-permute-start | bytes 3686408 | tf_op jit(solution)/shard_map/ppermute | solution.py:964
  11.8 16.4 %collective-permute-start.4 = (bf16[240,1280]{1,0:T(8,128)(2,1)}, bf16[240,1280]{1,0:T(8,128)(2,1)S(1)}, u32[]{:S(2)}, u32[]{:S(2)}) collective-permute-start(bf16[240,1280]{1,0:T(8,128)(2,1)} %get-tuple-element.151), channel_id=1, source_target_pairs={{0,2},{1,3},{2,0},{3,1},{4,6},{5,7},{6,4},{7,5},{8,10},{9,11},{10,... | collective-permute-start | bytes 1843208 | tf_op jit(solution)/shard_map/ppermute | solution.py:964
  28.2 15.3 %collective-permute-start.5 = (bf16[240,1280]{1,0:T(8,128)(2,1)S(1)}, bf16[240,1280]{1,0:T(8,128)(2,1)S(1)}, u32[]{:S(2)}, u32[]{:S(2)}) collective-permute-start(bf16[240,1280]{1,0:T(8,128)(2,1)S(1)} %collective-permute-done.4.refs_2_), channel_id=1, source_target_pairs={{0,4},{4,0},{8,12},{12,8},{16,20},{20,16},{24,28},{28,24},{1,5},{5... | collective-permute-start | bytes 1843208 | tf_op jit(solution)/shard_map/ppermute | solution.py:964
  29.9 17.0 %collective-permute-start.13 = (bf16[240,1280]{1,0:T(8,128)(2,1)}, bf16[240,1280]{1,0:T(8,128)(2,1)S(1)}, u32[]{:S(2)}, u32[]{:S(2)}) collective-permute-start(bf16[240,1280]{1,0:T(8,128)(2,1)} %get-tuple-element.152), channel_id=1, source_target_pairs={{0,2},{1,3},{2,0},{3,1},{4,6},{5,7},{6,4},{7,5},{8,10},{9,11},{10,... | collective-permute-start | bytes 1843208 | tf_op jit(solution)/shard_map/ppermute | solution.py:964
  31.4 26.7 %collective-permute-start.12 = (bf16[240,1280]{1,0:T(8,128)(2,1)}, bf16[240,1280]{1,0:T(8,128)(2,1)S(1)}, u32[]{:S(2)}, u32[]{:S(2)}) collective-permute-start(bf16[240,1280]{1,0:T(8,128)(2,1)} %get-tuple-element.153), channel_id=1, source_target_pairs={{0,2},{1,3},{2,0},{3,1},{4,6},{5,7},{6,4},{7,5},{8,10},{9,11},{10,... | collective-permute-start | bytes 1843208 | tf_op jit(solution)/shard_map/ppermute | solution.py:964
  32.0 28.2 %collective-permute-start.6 = (bf16[240,1280]{1,0:T(8,128)(2,1)S(1)}, bf16[240,1280]{1,0:T(8,128)(2,1)S(1)}, u32[]{:S(2)}, u32[]{:S(2)}) collective-permute-start(bf16[240,1280]{1,0:T(8,128)(2,1)S(1)} %collective-permute-done.4.refs_2_), channel_id=1, source_target_pairs={{0,1},{1,0},{2,3},{3,2},{4,5},{5,4},{6,7},{7,6},{8,9},{9,8},{10,11... | collective-permute-start | bytes 1843208 | tf_op jit(solution)/shard_map/ppermute | solution.py:964
  43.5 16.6 %collective-permute-start.7 = (bf16[240,1280]{1,0:T(8,128)(2,1)S(1)}, bf16[240,1280]{1,0:T(8,128)(2,1)S(1)}, u32[]{:S(2)}, u32[]{:S(2)}) collective-permute-start(bf16[240,1280]{1,0:T(8,128)(2,1)S(1)} %collective-permute-done.5.refs_3_), channel_id=1, source_target_pairs={{0,1},{1,0},{2,3},{3,2},{4,5},{5,4},{6,7},{7,6},{8,9},{9,8},{10,11... | collective-permute-start | bytes 1843208 | tf_op jit(solution)/shard_map/ppermute | solution.py:964
  46.9 27.1 %collective-permute-start.21 = (bf16[960,640]{1,0:T(8,128)(2,1)}, bf16[960,640]{1,0:T(8,128)(2,1)S(1)}, u32[]{:S(2)}, u32[]{:S(2)}) collective-permute-start(bf16[960,640]{1,0:T(8,128)(2,1)} %bitcast.133), channel_id=1, source_target_pairs={{0,1},{1,0},{2,3},{3,2},{4,5},{5,4},{6,7},{7,6},{8,9},{9,8},{10,11... | collective-permute-start | bytes 3686408 | tf_op jit(solution)/shard_map/ppermute | solution.py:964
  58.1 13.9 %collective-permute-start.14 = (bf16[240,1280]{1,0:T(8,128)(2,1)S(1)}, bf16[240,1280]{1,0:T(8,128)(2,1)S(1)}, u32[]{:S(2)}, u32[]{:S(2)}) collective-permute-start(bf16[240,1280]{1,0:T(8,128)(2,1)S(1)} %collective-permute-done.13.refs_12_), channel_id=1, source_target_pairs={{0,4},{4,0},{8,12},{12,8},{16,20},{20,16},{24,28},{28,24},{1,5},{5... | collective-permute-start | bytes 1843208 | tf_op jit(solution)/shard_map/ppermute | solution.py:964
  58.6 14.0 %collective-permute-start.22 = (bf16[480,640]{1,0:T(8,128)(2,1)}, bf16[480,640]{1,0:T(8,128)(2,1)S(1)}, u32[]{:S(2)}, u32[]{:S(2)}) collective-permute-start(bf16[480,640]{1,0:T(8,128)(2,1)} %slice_select_fusion), channel_id=1, source_target_pairs={{0,2},{1,3},{2,0},{3,1},{4,6},{5,7},{6,4},{7,5},{8,10},{9,11},{10,... | collective-permute-start | bytes 1843208 | tf_op jit(solution)/shard_map/ppermute | solution.py:964
  60.1 15.5 %collective-permute-start.11 = (bf16[240,2560]{1,0:T(8,128)(2,1)S(1)}, bf16[240,2560]{1,0:T(8,128)(2,1)S(1)}, u32[]{:S(2)}, u32[]{:S(2)}) collective-permute-start(bf16[240,2560]{1,0:T(8,128)(2,1)S(1)} %copy-done.3), channel_id=1, source_target_pairs={{0,1},{1,0},{2,3},{3,2},{4,5},{5,4},{6,7},{7,6},{8,9},{9,8},{10,11... | collective-permute-start | bytes 3686408 | tf_op jit(solution)/shard_map/ppermute | solution.py:964
  60.2 17.0 %collective-permute-start.17 = (bf16[240,2560]{1,0:T(8,128)(2,1)S(1)}, bf16[240,2560]{1,0:T(8,128)(2,1)S(1)}, u32[]{:S(2)}, u32[]{:S(2)}) collective-permute-start(bf16[240,2560]{1,0:T(8,128)(2,1)S(1)} %copy-done.4), channel_id=1, source_target_pairs={{0,1},{1,0},{2,3},{3,2},{4,5},{5,4},{6,7},{7,6},{8,9},{9,8},{10,11... | collective-permute-start | bytes 3686408 | tf_op jit(solution)/shard_map/ppermute | solution.py:964
  72.7 12.9 %collective-permute-start.23 = (bf16[480,640]{1,0:T(8,128)(2,1)S(1)}, bf16[480,640]{1,0:T(8,128)(2,1)S(1)}, u32[]{:S(2)}, u32[]{:S(2)}) collective-permute-start(bf16[480,640]{1,0:T(8,128)(2,1)S(1)} %collective-permute-done.22.refs_24_), channel_id=1, source_target_pairs={{0,4},{4,0},{8,12},{12,8},{16,20},{20,16},{24,28},{28,24},{1,5},{5... | collective-permute-start | bytes 1843208 | tf_op jit(solution)/shard_map/ppermute | solution.py:964
  74.0 12.2 %collective-permute-start.15 = (bf16[240,1280]{1,0:T(8,128)(2,1)S(1)}, bf16[240,1280]{1,0:T(8,128)(2,1)S(1)}, u32[]{:S(2)}, u32[]{:S(2)}) collective-permute-start(bf16[240,1280]{1,0:T(8,128)(2,1)S(1)} %collective-permute-done.13.refs_12_), channel_id=1, source_target_pairs={{0,1},{1,0},{2,3},{3,2},{4,5},{5,4},{6,7},{7,6},{8,9},{9,8},{10,11... | collective-permute-start | bytes 1843208 | tf_op jit(solution)/shard_map/ppermute | solution.py:964
  74.0 16.3 %collective-permute-start.18 = (bf16[240,1280]{1,0:T(8,128)(2,1)S(1)}, bf16[240,1280]{1,0:T(8,128)(2,1)S(1)}, u32[]{:S(2)}, u32[]{:S(2)}) collective-permute-start(bf16[240,1280]{1,0:T(8,128)(2,1)S(1)} %collective-permute-done.12.refs_18_), channel_id=1, source_target_pairs={{0,8},{4,12},{8,0},{12,4},{16,24},{20,28},{24,16},{28,20},{1,9},{5... | collective-permute-start | bytes 1843208 | tf_op jit(solution)/shard_map/ppermute | solution.py:964
  75.6 9.9 %collective-permute-start.9 = (bf16[640,256]{1,0:T(8,128)(2,1)S(1)}, bf16[640,256]{1,0:T(8,128)(2,1)S(1)}, u32[]{:S(2)}, u32[]{:S(2)}) collective-permute-start(bf16[640,256]{1,0:T(8,128)(2,1)S(1)} %get-tuple-element.162.refs_4_.kv0_ref), channel_id=1, source_target_pairs={{0,2},{1,3},{2,0},{3,1},{4,6},{5,7},{6,4},{7,5},{8,10},{9,11},{10,... | collective-permute-start | bytes 983048 | tf_op jit(solution)/shard_map/ppermute | solution.py:964
  112.6 10.4 %collective-permute-start.26 = (bf16[640,256]{1,0:T(8,128)(2,1)S(1)}, bf16[640,256]{1,0:T(8,128)(2,1)S(1)}, u32[]{:S(2)}, u32[]{:S(2)}) collective-permute-start(bf16[640,256]{1,0:T(8,128)(2,1)S(1)} %get-tuple-element.172.refs_4_.kv0_ref), channel_id=1, source_target_pairs={{0,1},{1,0},{2,3},{3,2},{4,5},{5,4},{6,7},{7,6},{8,9},{9,8},{10,11... | collective-permute-start | bytes 983048 | tf_op jit(solution)/shard_map/ppermute | solution.py:964
  160.0 13.7 %collective-permute-start.30 = (bf16[640,256]{1,0:T(8,128)(2,1)}, bf16[640,256]{1,0:T(8,128)(2,1)}, u32[]{:S(2)}, u32[]{:S(2)}) collective-permute-start(bf16[640,256]{1,0:T(8,128)(2,1)} %get-tuple-element.295), channel_id=1, source_target_pairs={{0,2},{1,3},{2,0},{3,1},{4,6},{5,7},{6,4},{7,5},{8,10},{9,11},{10,... | collective-permute-start | bytes 983048 | tf_op jit(solution)/shard_map/ppermute | solution.py:964
  190.3 18.9 %collective-permute-start.32 = (bf16[2,240,640]{2,1,0:T(8,128)(2,1)S(1)}, bf16[2,240,640]{2,1,0:T(8,128)(2,1)S(1)}, u32[]{:S(2)}, u32[]{:S(2)}) collective-permute-start(bf16[2,240,640]{2,1,0:T(8,128)(2,1)S(1)} %get-tuple-element.292), channel_id=1, source_target_pairs={{0,2},{1,3},{2,0},{3,1},{4,6},{5,7},{6,4},{7,5},{8,10},{9,11},{10,... | collective-permute-start | bytes 1843208 | tf_op jit(solution)/shard_map/ppermute | solution.py:964
  209.5 16.7 %collective-permute-start.34 = (bf16[2,240,640]{2,1,0:T(8,128)(2,1)S(1)}, bf16[2,240,640]{2,1,0:T(8,128)(2,1)S(1)}, u32[]{:S(2)}, u32[]{:S(2)}) collective-permute-start(bf16[2,240,640]{2,1,0:T(8,128)(2,1)S(1)} %get-tuple-element.291), channel_id=1, source_target_pairs={{0,2},{1,3},{2,0},{3,1},{4,6},{5,7},{6,4},{7,5},{8,10},{9,11},{10,... | collective-permute-start | bytes 1843208 | tf_op jit(solution)/shard_map/ppermute | solution.py:964
  214.5 24.4 %collective-permute-start.35 = (bf16[2,240,640]{2,1,0:T(8,128)(2,1)S(1)}, bf16[2,240,640]{2,1,0:T(8,128)(2,1)S(1)}, u32[]{:S(2)}, u32[]{:S(2)}) collective-permute-start(bf16[2,240,640]{2,1,0:T(8,128)(2,1)S(1)} %get-tuple-element.290), channel_id=1, source_target_pairs={{0,2},{1,3},{2,0},{3,1},{4,6},{5,7},{6,4},{7,5},{8,10},{9,11},{10,... | collective-permute-start | bytes 1843208 | tf_op jit(solution)/shard_map/ppermute | solution.py:964
  216.1 23.1 %collective-permute-start.36 = (bf16[2,240,640]{2,1,0:T(8,128)(2,1)S(1)}, bf16[2,240,640]{2,1,0:T(8,128)(2,1)S(1)}, u32[]{:S(2)}, u32[]{:S(2)}) collective-permute-start(bf16[2,240,640]{2,1,0:T(8,128)(2,1)S(1)} %fusion.3), channel_id=1, source_target_pairs={{0,4},{4,0},{8,12},{12,8},{16,20},{20,16},{24,28},{28,24},{1,5},{5... | collective-permute-start | bytes 1843208 | tf_op jit(solution)/shard_map/ppermute | solution.py:964
  226.2 39.2 %collective-permute-start.42 = (bf16[2,4,240,640]{3,2,1,0:T(8,128)(2,1)S(1)}, bf16[2,4,240,640]{3,2,1,0:T(8,128)(2,1)S(1)}, u32[]{:S(2)}, u32[]{:S(2)}) collective-permute-start(bf16[2,4,240,640]{3,2,1,0:T(8,128)(2,1)S(1)} %get-tuple-element.228), channel_id=1, source_target_pairs={{0,1},{1,0},{2,3},{3,2},{4,5},{5,4},{6,7},{7,6},{8,9},{9,8},{10,11... | collective-permute-start | bytes 7372808 | tf_op jit(solution)/shard_map/ppermute | solution.py:964
  239.5 16.3 %collective-permute-start.38 = (bf16[2,240,640]{2,1,0:T(8,128)(2,1)S(1)}, bf16[2,240,640]{2,1,0:T(8,128)(2,1)S(1)}, u32[]{:S(2)}, u32[]{:S(2)}) collective-permute-start(bf16[2,240,640]{2,1,0:T(8,128)(2,1)S(1)} %get-tuple-element.289), channel_id=1, source_target_pairs={{0,2},{1,3},{2,0},{3,1},{4,6},{5,7},{6,4},{7,5},{8,10},{9,11},{10,... | collective-permute-start | bytes 1843208 | tf_op jit(solution)/shard_map/ppermute | solution.py:964
  241.1 14.7 %collective-permute-start.39 = (bf16[240,640]{1,0:T(8,128)(2,1)S(1)}, bf16[240,640]{1,0:T(8,128)(2,1)S(1)}, u32[]{:S(2)}, u32[]{:S(2)}) collective-permute-start(bf16[240,640]{1,0:T(8,128)(2,1)S(1)} %fusion.21), channel_id=1, source_target_pairs={{0,8},{4,12},{8,0},{12,4},{16,24},{20,28},{24,16},{28,20},{1,9},{5... | collective-permute-start | bytes 921608 | tf_op jit(solution)/shard_map/ppermute | solution.py:964
  244.2 21.2 %collective-permute-start.41 = (bf16[2,240,640]{2,1,0:T(8,128)(2,1)S(1)}, bf16[2,240,640]{2,1,0:T(8,128)(2,1)S(1)}, u32[]{:S(2)}, u32[]{:S(2)}) collective-permute-start(bf16[2,240,640]{2,1,0:T(8,128)(2,1)S(1)} %fusion.2), channel_id=1, source_target_pairs={{0,4},{4,0},{8,12},{12,8},{16,20},{20,16},{24,28},{28,24},{1,5},{5... | collective-permute-start | bytes 1843208 | tf_op jit(solution)/shard_map/ppermute | solution.py:964
  265.9 14.6 %collective-permute-start.43 = (bf16[2,240,640]{2,1,0:T(8,128)(2,1)S(1)}, bf16[2,240,640]{2,1,0:T(8,128)(2,1)S(1)}, u32[]{:S(2)}, u32[]{:S(2)}) collective-permute-start(bf16[2,240,640]{2,1,0:T(8,128)(2,1)S(1)} %get-tuple-element.288), channel_id=1, source_target_pairs={{0,2},{1,3},{2,0},{3,1},{4,6},{5,7},{6,4},{7,5},{8,10},{9,11},{10,... | collective-permute-start | bytes 1843208 | tf_op jit(solution)/shard_map/ppermute | solution.py:964
  267.4 15.1 %collective-permute-start.44 = (bf16[240,640]{1,0:T(8,128)(2,1)S(1)}, bf16[240,640]{1,0:T(8,128)(2,1)S(1)}, u32[]{:S(2)}, u32[]{:S(2)}) collective-permute-start(bf16[240,640]{1,0:T(8,128)(2,1)S(1)} %fusion.23), channel_id=1, source_target_pairs={{0,16},{4,20},{8,24},{12,28},{16,0},{20,4},{24,8},{28,12},{1,17},{... | collective-permute-start | bytes 921608 | tf_op jit(solution)/shard_map/ppermute | solution.py:964
  269.6 13.0 %collective-permute-start.45 = (bf16[240,640]{1,0:T(8,128)(2,1)S(1)}, bf16[240,640]{1,0:T(8,128)(2,1)S(1)}, u32[]{:S(2)}, u32[]{:S(2)}) collective-permute-start(bf16[240,640]{1,0:T(8,128)(2,1)S(1)} %fusion.20), channel_id=1, source_target_pairs={{0,8},{4,12},{8,0},{12,4},{16,24},{20,28},{24,16},{28,20},{1,9},{5... | collective-permute-start | bytes 921608 | tf_op jit(solution)/shard_map/ppermute | solution.py:964
  282.9 16.7 %collective-permute-start.48 = (bf16[2,240,640]{2,1,0:T(8,128)(2,1)S(1)}, bf16[2,240,640]{2,1,0:T(8,128)(2,1)S(1)}, u32[]{:S(2)}, u32[]{:S(2)}) collective-permute-start(bf16[2,240,640]{2,1,0:T(8,128)(2,1)S(1)} %get-tuple-element.287), channel_id=1, source_target_pairs={{0,2},{1,3},{2,0},{3,1},{4,6},{5,7},{6,4},{7,5},{8,10},{9,11},{10,... | collective-permute-start | bytes 1843208 | tf_op jit(solution)/shard_map/ppermute | solution.py:964
  283.6 16.7 %collective-permute-start.47 = (bf16[2,240,640]{2,1,0:T(8,128)(2,1)S(1)}, bf16[2,240,640]{2,1,0:T(8,128)(2,1)S(1)}, u32[]{:S(2)}, u32[]{:S(2)}) collective-permute-start(bf16[2,240,640]{2,1,0:T(8,128)(2,1)S(1)} %fusion.1), channel_id=1, source_target_pairs={{0,4},{4,0},{8,12},{12,8},{16,20},{20,16},{24,28},{28,24},{1,5},{5... | collective-permute-start | bytes 1843208 | tf_op jit(solution)/shard_map/ppermute | solution.py:964
  288.2 27.0 %collective-permute-start.52 = (bf16[2,256,640]{2,1,0:T(8,128)(2,1)S(1)}, bf16[2,256,640]{2,1,0:T(8,128)(2,1)S(1)}, u32[]{:S(2)}, u32[]{:S(2)}) collective-permute-start(bf16[2,256,640]{2,1,0:T(8,128)(2,1)S(1)} %get-tuple-element.286), channel_id=1, source_target_pairs={{0,2},{1,3},{2,0},{3,1},{4,6},{5,7},{6,4},{7,5},{8,10},{9,11},{10,... | collective-permute-start | bytes 1966088 | tf_op jit(solution)/shard_map/ppermute | solution.py:964
  288.8 11.6 %collective-permute-start.49 = (bf16[240,640]{1,0:T(8,128)(2,1)S(1)}, bf16[240,640]{1,0:T(8,128)(2,1)S(1)}, u32[]{:S(2)}, u32[]{:S(2)}) collective-permute-start(bf16[240,640]{1,0:T(8,128)(2,1)S(1)} %add_convert_fusion.15.p0_ref), channel_id=1, source_target_pairs={{0,8},{4,12},{8,0},{12,4},{16,24},{20,28},{24,16},{28,20},{1,9},{5... | collective-permute-start | bytes 921608 | tf_op jit(solution)/shard_map/ppermute | solution.py:964
  291.0 15.8 %collective-permute-start.50 = (bf16[240,640]{1,0:T(8,128)(2,1)S(1)}, bf16[240,640]{1,0:T(8,128)(2,1)S(1)}, u32[]{:S(2)}, u32[]{:S(2)}) collective-permute-start(bf16[240,640]{1,0:T(8,128)(2,1)S(1)} %add_convert_fusion.15.p0_ref), channel_id=1, source_target_pairs={{0,4},{4,0},{8,12},{12,8},{16,20},{20,16},{24,28},{28,24},{1,5},{5... | collective-permute-start | bytes 921608 | tf_op jit(solution)/shard_map/ppermute | solution.py:964
  300.4 12.2 %collective-permute-start.51 = (bf16[240,640]{1,0:T(8,128)(2,1)S(1)}, bf16[240,640]{1,0:T(8,128)(2,1)S(1)}, u32[]{:S(2)}, u32[]{:S(2)}) collective-permute-start(bf16[240,640]{1,0:T(8,128)(2,1)S(1)} %collective-permute-done.49.p1_ref), channel_id=1, source_target_pairs={{0,4},{4,0},{8,12},{12,8},{16,20},{20,16},{24,28},{28,24},{1,5},{5... | collective-permute-start | bytes 921608 | tf_op jit(solution)/shard_map/ppermute | solution.py:964
  302.3 16.3 %collective-permute-start.54 = (bf16[240,640]{1,0:T(8,128)(2,1)S(1)}, bf16[240,640]{1,0:T(8,128)(2,1)S(1)}, u32[]{:S(2)}, u32[]{:S(2)}) collective-permute-start(bf16[240,640]{1,0:T(8,128)(2,1)S(1)} %fusion.19), channel_id=1, source_target_pairs={{0,16},{4,20},{8,24},{12,28},{16,0},{20,4},{24,8},{28,12},{1,17},{... | collective-permute-start | bytes 921608 | tf_op jit(solution)/shard_map/ppermute | solution.py:964
  303.6 25.8 %collective-permute-start.56 = (bf16[2,256,640]{2,1,0:T(8,128)(2,1)S(1)}, bf16[2,256,640]{2,1,0:T(8,128)(2,1)S(1)}, u32[]{:S(2)}, u32[]{:S(2)}) collective-permute-start(bf16[2,256,640]{2,1,0:T(8,128)(2,1)S(1)} %get-tuple-element.285), channel_id=1, source_target_pairs={{0,2},{1,3},{2,0},{3,1},{4,6},{5,7},{6,4},{7,5},{8,10},{9,11},{10,... | collective-permute-start | bytes 1966088 | tf_op jit(solution)/shard_map/ppermute | solution.py:964
  315.5 16.1 %collective-permute-start.53 = (bf16[2,256,640]{2,1,0:T(8,128)(2,1)S(1)}, bf16[2,256,640]{2,1,0:T(8,128)(2,1)S(1)}, u32[]{:S(2)}, u32[]{:S(2)}) collective-permute-start(bf16[2,256,640]{2,1,0:T(8,128)(2,1)S(1)} %fusion), channel_id=1, source_target_pairs={{0,4},{4,0},{8,12},{12,8},{16,20},{20,16},{24,28},{28,24},{1,5},{5... | collective-permute-start | bytes 1966088 | tf_op jit(solution)/shard_map/ppermute | solution.py:964
  317.3 10.2 %collective-permute-start.55 = (bf16[240,640]{1,0:T(8,128)(2,1)S(1)}, bf16[240,640]{1,0:T(8,128)(2,1)S(1)}, u32[]{:S(2)}, u32[]{:S(2)}) collective-permute-start(bf16[240,640]{1,0:T(8,128)(2,1)S(1)} %fusion.17), channel_id=1, source_target_pairs={{0,8},{4,12},{8,0},{12,4},{16,24},{20,28},{24,16},{28,20},{1,9},{5... | collective-permute-start | bytes 921608 | tf_op jit(solution)/shard_map/ppermute | solution.py:964
  318.7 20.6 %collective-permute-start.57 = (bf16[240,640]{1,0:T(8,128)(2,1)S(1)}, bf16[240,640]{1,0:T(8,128)(2,1)S(1)}, u32[]{:S(2)}, u32[]{:S(2)}) collective-permute-start(bf16[240,640]{1,0:T(8,128)(2,1)S(1)} %add_convert_fusion.14.p0_ref), channel_id=1, source_target_pairs={{0,8},{4,12},{8,0},{12,4},{16,24},{20,28},{24,16},{28,20},{1,9},{5... | collective-permute-start | bytes 921608 | tf_op jit(solution)/shard_map/ppermute | solution.py:964
  327.7 14.3 %collective-permute-start.58 = (bf16[240,640]{1,0:T(8,128)(2,1)S(1)}, bf16[240,640]{1,0:T(8,128)(2,1)S(1)}, u32[]{:S(2)}, u32[]{:S(2)}) collective-permute-start(bf16[240,640]{1,0:T(8,128)(2,1)S(1)} %fusion.16), channel_id=1, source_target_pairs={{0,16},{4,20},{8,24},{12,28},{16,0},{20,4},{24,8},{28,12},{1,17},{... | collective-permute-start | bytes 921608 | tf_op jit(solution)/shard_map/ppermute | solution.py:964
  331.7 16.0 %collective-permute-start.59 = (bf16[256,640]{1,0:T(8,128)(2,1)S(1)}, bf16[256,640]{1,0:T(8,128)(2,1)S(1)}, u32[]{:S(2)}, u32[]{:S(2)}) collective-permute-start(bf16[256,640]{1,0:T(8,128)(2,1)S(1)} %fusion.6), channel_id=1, source_target_pairs={{0,8},{4,12},{8,0},{12,4},{16,24},{20,28},{24,16},{28,20},{1,9},{5... | collective-permute-start | bytes 983048 | tf_op jit(solution)/shard_map/ppermute | solution.py:964
  333.9 17.4 %collective-permute-start.60 = (bf16[240,640]{1,0:T(8,128)(2,1)S(1)}, bf16[240,640]{1,0:T(8,128)(2,1)S(1)}, u32[]{:S(2)}, u32[]{:S(2)}) collective-permute-start(bf16[240,640]{1,0:T(8,128)(2,1)S(1)} %add_convert_fusion.14.p0_ref), channel_id=1, source_target_pairs={{0,4},{4,0},{8,12},{12,8},{16,20},{20,16},{24,28},{28,24},{1,5},{5... | collective-permute-start | bytes 921608 | tf_op jit(solution)/shard_map/ppermute | solution.py:964
  339.3 12.0 %collective-permute-start.61 = (bf16[240,640]{1,0:T(8,128)(2,1)S(1)}, bf16[240,640]{1,0:T(8,128)(2,1)S(1)}, u32[]{:S(2)}, u32[]{:S(2)}) collective-permute-start(bf16[240,640]{1,0:T(8,128)(2,1)S(1)} %collective-permute-done.57.p1_ref), channel_id=1, source_target_pairs={{0,4},{4,0},{8,12},{12,8},{16,20},{20,16},{24,28},{28,24},{1,5},{5... | collective-permute-start | bytes 921608 | tf_op jit(solution)/shard_map/ppermute | solution.py:964
  342.1 15.3 %collective-permute-start.62 = (bf16[240,640]{1,0:T(8,128)(2,1)S(1)}, bf16[240,640]{1,0:T(8,128)(2,1)S(1)}, u32[]{:S(2)}, u32[]{:S(2)}) collective-permute-start(bf16[240,640]{1,0:T(8,128)(2,1)S(1)} %add_convert_fusion.13.p0_ref), channel_id=1, source_target_pairs={{0,8},{4,12},{8,0},{12,4},{16,24},{20,28},{24,16},{28,20},{1,9},{5... | collective-permute-start | bytes 921608 | tf_op jit(solution)/shard_map/ppermute | solution.py:964
  347.9 19.1 %collective-permute-start.65 = (bf16[256,640]{1,0:T(8,128)(2,1)S(1)}, bf16[256,640]{1,0:T(8,128)(2,1)S(1)}, u32[]{:S(2)}, u32[]{:S(2)}) collective-permute-start(bf16[256,640]{1,0:T(8,128)(2,1)S(1)} %fusion.8), channel_id=1, source_target_pairs={{0,16},{4,20},{8,24},{12,28},{16,0},{20,4},{24,8},{28,12},{1,17},{... | collective-permute-start | bytes 983048 | tf_op jit(solution)/shard_map/ppermute | solution.py:964
  367.8 9.5 %collective-permute-start.67 = (bf16[256,640]{1,0:T(8,128)(2,1)S(1)}, bf16[256,640]{1,0:T(8,128)(2,1)S(1)}, u32[]{:S(2)}, u32[]{:S(2)}) collective-permute-start(bf16[256,640]{1,0:T(8,128)(2,1)S(1)} %add_convert_fusion.8.p0_ref), channel_id=1, source_target_pairs={{0,4},{4,0},{8,12},{12,8},{16,20},{20,16},{24,28},{28,24},{1,5},{5... | collective-permute-start | bytes 983048 | tf_op jit(solution)/shard_map/ppermute | solution.py:964
  (75 other events, 981.8 us)

commit v7 on v6

--- a/solution.py
+++ b/solution.py
@@ -699,7 +699,7 @@
         compiler_params=params(),
         cost_estimate=cost(2 * rows * width * wide, width * wide * 2 + rows * width * 14),
         name="leave",
-    )(hidden, d_middle, dq, own, got, gain, cos, sin, kept(weights_a))
+    )(hidden, d_middle, dq, own, got, gain, cos, sin, in_hbm(weights_a))
 
 
 def grad_parts(place_ref, right, keep_ref, send_ref, xt_ref):

time: 393 us -> 391 us (level)
  starting transfers between devices: 75.9 us -> 106 us
  Pallas kernels: 109 us -> 90.1 us
  waiting for transfers between devices: 176 us -> 165 us
    ppermute x69, starting transfers between devices: 75.9 us -> 106 us  [flip(): lax.ppermute(value, axis_name, [(i, i ^ distance) for i in range(size)])]
    ppermute x69, waiting for transfers between devices: 176 us -> 165 us  [flip(): lax.ppermute(value, axis_name, [(i, i ^ distance) for i in range(size)])]
    pallas_call x2, Pallas kernels: 18.8 us -> 7.95 us  [attend_back(): pl.pallas_call(attend_back_kernel, out_shape=(shape((width, rows), bf16),...]
    pallas_call x2, Pallas kernels: 30.6 us -> 21.4 us  [forward_block(): pl.pallas_call(functools.partial(forward_kernel, plans, counts), out_shap...]
    unnamed x108 -> x106, local copies, waits for them, and re-layouts: 8.47 us -> 6.15 us
  transfers between devices with their start and end apart: 69 -> 69, of which waited for: 36 -> 31; matrix products, arithmetic and copies ran while one was open for 3% -> 3% of each run, Pallas kernels for 12% -> 11%
where the time goes in v7:
time: 391 us; the launch traced here: 384 us
  waiting for transfers between devices  165 us (42%)
  starting transfers between devices  106 us (27%)
  Pallas kernels  90.1 us (23%)
  local copies, waits for them, and re-layouts  10.6 us (3%)
  other arithmetic  9.42 us (2%)
    ppermute x69, waiting for transfers between devices, flip(): lax.ppermute(value, axis_name, [(i, i ^ distance) for i in range(size)])  165 us
    ppermute x69, starting transfers between devices, flip(): lax.ppermute(value, axis_name, [(i, i ^ distance) for i in range(size)])  106 us
    pallas_call x2, Pallas kernels, forward_block(): pl.pallas_call(functools.partial(forward_kernel, plans, counts), out_shap...  21.4 us
    pallas_call x1, Pallas kernels, feed_back_gate(): pl.pallas_call(feed_back_gate_kernel, out_shape=(shape((rows, width), f32...  17 us
    pallas_call x1, Pallas kernels, feed_back(): pl.pallas_call(feed_back_kernel, out_shape=(shape((rows, width), bf16), s...  9.02 us
    pallas_call x2, Pallas kernels, attend_back(): pl.pallas_call(attend_back_kernel, out_shape=(shape((width, rows), bf16),...  7.95 us
  transfers between devices with their start and end apart: 69, of which 31 were waited for; matrix products, arithmetic and copies ran while one was open for 3% of the time, Pallas kernels for 11%

profile of v7, /device:TPU:0, one launch (start us, length us, event | category | flops | bytes accessed | tf_op | source)
XLA Modules:
  0.0 383.8 jit_solution(16023587274355638792)
XLA Ops:
  2.5 2.6 collective-permute-start.1
  5.2 4.0 %pack.1 = (bf16[240,2560]{1,0:T(8,128)(2,1)}, bf16[240,1280]{1,0:T(8,128)(2,1)}, bf16[240,1280]{1,0:T(8,128)(2,1)}, bf16[240,1280]{1,0:T(8,128)(2,1)}) custom-call(s32[3]{0:T(128)S(1)} %pad_add_fusion.bits_ref.index_ref.refs_1_, bf16[240,960]{1,0:T(8,128)(2,1)} %query_hbm.1, bf16[320,240]{1,0:T(8,128)(2,1)} %bitcast.136, bf16[320,240]{1,0:T(8,128)(2,1)} %bitcast.137, ...), custom_call_target="tpu_custom_call" | custom-call | bytes 4915200 | tf_op jit(solution)/shard_map/pack/pallas_call | solution.py:128
  9.5 2.3 slice_select_fusion
  18.5 9.7 %collective-permute-done.4.refs_2_ = bf16[240,1280]{1,0:T(8,128)(2,1)S(1)} collective-permute-done((bf16[240,1280]{1,0:T(8,128)(2,1)}, bf16[240,1280]{1,0:T(8,128)(2,1)S(1)}, u32[]{:S(2)}, u32[]{:S(2)}) %collective-permute-start.4) | collective-permute-done | bytes 614432 | tf_op jit(solution)/shard_map/ppermute | solution.py:964
  32.0 11.5 %collective-permute-done.5.refs_3_ = bf16[240,1280]{1,0:T(8,128)(2,1)S(1)} collective-permute-done((bf16[240,1280]{1,0:T(8,128)(2,1)S(1)}, bf16[240,1280]{1,0:T(8,128)(2,1)S(1)}, u32[]{:S(2)}, u32[]{:S(2)}) %collective-permute-start.5) | collective-permute-done | bytes 614432 | tf_op jit(solution)/shard_map/ppermute | solution.py:964
  43.5 3.4 collective-permute-done.13.refs_12_
  46.9 11.2 %collective-permute-done.12.refs_18_ = bf16[240,1280]{1,0:T(8,128)(2,1)S(1)} collective-permute-done((bf16[240,1280]{1,0:T(8,128)(2,1)}, bf16[240,1280]{1,0:T(8,128)(2,1)S(1)}, u32[]{:S(2)}, u32[]{:S(2)}) %collective-permute-start.12) | collective-permute-done | bytes 614432 | tf_op jit(solution)/shard_map/ppermute | solution.py:964
  63.0 3.4 enter_first.1
  67.2 4.8 %collective-permute-done.14.refs_13_ = bf16[240,1280]{1,0:T(8,128)(2,1)S(1)} collective-permute-done((bf16[240,1280]{1,0:T(8,128)(2,1)S(1)}, bf16[240,1280]{1,0:T(8,128)(2,1)S(1)}, u32[]{:S(2)}, u32[]{:S(2)}) %collective-permute-start.14) | collective-permute-done | bytes 614432 | tf_op jit(solution)/shard_map/ppermute | solution.py:964
  77.1 8.4 %collective-permute-done.23.refs_25_ = bf16[480,640]{1,0:T(8,128)(2,1)S(1)} collective-permute-done((bf16[480,640]{1,0:T(8,128)(2,1)S(1)}, bf16[480,640]{1,0:T(8,128)(2,1)S(1)}, u32[]{:S(2)}, u32[]{:S(2)}) %collective-permute-start.23) | collective-permute-done | bytes 614432 | tf_op jit(solution)/shard_map/ppermute | solution.py:964
  86.6 3.6 collective-permute-done.18.refs_19_
  92.8 11.5 %forward_first.1 = (f32[256,960]{1,0:T(8,128)S(1)}, bf16[256,960]{1,0:T(8,128)(2,1)S(1)}, bf16[960,256]{1,0:T(8,128)(2,1)S(1)}, f32[5,768]{1,0:T(8,128)S(1)}, f3...) custom-call(s32[4]{0:T(128)S(1)} %and_convert_fusion.refs_0_.visible, ...), custom_call_target="tpu_custom_call" | custom-call | flops 5033164800 | bytes 19988480 | tf_op jit(solution)/shard_map/forward_first/pallas_call | solution.py:416
  109.1 8.3 %collective-permute-done.27.refs_6_.kv2_ref = bf16[640,256]{1,0:T(8,128)(2,1)S(1)} collective-permute-done((bf16[640,256]{1,0:T(8,128)(2,1)S(1)}, bf16[640,256]{1,0:T(8,128)(2,1)S(1)}, u32[]{:S(2)}, u32[]{:S(2)}) %collective-permute-start.27) | collective-permute-done | bytes 327712 | tf_op jit(solution)/shard_map/ppermute | solution.py:964
  119.0 9.9 %forward_last.1 = (bf16[960,256]{1,0:T(8,128)(2,1)}, bf16[256,960]{1,0:T(8,128)(2,1)S(1)}, bf16[960,256]{1,0:T(8,128)(2,1)S(1)}, f32[5,768]{1,0:T(8,128)S(1)}, f...) custom-call(s32[4]{0:T(128)S(1)} %and_convert_fusion.refs_0_.visible, ...), custom_call_target="tpu_custom_call" | custom-call | flops 5033164800 | bytes 19988480 | tf_op jit(solution)/shard_map/forward_last/pallas_call | solution.py:416
  128.9 9.0 %feed_back.1 = (bf16[256,960]{1,0:T(8,128)(2,1)S(1)}, bf16[256,5120]{1,0:T(8,128)(2,1)S(1)}, f32[256,960]{1,0:T(8,128)S(1)}, bf16[256,1024]{1,0:T(8,128)(2,1)S(1...) custom-call(bf16[960,256]{1,0:T(8,128)(2,1)S(1)} %bitcast.131, f32[256,960]{1,0:T(8,128)S(1)} %get-tuple-element.176.middle_ref, ...), custom_call_target="tpu_custom_call" | custom-call | flops 5033164800 | bytes 19988480 | tf_op jit(solution)/shard_map/feed_back/pallas_call | solution.py:515
  138.0 3.9 %attend_back.2 = (bf16[960,256]{1,0:T(8,128)(2,1)S(1)}, bf16[2,640,256]{2,1,0:T(8,128)(2,1)S(1)}, bf16[2,640,256]{2,1,0:T(8,128)(2,1)S(1)}) custom-call(s32[4]{0:T(128)S(1)} %and_convert_fusion.refs_0_.visible_ref, bf16[960,256]{1,0:T(8,128)(2,1)S(1)} %get-tuple-element.171.refs_3_.q_ref, bf16[960,256]{1,0:T(8,128)(2,1)S(1)} %get-tuple-element.181.do_ref, ...), custom_call_target="tpu_custom_call" | custom-call | flops 5033164800 | bytes 4915200 | tf_op jit(solution)/shard_map/attend_back/pallas_call | solution.py:624
  146.6 8.5 %collective-permute-done.30.got_ref = bf16[640,256]{1,0:T(8,128)(2,1)} collective-permute-done((bf16[640,256]{1,0:T(8,128)(2,1)}, bf16[640,256]{1,0:T(8,128)(2,1)}, u32[]{:S(2)}, u32[]{:S(2)}) %collective-permute-start.30) | collective-permute-done | bytes 327712 | tf_op jit(solution)/shard_map/ppermute | solution.py:964
  156.2 4.0 %leave.1 = (f32[256,960]{1,0:T(8,128)S(1)}, bf16[256,1664]{1,0:T(8,128)(2,1)S(1)}, f32[1,960]{1,0:T(1,128)S(1)}) custom-call(f32[256,960]{1,0:T(8,128)S(1)} %get-tuple-element.170.h_ref.refs_2_, f32[256,960]{1,0:T(8,128)S(1)} %get-tuple-element.180.dmid_ref, bf16[960,256]{1,0:T(8,128)(2,1)S(1)} %copy-done.20, ...), custom_call_target="tpu_custom_call" | custom-call | flops 817889280 | bytes 6635520 | tf_op jit(solution)/shard_map/leave/pallas_call | solution.py:689
  160.3 5.4 %down_grad.1 = (bf16[2,4,240,640]{3,2,1,0:T(8,128)(2,1)S(1)}, bf16[2,4,240,640]{3,2,1,0:T(8,128)(2,1)S(1)}) custom-call(s32[3]{0:T(128)S(1)} %pad_add_fusion.1.place_ref.refs_0_, bf16[256,960]{1,0:T(8,128)(2,1)} %copy-done.41, f32[256,960]{1,0:T(8,128)S(1)} %get-tuple-element.194.g_ref.refs_1_, bf16[256,2560]{1,0:T(8,128)(2,1)} %copy-done.34, ...), custom_call_target="tpu_custom_call" | custom-call | flops 2516582400 | bytes 4915200 | tf_op jit(solution)/shard_map/down_grad/pallas_call | solution.py:835
  165.7 4.7 %collective-permute-done.31 = bf16[2,4,240,640]{3,2,1,0:T(8,128)(2,1)S(1)} collective-permute-done((bf16[2,4,240,640]{3,2,1,0:T(8,128)(2,1)S(1)}, bf16[2,4,240,640]{3,2,1,0:T(8,128)(2,1)S(1)}, u32[]{:S(2)}, u32[]{:S(2)}) %collective-permute-start.31) | collective-permute-done | bytes 2457632 | tf_op jit(solution)/shard_map/ppermute | solution.py:964
  172.4 17.0 %feed_back_gate.1 = (f32[256,960]{1,0:T(8,128)S(1)}, bf16[256,1024]{1,0:T(8,128)(2,1)S(1)}, bf16[960,256]{1,0:T(8,128)(2,1)S(1)}, f32[1,960]{1,0:T(1,128)S(1)}, ...) custom-call(s32[3]{0:T(128)S(1)} %pad_add_fusion.1.place_ref.refs_0_, ...), custom_call_target="tpu_custom_call" | custom-call | flops 10066329600 | bytes 19988480 | tf_op jit(solution)/shard_map/feed_back_gate/pallas_call | solution.py:746
  191.4 3.0 collective-permute-done.33
  196.3 19.0 %collective-permute-start.36 = (bf16[2,240,640]{2,1,0:T(8,128)(2,1)S(1)}, bf16[2,240,640]{2,1,0:T(8,128)(2,1)S(1)}, u32[]{:S(2)}, u32[]{:S(2)}) collective-permute-start(bf16[2,240,640]{2,1,0:T(8,128)(2,1)S(1)} %fusion.3), channel_id=1, source_target_pairs={{0,4},{4,0},{8,12},{12,8},{16,20},{20,16},{24,28},{28,24},{1,5},{5... | collective-permute-start | bytes 1843208 | tf_op jit(solution)/shard_map/ppermute | solution.py:964
  215.4 4.0 %attend_back.3 = (bf16[960,256]{1,0:T(8,128)(2,1)S(1)}, bf16[2,640,256]{2,1,0:T(8,128)(2,1)S(1)}, bf16[2,640,256]{2,1,0:T(8,128)(2,1)S(1)}) custom-call(s32[4]{0:T(128)S(1)} %and_convert_fusion.refs_0_.visible_ref, bf16[960,256]{1,0:T(8,128)(2,1)S(1)} %copy-done.18, bf16[960,256]{1,0:T(8,128)(2,1)S(1)} %get-tuple-element.210.do_ref, ...), custom_call_target="tpu_custom_call" | custom-call | flops 5033164800 | bytes 4915200 | tf_op jit(solution)/shard_map/attend_back/pallas_call | solution.py:624
  219.7 9.5 %collective-permute-done.36 = bf16[2,240,640]{2,1,0:T(8,128)(2,1)S(1)} collective-permute-done((bf16[2,240,640]{2,1,0:T(8,128)(2,1)S(1)}, bf16[2,240,640]{2,1,0:T(8,128)(2,1)S(1)}, u32[]{:S(2)}, u32[]{:S(2)}) %collective-permute-start.36) | collective-permute-done | bytes 614432 | tf_op jit(solution)/shard_map/ppermute | solution.py:964
  231.6 9.3 %collective-permute-start.41 = (bf16[2,240,640]{2,1,0:T(8,128)(2,1)S(1)}, bf16[2,240,640]{2,1,0:T(8,128)(2,1)S(1)}, u32[]{:S(2)}, u32[]{:S(2)}) collective-permute-start(bf16[2,240,640]{2,1,0:T(8,128)(2,1)S(1)} %fusion.2), channel_id=1, source_target_pairs={{0,4},{4,0},{8,12},{12,8},{16,20},{20,16},{24,28},{28,24},{1,5},{5... | collective-permute-start | bytes 1843208 | tf_op jit(solution)/shard_map/ppermute | solution.py:964
  241.1 4.6 %collective-permute-done.38 = bf16[2,240,640]{2,1,0:T(8,128)(2,1)S(1)} collective-permute-done((bf16[2,240,640]{2,1,0:T(8,128)(2,1)S(1)}, bf16[2,240,640]{2,1,0:T(8,128)(2,1)S(1)}, u32[]{:S(2)}, u32[]{:S(2)}) %collective-permute-start.38) | collective-permute-done | bytes 614432 | tf_op jit(solution)/shard_map/ppermute | solution.py:964
  246.5 8.8 %collective-permute-done.40.refs_5_ = bf16[640,256]{1,0:T(8,128)(2,1)S(1)} collective-permute-done((bf16[640,256]{1,0:T(8,128)(2,1)S(1)}, bf16[640,256]{1,0:T(8,128)(2,1)S(1)}, u32[]{:S(2)}, u32[]{:S(2)}) %collective-permute-start.40) | collective-permute-done | bytes 327712 | tf_op jit(solution)/shard_map/ppermute | solution.py:964
  256.9 6.4 %collective-permute-start.44 = (bf16[240,640]{1,0:T(8,128)(2,1)S(1)}, bf16[240,640]{1,0:T(8,128)(2,1)S(1)}, u32[]{:S(2)}, u32[]{:S(2)}) collective-permute-start(bf16[240,640]{1,0:T(8,128)(2,1)S(1)} %fusion.23), channel_id=1, source_target_pairs={{0,16},{4,20},{8,24},{12,28},{16,0},{20,4},{24,8},{28,12},{1,17},{... | collective-permute-start | bytes 921608 | tf_op jit(solution)/shard_map/ppermute | solution.py:964
  263.3 8.1 %collective-permute-start.45 = (bf16[240,640]{1,0:T(8,128)(2,1)S(1)}, bf16[240,640]{1,0:T(8,128)(2,1)S(1)}, u32[]{:S(2)}, u32[]{:S(2)}) collective-permute-start(bf16[240,640]{1,0:T(8,128)(2,1)S(1)} %fusion.20), channel_id=1, source_target_pairs={{0,8},{4,12},{8,0},{12,4},{16,24},{20,28},{24,16},{28,20},{1,9},{5... | collective-permute-start | bytes 921608 | tf_op jit(solution)/shard_map/ppermute | solution.py:964
  271.5 6.4 %leave_mixed.1 = (bf16[960,256]{1,0:T(8,128)(2,1)}, bf16[2,4,256,640]{3,2,1,0:T(8,128)(2,1)S(1)}, bf16[2,4,256,640]{3,2,1,0:T(8,128)(2,1)S(1)}) custom-call(s32[3]{0:T(128)S(1)} %pad_add_fusion.1.place_ref.refs_0_, f32[256,960]{1,0:T(8,128)S(1)} %copy-done.5, f32[256,960]{1,0:T(8,128)S(1)} %get-tuple-element.230.refs_2_, ...), custom_call_target="tpu_custom_call" | custom-call | flops 2453667840 | bytes 6635520 | tf_op jit(solution)/shard_map/leave_mixed/pallas_call | solution.py:795
  279.2 4.5 %collective-permute-start.47 = (bf16[2,240,640]{2,1,0:T(8,128)(2,1)S(1)}, bf16[2,240,640]{2,1,0:T(8,128)(2,1)S(1)}, u32[]{:S(2)}, u32[]{:S(2)}) collective-permute-start(bf16[2,240,640]{2,1,0:T(8,128)(2,1)S(1)} %fusion.1), channel_id=1, source_target_pairs={{0,4},{4,0},{8,12},{12,8},{16,20},{20,16},{24,28},{28,24},{1,5},{5... | collective-permute-start | bytes 1843208 | tf_op jit(solution)/shard_map/ppermute | solution.py:964
  286.6 3.3 collective-permute-start.50
  290.0 5.3 %collective-permute-done.48 = bf16[2,240,640]{2,1,0:T(8,128)(2,1)S(1)} collective-permute-done((bf16[2,240,640]{2,1,0:T(8,128)(2,1)S(1)}, bf16[2,240,640]{2,1,0:T(8,128)(2,1)S(1)}, u32[]{:S(2)}, u32[]{:S(2)}) %collective-permute-start.48) | collective-permute-done | bytes 614432 | tf_op jit(solution)/shard_map/ppermute | solution.py:964
  295.3 3.0 collective-permute-done.47
  304.9 6.1 %collective-permute-done.51.p3_ref = bf16[240,640]{1,0:T(8,128)(2,1)S(1)} collective-permute-done((bf16[240,640]{1,0:T(8,128)(2,1)S(1)}, bf16[240,640]{1,0:T(8,128)(2,1)S(1)}, u32[]{:S(2)}, u32[]{:S(2)}) %collective-permute-start.51) | collective-permute-done | bytes 307232 | tf_op jit(solution)/shard_map/ppermute | solution.py:964
  311.0 2.5 finish.3
  317.8 8.0 %collective-permute-done.55 = bf16[240,640]{1,0:T(8,128)(2,1)S(1)} collective-permute-done((bf16[240,640]{1,0:T(8,128)(2,1)S(1)}, bf16[240,640]{1,0:T(8,128)(2,1)S(1)}, u32[]{:S(2)}, u32[]{:S(2)}) %collective-permute-start.55) | collective-permute-done | bytes 307232 | tf_op jit(solution)/shard_map/ppermute | solution.py:964
  327.5 2.6 collective-permute-done.53
  332.9 4.7 %collective-permute-done.57.p1_ref = bf16[240,640]{1,0:T(8,128)(2,1)S(1)} collective-permute-done((bf16[240,640]{1,0:T(8,128)(2,1)S(1)}, bf16[240,640]{1,0:T(8,128)(2,1)S(1)}, u32[]{:S(2)}, u32[]{:S(2)}) %collective-permute-start.57) | collective-permute-done | bytes 307232 | tf_op jit(solution)/shard_map/ppermute | solution.py:964
  340.6 5.4 %collective-permute-done.59 = bf16[256,640]{1,0:T(8,128)(2,1)S(1)} collective-permute-done((bf16[256,640]{1,0:T(8,128)(2,1)S(1)}, bf16[256,640]{1,0:T(8,128)(2,1)S(1)}, u32[]{:S(2)}, u32[]{:S(2)}) %collective-permute-start.59) | collective-permute-done | bytes 327712 | tf_op jit(solution)/shard_map/ppermute | solution.py:964
  349.5 2.5 finish.4
  352.0 3.6 collective-permute-done.62.p1_ref
  357.2 5.9 %collective-permute-done.64.p3_ref = bf16[240,640]{1,0:T(8,128)(2,1)S(1)} collective-permute-done((bf16[240,640]{1,0:T(8,128)(2,1)S(1)}, bf16[240,640]{1,0:T(8,128)(2,1)S(1)}, u32[]{:S(2)}, u32[]{:S(2)}) %collective-permute-start.64) | collective-permute-done | bytes 307232 | tf_op jit(solution)/shard_map/ppermute | solution.py:964
  363.1 2.5 finish.5
  367.6 5.3 %collective-permute-done.66.p1_ref = bf16[256,640]{1,0:T(8,128)(2,1)S(1)} collective-permute-done((bf16[256,640]{1,0:T(8,128)(2,1)S(1)}, bf16[256,640]{1,0:T(8,128)(2,1)S(1)}, u32[]{:S(2)}, u32[]{:S(2)}) %collective-permute-start.66) | collective-permute-done | bytes 327712 | tf_op jit(solution)/shard_map/ppermute | solution.py:964
  374.6 5.4 %collective-permute-done.68.p3_ref = bf16[256,640]{1,0:T(8,128)(2,1)S(1)} collective-permute-done((bf16[256,640]{1,0:T(8,128)(2,1)S(1)}, bf16[256,640]{1,0:T(8,128)(2,1)S(1)}, u32[]{:S(2)}, u32[]{:S(2)}) %collective-permute-start.68) | collective-permute-done | bytes 327712 | tf_op jit(solution)/shard_map/ppermute | solution.py:964
  380.1 2.6 finish_mixed.1
  (256 shorter events, 81.5 us)
Async XLA Ops:
  2.0 9.8 %collective-permute-start = (bf16[2,240]{1,0:T(2,128)(2,1)S(1)}, bf16[2,240]{1,0:T(2,128)(2,1)S(1)}, u32[]{:S(2)}, u32[]{:S(2)}) collective-permute-start(bf16[2,240]{1,0:T(2,128)(2,1)S(1)} %pad_maximum_fusion), channel_id=1, source_target_pairs={{0,1},{1,0},{2,3},{3,2},{4,5},{5,4},{6,7},{7,6},{8,9},{9,8},{10,11... | collective-permute-start | bytes 2888 | tf_op jit(solution)/shard_map/ppermute | solution.py:964
  9.2 49.4 %collective-permute-start.3 = (bf16[240,2560]{1,0:T(8,128)(2,1)}, bf16[240,2560]{1,0:T(8,128)(2,1)}, u32[]{:S(2)}, u32[]{:S(2)}) collective-permute-start(bf16[240,2560]{1,0:T(8,128)(2,1)} %get-tuple-element.157.refs_0_), channel_id=1, source_target_pairs={{0,1},{1,0},{2,3},{3,2},{4,5},{5,4},{6,7},{7,6},{8,9},{9,8},{10,11... | collective-permute-start | bytes 3686408 | tf_op jit(solution)/shard_map/ppermute | solution.py:964
  11.8 16.4 %collective-permute-start.4 = (bf16[240,1280]{1,0:T(8,128)(2,1)}, bf16[240,1280]{1,0:T(8,128)(2,1)S(1)}, u32[]{:S(2)}, u32[]{:S(2)}) collective-permute-start(bf16[240,1280]{1,0:T(8,128)(2,1)} %get-tuple-element.151), channel_id=1, source_target_pairs={{0,2},{1,3},{2,0},{3,1},{4,6},{5,7},{6,4},{7,5},{8,10},{9,11},{10,... | collective-permute-start | bytes 1843208 | tf_op jit(solution)/shard_map/ppermute | solution.py:964
  28.2 15.3 %collective-permute-start.5 = (bf16[240,1280]{1,0:T(8,128)(2,1)S(1)}, bf16[240,1280]{1,0:T(8,128)(2,1)S(1)}, u32[]{:S(2)}, u32[]{:S(2)}) collective-permute-start(bf16[240,1280]{1,0:T(8,128)(2,1)S(1)} %collective-permute-done.4.refs_2_), channel_id=1, source_target_pairs={{0,4},{4,0},{8,12},{12,8},{16,20},{20,16},{24,28},{28,24},{1,5},{5... | collective-permute-start | bytes 1843208 | tf_op jit(solution)/shard_map/ppermute | solution.py:964
  29.9 17.0 %collective-permute-start.13 = (bf16[240,1280]{1,0:T(8,128)(2,1)}, bf16[240,1280]{1,0:T(8,128)(2,1)S(1)}, u32[]{:S(2)}, u32[]{:S(2)}) collective-permute-start(bf16[240,1280]{1,0:T(8,128)(2,1)} %get-tuple-element.152), channel_id=1, source_target_pairs={{0,2},{1,3},{2,0},{3,1},{4,6},{5,7},{6,4},{7,5},{8,10},{9,11},{10,... | collective-permute-start | bytes 1843208 | tf_op jit(solution)/shard_map/ppermute | solution.py:964
  31.4 26.7 %collective-permute-start.12 = (bf16[240,1280]{1,0:T(8,128)(2,1)}, bf16[240,1280]{1,0:T(8,128)(2,1)S(1)}, u32[]{:S(2)}, u32[]{:S(2)}) collective-permute-start(bf16[240,1280]{1,0:T(8,128)(2,1)} %get-tuple-element.153), channel_id=1, source_target_pairs={{0,2},{1,3},{2,0},{3,1},{4,6},{5,7},{6,4},{7,5},{8,10},{9,11},{10,... | collective-permute-start | bytes 1843208 | tf_op jit(solution)/shard_map/ppermute | solution.py:964
  32.0 28.2 %collective-permute-start.6 = (bf16[240,1280]{1,0:T(8,128)(2,1)S(1)}, bf16[240,1280]{1,0:T(8,128)(2,1)S(1)}, u32[]{:S(2)}, u32[]{:S(2)}) collective-permute-start(bf16[240,1280]{1,0:T(8,128)(2,1)S(1)} %collective-permute-done.4.refs_2_), channel_id=1, source_target_pairs={{0,1},{1,0},{2,3},{3,2},{4,5},{5,4},{6,7},{7,6},{8,9},{9,8},{10,11... | collective-permute-start | bytes 1843208 | tf_op jit(solution)/shard_map/ppermute | solution.py:964
  43.5 16.6 %collective-permute-start.7 = (bf16[240,1280]{1,0:T(8,128)(2,1)S(1)}, bf16[240,1280]{1,0:T(8,128)(2,1)S(1)}, u32[]{:S(2)}, u32[]{:S(2)}) collective-permute-start(bf16[240,1280]{1,0:T(8,128)(2,1)S(1)} %collective-permute-done.5.refs_3_), channel_id=1, source_target_pairs={{0,1},{1,0},{2,3},{3,2},{4,5},{5,4},{6,7},{7,6},{8,9},{9,8},{10,11... | collective-permute-start | bytes 1843208 | tf_op jit(solution)/shard_map/ppermute | solution.py:964
  46.9 27.1 %collective-permute-start.21 = (bf16[960,640]{1,0:T(8,128)(2,1)}, bf16[960,640]{1,0:T(8,128)(2,1)S(1)}, u32[]{:S(2)}, u32[]{:S(2)}) collective-permute-start(bf16[960,640]{1,0:T(8,128)(2,1)} %bitcast.133), channel_id=1, source_target_pairs={{0,1},{1,0},{2,3},{3,2},{4,5},{5,4},{6,7},{7,6},{8,9},{9,8},{10,11... | collective-permute-start | bytes 3686408 | tf_op jit(solution)/shard_map/ppermute | solution.py:964
  58.1 13.9 %collective-permute-start.14 = (bf16[240,1280]{1,0:T(8,128)(2,1)S(1)}, bf16[240,1280]{1,0:T(8,128)(2,1)S(1)}, u32[]{:S(2)}, u32[]{:S(2)}) collective-permute-start(bf16[240,1280]{1,0:T(8,128)(2,1)S(1)} %collective-permute-done.13.refs_12_), channel_id=1, source_target_pairs={{0,4},{4,0},{8,12},{12,8},{16,20},{20,16},{24,28},{28,24},{1,5},{5... | collective-permute-start | bytes 1843208 | tf_op jit(solution)/shard_map/ppermute | solution.py:964
  58.6 14.0 %collective-permute-start.22 = (bf16[480,640]{1,0:T(8,128)(2,1)}, bf16[480,640]{1,0:T(8,128)(2,1)S(1)}, u32[]{:S(2)}, u32[]{:S(2)}) collective-permute-start(bf16[480,640]{1,0:T(8,128)(2,1)} %slice_select_fusion), channel_id=1, source_target_pairs={{0,2},{1,3},{2,0},{3,1},{4,6},{5,7},{6,4},{7,5},{8,10},{9,11},{10,... | collective-permute-start | bytes 1843208 | tf_op jit(solution)/shard_map/ppermute | solution.py:964
  60.1 15.5 %collective-permute-start.11 = (bf16[240,2560]{1,0:T(8,128)(2,1)S(1)}, bf16[240,2560]{1,0:T(8,128)(2,1)S(1)}, u32[]{:S(2)}, u32[]{:S(2)}) collective-permute-start(bf16[240,2560]{1,0:T(8,128)(2,1)S(1)} %copy-done.2), channel_id=1, source_target_pairs={{0,1},{1,0},{2,3},{3,2},{4,5},{5,4},{6,7},{7,6},{8,9},{9,8},{10,11... | collective-permute-start | bytes 3686408 | tf_op jit(solution)/shard_map/ppermute | solution.py:964
  60.2 17.0 %collective-permute-start.17 = (bf16[240,2560]{1,0:T(8,128)(2,1)S(1)}, bf16[240,2560]{1,0:T(8,128)(2,1)S(1)}, u32[]{:S(2)}, u32[]{:S(2)}) collective-permute-start(bf16[240,2560]{1,0:T(8,128)(2,1)S(1)} %copy-done.3), channel_id=1, source_target_pairs={{0,1},{1,0},{2,3},{3,2},{4,5},{5,4},{6,7},{7,6},{8,9},{9,8},{10,11... | collective-permute-start | bytes 3686408 | tf_op jit(solution)/shard_map/ppermute | solution.py:964
  72.7 12.9 %collective-permute-start.23 = (bf16[480,640]{1,0:T(8,128)(2,1)S(1)}, bf16[480,640]{1,0:T(8,128)(2,1)S(1)}, u32[]{:S(2)}, u32[]{:S(2)}) collective-permute-start(bf16[480,640]{1,0:T(8,128)(2,1)S(1)} %collective-permute-done.22.refs_24_), channel_id=1, source_target_pairs={{0,4},{4,0},{8,12},{12,8},{16,20},{20,16},{24,28},{28,24},{1,5},{5... | collective-permute-start | bytes 1843208 | tf_op jit(solution)/shard_map/ppermute | solution.py:964
  74.0 12.2 %collective-permute-start.15 = (bf16[240,1280]{1,0:T(8,128)(2,1)S(1)}, bf16[240,1280]{1,0:T(8,128)(2,1)S(1)}, u32[]{:S(2)}, u32[]{:S(2)}) collective-permute-start(bf16[240,1280]{1,0:T(8,128)(2,1)S(1)} %collective-permute-done.13.refs_12_), channel_id=1, source_target_pairs={{0,1},{1,0},{2,3},{3,2},{4,5},{5,4},{6,7},{7,6},{8,9},{9,8},{10,11... | collective-permute-start | bytes 1843208 | tf_op jit(solution)/shard_map/ppermute | solution.py:964
  74.0 16.3 %collective-permute-start.18 = (bf16[240,1280]{1,0:T(8,128)(2,1)S(1)}, bf16[240,1280]{1,0:T(8,128)(2,1)S(1)}, u32[]{:S(2)}, u32[]{:S(2)}) collective-permute-start(bf16[240,1280]{1,0:T(8,128)(2,1)S(1)} %collective-permute-done.12.refs_18_), channel_id=1, source_target_pairs={{0,8},{4,12},{8,0},{12,4},{16,24},{20,28},{24,16},{28,20},{1,9},{5... | collective-permute-start | bytes 1843208 | tf_op jit(solution)/shard_map/ppermute | solution.py:964
  75.6 9.9 %collective-permute-start.9 = (bf16[640,256]{1,0:T(8,128)(2,1)S(1)}, bf16[640,256]{1,0:T(8,128)(2,1)S(1)}, u32[]{:S(2)}, u32[]{:S(2)}) collective-permute-start(bf16[640,256]{1,0:T(8,128)(2,1)S(1)} %get-tuple-element.162.refs_4_.kv0_ref), channel_id=1, source_target_pairs={{0,2},{1,3},{2,0},{3,1},{4,6},{5,7},{6,4},{7,5},{8,10},{9,11},{10,... | collective-permute-start | bytes 983048 | tf_op jit(solution)/shard_map/ppermute | solution.py:964
  107.5 9.8 %collective-permute-start.27 = (bf16[640,256]{1,0:T(8,128)(2,1)S(1)}, bf16[640,256]{1,0:T(8,128)(2,1)S(1)}, u32[]{:S(2)}, u32[]{:S(2)}) collective-permute-start(bf16[640,256]{1,0:T(8,128)(2,1)S(1)} %get-tuple-element.172.refs_4_.kv0_ref), channel_id=1, source_target_pairs={{0,2},{1,3},{2,0},{3,1},{4,6},{5,7},{6,4},{7,5},{8,10},{9,11},{10,... | collective-permute-start | bytes 983048 | tf_op jit(solution)/shard_map/ppermute | solution.py:964
  145.1 10.1 %collective-permute-start.30 = (bf16[640,256]{1,0:T(8,128)(2,1)}, bf16[640,256]{1,0:T(8,128)(2,1)}, u32[]{:S(2)}, u32[]{:S(2)}) collective-permute-start(bf16[640,256]{1,0:T(8,128)(2,1)} %get-tuple-element.295), channel_id=1, source_target_pairs={{0,2},{1,3},{2,0},{3,1},{4,6},{5,7},{6,4},{7,5},{8,10},{9,11},{10,... | collective-permute-start | bytes 983048 | tf_op jit(solution)/shard_map/ppermute | solution.py:964
  170.7 18.7 %collective-permute-start.32 = (bf16[2,240,640]{2,1,0:T(8,128)(2,1)S(1)}, bf16[2,240,640]{2,1,0:T(8,128)(2,1)S(1)}, u32[]{:S(2)}, u32[]{:S(2)}) collective-permute-start(bf16[2,240,640]{2,1,0:T(8,128)(2,1)S(1)} %get-tuple-element.292), channel_id=1, source_target_pairs={{0,2},{1,3},{2,0},{3,1},{4,6},{5,7},{6,4},{7,5},{8,10},{9,11},{10,... | collective-permute-start | bytes 1843208 | tf_op jit(solution)/shard_map/ppermute | solution.py:964
  189.9 25.4 %collective-permute-start.34 = (bf16[2,240,640]{2,1,0:T(8,128)(2,1)S(1)}, bf16[2,240,640]{2,1,0:T(8,128)(2,1)S(1)}, u32[]{:S(2)}, u32[]{:S(2)}) collective-permute-start(bf16[2,240,640]{2,1,0:T(8,128)(2,1)S(1)} %get-tuple-element.291), channel_id=1, source_target_pairs={{0,2},{1,3},{2,0},{3,1},{4,6},{5,7},{6,4},{7,5},{8,10},{9,11},{10,... | collective-permute-start | bytes 1843208 | tf_op jit(solution)/shard_map/ppermute | solution.py:964
  194.8 24.6 %collective-permute-start.35 = (bf16[2,240,640]{2,1,0:T(8,128)(2,1)S(1)}, bf16[2,240,640]{2,1,0:T(8,128)(2,1)S(1)}, u32[]{:S(2)}, u32[]{:S(2)}) collective-permute-start(bf16[2,240,640]{2,1,0:T(8,128)(2,1)S(1)} %get-tuple-element.290), channel_id=1, source_target_pairs={{0,2},{1,3},{2,0},{3,1},{4,6},{5,7},{6,4},{7,5},{8,10},{9,11},{10,... | collective-permute-start | bytes 1843208 | tf_op jit(solution)/shard_map/ppermute | solution.py:964
  196.3 32.8 %collective-permute-start.36 = (bf16[2,240,640]{2,1,0:T(8,128)(2,1)S(1)}, bf16[2,240,640]{2,1,0:T(8,128)(2,1)S(1)}, u32[]{:S(2)}, u32[]{:S(2)}) collective-permute-start(bf16[2,240,640]{2,1,0:T(8,128)(2,1)S(1)} %fusion.3), channel_id=1, source_target_pairs={{0,4},{4,0},{8,12},{12,8},{16,20},{20,16},{24,28},{28,24},{1,5},{5... | collective-permute-start | bytes 1843208 | tf_op jit(solution)/shard_map/ppermute | solution.py:964
  215.3 40.1 %collective-permute-start.42 = (bf16[2,4,240,640]{3,2,1,0:T(8,128)(2,1)S(1)}, bf16[2,4,240,640]{3,2,1,0:T(8,128)(2,1)S(1)}, u32[]{:S(2)}, u32[]{:S(2)}) collective-permute-start(bf16[2,4,240,640]{3,2,1,0:T(8,128)(2,1)S(1)} %get-tuple-element.228), channel_id=1, source_target_pairs={{0,1},{1,0},{2,3},{3,2},{4,5},{5,4},{6,7},{7,6},{8,9},{9,8},{10,11... | collective-permute-start | bytes 7372808 | tf_op jit(solution)/shard_map/ppermute | solution.py:964
  229.3 11.5 %collective-permute-start.37 = (bf16[2,640,256]{2,1,0:T(8,128)(2,1)S(1)}, bf16[2,640,256]{2,1,0:T(8,128)(2,1)S(1)}, u32[]{:S(2)}, u32[]{:S(2)}) collective-permute-start(bf16[2,640,256]{2,1,0:T(8,128)(2,1)S(1)} %get-tuple-element.220), channel_id=1, source_target_pairs={{0,1},{1,0},{2,3},{3,2},{4,5},{5,4},{6,7},{7,6},{8,9},{9,8},{10,11... | collective-permute-start | bytes 1966088 | tf_op jit(solution)/shard_map/ppermute | solution.py:964
  229.4 16.3 %collective-permute-start.38 = (bf16[2,240,640]{2,1,0:T(8,128)(2,1)S(1)}, bf16[2,240,640]{2,1,0:T(8,128)(2,1)S(1)}, u32[]{:S(2)}, u32[]{:S(2)}) collective-permute-start(bf16[2,240,640]{2,1,0:T(8,128)(2,1)S(1)} %get-tuple-element.289), channel_id=1, source_target_pairs={{0,2},{1,3},{2,0},{3,1},{4,6},{5,7},{6,4},{7,5},{8,10},{9,11},{10,... | collective-permute-start | bytes 1843208 | tf_op jit(solution)/shard_map/ppermute | solution.py:964
  230.0 15.7 %collective-permute-start.39 = (bf16[240,640]{1,0:T(8,128)(2,1)S(1)}, bf16[240,640]{1,0:T(8,128)(2,1)S(1)}, u32[]{:S(2)}, u32[]{:S(2)}) collective-permute-start(bf16[240,640]{1,0:T(8,128)(2,1)S(1)} %fusion.21), channel_id=1, source_target_pairs={{0,8},{4,12},{8,0},{12,4},{16,24},{20,28},{24,16},{28,20},{1,9},{5... | collective-permute-start | bytes 921608 | tf_op jit(solution)/shard_map/ppermute | solution.py:964
  231.6 23.6 %collective-permute-start.41 = (bf16[2,240,640]{2,1,0:T(8,128)(2,1)S(1)}, bf16[2,240,640]{2,1,0:T(8,128)(2,1)S(1)}, u32[]{:S(2)}, u32[]{:S(2)}) collective-permute-start(bf16[2,240,640]{2,1,0:T(8,128)(2,1)S(1)} %fusion.2), channel_id=1, source_target_pairs={{0,4},{4,0},{8,12},{12,8},{16,20},{20,16},{24,28},{28,24},{1,5},{5... | collective-permute-start | bytes 1843208 | tf_op jit(solution)/shard_map/ppermute | solution.py:964
  255.8 22.1 %collective-permute-start.43 = (bf16[2,240,640]{2,1,0:T(8,128)(2,1)S(1)}, bf16[2,240,640]{2,1,0:T(8,128)(2,1)S(1)}, u32[]{:S(2)}, u32[]{:S(2)}) collective-permute-start(bf16[2,240,640]{2,1,0:T(8,128)(2,1)S(1)} %get-tuple-element.288), channel_id=1, source_target_pairs={{0,2},{1,3},{2,0},{3,1},{4,6},{5,7},{6,4},{7,5},{8,10},{9,11},{10,... | collective-permute-start | bytes 1843208 | tf_op jit(solution)/shard_map/ppermute | solution.py:964
  256.9 21.3 %collective-permute-start.44 = (bf16[240,640]{1,0:T(8,128)(2,1)S(1)}, bf16[240,640]{1,0:T(8,128)(2,1)S(1)}, u32[]{:S(2)}, u32[]{:S(2)}) collective-permute-start(bf16[240,640]{1,0:T(8,128)(2,1)S(1)} %fusion.23), channel_id=1, source_target_pairs={{0,16},{4,20},{8,24},{12,28},{16,0},{20,4},{24,8},{28,12},{1,17},{... | collective-permute-start | bytes 921608 | tf_op jit(solution)/shard_map/ppermute | solution.py:964
  263.3 15.0 %collective-permute-start.45 = (bf16[240,640]{1,0:T(8,128)(2,1)S(1)}, bf16[240,640]{1,0:T(8,128)(2,1)S(1)}, u32[]{:S(2)}, u32[]{:S(2)}) collective-permute-start(bf16[240,640]{1,0:T(8,128)(2,1)S(1)} %fusion.20), channel_id=1, source_target_pairs={{0,8},{4,12},{8,0},{12,4},{16,24},{20,28},{24,16},{28,20},{1,9},{5... | collective-permute-start | bytes 921608 | tf_op jit(solution)/shard_map/ppermute | solution.py:964
  278.6 16.7 %collective-permute-start.48 = (bf16[2,240,640]{2,1,0:T(8,128)(2,1)S(1)}, bf16[2,240,640]{2,1,0:T(8,128)(2,1)S(1)}, u32[]{:S(2)}, u32[]{:S(2)}) collective-permute-start(bf16[2,240,640]{2,1,0:T(8,128)(2,1)S(1)} %get-tuple-element.287), channel_id=1, source_target_pairs={{0,2},{1,3},{2,0},{3,1},{4,6},{5,7},{6,4},{7,5},{8,10},{9,11},{10,... | collective-permute-start | bytes 1843208 | tf_op jit(solution)/shard_map/ppermute | solution.py:964
  279.2 19.1 %collective-permute-start.47 = (bf16[2,240,640]{2,1,0:T(8,128)(2,1)S(1)}, bf16[2,240,640]{2,1,0:T(8,128)(2,1)S(1)}, u32[]{:S(2)}, u32[]{:S(2)}) collective-permute-start(bf16[2,240,640]{2,1,0:T(8,128)(2,1)S(1)} %fusion.1), channel_id=1, source_target_pairs={{0,4},{4,0},{8,12},{12,8},{16,20},{20,16},{24,28},{28,24},{1,5},{5... | collective-permute-start | bytes 1843208 | tf_op jit(solution)/shard_map/ppermute | solution.py:964
  284.0 29.5 %collective-permute-start.52 = (bf16[2,256,640]{2,1,0:T(8,128)(2,1)S(1)}, bf16[2,256,640]{2,1,0:T(8,128)(2,1)S(1)}, u32[]{:S(2)}, u32[]{:S(2)}) collective-permute-start(bf16[2,256,640]{2,1,0:T(8,128)(2,1)S(1)} %get-tuple-element.286), channel_id=1, source_target_pairs={{0,2},{1,3},{2,0},{3,1},{4,6},{5,7},{6,4},{7,5},{8,10},{9,11},{10,... | collective-permute-start | bytes 1966088 | tf_op jit(solution)/shard_map/ppermute | solution.py:964
  285.6 12.9 %collective-permute-start.49 = (bf16[240,640]{1,0:T(8,128)(2,1)S(1)}, bf16[240,640]{1,0:T(8,128)(2,1)S(1)}, u32[]{:S(2)}, u32[]{:S(2)}) collective-permute-start(bf16[240,640]{1,0:T(8,128)(2,1)S(1)} %add_convert_fusion.15.p0_ref), channel_id=1, source_target_pairs={{0,8},{4,12},{8,0},{12,4},{16,24},{20,28},{24,16},{28,20},{1,9},{5... | collective-permute-start | bytes 921608 | tf_op jit(solution)/shard_map/ppermute | solution.py:964
  286.6 18.2 %collective-permute-start.50 = (bf16[240,640]{1,0:T(8,128)(2,1)S(1)}, bf16[240,640]{1,0:T(8,128)(2,1)S(1)}, u32[]{:S(2)}, u32[]{:S(2)}) collective-permute-start(bf16[240,640]{1,0:T(8,128)(2,1)S(1)} %add_convert_fusion.15.p0_ref), channel_id=1, source_target_pairs={{0,4},{4,0},{8,12},{12,8},{16,20},{20,16},{24,28},{28,24},{1,5},{5... | collective-permute-start | bytes 921608 | tf_op jit(solution)/shard_map/ppermute | solution.py:964
  298.5 12.5 %collective-permute-start.51 = (bf16[240,640]{1,0:T(8,128)(2,1)S(1)}, bf16[240,640]{1,0:T(8,128)(2,1)S(1)}, u32[]{:S(2)}, u32[]{:S(2)}) collective-permute-start(bf16[240,640]{1,0:T(8,128)(2,1)S(1)} %collective-permute-done.49.p1_ref), channel_id=1, source_target_pairs={{0,4},{4,0},{8,12},{12,8},{16,20},{20,16},{24,28},{28,24},{1,5},{5... | collective-permute-start | bytes 921608 | tf_op jit(solution)/shard_map/ppermute | solution.py:964
  300.6 16.1 %collective-permute-start.54 = (bf16[240,640]{1,0:T(8,128)(2,1)S(1)}, bf16[240,640]{1,0:T(8,128)(2,1)S(1)}, u32[]{:S(2)}, u32[]{:S(2)}) collective-permute-start(bf16[240,640]{1,0:T(8,128)(2,1)S(1)} %fusion.19), channel_id=1, source_target_pairs={{0,16},{4,20},{8,24},{12,28},{16,0},{20,4},{24,8},{28,12},{1,17},{... | collective-permute-start | bytes 921608 | tf_op jit(solution)/shard_map/ppermute | solution.py:964
  301.8 25.7 %collective-permute-start.56 = (bf16[2,256,640]{2,1,0:T(8,128)(2,1)S(1)}, bf16[2,256,640]{2,1,0:T(8,128)(2,1)S(1)}, u32[]{:S(2)}, u32[]{:S(2)}) collective-permute-start(bf16[2,256,640]{2,1,0:T(8,128)(2,1)S(1)} %get-tuple-element.285), channel_id=1, source_target_pairs={{0,2},{1,3},{2,0},{3,1},{4,6},{5,7},{6,4},{7,5},{8,10},{9,11},{10,... | collective-permute-start | bytes 1966088 | tf_op jit(solution)/shard_map/ppermute | solution.py:964
  313.8 16.4 %collective-permute-start.53 = (bf16[2,256,640]{2,1,0:T(8,128)(2,1)S(1)}, bf16[2,256,640]{2,1,0:T(8,128)(2,1)S(1)}, u32[]{:S(2)}, u32[]{:S(2)}) collective-permute-start(bf16[2,256,640]{2,1,0:T(8,128)(2,1)S(1)} %fusion), channel_id=1, source_target_pairs={{0,4},{4,0},{8,12},{12,8},{16,20},{20,16},{24,28},{28,24},{1,5},{5... | collective-permute-start | bytes 1966088 | tf_op jit(solution)/shard_map/ppermute | solution.py:964
  315.6 10.2 %collective-permute-start.55 = (bf16[240,640]{1,0:T(8,128)(2,1)S(1)}, bf16[240,640]{1,0:T(8,128)(2,1)S(1)}, u32[]{:S(2)}, u32[]{:S(2)}) collective-permute-start(bf16[240,640]{1,0:T(8,128)(2,1)S(1)} %fusion.17), channel_id=1, source_target_pairs={{0,8},{4,12},{8,0},{12,4},{16,24},{20,28},{24,16},{28,20},{1,9},{5... | collective-permute-start | bytes 921608 | tf_op jit(solution)/shard_map/ppermute | solution.py:964
  316.8 20.9 %collective-permute-start.57 = (bf16[240,640]{1,0:T(8,128)(2,1)S(1)}, bf16[240,640]{1,0:T(8,128)(2,1)S(1)}, u32[]{:S(2)}, u32[]{:S(2)}) collective-permute-start(bf16[240,640]{1,0:T(8,128)(2,1)S(1)} %add_convert_fusion.14.p0_ref), channel_id=1, source_target_pairs={{0,8},{4,12},{8,0},{12,4},{16,24},{20,28},{24,16},{28,20},{1,9},{5... | collective-permute-start | bytes 921608 | tf_op jit(solution)/shard_map/ppermute | solution.py:964
  326.0 14.2 %collective-permute-start.58 = (bf16[240,640]{1,0:T(8,128)(2,1)S(1)}, bf16[240,640]{1,0:T(8,128)(2,1)S(1)}, u32[]{:S(2)}, u32[]{:S(2)}) collective-permute-start(bf16[240,640]{1,0:T(8,128)(2,1)S(1)} %fusion.16), channel_id=1, source_target_pairs={{0,16},{4,20},{8,24},{12,28},{16,0},{20,4},{24,8},{28,12},{1,17},{... | collective-permute-start | bytes 921608 | tf_op jit(solution)/shard_map/ppermute | solution.py:964
  330.3 15.7 %collective-permute-start.59 = (bf16[256,640]{1,0:T(8,128)(2,1)S(1)}, bf16[256,640]{1,0:T(8,128)(2,1)S(1)}, u32[]{:S(2)}, u32[]{:S(2)}) collective-permute-start(bf16[256,640]{1,0:T(8,128)(2,1)S(1)} %fusion.6), channel_id=1, source_target_pairs={{0,8},{4,12},{8,0},{12,4},{16,24},{20,28},{24,16},{28,20},{1,9},{5... | collective-permute-start | bytes 983048 | tf_op jit(solution)/shard_map/ppermute | solution.py:964
  331.5 18.0 %collective-permute-start.60 = (bf16[240,640]{1,0:T(8,128)(2,1)S(1)}, bf16[240,640]{1,0:T(8,128)(2,1)S(1)}, u32[]{:S(2)}, u32[]{:S(2)}) collective-permute-start(bf16[240,640]{1,0:T(8,128)(2,1)S(1)} %add_convert_fusion.14.p0_ref), channel_id=1, source_target_pairs={{0,4},{4,0},{8,12},{12,8},{16,20},{20,16},{24,28},{28,24},{1,5},{5... | collective-permute-start | bytes 921608 | tf_op jit(solution)/shard_map/ppermute | solution.py:964
  337.7 11.8 %collective-permute-start.61 = (bf16[240,640]{1,0:T(8,128)(2,1)S(1)}, bf16[240,640]{1,0:T(8,128)(2,1)S(1)}, u32[]{:S(2)}, u32[]{:S(2)}) collective-permute-start(bf16[240,640]{1,0:T(8,128)(2,1)S(1)} %collective-permute-done.57.p1_ref), channel_id=1, source_target_pairs={{0,4},{4,0},{8,12},{12,8},{16,20},{20,16},{24,28},{28,24},{1,5},{5... | collective-permute-start | bytes 921608 | tf_op jit(solution)/shard_map/ppermute | solution.py:964
  340.3 15.3 %collective-permute-start.62 = (bf16[240,640]{1,0:T(8,128)(2,1)S(1)}, bf16[240,640]{1,0:T(8,128)(2,1)S(1)}, u32[]{:S(2)}, u32[]{:S(2)}) collective-permute-start(bf16[240,640]{1,0:T(8,128)(2,1)S(1)} %add_convert_fusion.13.p0_ref), channel_id=1, source_target_pairs={{0,8},{4,12},{8,0},{12,4},{16,24},{20,28},{24,16},{28,20},{1,9},{5... | collective-permute-start | bytes 921608 | tf_op jit(solution)/shard_map/ppermute | solution.py:964
  346.2 19.4 %collective-permute-start.65 = (bf16[256,640]{1,0:T(8,128)(2,1)S(1)}, bf16[256,640]{1,0:T(8,128)(2,1)S(1)}, u32[]{:S(2)}, u32[]{:S(2)}) collective-permute-start(bf16[256,640]{1,0:T(8,128)(2,1)S(1)} %fusion.8), channel_id=1, source_target_pairs={{0,16},{4,20},{8,24},{12,28},{16,0},{20,4},{24,8},{28,12},{1,17},{... | collective-permute-start | bytes 983048 | tf_op jit(solution)/shard_map/ppermute | solution.py:964
  (74 other events, 1006.1 us)
